TPU v7x, 128 devices: a whole 4x4x4 slice. The times are simulated.
128 devices in a mesh: row: 8 (over z_hi, y), col: 16 (over z_lo, x, core).
Axes of the slice: x: 4, y: 4, z: 4 (z_hi: 2, z_lo: 2; z = z_hi * 2 + z_lo), core: 2. Of those that a mesh axis runs over, the one named last changes fastest.
Arguments:
- query_vectors: bfloat16 [32, 1536, 128], P('row', 'col'), may hold values from -6.5 to 6.5
- key_vectors: bfloat16 [32, 1536, 128], P('row', 'col'), may hold values from -6.5 to 6.5
- value_vectors: bfloat16 [32, 1536, 128], P('row', 'col'), may hold values from -6 to 6
- gate_logits: bfloat16 [32, 1536, 128], P('row', 'col'), may hold values from -6 to 6
- pair_bias: bfloat16 [4, 1536, 1536], P(None, 'col'), may hold values from -6 to 6
- pair_mask: int32 [32, 1536], P('row', 'col'), may hold values 0 or 1
- output_weight: bfloat16 [128, 128], replicated, may hold values from -0.5 to 0.5
- output_cotangent: bfloat16 [32, 128, 1536], P('row', 'col'), may hold values from -48 to 48
Outputs:
- query_gradient: bfloat16 [32, 1536, 128], P('row', 'col')
- key_gradient: bfloat16 [32, 1536, 128], P('row', 'col')
- value_gradient: bfloat16 [32, 1536, 128], P('row', 'col')
- gate_gradient: bfloat16 [32, 1536, 128], P('row', 'col')
- bias_gradient: float32 [4, 1536, 1536], P(None, 'col', 'row')
All inputs are finite; a program needn't handle non-finite values. No bound on the sum of `pair_mask` on one device may be relied on, other than what follows from the above.
Results may differ from a plain program's by a relative error of at most 0.025.
Values may be sent and summed in bfloat16 or wider, within the bound.
No kernel may reach another device: no remote copies, remote signals or barrier semaphores. Data moves between devices by JAX's collectives and lax.ppermute only.
A program may use at most 64 MiB of HBM per device.

v0:
```python
import math

import jax
import jax.numpy as jnp
from jax import lax
from jax.sharding import PartitionSpec as P

HEADS = 4


NEG_FILL = -1000000000.0
START_MAX = -1e30


def shortened(x):

    def short(part):
        return part.astype(jnp.bfloat16) if part.dtype == jnp.float32 else part

    return jax.tree.map(short, x)


def shifted(value, axis, steps):
    count = lax.axis_size(axis)
    pairs = [(source, (source + steps) % count) for source in range(count)]
    return lax.ppermute(value, axis, pairs)


def split_heads(operand):
    return operand.reshape(operand.shape[0], operand.shape[1], HEADS, operand.shape[2] // HEADS)


def block_scores(query_heads, key_heads, mask_part, bias_part, scaling):
    raw_scores = jnp.einsum(
        "jihc,jkhc->jhik", query_heads, key_heads, preferred_element_type=jnp.float32
    )
    scores = raw_scores * scaling + bias_part.astype(jnp.float32)[None]
    return jnp.where(mask_part[:, None, None, :] > 0.5, scores, NEG_FILL)


def forward_visitor(query_heads, bias_rows, scaling):
    block_width = query_heads.shape[1]

    def visit_keys(folded, arrived, first_key):
        key_piece, value_piece, mask_piece = arrived
        key_count = key_piece.shape[1]
        step_width = math.gcd(key_count, block_width)

        def one_block(state, block_index):
            running_max, running_sum, accumulated = state
            block_offset = block_index * step_width
            key_heads = split_heads(
                lax.dynamic_slice_in_dim(key_piece, block_offset, step_width, 1)
            )
            value_heads = split_heads(
                lax.dynamic_slice_in_dim(value_piece, block_offset, step_width, 1)
            )
            mask_part = lax.dynamic_slice_in_dim(mask_piece, block_offset, step_width, 1)
            bias_part = lax.dynamic_slice_in_dim(bias_rows, block_offset, step_width, 2)
            scores = block_scores(query_heads, key_heads, mask_part, bias_part, scaling)
            new_max = jnp.maximum(running_max, jnp.max(scores, axis=-1))
            rescale = jnp.exp(running_max - new_max)
            weights = jnp.exp(scores - new_max[..., None])
            running_sum = running_sum * rescale + jnp.sum(weights, axis=-1)
            weights_high = weights.astype(jnp.bfloat16)
            weights_rest = (weights - weights_high.astype(jnp.float32)).astype(jnp.bfloat16)
            contribution = jnp.einsum(
                "jhik,jkhc->jhic", weights_high, value_heads, preferred_element_type=jnp.float32
            )
            contribution = contribution + jnp.einsum(
                "jhik,jkhc->jhic", weights_rest, value_heads, preferred_element_type=jnp.float32
            )
            accumulated = accumulated * rescale[..., None] + contribution
            return ((new_max, running_sum, accumulated), None)

        result, _ = lax.scan(
            one_block, folded, jnp.arange(key_count // step_width, dtype=jnp.int32)
        )
        return result

    return visit_keys


def backward_block(context, held_block, first_key):
    query_heads, grad_heads, log_total, row_delta, bias_rows, scaling = context
    key_piece, value_piece, mask_piece = held_block
    key_count = key_piece.shape[1]
    key_heads = split_heads(key_piece)
    value_heads = split_heads(value_piece)
    bias_part = lax.dynamic_slice_in_dim(bias_rows, first_key, key_count, 2)
    scores = block_scores(query_heads, key_heads, mask_piece, bias_part, scaling)
    attention = jnp.exp(scores - log_total[..., None])
    attention_grad = jnp.einsum(
        "jihc,jkhc->jhik", grad_heads, value_heads, preferred_element_type=jnp.float32
    )
    score_grad = attention * (attention_grad - row_delta[..., None])
    score_low = score_grad.astype(jnp.bfloat16)
    attention_low = attention.astype(jnp.bfloat16)
    query_part = jnp.einsum(
        "jhik,jkhc->jihc", score_low, key_heads, preferred_element_type=jnp.float32
    )
    key_part = jnp.einsum(
        "jhik,jihc->jkhc", score_low, query_heads, preferred_element_type=jnp.float32
    )
    value_part = jnp.einsum(
        "jhik,jihc->jkhc", attention_low, grad_heads, preferred_element_type=jnp.float32
    )
    tile_shape = key_piece.shape
    return (
        query_part,
        key_part.reshape(tile_shape),
        value_part.reshape(tile_shape),
        jnp.sum(score_grad, axis=0),
    )


def absorb(context, held_block, anchor, query_total, bias_total, grads):
    key_count = held_block[0].shape[1]
    first_key = anchor * key_count
    query_part, key_part, value_part, bias_part = backward_block(context, held_block, first_key)
    current = lax.dynamic_slice_in_dim(bias_total, first_key, key_count, 2)
    bias_total = lax.dynamic_update_slice_in_dim(bias_total, current + bias_part, first_key, 2)
    return (query_total + query_part, bias_total, (grads[0] + key_part, grads[1] + value_part))


def local(
    query_vectors,
    key_vectors,
    value_vectors,
    gate_logits,
    pair_bias,
    pair_mask,
    output_weight,
    output_cotangent,
):
    head_width = query_vectors.shape[2] // HEADS
    scaling = 1.0 / math.sqrt(head_width)
    column_count = lax.axis_size("col")
    column_here = lax.axis_index("col")
    rows_here = query_vectors.shape[0]
    tokens_here = query_vectors.shape[1]
    query_heads = split_heads(query_vectors)
    mask_low = pair_mask.astype(jnp.bfloat16)
    start_state = (
        jnp.full((rows_here, HEADS, tokens_here), START_MAX, jnp.float32),
        jnp.zeros((rows_here, HEADS, tokens_here), jnp.float32),
        jnp.zeros((rows_here, HEADS, tokens_here, head_width), jnp.float32),
    )
    visitor = forward_visitor(query_heads, pair_bias, scaling)
    running_max, running_sum, accumulated = visitor(
        start_state,
        (
            lax.all_gather(key_vectors, "col", axis=1, tiled=True),
            lax.all_gather(value_vectors, "col", axis=1, tiled=True),
            lax.all_gather(mask_low, "col", axis=1, tiled=True),
        ),
        jnp.int32(0),
    )
    log_total = running_max + jnp.log(running_sum)
    attended = jnp.transpose(accumulated / running_sum[..., None], (0, 2, 1, 3)).reshape(
        query_vectors.shape
    )
    regrouped = lax.all_to_all(output_cotangent, "col", split_axis=2, concat_axis=1, tiled=True)
    gated_grad = jnp.einsum(
        "jdi,ed->jie", regrouped, output_weight, preferred_element_type=jnp.float32
    )
    gate_sigma = jax.nn.sigmoid(gate_logits.astype(jnp.float32))
    gate_gradient = (gated_grad * attended * gate_sigma * (1.0 - gate_sigma)).astype(jnp.bfloat16)
    attended_grad = (gated_grad * gate_sigma).astype(jnp.bfloat16)
    grad_heads = split_heads(attended_grad)
    row_delta = jnp.transpose(
        jnp.sum(split_heads(attended_grad.astype(jnp.float32) * attended), axis=-1), (0, 2, 1)
    )
    context = (query_heads, grad_heads, log_total, row_delta, pair_bias, scaling)
    held_start = (key_vectors, value_vectors, mask_low)
    grads_start = (
        jnp.zeros(key_vectors.shape, jnp.float32),
        jnp.zeros(value_vectors.shape, jnp.float32),
    )
    query_start = jnp.zeros((rows_here, tokens_here, HEADS, head_width), jnp.float32)
    bias_start = jnp.zeros(pair_bias.shape, jnp.float32)

    def move_grads(grads):
        return jax.tree.map(
            lambda part, own: part.astype(own.dtype), shifted(shortened(grads), "col", 1), grads
        )

    def one_step(step_index, folded):
        held_block, grads, query_total, bias_total = folded
        anchor = (column_here - step_index) % column_count
        query_total, bias_total, grads = absorb(
            context, held_block, anchor, query_total, bias_total, grads
        )
        held_block = jax.tree.map(
            lambda part, own: part.astype(own.dtype),
            shifted(shortened(held_block), "col", 1),
            held_block,
        )
        return (held_block, move_grads(grads), query_total, bias_total)

    held_block, grads, query_total, bias_total = lax.fori_loop(
        0, column_count - 1, one_step, (held_start, grads_start, query_start, bias_start)
    )
    anchor = (column_here - (column_count - 1)) % column_count
    query_total, bias_total, grads = absorb(
        context, held_block, anchor, query_total, bias_total, grads
    )
    grads = move_grads(grads)
    query_gradient = (scaling * query_total).reshape(query_vectors.shape).astype(jnp.bfloat16)
    key_gradient = (scaling * grads[0]).astype(jnp.bfloat16)
    value_gradient = grads[1].astype(jnp.bfloat16)
    bias_gradient = lax.psum_scatter(
        bias_total.astype(jnp.bfloat16), "row", scatter_dimension=2, tiled=True
    ).astype(jnp.float32)
    return (query_gradient, key_gradient, value_gradient, gate_gradient, bias_gradient)


def solution(mesh):
    placed = (
        P("row", "col", None),
        P("row", "col", None),
        P("row", "col", None),
        P("row", "col", None),
        P(None, "col", None),
        P("row", "col"),
        P(),
        P("row", "col", None),
    )
    return jax.shard_map(
        local,
        mesh=mesh,
        in_specs=placed,
        out_specs=(
            P("row", "col", None),
            P("row", "col", None),
            P("row", "col", None),
            P("row", "col", None),
            P(None, "col", "row"),
        ),
        check_vma=False,
    )
```

profile of v0, /device:TPU:1, one launch (start us, length us, event | category | flops | bytes accessed | tf_op | source)
XLA Modules:
  0.0 486.5 jit_solution(13953133334544486383)
XLA Ops:
  7.2 1.6 copy.65
  8.9 1.6 copy.66
  10.5 2.2 copy.70
  12.7 2.3 reshape.119
  15.0 7.2 %all-to-all-start = ((bf16[16,2,1536]{2,1,0:T(2,128)(2,1)}), bf16[16,2,1536]{2,1,0:T(2,128)(2,1)S(1)}, u32[]{:S(2)}, u32[]{:S(2)}) async-start(bf16[16,2,1536]{2,1,0:T(2,128)(2,1)} %reshape.119), calls=%async_computation | async-start | bytes 196608 | tf_op jit(solution)/shard_map/all_to_all | solution.py:163
  23.8 20.1 %all-gather = bf16[16,96,4]{1,2,0:T(4,128)(2,1)S(1)} all-gather(bf16[1,96,4]{1,2,0:T(4,128)(2,1)S(1)} %convert_bitcast_fusion), channel_id=1, replica_groups=mesh['row'=8,'col'=16] {'col'}, dimensions={0}, use_global_device_ids=true | all-gather | bytes 13056 | tf_op jit(solution)/shard_map/all_gather | solution.py:155
  46.0 1.8 reshape.120
  47.8 1.6 copy.71
  49.4 33.5 %all-gather.6.cloned.1.call-done = bf16[4,1536,128]{2,0,1:T(4,128)(2,1)} async-done(((bf16[4,96,128]{2,0,1:T(4,128)(2,1)}), bf16[4,1536,128]{2,0,1:T(4,128)(2,1)}) %all-gather.6.cloned.1.call-update) | async-done | bytes 1572880 | tf_op jit(solution)/shard_map/all_gather | solution.py:154
  83.0 78.2 %while.43 = (s32[]{:T(128)}, f32[4,4,96]{2,1,0:T(4,128)S(1)}, f32[4,4,96]{2,1,0:T(4,128)S(1)}, f32[4,4,96,32]{2,3,1,0:T(8,128)S(1)}, s32[16]{0:T(128)S(1)}, /*in...) while((s32[]{:T(128)}, f32[4,4,96]{2,1,0:T(4,128)S(1)}, ...), condition=%wide.region_3.4_spmd.clone, body=%wide.region_0.3_spmd.clone.sunk | while | flops 30470792 | bytes 5095135 | solution.py:76
  162.9 224.8 %while.44 = (s32[]{:T(128)}, bf16[4,96,128]{1,2,0:T(8,128)(2,1)}, bf16[4,96,128]{1,2,0:T(8,128)(2,1)}, bf16[4,96]{1,0:T(4,128)(2,1)S(1)}, f32[4,96,128]{1,2,0:T(...) while((s32[]{:T(128)}, bf16[4,96,128]{1,2,0:T(8,128)(2,1)}, ...), condition=%wide.region_7.8_spmd.clone, body=%wide.region_5.7_spmd.clone.sunk | while | flops 49041808 | bytes 10513012 | solution.py:201
  176.3 1.4 collective-permute-start.2
  190.0 2.0 collective-permute-start.2
  193.0 2.1 collective-permute-start
  205.8 1.5 collective-permute-start.2
  208.2 1.4 collective-permute-start
  220.4 1.4 collective-permute-start.2
  222.7 1.9 collective-permute-start
  225.5 2.0 collective-permute-start.1
  236.1 1.4 collective-permute-start.2
  238.4 1.5 collective-permute-start
  240.8 1.5 collective-permute-start.1
  250.2 2.0 collective-permute-start.2
  253.2 2.5 collective-permute-start
  266.5 1.4 collective-permute-start.2
  268.8 1.4 collective-permute-start
  281.0 1.4 collective-permute-start.2
  283.3 1.9 collective-permute-start
  286.1 2.0 collective-permute-start.1
  296.7 1.4 collective-permute-start.2
  299.0 1.7 collective-permute-start
  310.8 2.0 collective-permute-start.2
  313.8 2.5 collective-permute-start
  327.1 1.4 collective-permute-start.2
  329.4 1.4 collective-permute-start
  341.6 1.4 collective-permute-start.2
  343.9 1.9 collective-permute-start
  346.6 2.0 collective-permute-start.1
  359.6 1.7 collective-permute-start
  371.5 2.0 collective-permute-start.2
  374.4 2.5 collective-permute-start
  387.7 2.3 copy.88
  392.2 2.0 fusion.43
  394.2 1.6 dynamic-slice_add_fusion.1
  399.4 2.6 copy.98
  402.1 1.9 reshape.117
  405.6 1.4 collective-permute-start.6
  411.1 66.3 %reduce-scatter.4.cloned.1.call-done = bf16[192,384]{1,0:T(8,128)(2,1)} async-done(((bf16[1536,384]{1,0:T(8,128)(2,1)}), bf16[192,384]{1,0:T(8,128)(2,1)}) %reduce-scatter.4.cloned.1.call-update) | async-done | bytes 147472
  (737 shorter events, 256.8 us)
Async XLA Ops:
  7.2 42.3 %all-gather.4.cloned.1.call-start = ((), (), s32[]{:S(2)}) async-start(), calls=%async_computation.2 | async-start | bytes 1671168 | tf_op jit(solution)/shard_map/all_gather | solution.py:153
  8.8 74.1 %all-gather.6.cloned.1.call-start = ((), (), s32[]{:S(2)}) async-start(), calls=%async_computation.3 | async-start | bytes 1671168 | tf_op jit(solution)/shard_map/all_gather | solution.py:154
  15.0 31.0 %all-to-all-start = ((bf16[16,2,1536]{2,1,0:T(2,128)(2,1)}), bf16[16,2,1536]{2,1,0:T(2,128)(2,1)S(1)}, u32[]{:S(2)}, u32[]{:S(2)}) async-start(bf16[16,2,1536]{2,1,0:T(2,128)(2,1)} %reshape.119), calls=%async_computation | async-start | bytes 196608 | tf_op jit(solution)/shard_map/all_to_all | solution.py:163
  22.2 455.2 %reduce-scatter.4.cloned.1.call-start = ((), (), s32[]{:S(2)}) async-start(), calls=%async_computation.4 | async-start | bytes 1327104
  162.9 13.3 %collective-permute-start.2 = (bf16[4,96]{1,0:T(4,128)(2,1)S(1)}, bf16[4,96]{1,0:T(4,128)(2,1)S(1)}, u32[]{:S(2)}, u32[]{:S(2)}) collective-permute-start(bf16[4,96]{1,0:T(4,128)(2,1)S(1)} %copy.133), channel_id=1, source_target_pairs={{0,1},{1,2},{2,3},{3,4},{4,5},{5,6},{6,7},{7,8},{8,9},{9,10},{10,1... | collective-permute-start | bytes 2312 | tf_op jit(solution)/shard_map/while/body/eval_jaxpr/ppermute | solution.py:26
  165.0 11.3 %collective-permute-start = (bf16[4,96,128]{1,2,0:T(8,128)(2,1)S(1)}, bf16[4,96,128]{1,2,0:T(8,128)(2,1)}, u32[]{:S(2)}, u32[]{:S(2)}) collective-permute-start(bf16[4,96,128]{1,2,0:T(8,128)(2,1)S(1)} %copy.131), channel_id=1, source_target_pairs={{0,1},{1,2},{2,3},{3,4},{4,5},{5,6},{6,7},{7,8},{8,9},{9,10},{10,1... | collective-permute-start | bytes 294920 | tf_op jit(solution)/shard_map/while/body/eval_jaxpr/ppermute | solution.py:26
  166.1 10.2 %collective-permute-start.1 = (bf16[4,96,128]{1,2,0:T(8,128)(2,1)S(1)}, bf16[4,96,128]{1,2,0:T(8,128)(2,1)}, u32[]{:S(2)}, u32[]{:S(2)}) collective-permute-start(bf16[4,96,128]{1,2,0:T(8,128)(2,1)S(1)} %copy.132), channel_id=1, source_target_pairs={{0,1},{1,2},{2,3},{3,4},{4,5},{5,6},{6,7},{7,8},{8,9},{9,10},{10,1... | collective-permute-start | bytes 294920 | tf_op jit(solution)/shard_map/while/body/eval_jaxpr/ppermute | solution.py:26
  176.3 13.7 %collective-permute-start.2 = (bf16[4,96]{1,0:T(4,128)(2,1)S(1)}, bf16[4,96]{1,0:T(4,128)(2,1)S(1)}, u32[]{:S(2)}, u32[]{:S(2)}) collective-permute-start(bf16[4,96]{1,0:T(4,128)(2,1)S(1)} %copy.133), channel_id=1, source_target_pairs={{0,1},{1,2},{2,3},{3,4},{4,5},{5,6},{6,7},{7,8},{8,9},{9,10},{10,1... | collective-permute-start | bytes 2312 | tf_op jit(solution)/shard_map/while/body/eval_jaxpr/ppermute | solution.py:26
  178.6 11.4 %collective-permute-start = (bf16[4,96,128]{1,2,0:T(8,128)(2,1)S(1)}, bf16[4,96,128]{1,2,0:T(8,128)(2,1)}, u32[]{:S(2)}, u32[]{:S(2)}) collective-permute-start(bf16[4,96,128]{1,2,0:T(8,128)(2,1)S(1)} %copy.131), channel_id=1, source_target_pairs={{0,1},{1,2},{2,3},{3,4},{4,5},{5,6},{6,7},{7,8},{8,9},{9,10},{10,1... | collective-permute-start | bytes 294920 | tf_op jit(solution)/shard_map/while/body/eval_jaxpr/ppermute | solution.py:26
  180.4 9.6 %collective-permute-start.1 = (bf16[4,96,128]{1,2,0:T(8,128)(2,1)S(1)}, bf16[4,96,128]{1,2,0:T(8,128)(2,1)}, u32[]{:S(2)}, u32[]{:S(2)}) collective-permute-start(bf16[4,96,128]{1,2,0:T(8,128)(2,1)S(1)} %copy.132), channel_id=1, source_target_pairs={{0,1},{1,2},{2,3},{3,4},{4,5},{5,6},{6,7},{7,8},{8,9},{9,10},{10,1... | collective-permute-start | bytes 294920 | tf_op jit(solution)/shard_map/while/body/eval_jaxpr/ppermute | solution.py:26
  190.0 15.7 %collective-permute-start.2 = (bf16[4,96]{1,0:T(4,128)(2,1)S(1)}, bf16[4,96]{1,0:T(4,128)(2,1)S(1)}, u32[]{:S(2)}, u32[]{:S(2)}) collective-permute-start(bf16[4,96]{1,0:T(4,128)(2,1)S(1)} %copy.133), channel_id=1, source_target_pairs={{0,1},{1,2},{2,3},{3,4},{4,5},{5,6},{6,7},{7,8},{8,9},{9,10},{10,1... | collective-permute-start | bytes 2312 | tf_op jit(solution)/shard_map/while/body/eval_jaxpr/ppermute | solution.py:26
  193.0 12.7 %collective-permute-start = (bf16[4,96,128]{1,2,0:T(8,128)(2,1)S(1)}, bf16[4,96,128]{1,2,0:T(8,128)(2,1)}, u32[]{:S(2)}, u32[]{:S(2)}) collective-permute-start(bf16[4,96,128]{1,2,0:T(8,128)(2,1)S(1)} %copy.131), channel_id=1, source_target_pairs={{0,1},{1,2},{2,3},{3,4},{4,5},{5,6},{6,7},{7,8},{8,9},{9,10},{10,1... | collective-permute-start | bytes 294920 | tf_op jit(solution)/shard_map/while/body/eval_jaxpr/ppermute | solution.py:26
  196.0 9.7 %collective-permute-start.1 = (bf16[4,96,128]{1,2,0:T(8,128)(2,1)S(1)}, bf16[4,96,128]{1,2,0:T(8,128)(2,1)}, u32[]{:S(2)}, u32[]{:S(2)}) collective-permute-start(bf16[4,96,128]{1,2,0:T(8,128)(2,1)S(1)} %copy.132), channel_id=1, source_target_pairs={{0,1},{1,2},{2,3},{3,4},{4,5},{5,6},{6,7},{7,8},{8,9},{9,10},{10,1... | collective-permute-start | bytes 294920 | tf_op jit(solution)/shard_map/while/body/eval_jaxpr/ppermute | solution.py:26
  205.8 14.6 %collective-permute-start.2 = (bf16[4,96]{1,0:T(4,128)(2,1)S(1)}, bf16[4,96]{1,0:T(4,128)(2,1)S(1)}, u32[]{:S(2)}, u32[]{:S(2)}) collective-permute-start(bf16[4,96]{1,0:T(4,128)(2,1)S(1)} %copy.133), channel_id=1, source_target_pairs={{0,1},{1,2},{2,3},{3,4},{4,5},{5,6},{6,7},{7,8},{8,9},{9,10},{10,1... | collective-permute-start | bytes 2312 | tf_op jit(solution)/shard_map/while/body/eval_jaxpr/ppermute | solution.py:26
  208.2 12.2 %collective-permute-start = (bf16[4,96,128]{1,2,0:T(8,128)(2,1)S(1)}, bf16[4,96,128]{1,2,0:T(8,128)(2,1)}, u32[]{:S(2)}, u32[]{:S(2)}) collective-permute-start(bf16[4,96,128]{1,2,0:T(8,128)(2,1)S(1)} %copy.131), channel_id=1, source_target_pairs={{0,1},{1,2},{2,3},{3,4},{4,5},{5,6},{6,7},{7,8},{8,9},{9,10},{10,1... | collective-permute-start | bytes 294920 | tf_op jit(solution)/shard_map/while/body/eval_jaxpr/ppermute | solution.py:26
  210.5 9.9 %collective-permute-start.1 = (bf16[4,96,128]{1,2,0:T(8,128)(2,1)S(1)}, bf16[4,96,128]{1,2,0:T(8,128)(2,1)}, u32[]{:S(2)}, u32[]{:S(2)}) collective-permute-start(bf16[4,96,128]{1,2,0:T(8,128)(2,1)S(1)} %copy.132), channel_id=1, source_target_pairs={{0,1},{1,2},{2,3},{3,4},{4,5},{5,6},{6,7},{7,8},{8,9},{9,10},{10,1... | collective-permute-start | bytes 294920 | tf_op jit(solution)/shard_map/while/body/eval_jaxpr/ppermute | solution.py:26
  220.4 15.6 %collective-permute-start.2 = (bf16[4,96]{1,0:T(4,128)(2,1)S(1)}, bf16[4,96]{1,0:T(4,128)(2,1)S(1)}, u32[]{:S(2)}, u32[]{:S(2)}) collective-permute-start(bf16[4,96]{1,0:T(4,128)(2,1)S(1)} %copy.133), channel_id=1, source_target_pairs={{0,1},{1,2},{2,3},{3,4},{4,5},{5,6},{6,7},{7,8},{8,9},{9,10},{10,1... | collective-permute-start | bytes 2312 | tf_op jit(solution)/shard_map/while/body/eval_jaxpr/ppermute | solution.py:26
  222.7 13.4 %collective-permute-start = (bf16[4,96,128]{1,2,0:T(8,128)(2,1)S(1)}, bf16[4,96,128]{1,2,0:T(8,128)(2,1)}, u32[]{:S(2)}, u32[]{:S(2)}) collective-permute-start(bf16[4,96,128]{1,2,0:T(8,128)(2,1)S(1)} %copy.131), channel_id=1, source_target_pairs={{0,1},{1,2},{2,3},{3,4},{4,5},{5,6},{6,7},{7,8},{8,9},{9,10},{10,1... | collective-permute-start | bytes 294920 | tf_op jit(solution)/shard_map/while/body/eval_jaxpr/ppermute | solution.py:26
  225.5 10.6 %collective-permute-start.1 = (bf16[4,96,128]{1,2,0:T(8,128)(2,1)S(1)}, bf16[4,96,128]{1,2,0:T(8,128)(2,1)}, u32[]{:S(2)}, u32[]{:S(2)}) collective-permute-start(bf16[4,96,128]{1,2,0:T(8,128)(2,1)S(1)} %copy.132), channel_id=1, source_target_pairs={{0,1},{1,2},{2,3},{3,4},{4,5},{5,6},{6,7},{7,8},{8,9},{9,10},{10,1... | collective-permute-start | bytes 294920 | tf_op jit(solution)/shard_map/while/body/eval_jaxpr/ppermute | solution.py:26
  236.1 14.1 %collective-permute-start.2 = (bf16[4,96]{1,0:T(4,128)(2,1)S(1)}, bf16[4,96]{1,0:T(4,128)(2,1)S(1)}, u32[]{:S(2)}, u32[]{:S(2)}) collective-permute-start(bf16[4,96]{1,0:T(4,128)(2,1)S(1)} %copy.133), channel_id=1, source_target_pairs={{0,1},{1,2},{2,3},{3,4},{4,5},{5,6},{6,7},{7,8},{8,9},{9,10},{10,1... | collective-permute-start | bytes 2312 | tf_op jit(solution)/shard_map/while/body/eval_jaxpr/ppermute | solution.py:26
  238.4 11.8 %collective-permute-start = (bf16[4,96,128]{1,2,0:T(8,128)(2,1)S(1)}, bf16[4,96,128]{1,2,0:T(8,128)(2,1)}, u32[]{:S(2)}, u32[]{:S(2)}) collective-permute-start(bf16[4,96,128]{1,2,0:T(8,128)(2,1)S(1)} %copy.131), channel_id=1, source_target_pairs={{0,1},{1,2},{2,3},{3,4},{4,5},{5,6},{6,7},{7,8},{8,9},{9,10},{10,1... | collective-permute-start | bytes 294920 | tf_op jit(solution)/shard_map/while/body/eval_jaxpr/ppermute | solution.py:26
  240.8 9.4 %collective-permute-start.1 = (bf16[4,96,128]{1,2,0:T(8,128)(2,1)S(1)}, bf16[4,96,128]{1,2,0:T(8,128)(2,1)}, u32[]{:S(2)}, u32[]{:S(2)}) collective-permute-start(bf16[4,96,128]{1,2,0:T(8,128)(2,1)S(1)} %copy.132), channel_id=1, source_target_pairs={{0,1},{1,2},{2,3},{3,4},{4,5},{5,6},{6,7},{7,8},{8,9},{9,10},{10,1... | collective-permute-start | bytes 294920 | tf_op jit(solution)/shard_map/while/body/eval_jaxpr/ppermute | solution.py:26
  250.2 16.2 %collective-permute-start.2 = (bf16[4,96]{1,0:T(4,128)(2,1)S(1)}, bf16[4,96]{1,0:T(4,128)(2,1)S(1)}, u32[]{:S(2)}, u32[]{:S(2)}) collective-permute-start(bf16[4,96]{1,0:T(4,128)(2,1)S(1)} %copy.133), channel_id=1, source_target_pairs={{0,1},{1,2},{2,3},{3,4},{4,5},{5,6},{6,7},{7,8},{8,9},{9,10},{10,1... | collective-permute-start | bytes 2312 | tf_op jit(solution)/shard_map/while/body/eval_jaxpr/ppermute | solution.py:26
  253.2 13.3 %collective-permute-start = (bf16[4,96,128]{1,2,0:T(8,128)(2,1)S(1)}, bf16[4,96,128]{1,2,0:T(8,128)(2,1)}, u32[]{:S(2)}, u32[]{:S(2)}) collective-permute-start(bf16[4,96,128]{1,2,0:T(8,128)(2,1)S(1)} %copy.131), channel_id=1, source_target_pairs={{0,1},{1,2},{2,3},{3,4},{4,5},{5,6},{6,7},{7,8},{8,9},{9,10},{10,1... | collective-permute-start | bytes 294920 | tf_op jit(solution)/shard_map/while/body/eval_jaxpr/ppermute | solution.py:26
  256.6 9.9 %collective-permute-start.1 = (bf16[4,96,128]{1,2,0:T(8,128)(2,1)S(1)}, bf16[4,96,128]{1,2,0:T(8,128)(2,1)}, u32[]{:S(2)}, u32[]{:S(2)}) collective-permute-start(bf16[4,96,128]{1,2,0:T(8,128)(2,1)S(1)} %copy.132), channel_id=1, source_target_pairs={{0,1},{1,2},{2,3},{3,4},{4,5},{5,6},{6,7},{7,8},{8,9},{9,10},{10,1... | collective-permute-start | bytes 294920 | tf_op jit(solution)/shard_map/while/body/eval_jaxpr/ppermute | solution.py:26
  266.5 14.5 %collective-permute-start.2 = (bf16[4,96]{1,0:T(4,128)(2,1)S(1)}, bf16[4,96]{1,0:T(4,128)(2,1)S(1)}, u32[]{:S(2)}, u32[]{:S(2)}) collective-permute-start(bf16[4,96]{1,0:T(4,128)(2,1)S(1)} %copy.133), channel_id=1, source_target_pairs={{0,1},{1,2},{2,3},{3,4},{4,5},{5,6},{6,7},{7,8},{8,9},{9,10},{10,1... | collective-permute-start | bytes 2312 | tf_op jit(solution)/shard_map/while/body/eval_jaxpr/ppermute | solution.py:26
  268.8 12.2 %collective-permute-start = (bf16[4,96,128]{1,2,0:T(8,128)(2,1)S(1)}, bf16[4,96,128]{1,2,0:T(8,128)(2,1)}, u32[]{:S(2)}, u32[]{:S(2)}) collective-permute-start(bf16[4,96,128]{1,2,0:T(8,128)(2,1)S(1)} %copy.131), channel_id=1, source_target_pairs={{0,1},{1,2},{2,3},{3,4},{4,5},{5,6},{6,7},{7,8},{8,9},{9,10},{10,1... | collective-permute-start | bytes 294920 | tf_op jit(solution)/shard_map/while/body/eval_jaxpr/ppermute | solution.py:26
  271.0 10.0 %collective-permute-start.1 = (bf16[4,96,128]{1,2,0:T(8,128)(2,1)S(1)}, bf16[4,96,128]{1,2,0:T(8,128)(2,1)}, u32[]{:S(2)}, u32[]{:S(2)}) collective-permute-start(bf16[4,96,128]{1,2,0:T(8,128)(2,1)S(1)} %copy.132), channel_id=1, source_target_pairs={{0,1},{1,2},{2,3},{3,4},{4,5},{5,6},{6,7},{7,8},{8,9},{9,10},{10,1... | collective-permute-start | bytes 294920 | tf_op jit(solution)/shard_map/while/body/eval_jaxpr/ppermute | solution.py:26
  281.0 15.6 %collective-permute-start.2 = (bf16[4,96]{1,0:T(4,128)(2,1)S(1)}, bf16[4,96]{1,0:T(4,128)(2,1)S(1)}, u32[]{:S(2)}, u32[]{:S(2)}) collective-permute-start(bf16[4,96]{1,0:T(4,128)(2,1)S(1)} %copy.133), channel_id=1, source_target_pairs={{0,1},{1,2},{2,3},{3,4},{4,5},{5,6},{6,7},{7,8},{8,9},{9,10},{10,1... | collective-permute-start | bytes 2312 | tf_op jit(solution)/shard_map/while/body/eval_jaxpr/ppermute | solution.py:26
  283.3 13.4 %collective-permute-start = (bf16[4,96,128]{1,2,0:T(8,128)(2,1)S(1)}, bf16[4,96,128]{1,2,0:T(8,128)(2,1)}, u32[]{:S(2)}, u32[]{:S(2)}) collective-permute-start(bf16[4,96,128]{1,2,0:T(8,128)(2,1)S(1)} %copy.131), channel_id=1, source_target_pairs={{0,1},{1,2},{2,3},{3,4},{4,5},{5,6},{6,7},{7,8},{8,9},{9,10},{10,1... | collective-permute-start | bytes 294920 | tf_op jit(solution)/shard_map/while/body/eval_jaxpr/ppermute | solution.py:26
  286.1 10.6 %collective-permute-start.1 = (bf16[4,96,128]{1,2,0:T(8,128)(2,1)S(1)}, bf16[4,96,128]{1,2,0:T(8,128)(2,1)}, u32[]{:S(2)}, u32[]{:S(2)}) collective-permute-start(bf16[4,96,128]{1,2,0:T(8,128)(2,1)S(1)} %copy.132), channel_id=1, source_target_pairs={{0,1},{1,2},{2,3},{3,4},{4,5},{5,6},{6,7},{7,8},{8,9},{9,10},{10,1... | collective-permute-start | bytes 294920 | tf_op jit(solution)/shard_map/while/body/eval_jaxpr/ppermute | solution.py:26
  296.7 14.1 %collective-permute-start.2 = (bf16[4,96]{1,0:T(4,128)(2,1)S(1)}, bf16[4,96]{1,0:T(4,128)(2,1)S(1)}, u32[]{:S(2)}, u32[]{:S(2)}) collective-permute-start(bf16[4,96]{1,0:T(4,128)(2,1)S(1)} %copy.133), channel_id=1, source_target_pairs={{0,1},{1,2},{2,3},{3,4},{4,5},{5,6},{6,7},{7,8},{8,9},{9,10},{10,1... | collective-permute-start | bytes 2312 | tf_op jit(solution)/shard_map/while/body/eval_jaxpr/ppermute | solution.py:26
  299.0 11.8 %collective-permute-start = (bf16[4,96,128]{1,2,0:T(8,128)(2,1)S(1)}, bf16[4,96,128]{1,2,0:T(8,128)(2,1)}, u32[]{:S(2)}, u32[]{:S(2)}) collective-permute-start(bf16[4,96,128]{1,2,0:T(8,128)(2,1)S(1)} %copy.131), channel_id=1, source_target_pairs={{0,1},{1,2},{2,3},{3,4},{4,5},{5,6},{6,7},{7,8},{8,9},{9,10},{10,1... | collective-permute-start | bytes 294920 | tf_op jit(solution)/shard_map/while/body/eval_jaxpr/ppermute | solution.py:26
  310.8 16.2 %collective-permute-start.2 = (bf16[4,96]{1,0:T(4,128)(2,1)S(1)}, bf16[4,96]{1,0:T(4,128)(2,1)S(1)}, u32[]{:S(2)}, u32[]{:S(2)}) collective-permute-start(bf16[4,96]{1,0:T(4,128)(2,1)S(1)} %copy.133), channel_id=1, source_target_pairs={{0,1},{1,2},{2,3},{3,4},{4,5},{5,6},{6,7},{7,8},{8,9},{9,10},{10,1... | collective-permute-start | bytes 2312 | tf_op jit(solution)/shard_map/while/body/eval_jaxpr/ppermute | solution.py:26
  313.8 13.3 %collective-permute-start = (bf16[4,96,128]{1,2,0:T(8,128)(2,1)S(1)}, bf16[4,96,128]{1,2,0:T(8,128)(2,1)}, u32[]{:S(2)}, u32[]{:S(2)}) collective-permute-start(bf16[4,96,128]{1,2,0:T(8,128)(2,1)S(1)} %copy.131), channel_id=1, source_target_pairs={{0,1},{1,2},{2,3},{3,4},{4,5},{5,6},{6,7},{7,8},{8,9},{9,10},{10,1... | collective-permute-start | bytes 294920 | tf_op jit(solution)/shard_map/while/body/eval_jaxpr/ppermute | solution.py:26
  317.2 9.9 %collective-permute-start.1 = (bf16[4,96,128]{1,2,0:T(8,128)(2,1)S(1)}, bf16[4,96,128]{1,2,0:T(8,128)(2,1)}, u32[]{:S(2)}, u32[]{:S(2)}) collective-permute-start(bf16[4,96,128]{1,2,0:T(8,128)(2,1)S(1)} %copy.132), channel_id=1, source_target_pairs={{0,1},{1,2},{2,3},{3,4},{4,5},{5,6},{6,7},{7,8},{8,9},{9,10},{10,1... | collective-permute-start | bytes 294920 | tf_op jit(solution)/shard_map/while/body/eval_jaxpr/ppermute | solution.py:26
  327.1 14.4 %collective-permute-start.2 = (bf16[4,96]{1,0:T(4,128)(2,1)S(1)}, bf16[4,96]{1,0:T(4,128)(2,1)S(1)}, u32[]{:S(2)}, u32[]{:S(2)}) collective-permute-start(bf16[4,96]{1,0:T(4,128)(2,1)S(1)} %copy.133), channel_id=1, source_target_pairs={{0,1},{1,2},{2,3},{3,4},{4,5},{5,6},{6,7},{7,8},{8,9},{9,10},{10,1... | collective-permute-start | bytes 2312 | tf_op jit(solution)/shard_map/while/body/eval_jaxpr/ppermute | solution.py:26
  329.4 12.2 %collective-permute-start = (bf16[4,96,128]{1,2,0:T(8,128)(2,1)S(1)}, bf16[4,96,128]{1,2,0:T(8,128)(2,1)}, u32[]{:S(2)}, u32[]{:S(2)}) collective-permute-start(bf16[4,96,128]{1,2,0:T(8,128)(2,1)S(1)} %copy.131), channel_id=1, source_target_pairs={{0,1},{1,2},{2,3},{3,4},{4,5},{5,6},{6,7},{7,8},{8,9},{9,10},{10,1... | collective-permute-start | bytes 294920 | tf_op jit(solution)/shard_map/while/body/eval_jaxpr/ppermute | solution.py:26
  331.7 9.9 %collective-permute-start.1 = (bf16[4,96,128]{1,2,0:T(8,128)(2,1)S(1)}, bf16[4,96,128]{1,2,0:T(8,128)(2,1)}, u32[]{:S(2)}, u32[]{:S(2)}) collective-permute-start(bf16[4,96,128]{1,2,0:T(8,128)(2,1)S(1)} %copy.132), channel_id=1, source_target_pairs={{0,1},{1,2},{2,3},{3,4},{4,5},{5,6},{6,7},{7,8},{8,9},{9,10},{10,1... | collective-permute-start | bytes 294920 | tf_op jit(solution)/shard_map/while/body/eval_jaxpr/ppermute | solution.py:26
  341.6 15.6 %collective-permute-start.2 = (bf16[4,96]{1,0:T(4,128)(2,1)S(1)}, bf16[4,96]{1,0:T(4,128)(2,1)S(1)}, u32[]{:S(2)}, u32[]{:S(2)}) collective-permute-start(bf16[4,96]{1,0:T(4,128)(2,1)S(1)} %copy.133), channel_id=1, source_target_pairs={{0,1},{1,2},{2,3},{3,4},{4,5},{5,6},{6,7},{7,8},{8,9},{9,10},{10,1... | collective-permute-start | bytes 2312 | tf_op jit(solution)/shard_map/while/body/eval_jaxpr/ppermute | solution.py:26
  343.9 13.4 %collective-permute-start = (bf16[4,96,128]{1,2,0:T(8,128)(2,1)S(1)}, bf16[4,96,128]{1,2,0:T(8,128)(2,1)}, u32[]{:S(2)}, u32[]{:S(2)}) collective-permute-start(bf16[4,96,128]{1,2,0:T(8,128)(2,1)S(1)} %copy.131), channel_id=1, source_target_pairs={{0,1},{1,2},{2,3},{3,4},{4,5},{5,6},{6,7},{7,8},{8,9},{9,10},{10,1... | collective-permute-start | bytes 294920 | tf_op jit(solution)/shard_map/while/body/eval_jaxpr/ppermute | solution.py:26
  346.6 10.6 %collective-permute-start.1 = (bf16[4,96,128]{1,2,0:T(8,128)(2,1)S(1)}, bf16[4,96,128]{1,2,0:T(8,128)(2,1)}, u32[]{:S(2)}, u32[]{:S(2)}) collective-permute-start(bf16[4,96,128]{1,2,0:T(8,128)(2,1)S(1)} %copy.132), channel_id=1, source_target_pairs={{0,1},{1,2},{2,3},{3,4},{4,5},{5,6},{6,7},{7,8},{8,9},{9,10},{10,1... | collective-permute-start | bytes 294920 | tf_op jit(solution)/shard_map/while/body/eval_jaxpr/ppermute | solution.py:26
  357.3 14.1 %collective-permute-start.2 = (bf16[4,96]{1,0:T(4,128)(2,1)S(1)}, bf16[4,96]{1,0:T(4,128)(2,1)S(1)}, u32[]{:S(2)}, u32[]{:S(2)}) collective-permute-start(bf16[4,96]{1,0:T(4,128)(2,1)S(1)} %copy.133), channel_id=1, source_target_pairs={{0,1},{1,2},{2,3},{3,4},{4,5},{5,6},{6,7},{7,8},{8,9},{9,10},{10,1... | collective-permute-start | bytes 2312 | tf_op jit(solution)/shard_map/while/body/eval_jaxpr/ppermute | solution.py:26
  359.6 11.8 %collective-permute-start = (bf16[4,96,128]{1,2,0:T(8,128)(2,1)S(1)}, bf16[4,96,128]{1,2,0:T(8,128)(2,1)}, u32[]{:S(2)}, u32[]{:S(2)}) collective-permute-start(bf16[4,96,128]{1,2,0:T(8,128)(2,1)S(1)} %copy.131), channel_id=1, source_target_pairs={{0,1},{1,2},{2,3},{3,4},{4,5},{5,6},{6,7},{7,8},{8,9},{9,10},{10,1... | collective-permute-start | bytes 294920 | tf_op jit(solution)/shard_map/while/body/eval_jaxpr/ppermute | solution.py:26
  362.2 9.2 %collective-permute-start.1 = (bf16[4,96,128]{1,2,0:T(8,128)(2,1)S(1)}, bf16[4,96,128]{1,2,0:T(8,128)(2,1)}, u32[]{:S(2)}, u32[]{:S(2)}) collective-permute-start(bf16[4,96,128]{1,2,0:T(8,128)(2,1)S(1)} %copy.132), channel_id=1, source_target_pairs={{0,1},{1,2},{2,3},{3,4},{4,5},{5,6},{6,7},{7,8},{8,9},{9,10},{10,1... | collective-permute-start | bytes 294920 | tf_op jit(solution)/shard_map/while/body/eval_jaxpr/ppermute | solution.py:26
  371.5 16.2 %collective-permute-start.2 = (bf16[4,96]{1,0:T(4,128)(2,1)S(1)}, bf16[4,96]{1,0:T(4,128)(2,1)S(1)}, u32[]{:S(2)}, u32[]{:S(2)}) collective-permute-start(bf16[4,96]{1,0:T(4,128)(2,1)S(1)} %copy.133), channel_id=1, source_target_pairs={{0,1},{1,2},{2,3},{3,4},{4,5},{5,6},{6,7},{7,8},{8,9},{9,10},{10,1... | collective-permute-start | bytes 2312 | tf_op jit(solution)/shard_map/while/body/eval_jaxpr/ppermute | solution.py:26
  374.4 13.3 %collective-permute-start = (bf16[4,96,128]{1,2,0:T(8,128)(2,1)S(1)}, bf16[4,96,128]{1,2,0:T(8,128)(2,1)}, u32[]{:S(2)}, u32[]{:S(2)}) collective-permute-start(bf16[4,96,128]{1,2,0:T(8,128)(2,1)S(1)} %copy.131), channel_id=1, source_target_pairs={{0,1},{1,2},{2,3},{3,4},{4,5},{5,6},{6,7},{7,8},{8,9},{9,10},{10,1... | collective-permute-start | bytes 294920 | tf_op jit(solution)/shard_map/while/body/eval_jaxpr/ppermute | solution.py:26
  377.8 9.9 %collective-permute-start.1 = (bf16[4,96,128]{1,2,0:T(8,128)(2,1)S(1)}, bf16[4,96,128]{1,2,0:T(8,128)(2,1)}, u32[]{:S(2)}, u32[]{:S(2)}) collective-permute-start(bf16[4,96,128]{1,2,0:T(8,128)(2,1)S(1)} %copy.132), channel_id=1, source_target_pairs={{0,1},{1,2},{2,3},{3,4},{4,5},{5,6},{6,7},{7,8},{8,9},{9,10},{10,1... | collective-permute-start | bytes 294920 | tf_op jit(solution)/shard_map/while/body/eval_jaxpr/ppermute | solution.py:26
  (74 other events, 487.0 us)
Sparse Core Ops, SparseCore 0:
  10.3 37.4 all-gather.3
  50.1 32.8 all-gather.5
  404.1 73.2 reduce-scatter.3
where the time goes:
time: 491 us; the launch traced here: 487 us
  local copies, waits for them, and re-layouts  131 us (27%)
  waiting for transfers between devices  100 us (20%)
  starting transfers between devices  87.8 us (18%)
  other arithmetic  75.7 us (15%)
  matrix products  43.6 us (9%)
  blocking collectives  20.1 us (4%)
  between operations  14.1 us (3%)
  loops' own time  13.5 us (3%)
    ppermute x77, starting transfers between devices, shifted(): return lax.ppermute(value, axis, pairs)  80.5 us
    unnamed x4, waiting for transfers between devices  66.4 us
    while x121, local copies, waits for them, and re-layouts  37.8 us
    all_gather x1, waiting for transfers between devices, local(): lax.all_gather(value_vectors, 'col', axis=1, tiled=True)  33.5 us
    convert_element_type x30, other arithmetic, move_grads(): part.astype(own.dtype)  27.7 us
    convert_element_type x32, other arithmetic, short(): return part.astype(jnp.bfloat16) if part.dtype == jnp.float32 else part  20.9 us
    unnamed x37, local copies, waits for them, and re-layouts  20.1 us
    all_gather x1, blocking collectives, local(): lax.all_gather(mask_low, 'col', axis=1, tiled=True)  20.1 us
  transfers between devices with their start and end apart: 81, of which 3 were waited for; matrix products, arithmetic and copies ran while one was open for 31% of the time, Pallas kernels for 0%

commit v1 on v0

v1 whole, which is shorter than its diff:
```python
import math

import jax
import jax.numpy as jnp
from jax import lax
from jax.experimental import pallas as pl
from jax.experimental.pallas import tpu as pltpu
from jax.sharding import PartitionSpec as P

HEADS = 4
NEG_FILL = -1000000000.0
LOG2E = math.log2(math.e)
CHUNK = 16


def attention_kernel(qd_ref, kv_ref, bias_ref, mask_ref, qa_ref, dkv_ref, dbias_ref, s_ref, b2_ref, acc_ref, de_ref, row_ref):
    step = pl.program_id(0)
    last = pl.num_programs(0) - 1
    rows = bias_ref.shape[0]
    queries = rows // 2
    keys = bias_ref.shape[1]
    head_width = qd_ref.shape[2] // 4
    scaling = 1.0 / math.sqrt(head_width)

    @pl.when(step == 0)
    def _():
        def fill(index, carry):
            part = pl.ds(index * CHUNK, CHUNK)
            b2_ref[part, :] = bias_ref[part, :].astype(jnp.float32) * LOG2E
            acc_ref[part, :] = jnp.zeros((CHUNK, keys), jnp.float32)
            return carry

        lax.fori_loop(0, rows // CHUNK, fill, 0)

    kv = kv_ref[...].reshape(keys, 4 * head_width)
    qd = qd_ref[0]
    lane = lax.broadcasted_iota(jnp.int32, (queries, 4 * head_width), 1)
    zero = jnp.zeros_like(qd)

    def only(part):
        return jnp.where((lane >= part * head_width) & (lane < (part + 1) * head_width), qd, zero)

    query_rows = jnp.concatenate([only(0), only(1)], axis=0)
    grad_rows = jnp.concatenate([only(2), only(3)], axis=0)
    transposed = (((1,), (1,)), ((), ()))
    s_ref[...] = lax.dot_general(query_rows, kv, transposed, preferred_element_type=jnp.float32)
    cap = jnp.where(mask_ref[0] > 0.5, 1e30, NEG_FILL * LOG2E)

    def soften(index, carry):
        part = pl.ds(index * CHUNK, CHUNK)
        scores = jnp.minimum(s_ref[part, :] * (scaling * LOG2E) + b2_ref[part, :], cap)
        weights = jnp.exp2(scores - jnp.max(scores, axis=1, keepdims=True))
        row_ref[part, :] = jnp.broadcast_to(jnp.sum(weights, axis=1, keepdims=True), (CHUNK, 128))
        de_ref[pl.ds(rows + index * CHUNK, CHUNK), :] = weights.astype(jnp.bfloat16)
        return carry

    lax.fori_loop(0, rows // CHUNK, soften, 0)
    weights_low = de_ref[rows:, :]
    inverse = 1.0 / row_ref[...]
    attended = jnp.dot(weights_low, kv, preferred_element_type=jnp.float32) * inverse
    grad_wide = grad_rows.astype(jnp.float32)
    delta = jnp.sum(grad_wide * attended, axis=1, keepdims=True)
    row_ref[...] = delta * inverse
    grad_scaled = (grad_wide * inverse).astype(jnp.bfloat16)
    s_ref[...] = lax.dot_general(grad_scaled, kv, transposed, preferred_element_type=jnp.float32)

    def backward(index, carry):
        part = pl.ds(index * CHUNK, CHUNK)
        weights = de_ref[pl.ds(rows + index * CHUNK, CHUNK), :].astype(jnp.float32)
        score_grad = weights * (s_ref[part, :] - row_ref[part, :1])
        acc_ref[part, :] += score_grad
        de_ref[part, :] = score_grad.astype(jnp.bfloat16)
        return carry

    lax.fori_loop(0, rows // CHUNK, backward, 0)
    query_part = jnp.dot(de_ref[:rows, :], kv, preferred_element_type=jnp.float32) * scaling
    merged = jnp.where(
        lane < 2 * head_width,
        jnp.where(lane < head_width, query_part[:queries], query_part[queries:]),
        jnp.where(lane < 3 * head_width, attended[:queries], attended[queries:]),
    )
    qa_ref[0] = merged.astype(jnp.bfloat16)
    sides = jnp.concatenate([query_rows, grad_scaled], axis=0)
    key_value = lax.dot_general(
        sides, de_ref[...], (((0,), (0,)), ((), ())), preferred_element_type=jnp.float32
    )
    dkv_ref[...] = key_value.T.astype(jnp.bfloat16).reshape(dkv_ref.shape)

    @pl.when(step == last)
    def _():
        width = dbias_ref.shape[2]
        for piece in range(dbias_ref.shape[0]):
            dbias_ref[piece] = acc_ref[:, piece * width : (piece + 1) * width].astype(jnp.bfloat16)


def attend(query_grad, key_value, bias, mask, row_count):
    columns, queries, lanes = query_grad.shape
    groups = key_value.shape[0]
    keys = bias.shape[1]
    rows = bias.shape[0]
    width = keys // row_count
    work = columns * rows * keys
    return pl.pallas_call(
        attention_kernel,
        grid=(columns,),
        in_specs=[
            pl.BlockSpec((1, queries, lanes), lambda j: (j, 0, 0)),
            pl.BlockSpec((groups, 1, queries, lanes), lambda j: (0, j, 0, 0)),
            pl.BlockSpec((rows, keys), lambda j: (0, 0)),
            pl.BlockSpec((1, 1, keys), lambda j: (j, 0, 0)),
        ],
        out_specs=[
            pl.BlockSpec((1, queries, lanes), lambda j: (j, 0, 0)),
            pl.BlockSpec((groups, 1, queries, lanes), lambda j: (0, j, 0, 0)),
            pl.BlockSpec((row_count, rows, width), lambda j: (0, 0, 0)),
        ],
        out_shape=[
            jax.ShapeDtypeStruct((columns, queries, lanes), jnp.bfloat16),
            jax.ShapeDtypeStruct((groups, columns, queries, lanes), jnp.bfloat16),
            jax.ShapeDtypeStruct((row_count, rows, width), jnp.bfloat16),
        ],
        scratch_shapes=[
            pltpu.VMEM((rows, keys), jnp.float32),
            pltpu.VMEM((rows, keys), jnp.float32),
            pltpu.VMEM((rows, keys), jnp.float32),
            pltpu.VMEM((2 * rows, keys), jnp.bfloat16),
            pltpu.VMEM((rows, 128), jnp.float32),
        ],
        compiler_params=pltpu.CompilerParams(vmem_limit_bytes=48 * 1024 * 1024),
        cost_estimate=pl.CostEstimate(flops=12 * 128 * work, bytes_accessed=16 * 2**20, transcendentals=work),
        name="attention_both",
    )(query_grad, key_value, bias, mask)


def local(
    query_vectors,
    key_vectors,
    value_vectors,
    gate_logits,
    pair_bias,
    pair_mask,
    output_weight,
    output_cotangent,
):
    columns, tokens, channels = query_vectors.shape
    half = channels // 2
    devices = lax.axis_size("col")
    row_count = lax.axis_size("row")
    chips = devices // 2
    core = lax.axis_index("col") % 2
    scaling = 1.0 / math.sqrt(channels // HEADS)
    swap = [(index, index ^ 1) for index in range(devices)]
    chip_groups = [[2 * chip + side for chip in range(chips)] for side in range(2)]
    keys = pair_bias.shape[2]

    def mine_other(array, axis):
        size = array.shape[axis] // 2
        low = lax.slice_in_dim(array, 0, size, axis=axis)
        high = lax.slice_in_dim(array, size, 2 * size, axis=axis)
        return jnp.where(core == 0, low, high), jnp.where(core == 0, high, low)

    def in_order(mine, other, axis):
        return jnp.where(
            core == 0,
            jnp.concatenate([mine, other], axis=axis),
            jnp.concatenate([other, mine], axis=axis),
        )

    def swapped(array):
        return lax.ppermute(array, "col", swap)

    bias_mine, bias_other = mine_other(pair_bias, 0)
    bias_pair = in_order(bias_mine, swapped(bias_other), 1).reshape(-1, keys)

    key_mine, key_other = mine_other(key_vectors, 2)
    value_mine, value_other = mine_other(value_vectors, 2)
    kv_mine = jnp.concatenate([key_mine, value_mine], axis=2)
    kv_other = swapped(jnp.concatenate([key_other, value_other], axis=2))
    mask_low = pair_mask.astype(jnp.bfloat16)
    kv_chip = in_order(kv_mine, kv_other, 1)
    mask_chip = in_order(mask_low, swapped(mask_low), 1)
    mask_rows = jnp.pad(mask_chip.reshape(-1, channels), ((0, 2), (0, 0)))
    payload = jnp.concatenate([kv_chip.reshape(-1, channels), mask_rows], axis=0)
    payload = jnp.broadcast_to(payload[None], (chips,) + payload.shape)
    gathered = lax.all_to_all(payload, "col", 0, 0, tiled=True, axis_index_groups=chip_groups)
    key_value = gathered[:, : columns * 2 * tokens].reshape(chips, columns, 2 * tokens, channels)
    mask_all = gathered[:, columns * 2 * tokens : -2].reshape(chips, columns, 2 * tokens)
    mask_all = jnp.transpose(mask_all, (1, 0, 2)).reshape(columns, 1, keys).astype(jnp.float32)

    regrouped = lax.all_to_all(output_cotangent, "col", split_axis=2, concat_axis=1, tiled=True)
    gated_grad = jnp.einsum(
        "jdi,ed->jie", regrouped, output_weight, preferred_element_type=jnp.float32
    )
    gate_sigma = jax.nn.sigmoid(gate_logits.astype(jnp.float32))
    attended_grad = (gated_grad * gate_sigma).astype(jnp.bfloat16)
    query_mine, query_other = mine_other(query_vectors, 2)
    grad_mine, grad_other = mine_other(attended_grad, 2)
    qd_mine = jnp.concatenate([query_mine, grad_mine], axis=2)
    qd_other = swapped(jnp.concatenate([query_other, grad_other], axis=2))
    query_grad = in_order(qd_mine, qd_other, 1)

    query_attended, kv_grads, bias_grads = attend(query_grad, key_value, bias_pair, mask_all, row_count)

    kv_parts = lax.all_to_all(kv_grads, "col", 0, 0, tiled=True, axis_index_groups=chip_groups)
    kv_sum = jnp.sum(kv_parts.astype(jnp.float32), axis=0).astype(jnp.bfloat16)
    kv_own, kv_away = mine_other(kv_sum, 1)
    kv_back = swapped(kv_away)
    key_gradient = in_order(kv_own[..., :half], kv_back[..., :half], 2)
    key_gradient = (key_gradient.astype(jnp.float32) * scaling).astype(jnp.bfloat16)
    value_gradient = in_order(kv_own[..., half:], kv_back[..., half:], 2)

    qa_own, qa_away = mine_other(query_attended, 1)
    qa_back = swapped(qa_away)
    query_gradient = in_order(qa_own[..., :half], qa_back[..., :half], 2)
    attended = in_order(qa_own[..., half:], qa_back[..., half:], 2).astype(jnp.float32)
    gate_gradient = (gated_grad * attended * gate_sigma * (1.0 - gate_sigma)).astype(jnp.bfloat16)

    bias_parts = lax.all_to_all(bias_grads, "row", 0, 0, tiled=True)
    bias_sum = jnp.sum(bias_parts.astype(jnp.float32), axis=0).astype(jnp.bfloat16)
    bias_sum = bias_sum.reshape(2, 2 * tokens, keys // row_count)
    bias_own, bias_away = mine_other(bias_sum, 1)
    bias_gradient = in_order(bias_own, swapped(bias_away), 0).astype(jnp.float32)
    return (query_gradient, key_gradient, value_gradient, gate_gradient, bias_gradient)


def solution(mesh):
    placed = (
        P("row", "col", None),
        P("row", "col", None),
        P("row", "col", None),
        P("row", "col", None),
        P(None, "col", None),
        P("row", "col"),
        P(),
        P("row", "col", None),
    )
    return jax.shard_map(
        local,
        mesh=mesh,
        in_specs=placed,
        out_specs=(
            P("row", "col", None),
            P("row", "col", None),
            P("row", "col", None),
            P("row", "col", None),
            P(None, "col", "row"),
        ),
        check_vma=False,
    )
```

time: 491 us -> 145 us (0.30)
  local copies, waits for them, and re-layouts: 131 us -> 14.2 us
  starting transfers between devices: 87.8 us -> 19.8 us
  other arithmetic: 75.7 us -> 10.3 us
  waiting for transfers between devices: 100 us -> 36.5 us
  matrix products: 43.6 us -> 0.21 us
  Pallas kernels: 0 us -> 37.6 us
  loops' own time: 13.5 us -> 0 us
  between operations: 14.1 us -> 0.88 us
    ppermute x77 -> x7, starting transfers between devices: 80.5 us -> 5.55 us  [swapped(): return lax.ppermute(array, 'col', swap)]
    unnamed x4 -> x0, waiting for transfers between devices: 66.4 us -> none
    convert_element_type x97 -> x4, other arithmetic: 67.8 us -> 3.15 us  [the longest x1 0.83 us: local(): in_order(bias_own, swapped(bias_away), 0).astype(jnp.float32)]
    dynamic_slice x96 -> x0, local copies, waits for them, and re-layouts: 48.2 us -> none  [the longest x32 18.5 us: one_block(): lax.dynamic_slice_in_dim(value_piece, block_offset, step_width, 1)]
    dot_general x128 -> x0, matrix products: 42.8 us -> none  [the longest x32 14 us: block_scores(): jnp.einsum('jihc,jkhc->jhik', query_heads, key_heads, preferred_element_t...]
    while x124 -> x0, local copies, waits for them, and re-layouts: 40.4 us -> none
    pallas_call x0 -> x1, Pallas kernels: none -> 37.6 us  [attend(): pl.pallas_call(attention_kernel, grid=(columns,), in_specs=[pl.BlockSpec(...]
    all_gather x2 -> x0, waiting for transfers between devices: 33.6 us -> none  [the longest x1 33.5 us: local(): lax.all_gather(value_vectors, 'col', axis=1, tiled=True)]
  transfers between devices with their start and end apart: 81 -> 10, of which waited for: 3 -> 7; matrix products, arithmetic and copies ran while one was open for 31% -> 11% of each run, Pallas kernels for 0% -> 0%
where the time goes in v1:
time: 145 us; the launch traced here: 144 us
  Pallas kernels  37.6 us (26%)
  waiting for transfers between devices  36.5 us (25%)
  blocking collectives  24.8 us (17%)
  starting transfers between devices  19.8 us (14%)
  local copies, waits for them, and re-layouts  14.2 us (10%)
  other arithmetic  10.3 us (7%)
    pallas_call x1, Pallas kernels, attend(): pl.pallas_call(attention_kernel, grid=(columns,), in_specs=[pl.BlockSpec(...  37.6 us
    all_to_all x1, blocking collectives, local(): bias_parts = lax.all_to_all(bias_grads, 'row', 0, 0, tiled=True)  24.8 us
    all_to_all x1, waiting for transfers between devices, local(): lax.all_to_all(kv_grads, 'col', 0, 0, tiled=True, axis_index_groups=chip_...  14.9 us
    all_to_all x1, waiting for transfers between devices, local(): lax.all_to_all(payload, 'col', 0, 0, tiled=True, axis_index_groups=chip_g...  13 us
    unnamed x13, local copies, waits for them, and re-layouts  6.28 us
    all_to_all x1, starting transfers between devices, local(): lax.all_to_all(output_cotangent, 'col', split_axis=2, concat_axis=1, tile...  6.24 us
    ppermute x7, starting transfers between devices, swapped(): return lax.ppermute(array, 'col', swap)  5.55 us
    all_to_all x1, waiting for transfers between devices, local(): lax.all_to_all(output_cotangent, 'col', split_axis=2, concat_axis=1, tile...  5.47 us
  transfers between devices with their start and end apart: 10, of which 7 were waited for; matrix products, arithmetic and copies ran while one was open for 11% of the time, Pallas kernels for 0%

profile of v1, /device:TPU:1, one launch (start us, length us, event | category | flops | bytes accessed | tf_op | source)
XLA Modules:
  0.0 144.4 jit_solution(6728450087209314448)
XLA Ops:
  0.6 0.7 convert_element_type.41
  1.3 1.4 collective-permute-start.2
  2.8 1.2 broadcast_select_fusion.6
  3.9 0.1 pad_maximum_fusion.1
  4.1 2.2 %copy.22 = bf16[4,8,1536]{1,0,2:T(4,128)(2,1)S(1)} copy(bf16[4,8,1536]{2,1,0:T(8,128)(2,1)} %param.15) | data formatting | bytes 196608 | tf_op args[7]
  6.3 2.3 %reshape.55 = bf16[16,2,1536]{2,1,0:T(2,128)(2,1)} reshape(bf16[1536,4,8]{2,1,0:T(4,128)(2,1)S(1)} %bitcast.22) | data formatting | bytes 196608
  8.6 6.2 %all-to-all-start = ((bf16[16,2,1536]{2,1,0:T(2,128)(2,1)}), bf16[16,2,1536]{2,1,0:T(2,128)(2,1)S(1)}, u32[]{:S(2)}, u32[]{:S(2)}) async-start(bf16[16,2,1536]{2,1,0:T(2,128)(2,1)} %reshape.55), calls=%async_computation | async-start | bytes 196608 | tf_op jit(solution)/shard_map/all_to_all | solution.py:190
  14.9 0.1 select_n.168
  15.0 0.2 maximum_select_fusion.2
  15.2 5.5 %all-to-all-done = bf16[16,2,1536]{2,1,0:T(2,128)(2,1)S(1)} async-done(((bf16[16,2,1536]{2,1,0:T(2,128)(2,1)}), bf16[16,2,1536]{2,1,0:T(2,128)(2,1)S(1)}, u32[]{:S(2)}, u32[]{:S(2)}) %all-to-all-start) | async-done | bytes 98336 | tf_op jit(solution)/shard_map/all_to_all | solution.py:190
  20.7 1.3 broadcast_in_dim.2
  22.0 4.4 %all-to-all-start.1 = ((bf16[8,776,128]{2,1,0:T(8,128)(2,1)}), bf16[8,776,128]{2,1,0:T(8,128)(2,1)}, u32[]{:S(2)}, u32[]{:S(2)}) async-start(bf16[8,776,128]{2,1,0:T(8,128)(2,1)} %broadcast_in_dim.2), calls=%async_computation.1 | async-start | bytes 3178496 | tf_op jit(solution)/shard_map/all_to_all | solution.py:185
  26.5 0.9 broadcast_select_fusion.1
  27.4 0.6 collective-permute-start.3
  27.9 1.8 %reshape.56 = bf16[1536,4,8]{2,1,0:T(4,128)(2,1)S(1)} reshape(bf16[16,2,1536]{2,1,0:T(2,128)(2,1)S(1)} %all-to-all-done) | data formatting | bytes 196608
  29.8 1.6 %copy.23 = bf16[4,8,16,96]{3,1,2,0:T(8,128)(2,1)S(1)} copy(bf16[4,8,16,96]{1,0,3,2:T(4,128)(2,1)S(1)} %bitcast.21) | data formatting | bytes 196608 | tf_op jit(solution)/shard_map/all_to_all | solution.py:190
  31.4 0.2 multiply_convert_fusion.2
  31.6 0.1 broadcast_select_fusion.10
  31.8 0.1 pad_maximum_fusion
  32.0 1.3 collective-permute-done
  33.2 0.2 maximum_select_fusion.1.qd_ref
  33.4 1.7 %maximum_select_fusion = bf16[2,192,1536]{2,1,0:T(8,128)(2,1)S(1)} fusion(bf16[2,96,1536]{2,1,0:T(8,128)(2,1)} %collective-permute-done.3, bf16[2,96,1536]{2,1,0:T(8,128)(2,1)S(1)} %copy-done.1, pred[]{:T(512)S(6)} %eq.4), kind=kLoop, calls=%fused_computation | loop fusion | flops 5308416 | bytes 2359297 | tf_op jit(solution)/shard_map/jit(_where)/select_n | solution.py:163
  35.1 13.0 %all-to-all-done.1 = bf16[8,776,128]{2,1,0:T(8,128)(2,1)} async-done(((bf16[8,776,128]{2,1,0:T(8,128)(2,1)}), bf16[8,776,128]{2,1,0:T(8,128)(2,1)}, u32[]{:S(2)}, u32[]{:S(2)}) %all-to-all-start.1) | async-done | bytes 1589280 | tf_op jit(solution)/shard_map/all_to_all | solution.py:185
  48.1 0.7 slice_convert_fusion
  49.0 2.7 %slice.106 = bf16[8,768,128]{2,1,0:T(8,128)(2,1)} slice(bf16[8,776,128]{2,1,0:T(8,128)(2,1)} %all-to-all-done.1), slice={[0:8], [0:768], [0:128]} | slice | bytes 3145728 | tf_op jit(solution)/shard_map/slice | solution.py:186
  51.7 37.6 %attention_both.1 = (bf16[4,192,128]{2,1,0:T(8,128)(2,1)S(1)}, bf16[8,4,192,128]{3,2,1,0:T(8,128)(2,1)}, bf16[8,384,192]{2,1,0:T(8,128)(2,1)S(1)}) custom-call(bf16[4,192,128]{2,1,0:T(8,128)(2,1)S(1)} %maximum_select_fusion.1.qd_ref, bf16[8,4,192,128]{3,2,1,0:T(8,128)(2,1)} %bitcast.23, bf16[384,1536]{1,0:T(8,128)(2,1)S(1)} %bitcast.20, ...), custom_call_target="tpu_custom_call" | custom-call | flops 3623878656 | bytes 16777216 | tf_op jit(solution)/shard_map/attention_both/pallas_call | solution.py:103
  89.3 1.5 %copy.26 = bf16[8,384,192]{1,2,0:T(8,128)(2,1)} copy(bf16[8,384,192]{2,1,0:T(8,128)(2,1)S(1)} %get-tuple-element.10) | data formatting | bytes 2359296 | tf_op jit(solution)/shard_map/attention_both/pallas_call | solution.py:103
  90.8 24.8 %all_to_all.33 = bf16[8,384,192]{1,2,0:T(8,128)(2,1)S(1)} all-to-all(bf16[8,384,192]{1,2,0:T(8,128)(2,1)} %copy.26), channel_id=1, replica_groups=mesh['row'=8,'col'=16] {'row'}, dimensions={0} | all-to-all | bytes 2359296 | tf_op jit(solution)/shard_map/all_to_all | solution.py:218
  115.6 3.6 %all-to-all-start.2 = ((bf16[8,4,192,128]{3,2,1,0:T(8,128)(2,1)}), bf16[8,4,192,128]{3,2,1,0:T(8,128)(2,1)S(1)}, u32[]{:S(2)}, u32[]{:S(2)}) async-start(bf16[8,4,192,128]{3,2,1,0:T(8,128)(2,1)} %get-tuple-element.9), calls=%async_computation.2 | async-start | bytes 3145728 | tf_op jit(solution)/shard_map/all_to_all | solution.py:204
  119.2 2.0 %collective-permute-start.4 = (bf16[4,96,128]{2,1,0:T(8,128)(2,1)S(1)}, bf16[4,96,128]{2,1,0:T(8,128)(2,1)S(1)}, u32[]{:S(2)}, u32[]{:S(2)}) collective-permute-start(bf16[4,96,128]{2,1,0:T(8,128)(2,1)S(1)} %get-tuple-element.18), channel_id=1, source_target_pairs={{0,1},{1,0},{2,3},{3,2},{4,5},{5,4},{6,7},{7,6},{8,9},{9,8},{10,11... | collective-permute-start | bytes 294920 | tf_op jit(solution)/shard_map/ppermute | solution.py:170
  121.3 0.1 fusion.6
  121.4 0.8 collective-permute-done.4
  122.2 0.1 fusion.7
  122.3 0.8 multiply_convert_fusion
  123.1 0.2 reduce_sum.25
  123.3 0.1 copy.30
  123.5 0.4 collective-permute-start.6
  123.9 0.8 maximum_select_fusion.4
  124.7 0.2 collective-permute-done.6
  124.9 0.8 fusion.2
  125.7 14.9 %all-to-all-done.2 = bf16[8,4,192,128]{3,2,1,0:T(8,128)(2,1)S(1)} async-done(((bf16[8,4,192,128]{3,2,1,0:T(8,128)(2,1)}), bf16[8,4,192,128]{3,2,1,0:T(8,128)(2,1)S(1)}, u32[]{:S(2)}, u32[]{:S(2)}) %all-to-all-start.2) | async-done | bytes 1572896 | tf_op jit(solution)/shard_map/all_to_all | solution.py:204
  140.6 0.3 reduce_sum.24
  140.9 0.9 collective-permute-start.5
  141.8 0.1 fusion.8
  141.9 0.8 collective-permute-done.5
  142.7 0.1 fusion.9
  142.8 0.8 maximum_select_fusion.6
  143.6 0.8 multiply_convert_fusion.1
  (23 shorter events, 0.5 us)
Async XLA Ops:
  0.6 30.7 %copy-start = (bf16[128,128]{1,0:T(8,128)(2,1)S(1)}, bf16[128,128]{1,0:T(8,128)(2,1)}, u32[]{:S(2)}) copy-start(bf16[128,128]{1,0:T(8,128)(2,1)} %param.14) | copy-start | bytes 98308
  1.3 13.5 %collective-permute-start.2 = (bf16[4,96]{1,0:T(4,128)(2,1)S(1)}, bf16[4,96]{1,0:T(4,128)(2,1)S(1)}, u32[]{:S(2)}, u32[]{:S(2)}) collective-permute-start(bf16[4,96]{1,0:T(4,128)(2,1)S(1)} %convert_element_type.41), channel_id=1, source_target_pairs={{0,1},{1,0},{2,3},{3,2},{4,5},{5,4},{6,7},{7,6},{8,9},{9,8},{10,11... | collective-permute-start | bytes 2312 | tf_op jit(solution)/shard_map/ppermute | solution.py:170
  4.0 11.0 %collective-permute-start.1 = (bf16[4,96,128]{2,1,0:T(8,128)(2,1)S(1)}, bf16[4,96,128]{2,1,0:T(8,128)(2,1)S(1)}, u32[]{:S(2)}, u32[]{:S(2)}) collective-permute-start(bf16[4,96,128]{2,1,0:T(8,128)(2,1)S(1)} %pad_maximum_fusion.1), channel_id=1, source_target_pairs={{0,1},{1,0},{2,3},{3,2},{4,5},{5,4},{6,7},{7,6},{8,9},{9,8},{10,11... | collective-permute-start | bytes 294920 | tf_op jit(solution)/shard_map/ppermute | solution.py:170
  8.6 12.1 %all-to-all-start = ((bf16[16,2,1536]{2,1,0:T(2,128)(2,1)}), bf16[16,2,1536]{2,1,0:T(2,128)(2,1)S(1)}, u32[]{:S(2)}, u32[]{:S(2)}) async-start(bf16[16,2,1536]{2,1,0:T(2,128)(2,1)} %reshape.55), calls=%async_computation | async-start | bytes 196608 | tf_op jit(solution)/shard_map/all_to_all | solution.py:190
  22.0 4.4 %copy-start.2 = (bf16[4,96,1536]{2,1,0:T(8,128)(2,1)S(1)}, bf16[4,96,1536]{2,1,0:T(8,128)(2,1)}, u32[]{:S(2)}) copy-start(bf16[4,96,1536]{2,1,0:T(8,128)(2,1)} %param.12) | copy-start | bytes 3538948
  22.0 26.1 %all-to-all-start.1 = ((bf16[8,776,128]{2,1,0:T(8,128)(2,1)}), bf16[8,776,128]{2,1,0:T(8,128)(2,1)}, u32[]{:S(2)}, u32[]{:S(2)}) async-start(bf16[8,776,128]{2,1,0:T(8,128)(2,1)} %broadcast_in_dim.2), calls=%async_computation.1 | async-start | bytes 3178496 | tf_op jit(solution)/shard_map/all_to_all | solution.py:185
  27.4 4.0 %copy-start.4 = (bf16[4,96,128]{2,1,0:T(8,128)(2,1)S(1)}, bf16[4,96,128]{2,1,0:T(8,128)(2,1)}, u32[]{:S(2)}) copy-start(bf16[4,96,128]{2,1,0:T(8,128)(2,1)} %param.11) | copy-start | bytes 294916
  27.4 6.0 %collective-permute-start.3 = (bf16[2,96,1536]{2,1,0:T(8,128)(2,1)S(1)}, bf16[2,96,1536]{2,1,0:T(8,128)(2,1)}, u32[]{:S(2)}, u32[]{:S(2)}) collective-permute-start(bf16[2,96,1536]{2,1,0:T(8,128)(2,1)S(1)} %get-tuple-element.12), channel_id=1, source_target_pairs={{0,1},{1,0},{2,3},{3,2},{4,5},{5,4},{6,7},{7,6},{8,9},{9,8},{10,11... | collective-permute-start | bytes 1769480 | tf_op jit(solution)/shard_map/ppermute | solution.py:170
  29.8 1.9 %copy-start.3 = (bf16[4,96,128]{2,1,0:T(8,128)(2,1)S(1)}, bf16[4,96,128]{2,1,0:T(8,128)(2,1)}, u32[]{:S(2)}) copy-start(bf16[4,96,128]{2,1,0:T(8,128)(2,1)} %param.8) | copy-start | bytes 294916
  31.4 2.0 %copy-start.1 = (bf16[2,96,1536]{2,1,0:T(8,128)(2,1)S(1)}, bf16[2,96,1536]{2,1,0:T(8,128)(2,1)}, u32[]{:S(2)}) copy-start(bf16[2,96,1536]{2,1,0:T(8,128)(2,1)} %get-tuple-element.11) | copy-start | bytes 1769476
  31.9 1.4 collective-permute-start
  115.6 24.9 %all-to-all-start.2 = ((bf16[8,4,192,128]{3,2,1,0:T(8,128)(2,1)}), bf16[8,4,192,128]{3,2,1,0:T(8,128)(2,1)S(1)}, u32[]{:S(2)}, u32[]{:S(2)}) async-start(bf16[8,4,192,128]{3,2,1,0:T(8,128)(2,1)} %get-tuple-element.9), calls=%async_computation.2 | async-start | bytes 3145728 | tf_op jit(solution)/shard_map/all_to_all | solution.py:204
  119.2 3.0 %collective-permute-start.4 = (bf16[4,96,128]{2,1,0:T(8,128)(2,1)S(1)}, bf16[4,96,128]{2,1,0:T(8,128)(2,1)S(1)}, u32[]{:S(2)}, u32[]{:S(2)}) collective-permute-start(bf16[4,96,128]{2,1,0:T(8,128)(2,1)S(1)} %get-tuple-element.18), channel_id=1, source_target_pairs={{0,1},{1,0},{2,3},{3,2},{4,5},{5,4},{6,7},{7,6},{8,9},{9,8},{10,11... | collective-permute-start | bytes 294920 | tf_op jit(solution)/shard_map/ppermute | solution.py:170
  123.5 1.4 collective-permute-start.6
  140.9 1.9 %collective-permute-start.5 = (bf16[4,96,128]{2,1,0:T(8,128)(2,1)S(1)}, bf16[4,96,128]{2,1,0:T(8,128)(2,1)S(1)}, u32[]{:S(2)}, u32[]{:S(2)}) collective-permute-start(bf16[4,96,128]{2,1,0:T(8,128)(2,1)S(1)} %get-tuple-element.16), channel_id=1, source_target_pairs={{0,1},{1,0},{2,3},{3,2},{4,5},{5,4},{6,7},{7,6},{8,9},{9,8},{10,11... | collective-permute-start | bytes 294920 | tf_op jit(solution)/shard_map/ppermute | solution.py:170

commit v2 on v1

--- a/solution.py
+++ b/solution.py
@@ -11,9 +11,10 @@
 NEG_FILL = -1000000000.0
 LOG2E = math.log2(math.e)
 CHUNK = 16
-
-
-def attention_kernel(qd_ref, kv_ref, bias_ref, mask_ref, qa_ref, dkv_ref, dbias_ref, s_ref, b2_ref, acc_ref, de_ref, row_ref):
+UNROLL = 12
+
+
+def attention_kernel(qd_ref, kv_ref, bias_ref, mask_ref, qa_ref, dkv_ref, dbias_ref, s_ref, b2_ref, acc_ref, dp_ref, de_ref, row_ref):
     step = pl.program_id(0)
     last = pl.num_programs(0) - 1
     rows = bias_ref.shape[0]
@@ -32,7 +33,7 @@
 
         lax.fori_loop(0, rows // CHUNK, fill, 0)
 
-    kv = kv_ref[...].reshape(keys, 4 * head_width)
+    kv = kv_ref[:, pl.ds(step * queries, queries), :].reshape(keys, 4 * head_width)
     qd = qd_ref[0]
     lane = lax.broadcasted_iota(jnp.int32, (queries, 4 * head_width), 1)
     zero = jnp.zeros_like(qd)
@@ -40,47 +41,74 @@
     def only(part):
         return jnp.where((lane >= part * head_width) & (lane < (part + 1) * head_width), qd, zero)
 
-    query_rows = jnp.concatenate([only(0), only(1)], axis=0)
-    grad_rows = jnp.concatenate([only(2), only(3)], axis=0)
     transposed = (((1,), (1,)), ((), ()))
-    s_ref[...] = lax.dot_general(query_rows, kv, transposed, preferred_element_type=jnp.float32)
     cap = jnp.where(mask_ref[0] > 0.5, 1e30, NEG_FILL * LOG2E)
-
-    def soften(index, carry):
-        part = pl.ds(index * CHUNK, CHUNK)
-        scores = jnp.minimum(s_ref[part, :] * (scaling * LOG2E) + b2_ref[part, :], cap)
-        weights = jnp.exp2(scores - jnp.max(scores, axis=1, keepdims=True))
-        row_ref[part, :] = jnp.broadcast_to(jnp.sum(weights, axis=1, keepdims=True), (CHUNK, 128))
-        de_ref[pl.ds(rows + index * CHUNK, CHUNK), :] = weights.astype(jnp.bfloat16)
-        return carry
-
-    lax.fori_loop(0, rows // CHUNK, soften, 0)
-    weights_low = de_ref[rows:, :]
-    inverse = 1.0 / row_ref[...]
-    attended = jnp.dot(weights_low, kv, preferred_element_type=jnp.float32) * inverse
-    grad_wide = grad_rows.astype(jnp.float32)
-    delta = jnp.sum(grad_wide * attended, axis=1, keepdims=True)
-    row_ref[...] = delta * inverse
-    grad_scaled = (grad_wide * inverse).astype(jnp.bfloat16)
-    s_ref[...] = lax.dot_general(grad_scaled, kv, transposed, preferred_element_type=jnp.float32)
-
-    def backward(index, carry):
-        part = pl.ds(index * CHUNK, CHUNK)
-        weights = de_ref[pl.ds(rows + index * CHUNK, CHUNK), :].astype(jnp.float32)
-        score_grad = weights * (s_ref[part, :] - row_ref[part, :1])
-        acc_ref[part, :] += score_grad
-        de_ref[part, :] = score_grad.astype(jnp.bfloat16)
-        return carry
-
-    lax.fori_loop(0, rows // CHUNK, backward, 0)
-    query_part = jnp.dot(de_ref[:rows, :], kv, preferred_element_type=jnp.float32) * scaling
+    query_rows = [only(0), only(1)]
+    grad_rows = [only(2), only(3)]
+
+    def scores_of(head):
+        s_ref[head * queries : (head + 1) * queries, :] = lax.dot_general(
+            query_rows[head], kv, transposed, preferred_element_type=jnp.float32
+        )
+
+    def soften(head):
+        def one(index, carry):
+            start = head * queries + index * CHUNK
+            part = pl.ds(start, CHUNK)
+            scores = jnp.minimum(s_ref[part, :] * (scaling * LOG2E) + b2_ref[part, :], cap)
+            weights = jnp.exp2(scores - jnp.max(scores, axis=1, keepdims=True))
+            row_ref[part, :] = jnp.broadcast_to(jnp.sum(weights, axis=1, keepdims=True), (CHUNK, 128))
+            de_ref[pl.ds(rows + start, CHUNK), :] = weights.astype(jnp.bfloat16)
+            return carry
+
+        lax.fori_loop(0, queries // CHUNK, one, 0, unroll=UNROLL)
+
+    def cotangents(head):
+        part = slice(head * queries, (head + 1) * queries)
+        weights_low = de_ref[rows + head * queries : rows + (head + 1) * queries, :]
+        inverse = 1.0 / row_ref[part, :]
+        attended = jnp.dot(weights_low, kv, preferred_element_type=jnp.float32) * inverse
+        grad_wide = grad_rows[head].astype(jnp.float32)
+        delta = jnp.sum(grad_wide * attended, axis=1, keepdims=True)
+        row_ref[part, :] = delta * inverse
+        grad_scaled = (grad_wide * inverse).astype(jnp.bfloat16)
+        dp_ref[part, :] = lax.dot_general(grad_scaled, kv, transposed, preferred_element_type=jnp.float32)
+        return attended, grad_scaled
+
+    def backward(head):
+        def one(index, carry):
+            start = head * queries + index * CHUNK
+            part = pl.ds(start, CHUNK)
+            weights = de_ref[pl.ds(rows + start, CHUNK), :].astype(jnp.float32)
+            score_grad = weights * (dp_ref[part, :] - row_ref[part, :1])
+            acc_ref[part, :] += score_grad
+            de_ref[part, :] = score_grad.astype(jnp.bfloat16)
+            return carry
+
+        lax.fori_loop(0, queries // CHUNK, one, 0, unroll=UNROLL)
+
+    def query_of(head):
+        return jnp.dot(
+            de_ref[head * queries : (head + 1) * queries, :], kv, preferred_element_type=jnp.float32
+        ) * scaling
+
+    scores_of(0)
+    scores_of(1)
+    soften(0)
+    att0, sc0 = cotangents(0)
+    soften(1)
+    att1, sc1 = cotangents(1)
+    backward(0)
+    q0 = query_of(0)
+    backward(1)
+    q1 = query_of(1)
     merged = jnp.where(
         lane < 2 * head_width,
-        jnp.where(lane < head_width, query_part[:queries], query_part[queries:]),
-        jnp.where(lane < 3 * head_width, attended[:queries], attended[queries:]),
+        jnp.where(lane < head_width, q0, q1),
+        jnp.where(lane < 3 * head_width, att0, att1),
     )
     qa_ref[0] = merged.astype(jnp.bfloat16)
-    sides = jnp.concatenate([query_rows, grad_scaled], axis=0)
+    sides = jnp.concatenate(query_rows + [sc0, sc1], axis=0)
     key_value = lax.dot_general(
         sides, de_ref[...], (((0,), (0,)), ((), ())), preferred_element_type=jnp.float32
     )
@@ -91,6 +119,48 @@
         width = dbias_ref.shape[2]
         for piece in range(dbias_ref.shape[0]):
             dbias_ref[piece] = acc_ref[:, piece * width : (piece + 1) * width].astype(jnp.bfloat16)
+
+
+def pack_kernel(cotangent_ref, packed_ref):
+    width = cotangent_ref.shape[2] // packed_ref.shape[0]
+    rows = packed_ref.shape[1]
+    whole = cotangent_ref[...].astype(jnp.float32).reshape(rows, cotangent_ref.shape[2])
+    filler = jnp.zeros((rows, packed_ref.shape[2] - width), jnp.float32)
+    for piece in range(packed_ref.shape[0]):
+        part = whole[:, piece * width : (piece + 1) * width]
+        packed_ref[piece] = jnp.concatenate([part, filler], axis=1).astype(jnp.bfloat16)
+
+
+def pack(cotangent, pieces):
+    return pl.pallas_call(
+        pack_kernel,
+        out_shape=jax.ShapeDtypeStruct((pieces, cotangent.shape[0] * cotangent.shape[1], 128), jnp.bfloat16),
+        name="pack_cotangent",
+    )(cotangent)
+
+
+def project_kernel(packed_ref, weight_ref, gate_ref, grad_ref, slope_ref):
+    pieces, rows, lanes = packed_ref.shape
+    columns, tokens, channels = gate_ref.shape
+    whole = packed_ref[...].astype(jnp.float32).reshape(pieces, columns, rows // columns, lanes)
+    for column in range(columns):
+        part = whole[:, column].reshape(channels, lanes).astype(jnp.bfloat16)
+        gated = jnp.dot(weight_ref[...], part, preferred_element_type=jnp.float32).T[:tokens]
+        sigma = jax.nn.sigmoid(gate_ref[column].astype(jnp.float32))
+        grad = gated * sigma
+        grad_ref[column] = grad.astype(jnp.bfloat16)
+        slope_ref[column] = grad * (1.0 - sigma)
+
+
+def project(packed, weight, gate):
+    return pl.pallas_call(
+        project_kernel,
+        out_shape=[
+            jax.ShapeDtypeStruct(gate.shape, jnp.bfloat16),
+            jax.ShapeDtypeStruct(gate.shape, jnp.float32),
+        ],
+        name="project_cotangent",
+    )(packed, weight, gate)
 
 
 def attend(query_grad, key_value, bias, mask, row_count):
@@ -105,7 +175,7 @@
         grid=(columns,),
         in_specs=[
             pl.BlockSpec((1, queries, lanes), lambda j: (j, 0, 0)),
-            pl.BlockSpec((groups, 1, queries, lanes), lambda j: (0, j, 0, 0)),
+            pl.BlockSpec((groups,) + key_value.shape[1:], lambda j: (0, 0, 0)),
             pl.BlockSpec((rows, keys), lambda j: (0, 0)),
             pl.BlockSpec((1, 1, keys), lambda j: (j, 0, 0)),
         ],
@@ -120,6 +190,7 @@
             jax.ShapeDtypeStruct((row_count, rows, width), jnp.bfloat16),
         ],
         scratch_shapes=[
+            pltpu.VMEM((rows, keys), jnp.float32),
             pltpu.VMEM((rows, keys), jnp.float32),
             pltpu.VMEM((rows, keys), jnp.float32),
             pltpu.VMEM((rows, keys), jnp.float32),
@@ -183,23 +254,18 @@
     payload = jnp.concatenate([kv_chip.reshape(-1, channels), mask_rows], axis=0)
     payload = jnp.broadcast_to(payload[None], (chips,) + payload.shape)
     gathered = lax.all_to_all(payload, "col", 0, 0, tiled=True, axis_index_groups=chip_groups)
-    key_value = gathered[:, : columns * 2 * tokens].reshape(chips, columns, 2 * tokens, channels)
     mask_all = gathered[:, columns * 2 * tokens : -2].reshape(chips, columns, 2 * tokens)
     mask_all = jnp.transpose(mask_all, (1, 0, 2)).reshape(columns, 1, keys).astype(jnp.float32)
 
-    regrouped = lax.all_to_all(output_cotangent, "col", split_axis=2, concat_axis=1, tiled=True)
-    gated_grad = jnp.einsum(
-        "jdi,ed->jie", regrouped, output_weight, preferred_element_type=jnp.float32
-    )
-    gate_sigma = jax.nn.sigmoid(gate_logits.astype(jnp.float32))
-    attended_grad = (gated_grad * gate_sigma).astype(jnp.bfloat16)
+    regrouped = lax.all_to_all(pack(output_cotangent, devices), "col", 0, 0, tiled=True)
+    attended_grad, gate_slope = project(regrouped, output_weight, gate_logits)
     query_mine, query_other = mine_other(query_vectors, 2)
     grad_mine, grad_other = mine_other(attended_grad, 2)
     qd_mine = jnp.concatenate([query_mine, grad_mine], axis=2)
     qd_other = swapped(jnp.concatenate([query_other, grad_other], axis=2))
     query_grad = in_order(qd_mine, qd_other, 1)
 
-    query_attended, kv_grads, bias_grads = attend(query_grad, key_value, bias_pair, mask_all, row_count)
+    query_attended, kv_grads, bias_grads = attend(query_grad, gathered, bias_pair, mask_all, row_count)
 
     kv_parts = lax.all_to_all(kv_grads, "col", 0, 0, tiled=True, axis_index_groups=chip_groups)
     kv_sum = jnp.sum(kv_parts.astype(jnp.float32), axis=0).astype(jnp.bfloat16)
@@ -213,10 +279,22 @@
     qa_back = swapped(qa_away)
     query_gradient = in_order(qa_own[..., :half], qa_back[..., :half], 2)
     attended = in_order(qa_own[..., half:], qa_back[..., half:], 2).astype(jnp.float32)
-    gate_gradient = (gated_grad * attended * gate_sigma * (1.0 - gate_sigma)).astype(jnp.bfloat16)
-
-    bias_parts = lax.all_to_all(bias_grads, "row", 0, 0, tiled=True)
-    bias_sum = jnp.sum(bias_parts.astype(jnp.float32), axis=0).astype(jnp.bfloat16)
+    gate_gradient = (gate_slope * attended).astype(jnp.bfloat16)
+
+    place = lax.axis_index("row")
+    high_step = row_count // 2
+    bias_sum = lax.dynamic_index_in_dim(bias_grads, place, 0, keepdims=False).astype(jnp.float32)
+    for high in range(2):
+        for low in range(high_step):
+            if high or low:
+                pairs = [
+                    (index, ((index // high_step + high) % 2) * high_step + (index + low) % high_step)
+                    for index in range(row_count)
+                ]
+                target = ((place // high_step + high) % 2) * high_step + (place + low) % high_step
+                part = lax.dynamic_index_in_dim(bias_grads, target, 0, keepdims=False)
+                bias_sum = bias_sum + lax.ppermute(part, "row", pairs).astype(jnp.float32)
+    bias_sum = bias_sum.astype(jnp.bfloat16)
     bias_sum = bias_sum.reshape(2, 2 * tokens, keys // row_count)
     bias_own, bias_away = mine_other(bias_sum, 1)
     bias_gradient = in_order(bias_own, swapped(bias_away), 0).astype(jnp.float32)

time: 145 us -> 109 us (0.75)
  blocking collectives: 24.8 us -> 0 us
  Pallas kernels: 37.6 us -> 15.8 us
  starting transfers between devices: 19.8 us -> 33.8 us
  local copies, waits for them, and re-layouts: 14.2 us -> 3.07 us
  waiting for transfers between devices: 36.5 us -> 42.7 us
  other arithmetic: 10.3 us -> 11.9 us
    pallas_call x1, Pallas kernels: 37.6 us -> 12.2 us  [attend(): pl.pallas_call(attention_kernel, grid=(columns,), in_specs=[pl.BlockSpec(...]
    all_to_all x1 -> x0, blocking collectives: 24.8 us -> none  [local(): bias_parts = lax.all_to_all(bias_grads, 'row', 0, 0, tiled=True)]
    ppermute x0 -> x7, waiting for transfers between devices: none -> 18.9 us  [local(): bias_sum = bias_sum + lax.ppermute(part, 'row', pairs).astype(jnp.float32)]
    all_to_all x1, waiting for transfers between devices: 14.9 us -> 0.01 us  [local(): lax.all_to_all(kv_grads, 'col', 0, 0, tiled=True, axis_index_groups=chip_...]
    ppermute x0 -> x7, starting transfers between devices: none -> 14.1 us  [local(): bias_sum = bias_sum + lax.ppermute(part, 'row', pairs).astype(jnp.float32)]
    unnamed x13 -> x6, local copies, waits for them, and re-layouts: 6.28 us -> 0.01 us
    pallas_call x0 -> x2, Pallas kernels: none -> 3.62 us  [the longest x1 1.95 us: project(): pl.pallas_call(project_kernel, out_shape=[jax.ShapeDtypeStruct(gate.shape...]
    all_to_all x1, waiting for transfers between devices: 13 us -> 15.9 us  [local(): lax.all_to_all(payload, 'col', 0, 0, tiled=True, axis_index_groups=chip_g...]
  transfers between devices with their start and end apart: 10 -> 17, of which waited for: 7 -> 8; matrix products, arithmetic and copies ran while one was open for 11% -> 8% of each run, Pallas kernels for 0% -> 3%
where the time goes in v2:
time: 109 us; the launch traced here: 108 us
  waiting for transfers between devices  42.7 us (39%)
  starting transfers between devices  33.8 us (31%)
  Pallas kernels  15.8 us (14%)
  other arithmetic  11.9 us (11%)
  local copies, waits for them, and re-layouts  3.07 us (3%)
    ppermute x7, waiting for transfers between devices, local(): bias_sum = bias_sum + lax.ppermute(part, 'row', pairs).astype(jnp.float32)  18.9 us
    all_to_all x1, waiting for transfers between devices, local(): lax.all_to_all(payload, 'col', 0, 0, tiled=True, axis_index_groups=chip_g...  15.9 us
    ppermute x7, starting transfers between devices, local(): bias_sum = bias_sum + lax.ppermute(part, 'row', pairs).astype(jnp.float32)  14.1 us
    pallas_call x1, Pallas kernels, attend(): pl.pallas_call(attention_kernel, grid=(columns,), in_specs=[pl.BlockSpec(...  12.2 us
    all_to_all x1, starting transfers between devices, local(): lax.all_to_all(pack(output_cotangent, devices), 'col', 0, 0, tiled=True)  6.24 us
    all_to_all x1, waiting for transfers between devices, local(): lax.all_to_all(pack(output_cotangent, devices), 'col', 0, 0, tiled=True)  5.71 us
    ppermute x7, starting transfers between devices, swapped(): return lax.ppermute(array, 'col', swap)  5.14 us
    all_to_all x1, starting transfers between devices, local(): lax.all_to_all(payload, 'col', 0, 0, tiled=True, axis_index_groups=chip_g...  4.42 us
  transfers between devices with their start and end apart: 17, of which 8 were waited for; matrix products, arithmetic and copies ran while one was open for 8% of the time, Pallas kernels for 3%

profile of v2, /device:TPU:1, one launch (start us, length us, event | category | flops | bytes accessed | tf_op | source)
XLA Modules:
  0.0 108.2 jit_solution(9655258261268144671)
XLA Ops:
  0.6 0.7 convert_element_type.61
  1.3 1.4 %collective-permute-start.2 = (bf16[4,96]{1,0:T(4,128)(2,1)S(1)}, bf16[4,96]{1,0:T(4,128)(2,1)S(1)}, u32[]{:S(2)}, u32[]{:S(2)}) collective-permute-start(bf16[4,96]{1,0:T(4,128)(2,1)S(1)} %convert_element_type.61), channel_id=1, source_target_pairs={{0,1},{1,0},{2,3},{3,2},{4,5},{5,4},{6,7},{7,6},{8,9},{9,8},{10,11... | collective-permute-start | bytes 2312 | tf_op jit(solution)/shard_map/ppermute | solution.py:241
  2.7 1.2 %broadcast_select_fusion.6 = (bf16[4,96,64]{2,1,0:T(8,128)(2,1)S(1)}, bf16[4,96,64]{2,1,0:T(8,128)(2,1)S(1)}, bf16[4,96,64]{2,1,0:T(8,128)(2,1)S(1)}, bf16[4,96,64]{2,1,0:T(8,128)(2,1)S(1)}) fusion(pred[]{:T(512)S(6)} %eq.18, bf16[4,96,128]{2,1,0:T(8,128)(2,1)} %param.10, bf16[4,96,128]{2,1,0:T(8,128)(2,1)} %param.9), kind=kLoop, calls=%fused_computation.37 | loop fusion | flops 98304 | bytes 393217 | tf_op jit(solution)/shard_map/jit(_where)/select_n | solution.py:231
  3.9 0.1 pad_maximum_fusion.1
  4.1 1.7 %pack_cotangent.1 = bf16[16,32,128]{2,1,0:T(8,128)(2,1)} custom-call(bf16[4,8,1536]{2,1,0:T(8,128)(2,1)} %cotangent_ref.1), custom_call_target="tpu_custom_call" | custom-call | tf_op jit(solution)/shard_map/pack_cotangent/pallas_call | solution.py:135
  5.8 6.2 %all-to-all-start = ((bf16[16,32,128]{2,1,0:T(8,128)(2,1)}), bf16[16,32,128]{2,1,0:T(8,128)(2,1)S(1)}, u32[]{:S(2)}, u32[]{:S(2)}) async-start(bf16[16,32,128]{2,1,0:T(8,128)(2,1)} %pack_cotangent.1), calls=%async_computation | async-start | bytes 262144 | tf_op jit(solution)/shard_map/all_to_all | solution.py:260
  12.2 0.2 maximum_select_fusion.2
  12.4 5.7 %all-to-all-done.packed_ref = bf16[16,32,128]{2,1,0:T(8,128)(2,1)S(1)} async-done(((bf16[16,32,128]{2,1,0:T(8,128)(2,1)}), bf16[16,32,128]{2,1,0:T(8,128)(2,1)S(1)}, u32[]{:S(2)}, u32[]{:S(2)}) %all-to-all-start) | async-done | bytes 131104 | tf_op jit(solution)/shard_map/all_to_all | solution.py:260
  18.1 1.4 %broadcast_in_dim.2 = bf16[8,776,128]{2,1,0:T(8,128)(2,1)} broadcast(bf16[776,128]{1,0:T(8,128)(2,1)S(1)} %fusion.8), dimensions={1,2} | broadcast | bytes 1787904 | tf_op jit(solution)/shard_map/broadcast_in_dim | solution.py:255
  19.5 4.4 %all-to-all-start.1 = ((bf16[8,776,128]{2,1,0:T(8,128)(2,1)}), bf16[8,776,128]{2,1,0:T(8,128)(2,1)}, u32[]{:S(2)}, u32[]{:S(2)}) async-start(bf16[8,776,128]{2,1,0:T(8,128)(2,1)} %broadcast_in_dim.2), calls=%async_computation.1 | async-start | bytes 3178496 | tf_op jit(solution)/shard_map/all_to_all | solution.py:256
  24.0 0.6 collective-permute-start.3
  24.6 2.0 %project_cotangent.1 = (bf16[4,96,128]{2,1,0:T(8,128)(2,1)}, f32[4,96,128]{2,1,0:T(8,128)}) custom-call(bf16[16,32,128]{2,1,0:T(8,128)(2,1)} %copy-done.1, bf16[128,128]{1,0:T(8,128)(2,1)} %weight_ref.1, bf16[4,96,128]{2,1,0:T(8,128)(2,1)} %gate_ref.1), custom_call_target="tpu_custom_call" | custom-call | tf_op jit(solution)/shard_map/project_cotangent/pallas_call | solution.py:156
  26.5 1.1 %broadcast_select_fusion.10 = (bf16[4,96,64]{2,1,0:T(8,128)(2,1)S(1)}, bf16[4,96,64]{2,1,0:T(8,128)(2,1)S(1)}, bf16[4,96,64]{2,1,0:T(8,128)(2,1)S(1)}, bf16[4,96,64]{2,1,0:T(8,128)(2,1)S(1)}) fusion(pred[]{:T(512)S(6)} %eq.18, bf16[4,96,128]{2,1,0:T(8,128)(2,1)} %get-tuple-element.10, bf16[4,96,128]{2,1,0:T(8,128)(2,1)S(1)} %copy-done.2), kind=kLoop, calls=%fused_computation.41 | loop fusion | flops 98304 | bytes 393217 | tf_op jit(solution)/shard_map/jit(_where)/select_n | solution.py:231
  27.6 0.1 pad_maximum_fusion
  27.7 0.1 collective-permute-start
  27.9 1.2 %collective-permute-done = bf16[4,96,128]{2,1,0:T(8,128)(2,1)S(1)} collective-permute-done((bf16[4,96,128]{2,1,0:T(8,128)(2,1)S(1)}, bf16[4,96,128]{2,1,0:T(8,128)(2,1)S(1)}, u32[]{:S(2)}, u32[]{:S(2)}) %collective-permute-start) | collective-permute-done | bytes 98336 | tf_op jit(solution)/shard_map/ppermute | solution.py:241
  29.1 0.2 maximum_select_fusion.1.qd_ref
  29.3 0.4 maximum_select_fusion
  29.7 15.9 %all-to-all-done.1.kv_ref = bf16[8,776,128]{2,1,0:T(8,128)(2,1)} async-done(((bf16[8,776,128]{2,1,0:T(8,128)(2,1)}), bf16[8,776,128]{2,1,0:T(8,128)(2,1)}, u32[]{:S(2)}, u32[]{:S(2)}) %all-to-all-start.1) | async-done | bytes 1589280 | tf_op jit(solution)/shard_map/all_to_all | solution.py:256
  45.6 0.7 slice_convert_fusion
  46.5 12.2 %attention_both.1 = (bf16[4,192,128]{2,1,0:T(8,128)(2,1)S(1)}, bf16[8,4,192,128]{3,2,1,0:T(8,128)(2,1)}, bf16[8,384,192]{2,1,0:T(8,128)(2,1)S(1)}) custom-call(bf16[4,192,128]{2,1,0:T(8,128)(2,1)S(1)} %maximum_select_fusion.1.qd_ref, bf16[8,776,128]{2,1,0:T(8,128)(2,1)} %all-to-all-done.1.kv_ref, bf16[384,1536]{1,0:T(8,128)(2,1)S(1)} %bitcast.21, ...), custom_call_target="tpu_custom_call" | custom-call | flops 3623878656 | bytes 16777216 | tf_op jit(solution)/shard_map/attention_both/pallas_call | solution.py:173
  58.7 1.0 dynamic-slice_bitcast_fusion.6
  59.8 4.3 %collective-permute-start.10 = (bf16[384,192]{1,0:T(8,128)(2,1)}, bf16[384,192]{1,0:T(8,128)(2,1)}, u32[]{:S(2)}, u32[]{:S(2)}) collective-permute-start(bf16[384,192]{1,0:T(8,128)(2,1)} %get-tuple-element.18), channel_id=1, source_target_pairs={{0,80},{16,96},{32,112},{48,64},{64,16},{80,32},{96,48},{112,0},{1... | collective-permute-start | bytes 442376 | tf_op jit(solution)/shard_map/ppermute | solution.py:296
  64.1 2.0 %collective-permute-start.11 = (bf16[384,192]{1,0:T(8,128)(2,1)}, bf16[384,192]{1,0:T(8,128)(2,1)}, u32[]{:S(2)}, u32[]{:S(2)}) collective-permute-start(bf16[384,192]{1,0:T(8,128)(2,1)} %get-tuple-element.17), channel_id=1, source_target_pairs={{0,96},{16,112},{32,64},{48,80},{64,32},{80,48},{96,0},{112,16},{1... | collective-permute-start | bytes 442376 | tf_op jit(solution)/shard_map/ppermute | solution.py:296
  66.1 4.1 %collective-permute-start.12 = (bf16[384,192]{1,0:T(8,128)(2,1)}, bf16[384,192]{1,0:T(8,128)(2,1)}, u32[]{:S(2)}, u32[]{:S(2)}) collective-permute-start(bf16[384,192]{1,0:T(8,128)(2,1)} %get-tuple-element.16), channel_id=1, source_target_pairs={{0,112},{16,64},{32,80},{48,96},{64,48},{80,0},{96,16},{112,32},{1... | collective-permute-start | bytes 442376 | tf_op jit(solution)/shard_map/ppermute | solution.py:296
  70.2 0.4 collective-permute-start.6
  70.6 0.7 broadcast_select_fusion.15
  71.2 1.9 %collective-permute-start.4 = (bf16[4,96,128]{2,1,0:T(8,128)(2,1)}, bf16[4,96,128]{2,1,0:T(8,128)(2,1)S(1)}, u32[]{:S(2)}, u32[]{:S(2)}) collective-permute-start(bf16[4,96,128]{2,1,0:T(8,128)(2,1)} %get-tuple-element.29), channel_id=1, source_target_pairs={{0,1},{1,0},{2,3},{3,2},{4,5},{5,4},{6,7},{7,6},{8,9},{9,8},{10,11... | collective-permute-start | bytes 294920 | tf_op jit(solution)/shard_map/ppermute | solution.py:241
  73.1 3.8 %all-to-all-start.2 = ((bf16[8,4,192,128]{3,2,1,0:T(8,128)(2,1)}), bf16[8,4,192,128]{3,2,1,0:T(8,128)(2,1)S(1)}, u32[]{:S(2)}, u32[]{:S(2)}) async-start(bf16[8,4,192,128]{3,2,1,0:T(8,128)(2,1)} %get-tuple-element.12), calls=%async_computation.2 | async-start | bytes 3145728 | tf_op jit(solution)/shard_map/all_to_all | solution.py:270
  77.0 0.1 fusion.10
  77.1 0.4 collective-permute-start.7
  77.5 0.1 fusion.11
  77.6 2.0 %collective-permute-start.8 = (bf16[384,192]{1,0:T(8,128)(2,1)}, bf16[384,192]{1,0:T(8,128)(2,1)S(1)}, u32[]{:S(2)}, u32[]{:S(2)}) collective-permute-start(bf16[384,192]{1,0:T(8,128)(2,1)} %get-tuple-element.20), channel_id=1, source_target_pairs={{0,48},{16,0},{32,16},{48,32},{64,112},{80,64},{96,80},{112,96},{1... | collective-permute-start | bytes 442376 | tf_op jit(solution)/shard_map/ppermute | solution.py:296
  79.6 0.9 collective-permute-start.9
  80.5 1.7 %multiply_convert_fusion = bf16[4,96,128]{2,1,0:T(8,128)(2,1)} fusion(f32[4,96,128]{2,1,0:T(8,128)} %get-tuple-element.13, bf16[4,96,64]{2,1,0:T(8,128)(2,1)S(1)} %get-tuple-element.32, bf16[4,96,64]{2,1,0:T(8,128)(2,1)S(1)} %get-tuple-element.30, pred[]{:T(512)S(6)} %eq.18), kind=kLoop, calls=%fused_computation.25 | loop fusion | flops 589824 | bytes 393217 | tf_op jit(solution)/shard_map/convert_element_type | solution.py:282
  82.2 3.5 %collective-permute-done.7 = bf16[384,192]{1,0:T(8,128)(2,1)S(1)} collective-permute-done((bf16[384,192]{1,0:T(8,128)(2,1)}, bf16[384,192]{1,0:T(8,128)(2,1)S(1)}, u32[]{:S(2)}, u32[]{:S(2)}) %collective-permute-start.7) | collective-permute-done | bytes 147488 | tf_op jit(solution)/shard_map/ppermute | solution.py:296
  85.7 3.5 %collective-permute-done.8 = bf16[384,192]{1,0:T(8,128)(2,1)S(1)} collective-permute-done((bf16[384,192]{1,0:T(8,128)(2,1)}, bf16[384,192]{1,0:T(8,128)(2,1)S(1)}, u32[]{:S(2)}, u32[]{:S(2)}) %collective-permute-start.8) | collective-permute-done | bytes 147488 | tf_op jit(solution)/shard_map/ppermute | solution.py:296
  89.2 11.9 %collective-permute-done.9 = bf16[384,192]{1,0:T(8,128)(2,1)S(1)} collective-permute-done((bf16[384,192]{1,0:T(8,128)(2,1)S(1)}, bf16[384,192]{1,0:T(8,128)(2,1)S(1)}, u32[]{:S(2)}, u32[]{:S(2)}) %collective-permute-start.9) | collective-permute-done | bytes 147488 | tf_op jit(solution)/shard_map/ppermute | solution.py:296
  101.1 1.4 %fusion.7 = bf16[384,192]{1,0:T(8,128)(2,1)S(1)} fusion(bf16[384,192]{1,0:T(8,128)(2,1)} %collective-permute-done.12, bf16[384,192]{1,0:T(8,128)(2,1)} %collective-permute-done.11, bf16[384,192]{1,0:T(8,128)(2,1)} %collective-permute-done.10, bf16[384,192]{1,0:T(8,128)(2,1)S(1)} %collective-permute-done.9, bf16[384,192]{1,0:T(8,128)(2,1)S(1)} %collective-permute-done.8, ...), kind=kLoop, calls=%fused_computation.12 | loop fusion | flops 1179648 | bytes 1327108 | tf_op jit(solution)/shard_map/convert_element_type | solution.py:297
  102.5 0.6 collective-permute-start.13
  103.2 0.8 maximum_select_fusion.4
  103.9 0.2 collective-permute-done.13
  104.1 0.8 fusion.9
  104.9 0.3 reduce_sum.12
  105.2 0.4 collective-permute-start.5
  105.8 0.8 collective-permute-done.5
  106.7 0.8 maximum_select_fusion.6
  107.5 0.8 multiply_convert_fusion.1
  (27 shorter events, 0.8 us)
Async XLA Ops:
  1.3 10.7 %collective-permute-start.2 = (bf16[4,96]{1,0:T(4,128)(2,1)S(1)}, bf16[4,96]{1,0:T(4,128)(2,1)S(1)}, u32[]{:S(2)}, u32[]{:S(2)}) collective-permute-start(bf16[4,96]{1,0:T(4,128)(2,1)S(1)} %convert_element_type.61), channel_id=1, source_target_pairs={{0,1},{1,0},{2,3},{3,2},{4,5},{5,4},{6,7},{7,6},{8,9},{9,8},{10,11... | collective-permute-start | bytes 2312 | tf_op jit(solution)/shard_map/ppermute | solution.py:241
  4.0 8.2 %collective-permute-start.1 = (bf16[4,96,128]{2,1,0:T(8,128)(2,1)S(1)}, bf16[4,96,128]{2,1,0:T(8,128)(2,1)S(1)}, u32[]{:S(2)}, u32[]{:S(2)}) collective-permute-start(bf16[4,96,128]{2,1,0:T(8,128)(2,1)S(1)} %pad_maximum_fusion.1), channel_id=1, source_target_pairs={{0,1},{1,0},{2,3},{3,2},{4,5},{5,4},{6,7},{7,6},{8,9},{9,8},{10,11... | collective-permute-start | bytes 294920 | tf_op jit(solution)/shard_map/ppermute | solution.py:241
  5.8 12.3 %all-to-all-start = ((bf16[16,32,128]{2,1,0:T(8,128)(2,1)}), bf16[16,32,128]{2,1,0:T(8,128)(2,1)S(1)}, u32[]{:S(2)}, u32[]{:S(2)}) async-start(bf16[16,32,128]{2,1,0:T(8,128)(2,1)} %pack_cotangent.1), calls=%async_computation | async-start | bytes 262144 | tf_op jit(solution)/shard_map/all_to_all | solution.py:260
  18.1 1.4 %copy-start.1 = (bf16[16,32,128]{2,1,0:T(8,128)(2,1)}, bf16[16,32,128]{2,1,0:T(8,128)(2,1)S(1)}, u32[]{:S(2)}) copy-start(bf16[16,32,128]{2,1,0:T(8,128)(2,1)S(1)} %all-to-all-done.packed_ref) | copy-start | bytes 393220
  19.5 4.4 %copy-start = (bf16[4,96,1536]{2,1,0:T(8,128)(2,1)S(1)}, bf16[4,96,1536]{2,1,0:T(8,128)(2,1)}, u32[]{:S(2)}) copy-start(bf16[4,96,1536]{2,1,0:T(8,128)(2,1)} %param.12) | copy-start | bytes 3538948
  19.5 26.1 %all-to-all-start.1 = ((bf16[8,776,128]{2,1,0:T(8,128)(2,1)}), bf16[8,776,128]{2,1,0:T(8,128)(2,1)}, u32[]{:S(2)}, u32[]{:S(2)}) async-start(bf16[8,776,128]{2,1,0:T(8,128)(2,1)} %broadcast_in_dim.2), calls=%async_computation.1 | async-start | bytes 3178496 | tf_op jit(solution)/shard_map/all_to_all | solution.py:256
  23.9 2.6 %copy-start.2 = (bf16[4,96,128]{2,1,0:T(8,128)(2,1)S(1)}, bf16[4,96,128]{2,1,0:T(8,128)(2,1)}, u32[]{:S(2)}) copy-start(bf16[4,96,128]{2,1,0:T(8,128)(2,1)} %param.8) | copy-start | bytes 294916
  24.0 5.3 %collective-permute-start.3 = (bf16[2,96,1536]{2,1,0:T(8,128)(2,1)S(1)}, bf16[2,96,1536]{2,1,0:T(8,128)(2,1)S(1)}, u32[]{:S(2)}, u32[]{:S(2)}) collective-permute-start(bf16[2,96,1536]{2,1,0:T(8,128)(2,1)S(1)} %get-tuple-element.23), channel_id=1, source_target_pairs={{0,1},{1,0},{2,3},{3,2},{4,5},{5,4},{6,7},{7,6},{8,9},{9,8},{10,11... | collective-permute-start | bytes 1769480 | tf_op jit(solution)/shard_map/ppermute | solution.py:241
  27.7 1.4 %collective-permute-start = (bf16[4,96,128]{2,1,0:T(8,128)(2,1)S(1)}, bf16[4,96,128]{2,1,0:T(8,128)(2,1)S(1)}, u32[]{:S(2)}, u32[]{:S(2)}) collective-permute-start(bf16[4,96,128]{2,1,0:T(8,128)(2,1)S(1)} %pad_maximum_fusion), channel_id=1, source_target_pairs={{0,1},{1,0},{2,3},{3,2},{4,5},{5,4},{6,7},{7,6},{8,9},{9,8},{10,11... | collective-permute-start | bytes 294920 | tf_op jit(solution)/shard_map/ppermute | solution.py:241
  59.8 17.8 %collective-permute-start.10 = (bf16[384,192]{1,0:T(8,128)(2,1)}, bf16[384,192]{1,0:T(8,128)(2,1)}, u32[]{:S(2)}, u32[]{:S(2)}) collective-permute-start(bf16[384,192]{1,0:T(8,128)(2,1)} %get-tuple-element.18), channel_id=1, source_target_pairs={{0,80},{16,96},{32,112},{48,64},{64,16},{80,32},{96,48},{112,0},{1... | collective-permute-start | bytes 442376 | tf_op jit(solution)/shard_map/ppermute | solution.py:296
  64.1 15.6 %collective-permute-start.11 = (bf16[384,192]{1,0:T(8,128)(2,1)}, bf16[384,192]{1,0:T(8,128)(2,1)}, u32[]{:S(2)}, u32[]{:S(2)}) collective-permute-start(bf16[384,192]{1,0:T(8,128)(2,1)} %get-tuple-element.17), channel_id=1, source_target_pairs={{0,96},{16,112},{32,64},{48,80},{64,32},{80,48},{96,0},{112,16},{1... | collective-permute-start | bytes 442376 | tf_op jit(solution)/shard_map/ppermute | solution.py:296
  66.1 16.1 %collective-permute-start.12 = (bf16[384,192]{1,0:T(8,128)(2,1)}, bf16[384,192]{1,0:T(8,128)(2,1)}, u32[]{:S(2)}, u32[]{:S(2)}) collective-permute-start(bf16[384,192]{1,0:T(8,128)(2,1)} %get-tuple-element.16), channel_id=1, source_target_pairs={{0,112},{16,64},{32,80},{48,96},{64,48},{80,0},{96,16},{112,32},{1... | collective-permute-start | bytes 442376 | tf_op jit(solution)/shard_map/ppermute | solution.py:296
  70.2 12.0 %collective-permute-start.6 = (bf16[384,192]{1,0:T(8,128)(2,1)}, bf16[384,192]{1,0:T(8,128)(2,1)}, u32[]{:S(2)}, u32[]{:S(2)}) collective-permute-start(bf16[384,192]{1,0:T(8,128)(2,1)} %get-tuple-element.15), channel_id=1, source_target_pairs={{0,16},{16,32},{32,48},{48,0},{64,80},{80,96},{96,112},{112,64},{1... | collective-permute-start | bytes 442376 | tf_op jit(solution)/shard_map/ppermute | solution.py:296
  71.2 5.8 %collective-permute-start.4 = (bf16[4,96,128]{2,1,0:T(8,128)(2,1)}, bf16[4,96,128]{2,1,0:T(8,128)(2,1)S(1)}, u32[]{:S(2)}, u32[]{:S(2)}) collective-permute-start(bf16[4,96,128]{2,1,0:T(8,128)(2,1)} %get-tuple-element.29), channel_id=1, source_target_pairs={{0,1},{1,0},{2,3},{3,2},{4,5},{5,4},{6,7},{7,6},{8,9},{9,8},{10,11... | collective-permute-start | bytes 294920 | tf_op jit(solution)/shard_map/ppermute | solution.py:241
  73.1 31.8 %all-to-all-start.2 = ((bf16[8,4,192,128]{3,2,1,0:T(8,128)(2,1)}), bf16[8,4,192,128]{3,2,1,0:T(8,128)(2,1)S(1)}, u32[]{:S(2)}, u32[]{:S(2)}) async-start(bf16[8,4,192,128]{3,2,1,0:T(8,128)(2,1)} %get-tuple-element.12), calls=%async_computation.2 | async-start | bytes 3145728 | tf_op jit(solution)/shard_map/all_to_all | solution.py:270
  77.1 8.7 %collective-permute-start.7 = (bf16[384,192]{1,0:T(8,128)(2,1)}, bf16[384,192]{1,0:T(8,128)(2,1)S(1)}, u32[]{:S(2)}, u32[]{:S(2)}) collective-permute-start(bf16[384,192]{1,0:T(8,128)(2,1)} %get-tuple-element.21), channel_id=1, source_target_pairs={{0,32},{16,48},{32,0},{48,16},{64,96},{80,112},{96,64},{112,80},{1... | collective-permute-start | bytes 442376 | tf_op jit(solution)/shard_map/ppermute | solution.py:296
  77.6 11.6 %collective-permute-start.8 = (bf16[384,192]{1,0:T(8,128)(2,1)}, bf16[384,192]{1,0:T(8,128)(2,1)S(1)}, u32[]{:S(2)}, u32[]{:S(2)}) collective-permute-start(bf16[384,192]{1,0:T(8,128)(2,1)} %get-tuple-element.20), channel_id=1, source_target_pairs={{0,48},{16,0},{32,16},{48,32},{64,112},{80,64},{96,80},{112,96},{1... | collective-permute-start | bytes 442376 | tf_op jit(solution)/shard_map/ppermute | solution.py:296
  79.6 21.5 %collective-permute-start.9 = (bf16[384,192]{1,0:T(8,128)(2,1)S(1)}, bf16[384,192]{1,0:T(8,128)(2,1)S(1)}, u32[]{:S(2)}, u32[]{:S(2)}) collective-permute-start(bf16[384,192]{1,0:T(8,128)(2,1)S(1)} %get-tuple-element.19), channel_id=1, source_target_pairs={{0,64},{16,80},{32,96},{48,112},{64,0},{80,16},{96,32},{112,48},{1... | collective-permute-start | bytes 442376 | tf_op jit(solution)/shard_map/ppermute | solution.py:296
  102.5 1.6 %collective-permute-start.13 = (bf16[2,96,192]{2,1,0:T(8,128)(2,1)S(1)}, bf16[2,96,192]{2,1,0:T(8,128)(2,1)S(1)}, u32[]{:S(2)}, u32[]{:S(2)}) collective-permute-start(bf16[2,96,192]{2,1,0:T(8,128)(2,1)S(1)} %get-tuple-element.25), channel_id=1, source_target_pairs={{0,1},{1,0},{2,3},{3,2},{4,5},{5,4},{6,7},{7,6},{8,9},{9,8},{10,11... | collective-permute-start | bytes 221192 | tf_op jit(solution)/shard_map/ppermute | solution.py:241
  105.2 1.4 %collective-permute-start.5 = (bf16[4,96,128]{2,1,0:T(8,128)(2,1)S(1)}, bf16[4,96,128]{2,1,0:T(8,128)(2,1)S(1)}, u32[]{:S(2)}, u32[]{:S(2)}) collective-permute-start(bf16[4,96,128]{2,1,0:T(8,128)(2,1)S(1)} %get-tuple-element.27), channel_id=1, source_target_pairs={{0,1},{1,0},{2,3},{3,2},{4,5},{5,4},{6,7},{7,6},{8,9},{9,8},{10,11... | collective-permute-start | bytes 294920 | tf_op jit(solution)/shard_map/ppermute | solution.py:241

commit v3 on v2

--- a/solution.py
+++ b/solution.py
@@ -12,9 +12,33 @@
 LOG2E = math.log2(math.e)
 CHUNK = 16
 UNROLL = 12
-
-
-def attention_kernel(qd_ref, kv_ref, bias_ref, mask_ref, qa_ref, dkv_ref, dbias_ref, s_ref, b2_ref, acc_ref, dp_ref, de_ref, row_ref):
+MASK_ROWS = 16
+
+
+def attention_kernel(
+    place_ref,
+    qd_ref,
+    own_ref,
+    left_ref,
+    right_ref,
+    across_ref,
+    left_pair_ref,
+    right_pair_ref,
+    left_far_ref,
+    right_far_ref,
+    bias_ref,
+    qa_ref,
+    dkv_ref,
+    dbias_ref,
+    kv_ref,
+    cap_ref,
+    s_ref,
+    b2_ref,
+    acc_ref,
+    dp_ref,
+    de_ref,
+    row_ref,
+):
     step = pl.program_id(0)
     last = pl.num_programs(0) - 1
     rows = bias_ref.shape[0]
@@ -32,6 +56,28 @@
             return carry
 
         lax.fori_loop(0, rows // CHUNK, fill, 0)
+        height = own_ref.shape[0]
+        cut = left_far_ref.shape[0]
+        kv_ref[place_ref[0]] = own_ref[...]
+        kv_ref[place_ref[1]] = left_ref[...]
+        kv_ref[place_ref[2]] = right_ref[...]
+        kv_ref[place_ref[3], :cut] = left_pair_ref[height:]
+        kv_ref[place_ref[3], cut:] = right_pair_ref[height:]
+        kv_ref[place_ref[4]] = across_ref[...]
+        kv_ref[place_ref[5]] = left_pair_ref[:height]
+        kv_ref[place_ref[6]] = right_pair_ref[:height]
+        kv_ref[place_ref[7], :cut] = left_far_ref[...]
+        kv_ref[place_ref[7], cut:] = right_far_ref[...]
+        first = height - MASK_ROWS
+        masks = kv_ref[:, first:, :].astype(jnp.float32)
+        for column in range(cap_ref.shape[0]):
+            pieces = []
+            for group in range(masks.shape[0]):
+                pieces.append(masks[group, 2 * column : 2 * column + 1, :])
+                pieces.append(masks[group, 2 * column + 1 : 2 * column + 2, : queries - 128])
+            cap_ref[column] = jnp.where(
+                jnp.concatenate(pieces, axis=1) > 0.5, 1e30, NEG_FILL * LOG2E
+            )
 
     kv = kv_ref[:, pl.ds(step * queries, queries), :].reshape(keys, 4 * head_width)
     qd = qd_ref[0]
@@ -42,7 +88,7 @@
         return jnp.where((lane >= part * head_width) & (lane < (part + 1) * head_width), qd, zero)
 
     transposed = (((1,), (1,)), ((), ()))
-    cap = jnp.where(mask_ref[0] > 0.5, 1e30, NEG_FILL * LOG2E)
+    cap = cap_ref[step]
     query_rows = [only(0), only(1)]
     grad_rows = [only(2), only(3)]
 
@@ -118,7 +164,8 @@
     def _():
         width = dbias_ref.shape[2]
         for piece in range(dbias_ref.shape[0]):
-            dbias_ref[piece] = acc_ref[:, piece * width : (piece + 1) * width].astype(jnp.bfloat16)
+            part = acc_ref[:, piece * width : (piece + 1) * width]
+            dbias_ref[place_ref[8 + piece]] = part.astype(jnp.bfloat16)
 
 
 def pack_kernel(cotangent_ref, packed_ref):
@@ -163,44 +210,49 @@
     )(packed, weight, gate)
 
 
-def attend(query_grad, key_value, bias, mask, row_count):
+def attend(places, query_grad, blocks, bias, chips, row_count):
     columns, queries, lanes = query_grad.shape
-    groups = key_value.shape[0]
-    keys = bias.shape[1]
-    rows = bias.shape[0]
+    rows, keys = bias.shape
+    height = blocks[0].shape[0]
     width = keys // row_count
     work = columns * rows * keys
+
+    def whole(array):
+        return pl.BlockSpec(array.shape, lambda j, places: (0,) * array.ndim)
+
     return pl.pallas_call(
         attention_kernel,
-        grid=(columns,),
-        in_specs=[
-            pl.BlockSpec((1, queries, lanes), lambda j: (j, 0, 0)),
-            pl.BlockSpec((groups,) + key_value.shape[1:], lambda j: (0, 0, 0)),
-            pl.BlockSpec((rows, keys), lambda j: (0, 0)),
-            pl.BlockSpec((1, 1, keys), lambda j: (j, 0, 0)),
-        ],
-        out_specs=[
-            pl.BlockSpec((1, queries, lanes), lambda j: (j, 0, 0)),
-            pl.BlockSpec((groups, 1, queries, lanes), lambda j: (0, j, 0, 0)),
-            pl.BlockSpec((row_count, rows, width), lambda j: (0, 0, 0)),
-        ],
+        grid_spec=pltpu.PrefetchScalarGridSpec(
+            num_scalar_prefetch=1,
+            grid=(columns,),
+            in_specs=[pl.BlockSpec((1, queries, lanes), lambda j, places: (j, 0, 0))]
+            + [whole(block) for block in blocks]
+            + [whole(bias)],
+            out_specs=[
+                pl.BlockSpec((1, queries, lanes), lambda j, places: (j, 0, 0)),
+                pl.BlockSpec((chips, 1, queries, lanes), lambda j, places: (0, j, 0, 0)),
+                pl.BlockSpec((row_count, rows, width), lambda j, places: (0, 0, 0)),
+            ],
+            scratch_shapes=[
+                pltpu.VMEM((chips, height, lanes), jnp.bfloat16),
+                pltpu.VMEM((columns, 1, keys), jnp.float32),
+                pltpu.VMEM((rows, keys), jnp.float32),
+                pltpu.VMEM((rows, keys), jnp.float32),
+                pltpu.VMEM((rows, keys), jnp.float32),
+                pltpu.VMEM((rows, keys), jnp.float32),
+                pltpu.VMEM((2 * rows, keys), jnp.bfloat16),
+                pltpu.VMEM((rows, 128), jnp.float32),
+            ],
+        ),
         out_shape=[
             jax.ShapeDtypeStruct((columns, queries, lanes), jnp.bfloat16),
-            jax.ShapeDtypeStruct((groups, columns, queries, lanes), jnp.bfloat16),
+            jax.ShapeDtypeStruct((chips, columns, queries, lanes), jnp.bfloat16),
             jax.ShapeDtypeStruct((row_count, rows, width), jnp.bfloat16),
-        ],
-        scratch_shapes=[
-            pltpu.VMEM((rows, keys), jnp.float32),
-            pltpu.VMEM((rows, keys), jnp.float32),
-            pltpu.VMEM((rows, keys), jnp.float32),
-            pltpu.VMEM((rows, keys), jnp.float32),
-            pltpu.VMEM((2 * rows, keys), jnp.bfloat16),
-            pltpu.VMEM((rows, 128), jnp.float32),
         ],
         compiler_params=pltpu.CompilerParams(vmem_limit_bytes=48 * 1024 * 1024),
         cost_estimate=pl.CostEstimate(flops=12 * 128 * work, bytes_accessed=16 * 2**20, transcendentals=work),
         name="attention_both",
-    )(query_grad, key_value, bias, mask)
+    )(places, query_grad, *blocks, bias)
 
 
 def local(
@@ -250,12 +302,38 @@
     mask_low = pair_mask.astype(jnp.bfloat16)
     kv_chip = in_order(kv_mine, kv_other, 1)
     mask_chip = in_order(mask_low, swapped(mask_low), 1)
-    mask_rows = jnp.pad(mask_chip.reshape(-1, channels), ((0, 2), (0, 0)))
-    payload = jnp.concatenate([kv_chip.reshape(-1, channels), mask_rows], axis=0)
-    payload = jnp.broadcast_to(payload[None], (chips,) + payload.shape)
-    gathered = lax.all_to_all(payload, "col", 0, 0, tiled=True, axis_index_groups=chip_groups)
-    mask_all = gathered[:, columns * 2 * tokens : -2].reshape(chips, columns, 2 * tokens)
-    mask_all = jnp.transpose(mask_all, (1, 0, 2)).reshape(columns, 1, keys).astype(jnp.float32)
+    mask_rows = jnp.pad(mask_chip, ((0, 0), (0, 256 - 2 * tokens))).reshape(-1, channels)
+    mask_rows = jnp.pad(mask_rows, ((0, MASK_ROWS - 2 * columns), (0, 0)))
+    block = jnp.concatenate([kv_chip.reshape(-1, channels), mask_rows], axis=0)
+    ring = chips // 2
+
+    def along(array, turn, side):
+        pairs = []
+        for index in range(devices):
+            high, low = index // (2 * ring), index // 2 % ring
+            target = ((high + side) % 2) * ring + (low + turn) % ring
+            pairs.append((index, 2 * target + index % 2))
+        return lax.ppermute(array, "col", pairs)
+
+    cut = columns * tokens
+    left, right, across = along(block, 1, 0), along(block, -1, 0), along(block, 0, 1)
+    left_pair = along(jnp.concatenate([across, left[:cut]], axis=0), 1, 0)
+    right_pair = along(jnp.concatenate([across, right[cut:]], axis=0), -1, 0)
+    left_far = along(left_pair[:cut], 1, 0)
+    right_far = along(right_pair[cut : block.shape[0]], -1, 0)
+    blocks = [block, left, right, across, left_pair, right_pair, left_far, right_far]
+    chip = lax.axis_index("col") // 2
+    place = lax.axis_index("row")
+    row_ring = row_count // 2
+    places = [
+        ((chip // ring + side) % 2) * ring + (chip % ring + turn) % ring
+        for side in range(2)
+        for turn in (0, ring - 1, 1, 2)
+    ] + [
+        2 * ((index % row_ring - place) % row_ring) + (index // row_ring - place // row_ring) % 2
+        for index in range(row_count)
+    ]
+    places = jnp.stack(places).astype(jnp.int32)
 
     regrouped = lax.all_to_all(pack(output_cotangent, devices), "col", 0, 0, tiled=True)
     attended_grad, gate_slope = project(regrouped, output_weight, gate_logits)
@@ -265,7 +343,7 @@
     qd_other = swapped(jnp.concatenate([query_other, grad_other], axis=2))
     query_grad = in_order(qd_mine, qd_other, 1)
 
-    query_attended, kv_grads, bias_grads = attend(query_grad, gathered, bias_pair, mask_all, row_count)
+    query_attended, kv_grads, bias_grads = attend(places, query_grad, blocks, bias_pair, chips, row_count)
 
     kv_parts = lax.all_to_all(kv_grads, "col", 0, 0, tiled=True, axis_index_groups=chip_groups)
     kv_sum = jnp.sum(kv_parts.astype(jnp.float32), axis=0).astype(jnp.bfloat16)
@@ -281,19 +359,24 @@
     attended = in_order(qa_own[..., half:], qa_back[..., half:], 2).astype(jnp.float32)
     gate_gradient = (gate_slope * attended).astype(jnp.bfloat16)
 
-    place = lax.axis_index("row")
-    high_step = row_count // 2
-    bias_sum = lax.dynamic_index_in_dim(bias_grads, place, 0, keepdims=False).astype(jnp.float32)
-    for high in range(2):
-        for low in range(high_step):
-            if high or low:
-                pairs = [
-                    (index, ((index // high_step + high) % 2) * high_step + (index + low) % high_step)
-                    for index in range(row_count)
-                ]
-                target = ((place // high_step + high) % 2) * high_step + (place + low) % high_step
-                part = lax.dynamic_index_in_dim(bias_grads, target, 0, keepdims=False)
-                bias_sum = bias_sum + lax.ppermute(part, "row", pairs).astype(jnp.float32)
+    def along_row(array, turn, side):
+        pairs = []
+        for index in range(row_count):
+            high, low = index // row_ring, index % row_ring
+            pairs.append((index, ((high + side) % 2) * row_ring + (low + turn) % row_ring))
+        return lax.ppermute(array, "row", pairs)
+
+    def added(*parts):
+        return sum(part.astype(jnp.float32) for part in parts)
+
+    from_left = along_row(bias_grads[4], 1, 0)
+    from_right = along_row(bias_grads[5], -1, 0)
+    onward = jnp.stack([added(bias_grads[2], from_left).astype(jnp.bfloat16), bias_grads[3]])
+    backward = jnp.stack([bias_grads[6], added(bias_grads[7], from_right).astype(jnp.bfloat16)])
+    from_left = along_row(onward, 1, 0)
+    from_right = along_row(backward, -1, 0)
+    bias_away = added(bias_grads[1], from_left[1], from_right[1]).astype(jnp.bfloat16)
+    bias_sum = added(bias_grads[0], from_left[0], from_right[0], along_row(bias_away, 0, 1))
     bias_sum = bias_sum.astype(jnp.bfloat16)
     bias_sum = bias_sum.reshape(2, 2 * tokens, keys // row_count)
     bias_own, bias_away = mine_other(bias_sum, 1)

time: 109 us -> 95.5 us (0.88)
  waiting for transfers between devices: 42.7 us -> 18.3 us
  starting transfers between devices: 33.8 us -> 43.7 us
  other arithmetic: 11.9 us -> 13.4 us
    all_to_all x1 -> x0, waiting for transfers between devices: 15.9 us -> none  [local(): lax.all_to_all(payload, 'col', 0, 0, tiled=True, axis_index_groups=chip_g...]
    ppermute x7, starting transfers between devices: 5.14 us -> 16.5 us  [swapped(): return lax.ppermute(array, 'col', swap)]
    all_to_all x1, waiting for transfers between devices: 5.71 us -> 0.01 us  [local(): lax.all_to_all(pack(output_cotangent, devices), 'col', 0, 0, tiled=True)]
    all_to_all x1 -> x0, starting transfers between devices: 4.42 us -> none  [local(): lax.all_to_all(payload, 'col', 0, 0, tiled=True, axis_index_groups=chip_g...]
    ppermute x7 -> x12, waiting for transfers between devices: 18.9 us -> 15.2 us  [the longest x5 10.6 us: along_row(): return lax.ppermute(array, 'row', pairs)]
    ppermute x7 -> x12, starting transfers between devices: 14.1 us -> 17.3 us  [the longest x7 9.34 us: along(): return lax.ppermute(array, 'col', pairs)]
    select_n x6, other arithmetic: 2.31 us -> 4.21 us  [in_order(): jnp.where(core == 0, jnp.concatenate([mine, other], axis=axis), jnp.conca...]
    concatenate x1 -> x3, other arithmetic: 0.02 us -> 1.49 us  [the longest x1 0.74 us: local(): right_pair = along(jnp.concatenate([across, right[cut:]], axis=0), -1, 0)]
  transfers between devices with their start and end apart: 17 -> 21, of which waited for: 8 -> 9; matrix products, arithmetic and copies ran while one was open for 8% -> 13% of each run, Pallas kernels for 3% -> 4%
where the time goes in v3:
time: 95.5 us; the launch traced here: 95 us
  starting transfers between devices  43.7 us (46%)
  waiting for transfers between devices  18.3 us (19%)
  Pallas kernels  16.2 us (17%)
  other arithmetic  13.4 us (14%)
  local copies, waits for them, and re-layouts  2.59 us (3%)
    ppermute x7, starting transfers between devices, swapped(): return lax.ppermute(array, 'col', swap)  16.5 us
    pallas_call x1, Pallas kernels, attend(): pl.pallas_call(attention_kernel, grid_spec=pltpu.PrefetchScalarGridSpec(n...  12.6 us
    ppermute x5, waiting for transfers between devices, along_row(): return lax.ppermute(array, 'row', pairs)  10.6 us
    ppermute x7, starting transfers between devices, along(): return lax.ppermute(array, 'col', pairs)  9.34 us
    ppermute x5, starting transfers between devices, along_row(): return lax.ppermute(array, 'row', pairs)  7.92 us
    all_to_all x1, starting transfers between devices, local(): lax.all_to_all(pack(output_cotangent, devices), 'col', 0, 0, tiled=True)  5.86 us
    ppermute x7, waiting for transfers between devices, along(): return lax.ppermute(array, 'col', pairs)  4.64 us
    select_n x6, other arithmetic, in_order(): jnp.where(core == 0, jnp.concatenate([mine, other], axis=axis), jnp.conca...  4.21 us
  transfers between devices with their start and end apart: 21, of which 9 were waited for; matrix products, arithmetic and copies ran while one was open for 13% of the time, Pallas kernels for 4%

profile of v3, /device:TPU:1, one launch (start us, length us, event | category | flops | bytes accessed | tf_op | source)
XLA Modules:
  0.0 95.0 jit_solution(16907249185944727649)
XLA Ops:
  0.6 0.8 convert_element_type.84
  1.4 1.4 %collective-permute-start.2 = (bf16[4,96]{1,0:T(4,128)(2,1)S(1)}, bf16[4,96]{1,0:T(4,128)(2,1)S(1)}, u32[]{:S(2)}, u32[]{:S(2)}) collective-permute-start(bf16[4,96]{1,0:T(4,128)(2,1)S(1)} %convert_element_type.84), channel_id=1, source_target_pairs={{0,1},{1,0},{2,3},{3,2},{4,5},{5,4},{6,7},{7,6},{8,9},{9,8},{10,11... | collective-permute-start | bytes 2312 | tf_op jit(solution)/shard_map/ppermute | solution.py:293
  2.8 1.7 %pack_cotangent.1 = bf16[16,32,128]{2,1,0:T(8,128)(2,1)} custom-call(bf16[4,8,1536]{2,1,0:T(8,128)(2,1)} %cotangent_ref.1), custom_call_target="tpu_custom_call" | custom-call | tf_op jit(solution)/shard_map/pack_cotangent/pallas_call | solution.py:182
  4.5 5.9 %all-to-all-start = ((bf16[16,32,128]{2,1,0:T(8,128)(2,1)}), bf16[16,32,128]{2,1,0:T(8,128)(2,1)S(1)}, u32[]{:S(2)}, u32[]{:S(2)}) async-start(bf16[16,32,128]{2,1,0:T(8,128)(2,1)} %pack_cotangent.1), calls=%async_computation | async-start | bytes 262144 | tf_op jit(solution)/shard_map/all_to_all | solution.py:338
  10.4 1.2 %broadcast_select_fusion.6 = (bf16[4,96,64]{2,1,0:T(8,128)(2,1)S(1)}, bf16[4,96,64]{2,1,0:T(8,128)(2,1)S(1)}, bf16[4,96,64]{2,1,0:T(8,128)(2,1)S(1)}, bf16[4,96,64]{2,1,0:T(8,128)(2,1)S(1)}) fusion(pred[]{:T(512)S(6)} %eq.69, bf16[4,96,128]{2,1,0:T(8,128)(2,1)} %param.10, bf16[4,96,128]{2,1,0:T(8,128)(2,1)} %param.9), kind=kLoop, calls=%fused_computation.38 | loop fusion | flops 98304 | bytes 393217 | tf_op jit(solution)/shard_map/jit(_where)/select_n | solution.py:283
  11.5 0.7 pad_maximum_fusion.5
  12.3 0.1 collective-permute-start.1
  12.5 0.5 collective-permute-start.10
  13.1 0.9 collective-permute-done.1
  13.9 1.1 %maximum_select_fusion.2 = bf16[4,192,128]{2,1,0:T(8,128)(2,1)S(1)} fusion(bf16[4,96,128]{2,1,0:T(8,128)(2,1)} %collective-permute-done.1, bf16[4,96,64]{2,1,0:T(8,128)(2,1)S(1)} %get-tuple-element.39, bf16[4,96,64]{2,1,0:T(8,128)(2,1)S(1)} %get-tuple-element.46, pred[]{:T(512)S(6)} %eq.69), kind=kLoop, calls=%fused_computation.21 | loop fusion | flops 1277952 | bytes 393217 | tf_op jit(solution)/shard_map/jit(_where)/select_n | solution.py:286
  15.1 1.5 %collective-permute-start.5 = (bf16[784,128]{1,0:T(8,128)(2,1)S(1)}, bf16[784,128]{1,0:T(8,128)(2,1)S(1)}, u32[]{:S(2)}, u32[]{:S(2)}) collective-permute-start(bf16[784,128]{1,0:T(8,128)(2,1)S(1)} %fusion.4.own_ref), channel_id=1, source_target_pairs={{0,8},{1,9},{2,10},{3,11},{4,12},{5,13},{6,14},{7,15},{8,0},{9,1},... | collective-permute-start | bytes 602120 | tf_op jit(solution)/shard_map/ppermute | solution.py:316
  16.5 2.4 %collective-permute-start.4 = (bf16[784,128]{1,0:T(8,128)(2,1)S(1)}, bf16[784,128]{1,0:T(8,128)(2,1)S(1)}, u32[]{:S(2)}, u32[]{:S(2)}) collective-permute-start(bf16[784,128]{1,0:T(8,128)(2,1)S(1)} %fusion.4.own_ref), channel_id=1, source_target_pairs={{0,6},{1,7},{2,0},{3,1},{4,2},{5,3},{6,4},{7,5},{8,14},{9,15},{10,... | collective-permute-start | bytes 602120 | tf_op jit(solution)/shard_map/ppermute | solution.py:316
  18.9 0.7 copy-done.2
  19.6 1.9 %project_cotangent.1 = (bf16[4,96,128]{2,1,0:T(8,128)(2,1)}, f32[4,96,128]{2,1,0:T(8,128)}) custom-call(bf16[16,32,128]{2,1,0:T(8,128)(2,1)} %copy-done.2, bf16[128,128]{1,0:T(8,128)(2,1)} %weight_ref.1, bf16[4,96,128]{2,1,0:T(8,128)(2,1)} %gate_ref.1), custom_call_target="tpu_custom_call" | custom-call | tf_op jit(solution)/shard_map/project_cotangent/pallas_call | solution.py:203
  21.5 1.1 %broadcast_select_fusion.10 = (bf16[4,96,64]{2,1,0:T(8,128)(2,1)S(1)}, bf16[4,96,64]{2,1,0:T(8,128)(2,1)S(1)}, bf16[4,96,64]{2,1,0:T(8,128)(2,1)S(1)}, bf16[4,96,64]{2,1,0:T(8,128)(2,1)S(1)}) fusion(pred[]{:T(512)S(6)} %eq.69, bf16[4,96,128]{2,1,0:T(8,128)(2,1)} %get-tuple-element.10, bf16[4,96,128]{2,1,0:T(8,128)(2,1)S(1)} %copy-done.3), kind=kLoop, calls=%fused_computation.42 | loop fusion | flops 98304 | bytes 393217 | tf_op jit(solution)/shard_map/jit(_where)/select_n | solution.py:283
  22.6 3.1 %collective-permute-done.3.left_ref = bf16[784,128]{1,0:T(8,128)(2,1)S(1)} collective-permute-done((bf16[784,128]{1,0:T(8,128)(2,1)S(1)}, bf16[784,128]{1,0:T(8,128)(2,1)S(1)}, u32[]{:S(2)}, u32[]{:S(2)}) %collective-permute-start.3) | collective-permute-done | bytes 200736 | tf_op jit(solution)/shard_map/ppermute | solution.py:316
  25.7 0.7 pad_maximum_fusion.3
  26.5 0.7 pad_maximum_fusion.2
  27.2 2.7 %collective-permute-start.7 = (bf16[1184,128]{1,0:T(8,128)(2,1)}, bf16[1184,128]{1,0:T(8,128)(2,1)S(1)}, u32[]{:S(2)}, u32[]{:S(2)}) collective-permute-start(bf16[1184,128]{1,0:T(8,128)(2,1)} %pad_maximum_fusion.2), channel_id=1, source_target_pairs={{0,6},{1,7},{2,0},{3,1},{4,2},{5,3},{6,4},{7,5},{8,14},{9,15},{10,... | collective-permute-start | bytes 909320 | tf_op jit(solution)/shard_map/ppermute | solution.py:316
  29.9 0.7 pad_maximum_fusion.4
  30.6 2.4 %collective-permute-start = (bf16[4,96,128]{2,1,0:T(8,128)(2,1)}, bf16[4,96,128]{2,1,0:T(8,128)(2,1)}, u32[]{:S(2)}, u32[]{:S(2)}) collective-permute-start(bf16[4,96,128]{2,1,0:T(8,128)(2,1)} %pad_maximum_fusion.4), channel_id=1, source_target_pairs={{0,1},{1,0},{2,3},{3,2},{4,5},{5,4},{6,7},{7,6},{8,9},{9,8},{10,11... | collective-permute-start | bytes 294920 | tf_op jit(solution)/shard_map/ppermute | solution.py:293
  33.1 1.2 %collective-permute-done = bf16[4,96,128]{2,1,0:T(8,128)(2,1)} collective-permute-done((bf16[4,96,128]{2,1,0:T(8,128)(2,1)}, bf16[4,96,128]{2,1,0:T(8,128)(2,1)}, u32[]{:S(2)}, u32[]{:S(2)}) %collective-permute-start) | collective-permute-done | bytes 98336 | tf_op jit(solution)/shard_map/ppermute | solution.py:293
  34.3 1.1 %maximum_select_fusion.1.qd_ref = bf16[4,192,128]{2,1,0:T(8,128)(2,1)S(1)} fusion(bf16[4,96,128]{2,1,0:T(8,128)(2,1)} %collective-permute-done, bf16[4,96,64]{2,1,0:T(8,128)(2,1)S(1)} %get-tuple-element.43, bf16[4,96,64]{2,1,0:T(8,128)(2,1)S(1)} %get-tuple-element.48, pred[]{:T(512)S(6)} %eq.69), kind=kLoop, calls=%fused_computation.20 | loop fusion | flops 1277952 | bytes 393217 | tf_op jit(solution)/shard_map/jit(_where)/select_n | solution.py:286
  35.6 2.7 %collective-permute-start.9 = (bf16[400,128]{1,0:T(8,128)(2,1)S(1)}, bf16[400,128]{1,0:T(8,128)(2,1)S(1)}, u32[]{:S(2)}, u32[]{:S(2)}) collective-permute-start(bf16[400,128]{1,0:T(8,128)(2,1)S(1)} %slice.163), channel_id=1, source_target_pairs={{0,6},{1,7},{2,0},{3,1},{4,2},{5,3},{6,4},{7,5},{8,14},{9,15},{10,... | collective-permute-start | bytes 307208 | tf_op jit(solution)/shard_map/ppermute | solution.py:316
  38.3 0.4 maximum_select_fusion
  38.7 1.5 %collective-permute-done.8.left_far_ref = bf16[384,128]{1,0:T(8,128)(2,1)S(1)} collective-permute-done((bf16[384,128]{1,0:T(8,128)(2,1)S(1)}, bf16[384,128]{1,0:T(8,128)(2,1)S(1)}, u32[]{:S(2)}, u32[]{:S(2)}) %collective-permute-start.8) | collective-permute-done | bytes 98336 | tf_op jit(solution)/shard_map/ppermute | solution.py:316
  40.2 12.6 %attention_both.1 = (bf16[4,192,128]{2,1,0:T(8,128)(2,1)S(1)}, bf16[8,4,192,128]{3,2,1,0:T(8,128)(2,1)}, bf16[8,384,192]{2,1,0:T(8,128)(2,1)}) custom-call(s32[16]{0:T(128)S(1)} %stack.79.place_ref, bf16[4,192,128]{2,1,0:T(8,128)(2,1)S(1)} %maximum_select_fusion.1.qd_ref, bf16[784,128]{1,0:T(8,128)(2,1)S(1)} %fusion.4.own_ref, ...), custom_call_target="tpu_custom_call" | custom-call | flops 3623878656 | bytes 16777216 | tf_op jit(solution)/shard_map/attention_both/pallas_call | solution.py:223
  52.8 4.1 %all-to-all-start.1 = ((bf16[8,4,192,128]{3,2,1,0:T(8,128)(2,1)}), bf16[8,4,192,128]{3,2,1,0:T(8,128)(2,1)S(1)}, u32[]{:S(2)}, u32[]{:S(2)}) async-start(bf16[8,4,192,128]{3,2,1,0:T(8,128)(2,1)} %get-tuple-element.12), calls=%async_computation.1 | async-start | bytes 3145728 | tf_op jit(solution)/shard_map/all_to_all | solution.py:348
  56.9 1.4 %slice_bitcast_fusion.1 = (bf16[384,192]{1,0:T(8,128)(2,1)S(1)}, bf16[384,192]{1,0:T(8,128)(2,1)S(1)}, bf16[1,384,192]{2,1,0:T(8,128)(2,1)S(1)}, bf16[1,384,192]{2,1,0:T(8,128)(2,1)S(1)}) fusion(bf16[8,384,192]{2,1,0:T(8,128)(2,1)} %get-tuple-element.14), kind=kLoop, calls=%fused_computation.25 | loop fusion | bytes 1179648 | tf_op jit(solution)/shard_map/squeeze | solution.py:372
  58.3 1.4 %collective-permute-start.13 = (bf16[384,192]{1,0:T(8,128)(2,1)S(1)}, bf16[384,192]{1,0:T(8,128)(2,1)S(1)}, u32[]{:S(2)}, u32[]{:S(2)}) collective-permute-start(bf16[384,192]{1,0:T(8,128)(2,1)S(1)} %get-tuple-element.17), channel_id=1, source_target_pairs={{0,16},{16,32},{32,48},{48,0},{64,80},{80,96},{96,112},{112,64},{1... | collective-permute-start | bytes 442376 | tf_op jit(solution)/shard_map/ppermute | solution.py:367
  59.6 1.5 %collective-permute-start.15 = (bf16[384,192]{1,0:T(8,128)(2,1)S(1)}, bf16[384,192]{1,0:T(8,128)(2,1)S(1)}, u32[]{:S(2)}, u32[]{:S(2)}) collective-permute-start(bf16[384,192]{1,0:T(8,128)(2,1)S(1)} %get-tuple-element.18), channel_id=1, source_target_pairs={{0,48},{16,0},{32,16},{48,32},{64,112},{80,64},{96,80},{112,96},{1... | collective-permute-start | bytes 442376 | tf_op jit(solution)/shard_map/ppermute | solution.py:367
  61.2 4.6 %collective-permute-start.11 = (bf16[4,96,128]{2,1,0:T(8,128)(2,1)S(1)}, bf16[4,96,128]{2,1,0:T(8,128)(2,1)S(1)}, u32[]{:S(2)}, u32[]{:S(2)}) collective-permute-start(bf16[4,96,128]{2,1,0:T(8,128)(2,1)S(1)} %get-tuple-element.28), channel_id=1, source_target_pairs={{0,1},{1,0},{2,3},{3,2},{4,5},{5,4},{6,7},{7,6},{8,9},{9,8},{10,11... | collective-permute-start | bytes 294920 | tf_op jit(solution)/shard_map/ppermute | solution.py:293
  66.0 1.6 %collective-permute-start.16 = (bf16[2,384,192]{2,1,0:T(8,128)(2,1)S(1)}, bf16[2,384,192]{2,1,0:T(8,128)(2,1)S(1)}, u32[]{:S(2)}, u32[]{:S(2)}) collective-permute-start(bf16[2,384,192]{2,1,0:T(8,128)(2,1)S(1)} %pad_maximum_fusion.1), channel_id=1, source_target_pairs={{0,48},{16,0},{32,16},{48,32},{64,112},{80,64},{96,80},{112,96},{1... | collective-permute-start | bytes 884744 | tf_op jit(solution)/shard_map/ppermute | solution.py:367
  68.0 5.6 %collective-permute-done.16 = bf16[2,384,192]{2,1,0:T(8,128)(2,1)S(1)} collective-permute-done((bf16[2,384,192]{2,1,0:T(8,128)(2,1)S(1)}, bf16[2,384,192]{2,1,0:T(8,128)(2,1)S(1)}, u32[]{:S(2)}, u32[]{:S(2)}) %collective-permute-start.16) | collective-permute-done | bytes 294944 | tf_op jit(solution)/shard_map/ppermute | solution.py:367
  73.6 2.3 %collective-permute-done.14 = bf16[2,384,192]{2,1,0:T(8,128)(2,1)S(1)} collective-permute-done((bf16[2,384,192]{2,1,0:T(8,128)(2,1)S(1)}, bf16[2,384,192]{2,1,0:T(8,128)(2,1)S(1)}, u32[]{:S(2)}, u32[]{:S(2)}) %collective-permute-start.14) | collective-permute-done | bytes 294944 | tf_op jit(solution)/shard_map/ppermute | solution.py:367
  76.0 3.4 %collective-permute-start.17 = (bf16[384,192]{1,0:T(8,128)(2,1)S(1)}, bf16[384,192]{1,0:T(8,128)(2,1)S(1)}, u32[]{:S(2)}, u32[]{:S(2)}) collective-permute-start(bf16[384,192]{1,0:T(8,128)(2,1)S(1)} %fusion.5), channel_id=1, source_target_pairs={{0,64},{16,80},{32,96},{48,112},{64,0},{80,16},{96,32},{112,48},{1... | collective-permute-start | bytes 442376 | tf_op jit(solution)/shard_map/ppermute | solution.py:367
  79.4 0.8 multiply_convert_fusion
  80.1 2.7 %collective-permute-done.17 = bf16[384,192]{1,0:T(8,128)(2,1)S(1)} collective-permute-done((bf16[384,192]{1,0:T(8,128)(2,1)S(1)}, bf16[384,192]{1,0:T(8,128)(2,1)S(1)}, u32[]{:S(2)}, u32[]{:S(2)}) %collective-permute-start.17) | collective-permute-done | bytes 147488 | tf_op jit(solution)/shard_map/ppermute | solution.py:367
  82.8 0.1 fusion.3
  82.9 7.0 %collective-permute-start.18 = (bf16[2,96,192]{2,1,0:T(8,128)(2,1)S(1)}, bf16[2,96,192]{2,1,0:T(8,128)(2,1)S(1)}, u32[]{:S(2)}, u32[]{:S(2)}) collective-permute-start(bf16[2,96,192]{2,1,0:T(8,128)(2,1)S(1)} %get-tuple-element.24), channel_id=1, source_target_pairs={{0,1},{1,0},{2,3},{3,2},{4,5},{5,4},{6,7},{7,6},{8,9},{9,8},{10,11... | collective-permute-start | bytes 221192 | tf_op jit(solution)/shard_map/ppermute | solution.py:293
  89.9 0.8 maximum_select_fusion.4
  90.7 0.2 collective-permute-done.18
  90.9 0.8 fusion.8
  91.7 0.3 reduce_sum.12
  92.0 0.4 collective-permute-start.12
  92.5 0.8 collective-permute-done.12
  93.5 0.8 maximum_select_fusion.6
  94.3 0.8 multiply_convert_fusion.1
  (46 shorter events, 1.3 us)
Async XLA Ops:
  0.6 11.8 %copy-start.1 = (bf16[4,96,1536]{2,1,0:T(8,128)(2,1)S(1)}, bf16[4,96,1536]{2,1,0:T(8,128)(2,1)}, u32[]{:S(2)}) copy-start(bf16[4,96,1536]{2,1,0:T(8,128)(2,1)} %param.12) | copy-start | bytes 3538948
  1.4 11.5 %collective-permute-start.2 = (bf16[4,96]{1,0:T(4,128)(2,1)S(1)}, bf16[4,96]{1,0:T(4,128)(2,1)S(1)}, u32[]{:S(2)}, u32[]{:S(2)}) collective-permute-start(bf16[4,96]{1,0:T(4,128)(2,1)S(1)} %convert_element_type.84), channel_id=1, source_target_pairs={{0,1},{1,0},{2,3},{3,2},{4,5},{5,4},{6,7},{7,6},{8,9},{9,8},{10,11... | collective-permute-start | bytes 2312 | tf_op jit(solution)/shard_map/ppermute | solution.py:293
  4.5 14.4 %all-to-all-start = ((bf16[16,32,128]{2,1,0:T(8,128)(2,1)}), bf16[16,32,128]{2,1,0:T(8,128)(2,1)S(1)}, u32[]{:S(2)}, u32[]{:S(2)}) async-start(bf16[16,32,128]{2,1,0:T(8,128)(2,1)} %pack_cotangent.1), calls=%async_computation | async-start | bytes 262144 | tf_op jit(solution)/shard_map/all_to_all | solution.py:338
  12.3 9.3 %copy-start.3 = (bf16[4,96,128]{2,1,0:T(8,128)(2,1)S(1)}, bf16[4,96,128]{2,1,0:T(8,128)(2,1)}, u32[]{:S(2)}) copy-start(bf16[4,96,128]{2,1,0:T(8,128)(2,1)} %param.8) | copy-start | bytes 294916
  12.3 1.6 %collective-permute-start.1 = (bf16[4,96,128]{2,1,0:T(8,128)(2,1)}, bf16[4,96,128]{2,1,0:T(8,128)(2,1)}, u32[]{:S(2)}, u32[]{:S(2)}) collective-permute-start(bf16[4,96,128]{2,1,0:T(8,128)(2,1)} %pad_maximum_fusion.5), channel_id=1, source_target_pairs={{0,1},{1,0},{2,3},{3,2},{4,5},{5,4},{6,7},{7,6},{8,9},{9,8},{10,11... | collective-permute-start | bytes 294920 | tf_op jit(solution)/shard_map/ppermute | solution.py:293
  12.5 25.8 %collective-permute-start.10 = (bf16[2,96,1536]{2,1,0:T(8,128)(2,1)S(1)}, bf16[2,96,1536]{2,1,0:T(8,128)(2,1)S(1)}, u32[]{:S(2)}, u32[]{:S(2)}) collective-permute-start(bf16[2,96,1536]{2,1,0:T(8,128)(2,1)S(1)} %get-tuple-element.22), channel_id=1, source_target_pairs={{0,1},{1,0},{2,3},{3,2},{4,5},{5,4},{6,7},{7,6},{8,9},{9,8},{10,11... | collective-permute-start | bytes 1769480 | tf_op jit(solution)/shard_map/ppermute | solution.py:293
  15.1 10.7 %collective-permute-start.5 = (bf16[784,128]{1,0:T(8,128)(2,1)S(1)}, bf16[784,128]{1,0:T(8,128)(2,1)S(1)}, u32[]{:S(2)}, u32[]{:S(2)}) collective-permute-start(bf16[784,128]{1,0:T(8,128)(2,1)S(1)} %fusion.4.own_ref), channel_id=1, source_target_pairs={{0,8},{1,9},{2,10},{3,11},{4,12},{5,13},{6,14},{7,15},{8,0},{9,1},... | collective-permute-start | bytes 602120 | tf_op jit(solution)/shard_map/ppermute | solution.py:316
  16.5 9.9 %collective-permute-start.4 = (bf16[784,128]{1,0:T(8,128)(2,1)S(1)}, bf16[784,128]{1,0:T(8,128)(2,1)S(1)}, u32[]{:S(2)}, u32[]{:S(2)}) collective-permute-start(bf16[784,128]{1,0:T(8,128)(2,1)S(1)} %fusion.4.own_ref), channel_id=1, source_target_pairs={{0,6},{1,7},{2,0},{3,1},{4,2},{5,3},{6,4},{7,5},{8,14},{9,15},{10,... | collective-permute-start | bytes 602120 | tf_op jit(solution)/shard_map/ppermute | solution.py:316
  18.9 6.8 %collective-permute-start.3 = (bf16[784,128]{1,0:T(8,128)(2,1)S(1)}, bf16[784,128]{1,0:T(8,128)(2,1)S(1)}, u32[]{:S(2)}, u32[]{:S(2)}) collective-permute-start(bf16[784,128]{1,0:T(8,128)(2,1)S(1)} %fusion.4.own_ref), channel_id=1, source_target_pairs={{0,2},{1,3},{2,4},{3,5},{4,6},{5,7},{6,0},{7,1},{8,10},{9,11},{10,... | collective-permute-start | bytes 602120 | tf_op jit(solution)/shard_map/ppermute | solution.py:316
  18.9 0.7 copy-start.2
  26.5 9.0 %collective-permute-start.6 = (bf16[1168,128]{1,0:T(8,128)(2,1)}, bf16[1168,128]{1,0:T(8,128)(2,1)S(1)}, u32[]{:S(2)}, u32[]{:S(2)}) collective-permute-start(bf16[1168,128]{1,0:T(8,128)(2,1)} %pad_maximum_fusion.3), channel_id=1, source_target_pairs={{0,2},{1,3},{2,4},{3,5},{4,6},{5,7},{6,0},{7,1},{8,10},{9,11},{10,... | collective-permute-start | bytes 897032 | tf_op jit(solution)/shard_map/ppermute | solution.py:316
  27.2 8.3 %collective-permute-start.7 = (bf16[1184,128]{1,0:T(8,128)(2,1)}, bf16[1184,128]{1,0:T(8,128)(2,1)S(1)}, u32[]{:S(2)}, u32[]{:S(2)}) collective-permute-start(bf16[1184,128]{1,0:T(8,128)(2,1)} %pad_maximum_fusion.2), channel_id=1, source_target_pairs={{0,6},{1,7},{2,0},{3,1},{4,2},{5,3},{6,4},{7,5},{8,14},{9,15},{10,... | collective-permute-start | bytes 909320 | tf_op jit(solution)/shard_map/ppermute | solution.py:316
  30.6 3.7 %collective-permute-start = (bf16[4,96,128]{2,1,0:T(8,128)(2,1)}, bf16[4,96,128]{2,1,0:T(8,128)(2,1)}, u32[]{:S(2)}, u32[]{:S(2)}) collective-permute-start(bf16[4,96,128]{2,1,0:T(8,128)(2,1)} %pad_maximum_fusion.4), channel_id=1, source_target_pairs={{0,1},{1,0},{2,3},{3,2},{4,5},{5,4},{6,7},{7,6},{8,9},{9,8},{10,11... | collective-permute-start | bytes 294920 | tf_op jit(solution)/shard_map/ppermute | solution.py:293
  35.5 4.7 %collective-permute-start.8 = (bf16[384,128]{1,0:T(8,128)(2,1)S(1)}, bf16[384,128]{1,0:T(8,128)(2,1)S(1)}, u32[]{:S(2)}, u32[]{:S(2)}) collective-permute-start(bf16[384,128]{1,0:T(8,128)(2,1)S(1)} %slice.162), channel_id=1, source_target_pairs={{0,2},{1,3},{2,4},{3,5},{4,6},{5,7},{6,0},{7,1},{8,10},{9,11},{10,... | collective-permute-start | bytes 294920 | tf_op jit(solution)/shard_map/ppermute | solution.py:316
  35.6 4.6 %collective-permute-start.9 = (bf16[400,128]{1,0:T(8,128)(2,1)S(1)}, bf16[400,128]{1,0:T(8,128)(2,1)S(1)}, u32[]{:S(2)}, u32[]{:S(2)}) collective-permute-start(bf16[400,128]{1,0:T(8,128)(2,1)S(1)} %slice.163), channel_id=1, source_target_pairs={{0,6},{1,7},{2,0},{3,1},{4,2},{5,3},{6,4},{7,5},{8,14},{9,15},{10,... | collective-permute-start | bytes 307208 | tf_op jit(solution)/shard_map/ppermute | solution.py:316
  52.8 38.9 %all-to-all-start.1 = ((bf16[8,4,192,128]{3,2,1,0:T(8,128)(2,1)}), bf16[8,4,192,128]{3,2,1,0:T(8,128)(2,1)S(1)}, u32[]{:S(2)}, u32[]{:S(2)}) async-start(bf16[8,4,192,128]{3,2,1,0:T(8,128)(2,1)} %get-tuple-element.12), calls=%async_computation.1 | async-start | bytes 3145728 | tf_op jit(solution)/shard_map/all_to_all | solution.py:348
  56.9 8.9 %copy-start = (bf16[8,384,192]{2,1,0:T(8,128)(2,1)S(1)}, bf16[8,384,192]{2,1,0:T(8,128)(2,1)}, u32[]{:S(2)}) copy-start(bf16[8,384,192]{2,1,0:T(8,128)(2,1)} %get-tuple-element.14) | copy-start | bytes 3538948
  58.3 7.5 %collective-permute-start.13 = (bf16[384,192]{1,0:T(8,128)(2,1)S(1)}, bf16[384,192]{1,0:T(8,128)(2,1)S(1)}, u32[]{:S(2)}, u32[]{:S(2)}) collective-permute-start(bf16[384,192]{1,0:T(8,128)(2,1)S(1)} %get-tuple-element.17), channel_id=1, source_target_pairs={{0,16},{16,32},{32,48},{48,0},{64,80},{80,96},{96,112},{112,64},{1... | collective-permute-start | bytes 442376 | tf_op jit(solution)/shard_map/ppermute | solution.py:367
  59.6 6.2 %collective-permute-start.15 = (bf16[384,192]{1,0:T(8,128)(2,1)S(1)}, bf16[384,192]{1,0:T(8,128)(2,1)S(1)}, u32[]{:S(2)}, u32[]{:S(2)}) collective-permute-start(bf16[384,192]{1,0:T(8,128)(2,1)S(1)} %get-tuple-element.18), channel_id=1, source_target_pairs={{0,48},{16,0},{32,16},{48,32},{64,112},{80,64},{96,80},{112,96},{1... | collective-permute-start | bytes 442376 | tf_op jit(solution)/shard_map/ppermute | solution.py:367
  61.2 6.7 %collective-permute-start.11 = (bf16[4,96,128]{2,1,0:T(8,128)(2,1)S(1)}, bf16[4,96,128]{2,1,0:T(8,128)(2,1)S(1)}, u32[]{:S(2)}, u32[]{:S(2)}) collective-permute-start(bf16[4,96,128]{2,1,0:T(8,128)(2,1)S(1)} %get-tuple-element.28), channel_id=1, source_target_pairs={{0,1},{1,0},{2,3},{3,2},{4,5},{5,4},{6,7},{7,6},{8,9},{9,8},{10,11... | collective-permute-start | bytes 294920 | tf_op jit(solution)/shard_map/ppermute | solution.py:293
  65.9 13.4 %copy-start.4 = (f32[4,96,128]{2,1,0:T(8,128)S(1)}, f32[4,96,128]{2,1,0:T(8,128)}, u32[]{:S(2)}) copy-start(f32[4,96,128]{2,1,0:T(8,128)} %get-tuple-element.13) | copy-start | bytes 589828
  66.0 7.5 %collective-permute-start.16 = (bf16[2,384,192]{2,1,0:T(8,128)(2,1)S(1)}, bf16[2,384,192]{2,1,0:T(8,128)(2,1)S(1)}, u32[]{:S(2)}, u32[]{:S(2)}) collective-permute-start(bf16[2,384,192]{2,1,0:T(8,128)(2,1)S(1)} %pad_maximum_fusion.1), channel_id=1, source_target_pairs={{0,48},{16,0},{32,16},{48,32},{64,112},{80,64},{96,80},{112,96},{1... | collective-permute-start | bytes 884744 | tf_op jit(solution)/shard_map/ppermute | solution.py:367
  67.7 8.2 %collective-permute-start.14 = (bf16[2,384,192]{2,1,0:T(8,128)(2,1)S(1)}, bf16[2,384,192]{2,1,0:T(8,128)(2,1)S(1)}, u32[]{:S(2)}, u32[]{:S(2)}) collective-permute-start(bf16[2,384,192]{2,1,0:T(8,128)(2,1)S(1)} %pad_maximum_fusion), channel_id=1, source_target_pairs={{0,16},{16,32},{32,48},{48,0},{64,80},{80,96},{96,112},{112,64},{1... | collective-permute-start | bytes 884744 | tf_op jit(solution)/shard_map/ppermute | solution.py:367
  76.0 6.8 %collective-permute-start.17 = (bf16[384,192]{1,0:T(8,128)(2,1)S(1)}, bf16[384,192]{1,0:T(8,128)(2,1)S(1)}, u32[]{:S(2)}, u32[]{:S(2)}) collective-permute-start(bf16[384,192]{1,0:T(8,128)(2,1)S(1)} %fusion.5), channel_id=1, source_target_pairs={{0,64},{16,80},{32,96},{48,112},{64,0},{80,16},{96,32},{112,48},{1... | collective-permute-start | bytes 442376 | tf_op jit(solution)/shard_map/ppermute | solution.py:367
  82.9 7.9 %collective-permute-start.18 = (bf16[2,96,192]{2,1,0:T(8,128)(2,1)S(1)}, bf16[2,96,192]{2,1,0:T(8,128)(2,1)S(1)}, u32[]{:S(2)}, u32[]{:S(2)}) collective-permute-start(bf16[2,96,192]{2,1,0:T(8,128)(2,1)S(1)} %get-tuple-element.24), channel_id=1, source_target_pairs={{0,1},{1,0},{2,3},{3,2},{4,5},{5,4},{6,7},{7,6},{8,9},{9,8},{10,11... | collective-permute-start | bytes 221192 | tf_op jit(solution)/shard_map/ppermute | solution.py:293
  92.0 1.4 %collective-permute-start.12 = (bf16[4,96,128]{2,1,0:T(8,128)(2,1)S(1)}, bf16[4,96,128]{2,1,0:T(8,128)(2,1)S(1)}, u32[]{:S(2)}, u32[]{:S(2)}) collective-permute-start(bf16[4,96,128]{2,1,0:T(8,128)(2,1)S(1)} %get-tuple-element.26), channel_id=1, source_target_pairs={{0,1},{1,0},{2,3},{3,2},{4,5},{5,4},{6,7},{7,6},{8,9},{9,8},{10,11... | collective-permute-start | bytes 294920 | tf_op jit(solution)/shard_map/ppermute | solution.py:293

commit v4 on v3

--- a/solution.py
+++ b/solution.py
@@ -13,11 +13,13 @@
 CHUNK = 16
 UNROLL = 12
 MASK_ROWS = 16
+PIECES = 8
 
 
 def attention_kernel(
     place_ref,
-    qd_ref,
+    qd_mine_ref,
+    qd_other_ref,
     own_ref,
     left_ref,
     right_ref,
@@ -27,9 +29,12 @@
     left_far_ref,
     right_far_ref,
     bias_ref,
-    qa_ref,
+    qa_own_ref,
+    qa_away_ref,
     dkv_ref,
-    dbias_ref,
+    right_out_ref,
+    left_out_ref,
+    rest_out_ref,
     kv_ref,
     cap_ref,
     s_ref,
@@ -38,13 +43,15 @@
     dp_ref,
     de_ref,
     row_ref,
+    dbias_ref,
 ):
     step = pl.program_id(0)
     last = pl.num_programs(0) - 1
     rows = bias_ref.shape[0]
     queries = rows // 2
     keys = bias_ref.shape[1]
-    head_width = qd_ref.shape[2] // 4
+    head_width = qd_mine_ref.shape[2] // 4
+    core = place_ref[8 + PIECES]
     scaling = 1.0 / math.sqrt(head_width)
 
     @pl.when(step == 0)
@@ -56,31 +63,34 @@
             return carry
 
         lax.fori_loop(0, rows // CHUNK, fill, 0)
-        height = own_ref.shape[0]
-        cut = left_far_ref.shape[0]
         kv_ref[place_ref[0]] = own_ref[...]
         kv_ref[place_ref[1]] = left_ref[...]
         kv_ref[place_ref[2]] = right_ref[...]
-        kv_ref[place_ref[3], :cut] = left_pair_ref[height:]
-        kv_ref[place_ref[3], cut:] = right_pair_ref[height:]
+        kv_ref[place_ref[3], 0] = left_pair_ref[2]
+        kv_ref[place_ref[3], 1] = right_pair_ref[2]
         kv_ref[place_ref[4]] = across_ref[...]
-        kv_ref[place_ref[5]] = left_pair_ref[:height]
-        kv_ref[place_ref[6]] = right_pair_ref[:height]
-        kv_ref[place_ref[7], :cut] = left_far_ref[...]
-        kv_ref[place_ref[7], cut:] = right_far_ref[...]
-        first = height - MASK_ROWS
-        masks = kv_ref[:, first:, :].astype(jnp.float32)
+        kv_ref[place_ref[5]] = left_pair_ref[:2]
+        kv_ref[place_ref[6]] = right_pair_ref[:2]
+        kv_ref[place_ref[7], 0] = left_far_ref[...]
+        kv_ref[place_ref[7], 1] = right_far_ref[...]
+        first = own_ref.shape[1] - MASK_ROWS
+        masks = kv_ref[:, :, first:, :].astype(jnp.float32)
         for column in range(cap_ref.shape[0]):
             pieces = []
             for group in range(masks.shape[0]):
-                pieces.append(masks[group, 2 * column : 2 * column + 1, :])
-                pieces.append(masks[group, 2 * column + 1 : 2 * column + 2, : queries - 128])
+                for side in range(2):
+                    pieces.append(masks[group, side, column : column + 1, : queries // 2])
             cap_ref[column] = jnp.where(
                 jnp.concatenate(pieces, axis=1) > 0.5, 1e30, NEG_FILL * LOG2E
             )
 
-    kv = kv_ref[:, pl.ds(step * queries, queries), :].reshape(keys, 4 * head_width)
-    qd = qd_ref[0]
+    half = queries // 2
+    kv = kv_ref[:, :, pl.ds(step * half, half), :].reshape(keys, 4 * head_width)
+    qd_mine = qd_mine_ref[0]
+    qd_other = qd_other_ref[0]
+    qd = jnp.concatenate(
+        [jnp.where(core == 0, qd_mine, qd_other), jnp.where(core == 0, qd_other, qd_mine)], axis=0
+    )
     lane = lax.broadcasted_iota(jnp.int32, (queries, 4 * head_width), 1)
     zero = jnp.zeros_like(qd)
 
@@ -153,7 +163,8 @@
         jnp.where(lane < head_width, q0, q1),
         jnp.where(lane < 3 * head_width, att0, att1),
     )
-    qa_ref[0] = merged.astype(jnp.bfloat16)
+    qa_own_ref[0] = jnp.where(core == 0, merged[:half], merged[half:]).astype(jnp.bfloat16)
+    qa_away_ref[0] = jnp.where(core == 0, merged[half:], merged[:half]).astype(jnp.bfloat16)
     sides = jnp.concatenate(query_rows + [sc0, sc1], axis=0)
     key_value = lax.dot_general(
         sides, de_ref[...], (((0,), (0,)), ((), ())), preferred_element_type=jnp.float32
@@ -162,10 +173,50 @@
 
     @pl.when(step == last)
     def _():
-        width = dbias_ref.shape[2]
-        for piece in range(dbias_ref.shape[0]):
-            part = acc_ref[:, piece * width : (piece + 1) * width]
-            dbias_ref[place_ref[8 + piece]] = part.astype(jnp.bfloat16)
+        width = dbias_ref.shape[3]
+        for piece in range(PIECES):
+            for head in range(2):
+                for side in range(2):
+                    start = head * queries + side * half
+                    part = acc_ref[start : start + half, piece * width : (piece + 1) * width]
+                    target = 2 * place_ref[8 + piece] + (side + core) % 2
+                    dbias_ref[target, head] = part.astype(jnp.bfloat16)
+        right_out_ref[...] = dbias_ref[8:10]
+        left_out_ref[...] = dbias_ref[10:12]
+        rest_out_ref[:8] = dbias_ref[:8]
+        rest_out_ref[8:] = dbias_ref[12:]
+
+
+def prepare_kernel(core_ref, key_ref, value_ref, mask_ref, mine_ref, other_ref):
+    columns, tokens, channels = key_ref.shape
+    half = channels // 2
+    core = core_ref[0]
+    filler = jnp.zeros((MASK_ROWS - columns, channels), jnp.float32)
+    mask = mask_ref[...].astype(jnp.float32)
+    mask = jnp.concatenate([mask, jnp.zeros((columns, channels - tokens), jnp.float32)], axis=1)
+    mask = jnp.concatenate([mask, filler], axis=0).astype(jnp.bfloat16)
+    for column in range(columns):
+        key = key_ref[column]
+        value = value_ref[column]
+        low = jnp.concatenate([key[:, :half], value[:, :half]], axis=1)
+        high = jnp.concatenate([key[:, half:], value[:, half:]], axis=1)
+        part = slice(column * tokens, (column + 1) * tokens)
+        mine_ref[part, :] = jnp.where(core == 0, low, high)
+        other_ref[part, :] = jnp.where(core == 0, high, low)
+    mine_ref[columns * tokens :, :] = mask
+    other_ref[columns * tokens :, :] = mask
+
+
+def prepare(core, key, value, mask):
+    columns, tokens, channels = key.shape
+    out = jax.ShapeDtypeStruct((columns * tokens + MASK_ROWS, channels), jnp.bfloat16)
+    vmem = pl.BlockSpec(memory_space=pltpu.VMEM)
+    return pl.pallas_call(
+        prepare_kernel,
+        in_specs=[pl.BlockSpec(memory_space=pltpu.SMEM), vmem, vmem, vmem],
+        out_shape=[out, out],
+        name="prepare_key_value",
+    )(core, key, value, mask)
 
 
 def pack_kernel(cotangent_ref, packed_ref):
@@ -186,55 +237,87 @@
     )(cotangent)
 
 
-def project_kernel(packed_ref, weight_ref, gate_ref, grad_ref, slope_ref):
+def project_kernel(core_ref, packed_ref, weight_ref, gate_ref, query_ref, mine_ref, other_ref, slope_ref):
     pieces, rows, lanes = packed_ref.shape
     columns, tokens, channels = gate_ref.shape
+    half = channels // 2
+    core = core_ref[0]
     whole = packed_ref[...].astype(jnp.float32).reshape(pieces, columns, rows // columns, lanes)
     for column in range(columns):
         part = whole[:, column].reshape(channels, lanes).astype(jnp.bfloat16)
         gated = jnp.dot(weight_ref[...], part, preferred_element_type=jnp.float32).T[:tokens]
         sigma = jax.nn.sigmoid(gate_ref[column].astype(jnp.float32))
         grad = gated * sigma
-        grad_ref[column] = grad.astype(jnp.bfloat16)
         slope_ref[column] = grad * (1.0 - sigma)
-
-
-def project(packed, weight, gate):
+        grad = grad.astype(jnp.bfloat16)
+        query = query_ref[column]
+        low = jnp.concatenate([query[:, :half], grad[:, :half]], axis=1)
+        high = jnp.concatenate([query[:, half:], grad[:, half:]], axis=1)
+        mine_ref[column] = jnp.where(core == 0, low, high)
+        other_ref[column] = jnp.where(core == 0, high, low)
+
+
+def project(core, packed, weight, gate, query):
+    vmem = pl.BlockSpec(memory_space=pltpu.VMEM)
     return pl.pallas_call(
         project_kernel,
+        in_specs=[pl.BlockSpec(memory_space=pltpu.SMEM)] + [vmem] * 4,
         out_shape=[
+            jax.ShapeDtypeStruct(gate.shape, jnp.bfloat16),
             jax.ShapeDtypeStruct(gate.shape, jnp.bfloat16),
             jax.ShapeDtypeStruct(gate.shape, jnp.float32),
         ],
         name="project_cotangent",
-    )(packed, weight, gate)
-
-
-def attend(places, query_grad, blocks, bias, chips, row_count):
-    columns, queries, lanes = query_grad.shape
+    )(core, packed, weight, gate, query)
+
+
+def total_kernel(parts_ref, key_ref, value_ref):
+    half = key_ref.shape[2] // 2
+    scaling = 1.0 / math.sqrt(key_ref.shape[2] // HEADS)
+    for column in range(key_ref.shape[0]):
+        sums = [
+            jnp.sum(parts_ref[:, side, column].astype(jnp.float32), axis=0) for side in range(2)
+        ]
+        key = jnp.concatenate([part[:, :half] for part in sums], axis=1) * scaling
+        key_ref[column] = key.astype(jnp.bfloat16)
+        value = jnp.concatenate([part[:, half:] for part in sums], axis=1)
+        value_ref[column] = value.astype(jnp.bfloat16)
+
+
+def total(parts, like):
+    out = jax.ShapeDtypeStruct(like.shape, jnp.bfloat16)
+    return pl.pallas_call(total_kernel, out_shape=[out, out], name="total_key_value")(parts)
+
+
+def attend(places, mine, other, blocks, bias, chips, row_count):
+    columns, tokens, lanes = mine.shape
     rows, keys = bias.shape
-    height = blocks[0].shape[0]
     width = keys // row_count
     work = columns * rows * keys
 
-    def whole(array):
-        return pl.BlockSpec(array.shape, lambda j, places: (0,) * array.ndim)
-
+    def whole(shape):
+        return pl.BlockSpec(shape, lambda j, places: (0,) * len(shape))
+
+    column_spec = pl.BlockSpec((1, tokens, lanes), lambda j, places: (j, 0, 0))
+    piece = (2, tokens, width)
     return pl.pallas_call(
         attention_kernel,
         grid_spec=pltpu.PrefetchScalarGridSpec(
             num_scalar_prefetch=1,
             grid=(columns,),
-            in_specs=[pl.BlockSpec((1, queries, lanes), lambda j, places: (j, 0, 0))]
-            + [whole(block) for block in blocks]
-            + [whole(bias)],
+            in_specs=[column_spec, column_spec]
+            + [whole(block.shape) for block in blocks]
+            + [whole(bias.shape)],
             out_specs=[
-                pl.BlockSpec((1, queries, lanes), lambda j, places: (j, 0, 0)),
-                pl.BlockSpec((chips, 1, queries, lanes), lambda j, places: (0, j, 0, 0)),
-                pl.BlockSpec((row_count, rows, width), lambda j, places: (0, 0, 0)),
+                column_spec,
+                column_spec,
+                pl.BlockSpec((chips, 2, 1, tokens, lanes), lambda j, places: (0, 0, j, 0, 0)),
+                whole((2,) + piece),
+                whole((2,) + piece),
+                whole((12,) + piece),
             ],
             scratch_shapes=[
-                pltpu.VMEM((chips, height, lanes), jnp.bfloat16),
+                pltpu.VMEM((chips,) + blocks[0].shape, jnp.bfloat16),
                 pltpu.VMEM((columns, 1, keys), jnp.float32),
                 pltpu.VMEM((rows, keys), jnp.float32),
                 pltpu.VMEM((rows, keys), jnp.float32),
@@ -242,17 +325,21 @@
                 pltpu.VMEM((rows, keys), jnp.float32),
                 pltpu.VMEM((2 * rows, keys), jnp.bfloat16),
                 pltpu.VMEM((rows, 128), jnp.float32),
+                pltpu.VMEM((16,) + piece, jnp.bfloat16),
             ],
         ),
         out_shape=[
-            jax.ShapeDtypeStruct((columns, queries, lanes), jnp.bfloat16),
-            jax.ShapeDtypeStruct((chips, columns, queries, lanes), jnp.bfloat16),
-            jax.ShapeDtypeStruct((row_count, rows, width), jnp.bfloat16),
+            jax.ShapeDtypeStruct(mine.shape, jnp.bfloat16),
+            jax.ShapeDtypeStruct(mine.shape, jnp.bfloat16),
+            jax.ShapeDtypeStruct((chips, 2, columns, tokens, lanes), jnp.bfloat16),
+            jax.ShapeDtypeStruct((2,) + piece, jnp.bfloat16),
+            jax.ShapeDtypeStruct((2,) + piece, jnp.bfloat16),
+            jax.ShapeDtypeStruct((12,) + piece, jnp.bfloat16),
         ],
         compiler_params=pltpu.CompilerParams(vmem_limit_bytes=48 * 1024 * 1024),
         cost_estimate=pl.CostEstimate(flops=12 * 128 * work, bytes_accessed=16 * 2**20, transcendentals=work),
         name="attention_both",
-    )(places, query_grad, *blocks, bias)
+    )(places, mine, other, *blocks, bias)
 
 
 def local(
@@ -295,16 +382,9 @@
     bias_mine, bias_other = mine_other(pair_bias, 0)
     bias_pair = in_order(bias_mine, swapped(bias_other), 1).reshape(-1, keys)
 
-    key_mine, key_other = mine_other(key_vectors, 2)
-    value_mine, value_other = mine_other(value_vectors, 2)
-    kv_mine = jnp.concatenate([key_mine, value_mine], axis=2)
-    kv_other = swapped(jnp.concatenate([key_other, value_other], axis=2))
-    mask_low = pair_mask.astype(jnp.bfloat16)
-    kv_chip = in_order(kv_mine, kv_other, 1)
-    mask_chip = in_order(mask_low, swapped(mask_low), 1)
-    mask_rows = jnp.pad(mask_chip, ((0, 0), (0, 256 - 2 * tokens))).reshape(-1, channels)
-    mask_rows = jnp.pad(mask_rows, ((0, MASK_ROWS - 2 * columns), (0, 0)))
-    block = jnp.concatenate([kv_chip.reshape(-1, channels), mask_rows], axis=0)
+    core_word = core.astype(jnp.int32).reshape(1)
+    kv_mine, kv_away = prepare(core_word, key_vectors, value_vectors, pair_mask)
+    block = in_order(kv_mine[None], swapped(kv_away)[None], 0)
     ring = chips // 2
 
     def along(array, turn, side):
@@ -315,12 +395,12 @@
             pairs.append((index, 2 * target + index % 2))
         return lax.ppermute(array, "col", pairs)
 
-    cut = columns * tokens
+    block, output_cotangent = lax.optimization_barrier((block, output_cotangent))
     left, right, across = along(block, 1, 0), along(block, -1, 0), along(block, 0, 1)
-    left_pair = along(jnp.concatenate([across, left[:cut]], axis=0), 1, 0)
-    right_pair = along(jnp.concatenate([across, right[cut:]], axis=0), -1, 0)
-    left_far = along(left_pair[:cut], 1, 0)
-    right_far = along(right_pair[cut : block.shape[0]], -1, 0)
+    left_pair = along(jnp.concatenate([across, left[:1]], axis=0), 1, 0)
+    right_pair = along(jnp.concatenate([across, right[1:]], axis=0), -1, 0)
+    left_far = along(left_pair[0], 1, 0)
+    right_far = along(right_pair[1], -1, 0)
     blocks = [block, left, right, across, left_pair, right_pair, left_far, right_far]
     chip = lax.axis_index("col") // 2
     place = lax.axis_index("row")
@@ -333,27 +413,21 @@
         2 * ((index % row_ring - place) % row_ring) + (index // row_ring - place // row_ring) % 2
         for index in range(row_count)
     ]
+    places.append(core)
     places = jnp.stack(places).astype(jnp.int32)
 
     regrouped = lax.all_to_all(pack(output_cotangent, devices), "col", 0, 0, tiled=True)
-    attended_grad, gate_slope = project(regrouped, output_weight, gate_logits)
-    query_mine, query_other = mine_other(query_vectors, 2)
-    grad_mine, grad_other = mine_other(attended_grad, 2)
-    qd_mine = jnp.concatenate([query_mine, grad_mine], axis=2)
-    qd_other = swapped(jnp.concatenate([query_other, grad_other], axis=2))
-    query_grad = in_order(qd_mine, qd_other, 1)
-
-    query_attended, kv_grads, bias_grads = attend(places, query_grad, blocks, bias_pair, chips, row_count)
-
-    kv_parts = lax.all_to_all(kv_grads, "col", 0, 0, tiled=True, axis_index_groups=chip_groups)
-    kv_sum = jnp.sum(kv_parts.astype(jnp.float32), axis=0).astype(jnp.bfloat16)
-    kv_own, kv_away = mine_other(kv_sum, 1)
-    kv_back = swapped(kv_away)
-    key_gradient = in_order(kv_own[..., :half], kv_back[..., :half], 2)
-    key_gradient = (key_gradient.astype(jnp.float32) * scaling).astype(jnp.bfloat16)
-    value_gradient = in_order(kv_own[..., half:], kv_back[..., half:], 2)
-
-    qa_own, qa_away = mine_other(query_attended, 1)
+    qd_mine, qd_away, gate_slope = project(core_word, regrouped, output_weight, gate_logits, query_vectors)
+
+    qa_own, qa_away, kv_grads, bias_right, bias_left, bias_rest = attend(
+        places, qd_mine, swapped(qd_away), blocks, bias_pair, chips, row_count
+    )
+
+    kv_parts = lax.all_to_all(
+        kv_grads.reshape((devices,) + kv_grads.shape[2:]), "col", 0, 0, tiled=True
+    )
+    key_gradient, value_gradient = total(kv_parts.reshape(kv_grads.shape), key_vectors)
+
     qa_back = swapped(qa_away)
     query_gradient = in_order(qa_own[..., :half], qa_back[..., :half], 2)
     attended = in_order(qa_own[..., half:], qa_back[..., half:], 2).astype(jnp.float32)
@@ -369,18 +443,19 @@
     def added(*parts):
         return sum(part.astype(jnp.float32) for part in parts)
 
-    from_left = along_row(bias_grads[4], 1, 0)
-    from_right = along_row(bias_grads[5], -1, 0)
-    onward = jnp.stack([added(bias_grads[2], from_left).astype(jnp.bfloat16), bias_grads[3]])
-    backward = jnp.stack([bias_grads[6], added(bias_grads[7], from_right).astype(jnp.bfloat16)])
-    from_left = along_row(onward, 1, 0)
-    from_right = along_row(backward, -1, 0)
-    bias_away = added(bias_grads[1], from_left[1], from_right[1]).astype(jnp.bfloat16)
-    bias_sum = added(bias_grads[0], from_left[0], from_right[0], along_row(bias_away, 0, 1))
-    bias_sum = bias_sum.astype(jnp.bfloat16)
-    bias_sum = bias_sum.reshape(2, 2 * tokens, keys // row_count)
-    bias_own, bias_away = mine_other(bias_sum, 1)
-    bias_gradient = in_order(bias_own, swapped(bias_away), 0).astype(jnp.float32)
+    from_left = along_row(bias_right, 1, 0)
+    from_right = along_row(bias_left, -1, 0)
+    onward = jnp.concatenate([added(bias_rest[4:6], from_left).astype(jnp.bfloat16), bias_rest[6:8]])
+    backward = jnp.concatenate([bias_rest[8:10], added(bias_rest[10:], from_right).astype(jnp.bfloat16)])
+    sums = added(bias_rest[:4], along_row(onward, 1, 0), along_row(backward, -1, 0))
+    low_sums = sums.astype(jnp.bfloat16)
+    diagonal = []
+    for index in range(row_count * devices):
+        up = (index // devices + row_ring) % row_count
+        diagonal.append((index, up * devices + (index % devices ^ 1)))
+    bias_own = added(sums[0], along_row(low_sums[2], 0, 1))
+    bias_away = added(swapped(low_sums[1]), lax.ppermute(low_sums[3], ("row", "col"), diagonal))
+    bias_gradient = in_order(bias_own, bias_away, 0)
     return (query_gradient, key_gradient, value_gradient, gate_gradient, bias_gradient)
 
 

time: 95.5 us -> 97.2 us (1.018)
  waiting for transfers between devices: 18.3 us -> 37 us
  starting transfers between devices: 43.7 us -> 32.5 us
  other arithmetic: 13.4 us -> 5.82 us
  Pallas kernels: 16.2 us -> 19.7 us
  local copies, waits for them, and re-layouts: 2.59 us -> 1.04 us
    ppermute x7 -> x5, starting transfers between devices: 16.5 us -> 4.38 us  [swapped(): return lax.ppermute(array, 'col', swap)]
    ppermute x5, waiting for transfers between devices: 10.6 us -> 18.1 us  [along_row(): return lax.ppermute(array, 'row', pairs)]
    ppermute x7, waiting for transfers between devices: 4.64 us -> 11.2 us  [along(): return lax.ppermute(array, 'col', pairs)]
    ppermute x0 -> x1, starting transfers between devices: none -> 5.56 us  [local(): lax.ppermute(low_sums[3], ('row', 'col'), diagonal)]
    all_to_all x1, waiting for transfers between devices: 0.01 us -> 4.88 us  [local(): lax.all_to_all(pack(output_cotangent, devices), 'col', 0, 0, tiled=True)]
    pallas_call x1 -> x3, Pallas kernels: 1.94 us -> 6.24 us  [the longest x1 2.32 us: total(): pl.pallas_call(total_kernel, out_shape=[out, out], name='total_key_value')]
    ppermute x5, starting transfers between devices: 7.92 us -> 5.44 us  [along_row(): return lax.ppermute(array, 'row', pairs)]
    all_to_all x1, starting transfers between devices: 5.86 us -> 3.41 us  [local(): lax.all_to_all(pack(output_cotangent, devices), 'col', 0, 0, tiled=True)]
  transfers between devices with their start and end apart: 21 -> 20, of which waited for: 9 -> 12; matrix products, arithmetic and copies ran while one was open for 13% -> 5% of each run, Pallas kernels for 4% -> 4%
where the time goes in v4:
time: 97.2 us; the launch traced here: 96.8 us
  waiting for transfers between devices  37 us (38%)
  starting transfers between devices  32.5 us (33%)
  Pallas kernels  19.7 us (20%)
  other arithmetic  5.82 us (6%)
  local copies, waits for them, and re-layouts  1.04 us (1%)
    ppermute x5, waiting for transfers between devices, along_row(): return lax.ppermute(array, 'row', pairs)  18.1 us
    pallas_call x1, Pallas kernels, attend(): pl.pallas_call(attention_kernel, grid_spec=pltpu.PrefetchScalarGridSpec(n...  11.8 us
    ppermute x7, waiting for transfers between devices, along(): return lax.ppermute(array, 'col', pairs)  11.2 us
    ppermute x7, starting transfers between devices, along(): return lax.ppermute(array, 'col', pairs)  7.68 us
    all_to_all x1, starting transfers between devices, local(): lax.all_to_all(kv_grads.reshape((devices,) + kv_grads.shape[2:]), 'col',...  6 us
    ppermute x1, starting transfers between devices, local(): lax.ppermute(low_sums[3], ('row', 'col'), diagonal)  5.56 us
    ppermute x5, starting transfers between devices, along_row(): return lax.ppermute(array, 'row', pairs)  5.44 us
    all_to_all x1, waiting for transfers between devices, local(): lax.all_to_all(pack(output_cotangent, devices), 'col', 0, 0, tiled=True)  4.88 us
  transfers between devices with their start and end apart: 20, of which 12 were waited for; matrix products, arithmetic and copies ran while one was open for 5% of the time, Pallas kernels for 4%

profile of v4, /device:TPU:1, one launch (start us, length us, event | category | flops | bytes accessed | tf_op | source)
XLA Modules:
  0.0 96.8 jit_solution(8518151866032794792)
XLA Ops:
  0.7 1.8 %prepare_key_value.1 = (bf16[400,128]{1,0:T(8,128)(2,1)}, bf16[400,128]{1,0:T(8,128)(2,1)}) custom-call(s32[1]{0:T(128)} %bitcast.16.core_ref, bf16[4,96,128]{2,1,0:T(8,128)(2,1)} %key_ref.1, bf16[4,96,128]{2,1,0:T(8,128)(2,1)} %value_ref.1, s32[4,96]{1,0:T(4,128)} %mask_ref.1), custom_call_target="tpu_custom_call" | custom-call | tf_op jit(solution)/shard_map/prepare_key_value/pallas_call | solution.py:214
  2.5 1.4 %collective-permute-start = (bf16[400,128]{1,0:T(8,128)(2,1)}, bf16[400,128]{1,0:T(8,128)(2,1)S(1)}, u32[]{:S(2)}, u32[]{:S(2)}) collective-permute-start(bf16[400,128]{1,0:T(8,128)(2,1)} %get-tuple-element.21), channel_id=1, source_target_pairs={{0,1},{1,0},{2,3},{3,2},{4,5},{5,4},{6,7},{7,6},{8,9},{9,8},{10,11... | collective-permute-start | bytes 307208 | tf_op jit(solution)/shard_map/ppermute | solution.py:380
  3.9 1.2 %collective-permute-done = bf16[400,128]{1,0:T(8,128)(2,1)S(1)} collective-permute-done((bf16[400,128]{1,0:T(8,128)(2,1)}, bf16[400,128]{1,0:T(8,128)(2,1)S(1)}, u32[]{:S(2)}, u32[]{:S(2)}) %collective-permute-start) | collective-permute-done | bytes 102432 | tf_op jit(solution)/shard_map/ppermute | solution.py:380
  5.1 1.0 %maximum_select_fusion.2.own_ref = bf16[2,400,128]{2,1,0:T(8,128)(2,1)S(1)} fusion(bf16[1,400,128]{2,1,0:T(8,128)(2,1)S(1)} %bitcast.39, bf16[1,400,128]{2,1,0:T(8,128)(2,1)} %bitcast.38, pred[]{:T(512)S(6)} %eq.51), kind=kLoop, calls=%fused_computation.11 | loop fusion | flops 307200 | bytes 409601 | tf_op jit(solution)/shard_map/jit(_where)/select_n | solution.py:373
  6.1 2.6 %collective-permute-start.3 = (bf16[2,400,128]{2,1,0:T(8,128)(2,1)S(1)}, bf16[2,400,128]{2,1,0:T(8,128)(2,1)S(1)}, u32[]{:S(2)}, u32[]{:S(2)}) collective-permute-start(bf16[2,400,128]{2,1,0:T(8,128)(2,1)S(1)} %maximum_select_fusion.2.own_ref), channel_id=1, source_target_pairs={{0,6},{1,7},{2,0},{3,1},{4,2},{5,3},{6,4},{7,5},{8,14},{9,15},{10,... | collective-permute-start | bytes 614408 | tf_op jit(solution)/shard_map/ppermute | solution.py:396
  8.7 1.6 %collective-permute-start.4 = (bf16[2,400,128]{2,1,0:T(8,128)(2,1)S(1)}, bf16[2,400,128]{2,1,0:T(8,128)(2,1)S(1)}, u32[]{:S(2)}, u32[]{:S(2)}) collective-permute-start(bf16[2,400,128]{2,1,0:T(8,128)(2,1)S(1)} %maximum_select_fusion.2.own_ref), channel_id=1, source_target_pairs={{0,8},{1,9},{2,10},{3,11},{4,12},{5,13},{6,14},{7,15},{8,0},{9,1},... | collective-permute-start | bytes 614408 | tf_op jit(solution)/shard_map/ppermute | solution.py:396
  10.3 2.5 %collective-permute-done.3.right_ref = bf16[2,400,128]{2,1,0:T(8,128)(2,1)S(1)} collective-permute-done((bf16[2,400,128]{2,1,0:T(8,128)(2,1)S(1)}, bf16[2,400,128]{2,1,0:T(8,128)(2,1)S(1)}, u32[]{:S(2)}, u32[]{:S(2)}) %collective-permute-start.3) | collective-permute-done | bytes 204832 | tf_op jit(solution)/shard_map/ppermute | solution.py:396
  12.8 3.1 %collective-permute-done.2.left_ref = bf16[2,400,128]{2,1,0:T(8,128)(2,1)S(1)} collective-permute-done((bf16[2,400,128]{2,1,0:T(8,128)(2,1)S(1)}, bf16[2,400,128]{2,1,0:T(8,128)(2,1)S(1)}, u32[]{:S(2)}, u32[]{:S(2)}) %collective-permute-start.2) | collective-permute-done | bytes 204832 | tf_op jit(solution)/shard_map/ppermute | solution.py:396
  15.9 0.8 pad_maximum_fusion.2
  16.7 1.5 %collective-permute-start.6 = (bf16[3,400,128]{2,1,0:T(8,128)(2,1)}, bf16[3,400,128]{2,1,0:T(8,128)(2,1)S(1)}, u32[]{:S(2)}, u32[]{:S(2)}) collective-permute-start(bf16[3,400,128]{2,1,0:T(8,128)(2,1)} %get-tuple-element.46), channel_id=1, source_target_pairs={{0,6},{1,7},{2,0},{3,1},{4,2},{5,3},{6,4},{7,5},{8,14},{9,15},{10,... | collective-permute-start | bytes 921608 | tf_op jit(solution)/shard_map/ppermute | solution.py:396
  18.2 0.9 broadcast_select_fusion.1
  19.1 1.9 %collective-permute-start.9 = (bf16[2,96,1536]{2,1,0:T(8,128)(2,1)}, bf16[2,96,1536]{2,1,0:T(8,128)(2,1)S(1)}, u32[]{:S(2)}, u32[]{:S(2)}) collective-permute-start(bf16[2,96,1536]{2,1,0:T(8,128)(2,1)} %get-tuple-element.42), channel_id=1, source_target_pairs={{0,1},{1,0},{2,3},{3,2},{4,5},{5,4},{6,7},{7,6},{8,9},{9,8},{10,11... | collective-permute-start | bytes 1769480 | tf_op jit(solution)/shard_map/ppermute | solution.py:380
  21.0 1.7 %pack_cotangent.1 = bf16[16,32,128]{2,1,0:T(8,128)(2,1)} custom-call(bf16[4,8,1536]{2,1,0:T(8,128)(2,1)} %cotangent_ref), custom_call_target="tpu_custom_call" | custom-call | tf_op jit(solution)/shard_map/pack_cotangent/pallas_call | solution.py:233
  22.7 3.4 %all-to-all-start = ((bf16[16,32,128]{2,1,0:T(8,128)(2,1)}), bf16[16,32,128]{2,1,0:T(8,128)(2,1)S(1)}, u32[]{:S(2)}, u32[]{:S(2)}) async-start(bf16[16,32,128]{2,1,0:T(8,128)(2,1)} %pack_cotangent.1), calls=%async_computation | async-start | bytes 262144 | tf_op jit(solution)/shard_map/all_to_all | solution.py:419
  26.1 1.3 %collective-permute-start.5 = (bf16[3,400,128]{2,1,0:T(8,128)(2,1)S(1)}, bf16[3,400,128]{2,1,0:T(8,128)(2,1)S(1)}, u32[]{:S(2)}, u32[]{:S(2)}) collective-permute-start(bf16[3,400,128]{2,1,0:T(8,128)(2,1)S(1)} %get-tuple-element.47), channel_id=1, source_target_pairs={{0,2},{1,3},{2,4},{3,5},{4,6},{5,7},{6,0},{7,1},{8,10},{9,11},{10,... | collective-permute-start | bytes 921608 | tf_op jit(solution)/shard_map/ppermute | solution.py:396
  27.3 0.1 stack.71.place_ref
  27.4 4.9 %all-to-all-done.packed_ref = bf16[16,32,128]{2,1,0:T(8,128)(2,1)S(1)} async-done(((bf16[16,32,128]{2,1,0:T(8,128)(2,1)}), bf16[16,32,128]{2,1,0:T(8,128)(2,1)S(1)}, u32[]{:S(2)}, u32[]{:S(2)}) %all-to-all-start) | async-done | bytes 131104 | tf_op jit(solution)/shard_map/all_to_all | solution.py:419
  32.3 0.7 copy-done.2
  33.0 2.1 %project_cotangent.1 = (bf16[4,96,128]{2,1,0:T(8,128)(2,1)}, bf16[4,96,128]{2,1,0:T(8,128)(2,1)}, f32[4,96,128]{2,1,0:T(8,128)}) custom-call(s32[1]{0:T(128)} %bitcast.16.core_ref, bf16[16,32,128]{2,1,0:T(8,128)(2,1)} %copy-done.2, bf16[128,128]{1,0:T(8,128)(2,1)} %weight_ref.1, bf16[4,96,128]{2,1,0:T(8,128)(2,1)} %gate_ref.1, bf16[4,96,128]{2,1,0:T(8,128)(2,1)} %query_ref.1), custom_call_target="tpu_custom_call" | custom-call | tf_op jit(solution)/shard_map/project_cotangent/pallas_call | solution.py:262
  35.1 0.7 collective-permute-start.1
  35.8 0.6 collective-permute-start.8
  36.3 1.3 %collective-permute-done.5.left_pair_ref = bf16[3,400,128]{2,1,0:T(8,128)(2,1)S(1)} collective-permute-done((bf16[3,400,128]{2,1,0:T(8,128)(2,1)S(1)}, bf16[3,400,128]{2,1,0:T(8,128)(2,1)S(1)}, u32[]{:S(2)}, u32[]{:S(2)}) %collective-permute-start.5) | collective-permute-done | bytes 307232 | tf_op jit(solution)/shard_map/ppermute | solution.py:396
  37.7 0.1 collective-permute-start.7
  37.8 0.4 maximum_select_fusion
  38.2 2.2 %collective-permute-done.8.right_far_ref = bf16[400,128]{1,0:T(8,128)(2,1)S(1)} collective-permute-done((bf16[400,128]{1,0:T(8,128)(2,1)S(1)}, bf16[400,128]{1,0:T(8,128)(2,1)S(1)}, u32[]{:S(2)}, u32[]{:S(2)}) %collective-permute-start.8) | collective-permute-done | bytes 102432 | tf_op jit(solution)/shard_map/ppermute | solution.py:396
  40.4 2.1 %collective-permute-done.7.left_far_ref = bf16[400,128]{1,0:T(8,128)(2,1)S(1)} collective-permute-done((bf16[400,128]{1,0:T(8,128)(2,1)S(1)}, bf16[400,128]{1,0:T(8,128)(2,1)S(1)}, u32[]{:S(2)}, u32[]{:S(2)}) %collective-permute-start.7) | collective-permute-done | bytes 102432 | tf_op jit(solution)/shard_map/ppermute | solution.py:396
  42.5 11.8 %attention_both.1 = (bf16[4,96,128]{2,1,0:T(8,128)(2,1)S(1)}, bf16[4,96,128]{2,1,0:T(8,128)(2,1)S(1)}, bf16[8,2,4,96,128]{4,3,2,1,0:T(8,128)(2,1)}, bf16[2,2,96,...) custom-call(s32[17]{0:T(128)S(1)} %stack.71.place_ref, ...), custom_call_target="tpu_custom_call" | custom-call | flops 3623878656 | bytes 16777216 | tf_op jit(solution)/shard_map/attention_both/pallas_call | solution.py:303
  54.3 6.0 %all-to-all-start.1 = ((bf16[16,4,96,128]{3,2,1,0:T(8,128)(2,1)}), bf16[16,4,96,128]{3,2,1,0:T(8,128)(2,1)}, u32[]{:S(2)}, u32[]{:S(2)}) async-start(bf16[16,4,96,128]{3,2,1,0:T(8,128)(2,1)} %bitcast.37), calls=%async_computation.1 | async-start | bytes 3145728 | tf_op jit(solution)/shard_map/all_to_all | solution.py:426
  60.3 0.4 collective-permute-start.10
  60.7 1.3 %collective-permute-start.11 = (bf16[2,2,96,192]{3,2,1,0:T(8,128)(2,1)S(1)}, bf16[2,2,96,192]{3,2,1,0:T(8,128)(2,1)S(1)}, u32[]{:S(2)}, u32[]{:S(2)}) collective-permute-start(bf16[2,2,96,192]{3,2,1,0:T(8,128)(2,1)S(1)} %get-tuple-element.33), channel_id=1, source_target_pairs={{0,16},{16,32},{32,48},{48,0},{64,80},{80,96},{96,112},{112,64},{1... | collective-permute-start | bytes 442376 | tf_op jit(solution)/shard_map/ppermute | solution.py:441
  62.0 1.4 %collective-permute-start.13 = (bf16[2,2,96,192]{3,2,1,0:T(8,128)(2,1)S(1)}, bf16[2,2,96,192]{3,2,1,0:T(8,128)(2,1)S(1)}, u32[]{:S(2)}, u32[]{:S(2)}) collective-permute-start(bf16[2,2,96,192]{3,2,1,0:T(8,128)(2,1)S(1)} %get-tuple-element.34), channel_id=1, source_target_pairs={{0,48},{16,0},{32,16},{48,32},{64,112},{80,64},{96,80},{112,96},{1... | collective-permute-start | bytes 442376 | tf_op jit(solution)/shard_map/ppermute | solution.py:441
  63.5 0.1 fusion.3
  63.6 4.9 %collective-permute-done.11 = bf16[2,2,96,192]{3,2,1,0:T(8,128)(2,1)S(1)} collective-permute-done((bf16[2,2,96,192]{3,2,1,0:T(8,128)(2,1)S(1)}, bf16[2,2,96,192]{3,2,1,0:T(8,128)(2,1)S(1)}, u32[]{:S(2)}, u32[]{:S(2)}) %collective-permute-start.11) | collective-permute-done | bytes 147488 | tf_op jit(solution)/shard_map/ppermute | solution.py:441
  68.5 0.1 add_convert_fusion.1
  68.7 2.4 %collective-permute-start.14 = (bf16[4,2,96,192]{3,2,1,0:T(8,128)(2,1)S(1)}, bf16[4,2,96,192]{3,2,1,0:T(8,128)(2,1)S(1)}, u32[]{:S(2)}, u32[]{:S(2)}) collective-permute-start(bf16[4,2,96,192]{3,2,1,0:T(8,128)(2,1)S(1)} %pad_maximum_fusion.1), channel_id=1, source_target_pairs={{0,48},{16,0},{32,16},{48,32},{64,112},{80,64},{96,80},{112,96},{1... | collective-permute-start | bytes 884744 | tf_op jit(solution)/shard_map/ppermute | solution.py:441
  71.2 0.1 collective-permute-start.12
  71.3 0.1 fusion.4
  71.4 0.8 multiply_convert_fusion
  72.2 6.6 %collective-permute-done.14 = bf16[4,2,96,192]{3,2,1,0:T(8,128)(2,1)S(1)} collective-permute-done((bf16[4,2,96,192]{3,2,1,0:T(8,128)(2,1)S(1)}, bf16[4,2,96,192]{3,2,1,0:T(8,128)(2,1)S(1)}, u32[]{:S(2)}, u32[]{:S(2)}) %collective-permute-start.14) | collective-permute-done | bytes 294944 | tf_op jit(solution)/shard_map/ppermute | solution.py:441
  78.7 3.1 %collective-permute-done.12 = bf16[4,2,96,192]{3,2,1,0:T(8,128)(2,1)S(1)} collective-permute-done((bf16[4,2,96,192]{3,2,1,0:T(8,128)(2,1)S(1)}, bf16[4,2,96,192]{3,2,1,0:T(8,128)(2,1)S(1)}, u32[]{:S(2)}, u32[]{:S(2)}) %collective-permute-start.12) | collective-permute-done | bytes 294944 | tf_op jit(solution)/shard_map/ppermute | solution.py:441
  81.8 0.2 fusion.1
  82.0 5.6 %collective-permute-start.17 = (bf16[2,96,192]{2,1,0:T(8,128)(2,1)S(1)}, bf16[2,96,192]{2,1,0:T(8,128)(2,1)S(1)}, u32[]{:S(2)}, u32[]{:S(2)}) collective-permute-start(bf16[2,96,192]{2,1,0:T(8,128)(2,1)S(1)} %get-tuple-element.44), channel_id=1, source_target_pairs={{0,65},{1,64},{2,67},{3,66},{4,69},{5,68},{6,71},{7,70},{8,73},{9,... | collective-permute-start | bytes 221192 | tf_op jit(solution)/shard_map/ppermute | solution.py:457
  87.6 0.8 maximum_select_fusion.3
  88.4 0.2 collective-permute-start.15
  88.6 1.6 %collective-permute-done.17 = bf16[2,96,192]{2,1,0:T(8,128)(2,1)S(1)} collective-permute-done((bf16[2,96,192]{2,1,0:T(8,128)(2,1)S(1)}, bf16[2,96,192]{2,1,0:T(8,128)(2,1)S(1)}, u32[]{:S(2)}, u32[]{:S(2)}) %collective-permute-start.17) | collective-permute-done | bytes 73760 | tf_op jit(solution)/shard_map/ppermute | solution.py:457
  90.2 3.5 %collective-permute-done.15 = bf16[2,96,192]{2,1,0:T(8,128)(2,1)S(1)} collective-permute-done((bf16[2,96,192]{2,1,0:T(8,128)(2,1)S(1)}, bf16[2,96,192]{2,1,0:T(8,128)(2,1)S(1)}, u32[]{:S(2)}, u32[]{:S(2)}) %collective-permute-start.15) | collective-permute-done | bytes 73760 | tf_op jit(solution)/shard_map/ppermute | solution.py:441
  93.7 0.8 maximum_select_fusion.1
  94.5 2.3 %total_key_value.1 = (bf16[4,96,128]{2,1,0:T(8,128)(2,1)}, bf16[4,96,128]{2,1,0:T(8,128)(2,1)}) custom-call(bf16[8,2,4,96,128]{4,3,2,1,0:T(8,128)(2,1)} %bitcast.23.parts_ref), custom_call_target="tpu_custom_call" | custom-call | tf_op jit(solution)/shard_map/total_key_value/pallas_call | solution.py:289
  (27 shorter events, 0.3 us)
Async XLA Ops:
  0.6 17.6 %copy-start.1 = (bf16[4,96,1536]{2,1,0:T(8,128)(2,1)S(1)}, bf16[4,96,1536]{2,1,0:T(8,128)(2,1)}, u32[]{:S(2)}) copy-start(bf16[4,96,1536]{2,1,0:T(8,128)(2,1)} %param.12) | copy-start | bytes 3538948
  2.5 2.6 %collective-permute-start = (bf16[400,128]{1,0:T(8,128)(2,1)}, bf16[400,128]{1,0:T(8,128)(2,1)S(1)}, u32[]{:S(2)}, u32[]{:S(2)}) collective-permute-start(bf16[400,128]{1,0:T(8,128)(2,1)} %get-tuple-element.21), channel_id=1, source_target_pairs={{0,1},{1,0},{2,3},{3,2},{4,5},{5,4},{6,7},{7,6},{8,9},{9,8},{10,11... | collective-permute-start | bytes 307208 | tf_op jit(solution)/shard_map/ppermute | solution.py:380
  6.1 6.7 %collective-permute-start.3 = (bf16[2,400,128]{2,1,0:T(8,128)(2,1)S(1)}, bf16[2,400,128]{2,1,0:T(8,128)(2,1)S(1)}, u32[]{:S(2)}, u32[]{:S(2)}) collective-permute-start(bf16[2,400,128]{2,1,0:T(8,128)(2,1)S(1)} %maximum_select_fusion.2.own_ref), channel_id=1, source_target_pairs={{0,6},{1,7},{2,0},{3,1},{4,2},{5,3},{6,4},{7,5},{8,14},{9,15},{10,... | collective-permute-start | bytes 614408 | tf_op jit(solution)/shard_map/ppermute | solution.py:396
  8.7 7.2 %collective-permute-start.2 = (bf16[2,400,128]{2,1,0:T(8,128)(2,1)S(1)}, bf16[2,400,128]{2,1,0:T(8,128)(2,1)S(1)}, u32[]{:S(2)}, u32[]{:S(2)}) collective-permute-start(bf16[2,400,128]{2,1,0:T(8,128)(2,1)S(1)} %maximum_select_fusion.2.own_ref), channel_id=1, source_target_pairs={{0,2},{1,3},{2,4},{3,5},{4,6},{5,7},{6,0},{7,1},{8,10},{9,11},{10,... | collective-permute-start | bytes 614408 | tf_op jit(solution)/shard_map/ppermute | solution.py:396
  8.7 7.2 %collective-permute-start.4 = (bf16[2,400,128]{2,1,0:T(8,128)(2,1)S(1)}, bf16[2,400,128]{2,1,0:T(8,128)(2,1)S(1)}, u32[]{:S(2)}, u32[]{:S(2)}) collective-permute-start(bf16[2,400,128]{2,1,0:T(8,128)(2,1)S(1)} %maximum_select_fusion.2.own_ref), channel_id=1, source_target_pairs={{0,8},{1,9},{2,10},{3,11},{4,12},{5,13},{6,14},{7,15},{8,0},{9,1},... | collective-permute-start | bytes 614408 | tf_op jit(solution)/shard_map/ppermute | solution.py:396
  16.7 19.1 %collective-permute-start.6 = (bf16[3,400,128]{2,1,0:T(8,128)(2,1)}, bf16[3,400,128]{2,1,0:T(8,128)(2,1)S(1)}, u32[]{:S(2)}, u32[]{:S(2)}) collective-permute-start(bf16[3,400,128]{2,1,0:T(8,128)(2,1)} %get-tuple-element.46), channel_id=1, source_target_pairs={{0,6},{1,7},{2,0},{3,1},{4,2},{5,3},{6,4},{7,5},{8,14},{9,15},{10,... | collective-permute-start | bytes 921608 | tf_op jit(solution)/shard_map/ppermute | solution.py:396
  19.1 18.7 %collective-permute-start.9 = (bf16[2,96,1536]{2,1,0:T(8,128)(2,1)}, bf16[2,96,1536]{2,1,0:T(8,128)(2,1)S(1)}, u32[]{:S(2)}, u32[]{:S(2)}) collective-permute-start(bf16[2,96,1536]{2,1,0:T(8,128)(2,1)} %get-tuple-element.42), channel_id=1, source_target_pairs={{0,1},{1,0},{2,3},{3,2},{4,5},{5,4},{6,7},{7,6},{8,9},{9,8},{10,11... | collective-permute-start | bytes 1769480 | tf_op jit(solution)/shard_map/ppermute | solution.py:380
  22.7 9.7 %all-to-all-start = ((bf16[16,32,128]{2,1,0:T(8,128)(2,1)}), bf16[16,32,128]{2,1,0:T(8,128)(2,1)S(1)}, u32[]{:S(2)}, u32[]{:S(2)}) async-start(bf16[16,32,128]{2,1,0:T(8,128)(2,1)} %pack_cotangent.1), calls=%async_computation | async-start | bytes 262144 | tf_op jit(solution)/shard_map/all_to_all | solution.py:419
  26.1 11.6 %collective-permute-start.5 = (bf16[3,400,128]{2,1,0:T(8,128)(2,1)S(1)}, bf16[3,400,128]{2,1,0:T(8,128)(2,1)S(1)}, u32[]{:S(2)}, u32[]{:S(2)}) collective-permute-start(bf16[3,400,128]{2,1,0:T(8,128)(2,1)S(1)} %get-tuple-element.47), channel_id=1, source_target_pairs={{0,2},{1,3},{2,4},{3,5},{4,6},{5,7},{6,0},{7,1},{8,10},{9,11},{10,... | collective-permute-start | bytes 921608 | tf_op jit(solution)/shard_map/ppermute | solution.py:396
  32.3 0.7 copy-start.2
  35.1 3.1 %collective-permute-start.1 = (bf16[4,96,128]{2,1,0:T(8,128)(2,1)}, bf16[4,96,128]{2,1,0:T(8,128)(2,1)S(1)}, u32[]{:S(2)}, u32[]{:S(2)}) collective-permute-start(bf16[4,96,128]{2,1,0:T(8,128)(2,1)} %get-tuple-element.24), channel_id=1, source_target_pairs={{0,1},{1,0},{2,3},{3,2},{4,5},{5,4},{6,7},{7,6},{8,9},{9,8},{10,11... | collective-permute-start | bytes 294920 | tf_op jit(solution)/shard_map/ppermute | solution.py:380
  35.8 4.6 %collective-permute-start.8 = (bf16[400,128]{1,0:T(8,128)(2,1)S(1)}, bf16[400,128]{1,0:T(8,128)(2,1)S(1)}, u32[]{:S(2)}, u32[]{:S(2)}) collective-permute-start(bf16[400,128]{1,0:T(8,128)(2,1)S(1)} %slice_bitcast_fusion.1), channel_id=1, source_target_pairs={{0,6},{1,7},{2,0},{3,1},{4,2},{5,3},{6,4},{7,5},{8,14},{9,15},{10,... | collective-permute-start | bytes 307208 | tf_op jit(solution)/shard_map/ppermute | solution.py:396
  37.7 4.8 %collective-permute-start.7 = (bf16[400,128]{1,0:T(8,128)(2,1)S(1)}, bf16[400,128]{1,0:T(8,128)(2,1)S(1)}, u32[]{:S(2)}, u32[]{:S(2)}) collective-permute-start(bf16[400,128]{1,0:T(8,128)(2,1)S(1)} %slice_bitcast_fusion.2), channel_id=1, source_target_pairs={{0,2},{1,3},{2,4},{3,5},{4,6},{5,7},{6,0},{7,1},{8,10},{9,11},{10,... | collective-permute-start | bytes 307208 | tf_op jit(solution)/shard_map/ppermute | solution.py:396
  37.8 4.7 %copy-start = (bf16[4,96,128]{2,1,0:T(8,128)(2,1)S(1)}, bf16[4,96,128]{2,1,0:T(8,128)(2,1)}, u32[]{:S(2)}) copy-start(bf16[4,96,128]{2,1,0:T(8,128)(2,1)} %get-tuple-element.23.qd_mine_ref) | copy-start | bytes 294916
  54.3 40.2 %all-to-all-start.1 = ((bf16[16,4,96,128]{3,2,1,0:T(8,128)(2,1)}), bf16[16,4,96,128]{3,2,1,0:T(8,128)(2,1)}, u32[]{:S(2)}, u32[]{:S(2)}) async-start(bf16[16,4,96,128]{3,2,1,0:T(8,128)(2,1)} %bitcast.37), calls=%async_computation.1 | async-start | bytes 3145728 | tf_op jit(solution)/shard_map/all_to_all | solution.py:426
  60.3 10.9 %collective-permute-start.10 = (bf16[4,96,128]{2,1,0:T(8,128)(2,1)S(1)}, bf16[4,96,128]{2,1,0:T(8,128)(2,1)S(1)}, u32[]{:S(2)}, u32[]{:S(2)}) collective-permute-start(bf16[4,96,128]{2,1,0:T(8,128)(2,1)S(1)} %get-tuple-element.27), channel_id=1, source_target_pairs={{0,1},{1,0},{2,3},{3,2},{4,5},{5,4},{6,7},{7,6},{8,9},{9,8},{10,11... | collective-permute-start | bytes 294920 | tf_op jit(solution)/shard_map/ppermute | solution.py:380
  60.7 7.8 %collective-permute-start.11 = (bf16[2,2,96,192]{3,2,1,0:T(8,128)(2,1)S(1)}, bf16[2,2,96,192]{3,2,1,0:T(8,128)(2,1)S(1)}, u32[]{:S(2)}, u32[]{:S(2)}) collective-permute-start(bf16[2,2,96,192]{3,2,1,0:T(8,128)(2,1)S(1)} %get-tuple-element.33), channel_id=1, source_target_pairs={{0,16},{16,32},{32,48},{48,0},{64,80},{80,96},{96,112},{112,64},{1... | collective-permute-start | bytes 442376 | tf_op jit(solution)/shard_map/ppermute | solution.py:441
  62.0 6.5 %collective-permute-start.13 = (bf16[2,2,96,192]{3,2,1,0:T(8,128)(2,1)S(1)}, bf16[2,2,96,192]{3,2,1,0:T(8,128)(2,1)S(1)}, u32[]{:S(2)}, u32[]{:S(2)}) collective-permute-start(bf16[2,2,96,192]{3,2,1,0:T(8,128)(2,1)S(1)} %get-tuple-element.34), channel_id=1, source_target_pairs={{0,48},{16,0},{32,16},{48,32},{64,112},{80,64},{96,80},{112,96},{1... | collective-permute-start | bytes 442376 | tf_op jit(solution)/shard_map/ppermute | solution.py:441
  68.6 2.8 %copy-start.3 = (f32[4,96,128]{2,1,0:T(8,128)S(1)}, f32[4,96,128]{2,1,0:T(8,128)}, u32[]{:S(2)}) copy-start(f32[4,96,128]{2,1,0:T(8,128)} %get-tuple-element.31) | copy-start | bytes 589828
  68.7 10.0 %collective-permute-start.14 = (bf16[4,2,96,192]{3,2,1,0:T(8,128)(2,1)S(1)}, bf16[4,2,96,192]{3,2,1,0:T(8,128)(2,1)S(1)}, u32[]{:S(2)}, u32[]{:S(2)}) collective-permute-start(bf16[4,2,96,192]{3,2,1,0:T(8,128)(2,1)S(1)} %pad_maximum_fusion.1), channel_id=1, source_target_pairs={{0,48},{16,0},{32,16},{48,32},{64,112},{80,64},{96,80},{112,96},{1... | collective-permute-start | bytes 884744 | tf_op jit(solution)/shard_map/ppermute | solution.py:441
  71.2 10.6 %collective-permute-start.12 = (bf16[4,2,96,192]{3,2,1,0:T(8,128)(2,1)S(1)}, bf16[4,2,96,192]{3,2,1,0:T(8,128)(2,1)S(1)}, u32[]{:S(2)}, u32[]{:S(2)}) collective-permute-start(bf16[4,2,96,192]{3,2,1,0:T(8,128)(2,1)S(1)} %pad_maximum_fusion), channel_id=1, source_target_pairs={{0,16},{16,32},{32,48},{48,0},{64,80},{80,96},{96,112},{112,64},{1... | collective-permute-start | bytes 884744 | tf_op jit(solution)/shard_map/ppermute | solution.py:441
  82.0 8.2 %collective-permute-start.17 = (bf16[2,96,192]{2,1,0:T(8,128)(2,1)S(1)}, bf16[2,96,192]{2,1,0:T(8,128)(2,1)S(1)}, u32[]{:S(2)}, u32[]{:S(2)}) collective-permute-start(bf16[2,96,192]{2,1,0:T(8,128)(2,1)S(1)} %get-tuple-element.44), channel_id=1, source_target_pairs={{0,65},{1,64},{2,67},{3,66},{4,69},{5,68},{6,71},{7,70},{8,73},{9,... | collective-permute-start | bytes 221192 | tf_op jit(solution)/shard_map/ppermute | solution.py:457
  87.6 2.6 %collective-permute-start.16 = (bf16[2,96,192]{2,1,0:T(8,128)(2,1)S(1)}, bf16[2,96,192]{2,1,0:T(8,128)(2,1)S(1)}, u32[]{:S(2)}, u32[]{:S(2)}) collective-permute-start(bf16[2,96,192]{2,1,0:T(8,128)(2,1)S(1)} %get-tuple-element.45), channel_id=1, source_target_pairs={{0,1},{1,0},{2,3},{3,2},{4,5},{5,4},{6,7},{7,6},{8,9},{9,8},{10,11... | collective-permute-start | bytes 221192 | tf_op jit(solution)/shard_map/ppermute | solution.py:380
  88.4 5.4 %collective-permute-start.15 = (bf16[2,96,192]{2,1,0:T(8,128)(2,1)S(1)}, bf16[2,96,192]{2,1,0:T(8,128)(2,1)S(1)}, u32[]{:S(2)}, u32[]{:S(2)}) collective-permute-start(bf16[2,96,192]{2,1,0:T(8,128)(2,1)S(1)} %get-tuple-element.43), channel_id=1, source_target_pairs={{0,64},{16,80},{32,96},{48,112},{64,0},{80,16},{96,32},{112,48},{1... | collective-permute-start | bytes 221192 | tf_op jit(solution)/shard_map/ppermute | solution.py:441

commit v5 on v4

--- a/solution.py
+++ b/solution.py
@@ -31,10 +31,10 @@
     bias_ref,
     qa_own_ref,
     qa_away_ref,
-    dkv_ref,
     right_out_ref,
     left_out_ref,
     rest_out_ref,
+    dbias_ref,
     kv_ref,
     cap_ref,
     s_ref,
@@ -43,7 +43,7 @@
     dp_ref,
     de_ref,
     row_ref,
-    dbias_ref,
+    dkv_ref,
 ):
     step = pl.program_id(0)
     last = pl.num_programs(0) - 1
@@ -169,22 +169,26 @@
     key_value = lax.dot_general(
         sides, de_ref[...], (((0,), (0,)), ((), ())), preferred_element_type=jnp.float32
     )
-    dkv_ref[...] = key_value.T.astype(jnp.bfloat16).reshape(dkv_ref.shape)
+    key_value = key_value.T.astype(jnp.bfloat16)
+    for group in range(PIECES):
+        for side in range(2):
+            start = group * queries + side * half
+            target = 2 * place_ref[8 + group] + (side + core) % 2
+            dkv_ref[target, step] = key_value[start : start + half]
 
     @pl.when(step == last)
     def _():
-        width = dbias_ref.shape[3]
+        width = dbias_ref.shape[4]
         for piece in range(PIECES):
             for head in range(2):
                 for side in range(2):
                     start = head * queries + side * half
                     part = acc_ref[start : start + half, piece * width : (piece + 1) * width]
-                    target = 2 * place_ref[8 + piece] + (side + core) % 2
-                    dbias_ref[target, head] = part.astype(jnp.bfloat16)
-        right_out_ref[...] = dbias_ref[8:10]
-        left_out_ref[...] = dbias_ref[10:12]
-        rest_out_ref[:8] = dbias_ref[:8]
-        rest_out_ref[8:] = dbias_ref[12:]
+                    dbias_ref[piece, (side + core) % 2, head] = part.astype(jnp.bfloat16)
+        right_out_ref[...] = dkv_ref[12]
+        left_out_ref[...] = dkv_ref[13]
+        rest_out_ref[:12] = dkv_ref[:12]
+        rest_out_ref[12:] = dkv_ref[14:]
 
 
 def prepare_kernel(core_ref, key_ref, value_ref, mask_ref, mine_ref, other_ref):
@@ -271,24 +275,6 @@
     )(core, packed, weight, gate, query)
 
 
-def total_kernel(parts_ref, key_ref, value_ref):
-    half = key_ref.shape[2] // 2
-    scaling = 1.0 / math.sqrt(key_ref.shape[2] // HEADS)
-    for column in range(key_ref.shape[0]):
-        sums = [
-            jnp.sum(parts_ref[:, side, column].astype(jnp.float32), axis=0) for side in range(2)
-        ]
-        key = jnp.concatenate([part[:, :half] for part in sums], axis=1) * scaling
-        key_ref[column] = key.astype(jnp.bfloat16)
-        value = jnp.concatenate([part[:, half:] for part in sums], axis=1)
-        value_ref[column] = value.astype(jnp.bfloat16)
-
-
-def total(parts, like):
-    out = jax.ShapeDtypeStruct(like.shape, jnp.bfloat16)
-    return pl.pallas_call(total_kernel, out_shape=[out, out], name="total_key_value")(parts)
-
-
 def attend(places, mine, other, blocks, bias, chips, row_count):
     columns, tokens, lanes = mine.shape
     rows, keys = bias.shape
@@ -311,10 +297,10 @@
             out_specs=[
                 column_spec,
                 column_spec,
-                pl.BlockSpec((chips, 2, 1, tokens, lanes), lambda j, places: (0, 0, j, 0, 0)),
-                whole((2,) + piece),
-                whole((2,) + piece),
-                whole((12,) + piece),
+                whole(mine.shape),
+                whole(mine.shape),
+                whole((14,) + mine.shape),
+                whole((row_count, 2) + piece),
             ],
             scratch_shapes=[
                 pltpu.VMEM((chips,) + blocks[0].shape, jnp.bfloat16),
@@ -325,16 +311,16 @@
                 pltpu.VMEM((rows, keys), jnp.float32),
                 pltpu.VMEM((2 * rows, keys), jnp.bfloat16),
                 pltpu.VMEM((rows, 128), jnp.float32),
-                pltpu.VMEM((16,) + piece, jnp.bfloat16),
+                pltpu.VMEM((16,) + mine.shape, jnp.bfloat16),
             ],
         ),
         out_shape=[
             jax.ShapeDtypeStruct(mine.shape, jnp.bfloat16),
             jax.ShapeDtypeStruct(mine.shape, jnp.bfloat16),
-            jax.ShapeDtypeStruct((chips, 2, columns, tokens, lanes), jnp.bfloat16),
-            jax.ShapeDtypeStruct((2,) + piece, jnp.bfloat16),
-            jax.ShapeDtypeStruct((2,) + piece, jnp.bfloat16),
-            jax.ShapeDtypeStruct((12,) + piece, jnp.bfloat16),
+            jax.ShapeDtypeStruct(mine.shape, jnp.bfloat16),
+            jax.ShapeDtypeStruct(mine.shape, jnp.bfloat16),
+            jax.ShapeDtypeStruct((14,) + mine.shape, jnp.bfloat16),
+            jax.ShapeDtypeStruct((row_count, 2) + piece, jnp.bfloat16),
         ],
         compiler_params=pltpu.CompilerParams(vmem_limit_bytes=48 * 1024 * 1024),
         cost_estimate=pl.CostEstimate(flops=12 * 128 * work, bytes_accessed=16 * 2**20, transcendentals=work),
@@ -384,6 +370,8 @@
 
     core_word = core.astype(jnp.int32).reshape(1)
     kv_mine, kv_away = prepare(core_word, key_vectors, value_vectors, pair_mask)
+    kv_away, output_cotangent = lax.optimization_barrier((kv_away, output_cotangent))
+    packed = pack(output_cotangent, devices)
     block = in_order(kv_mine[None], swapped(kv_away)[None], 0)
     ring = chips // 2
 
@@ -395,67 +383,67 @@
             pairs.append((index, 2 * target + index % 2))
         return lax.ppermute(array, "col", pairs)
 
-    block, output_cotangent = lax.optimization_barrier((block, output_cotangent))
     left, right, across = along(block, 1, 0), along(block, -1, 0), along(block, 0, 1)
+    regrouped = lax.all_to_all(packed, "col", 0, 0, tiled=True)
+    left, right, across, regrouped = lax.optimization_barrier((left, right, across, regrouped))
     left_pair = along(jnp.concatenate([across, left[:1]], axis=0), 1, 0)
     right_pair = along(jnp.concatenate([across, right[1:]], axis=0), -1, 0)
     left_far = along(left_pair[0], 1, 0)
     right_far = along(right_pair[1], -1, 0)
     blocks = [block, left, right, across, left_pair, right_pair, left_far, right_far]
     chip = lax.axis_index("col") // 2
-    place = lax.axis_index("row")
-    row_ring = row_count // 2
     places = [
         ((chip // ring + side) % 2) * ring + (chip % ring + turn) % ring
         for side in range(2)
         for turn in (0, ring - 1, 1, 2)
     ] + [
-        2 * ((index % row_ring - place) % row_ring) + (index // row_ring - place // row_ring) % 2
-        for index in range(row_count)
+        ring * ((index // ring - chip // ring) % 2) + (index % ring - chip % ring) % ring
+        for index in range(chips)
     ]
     places.append(core)
     places = jnp.stack(places).astype(jnp.int32)
 
-    regrouped = lax.all_to_all(pack(output_cotangent, devices), "col", 0, 0, tiled=True)
     qd_mine, qd_away, gate_slope = project(core_word, regrouped, output_weight, gate_logits, query_vectors)
 
-    qa_own, qa_away, kv_grads, bias_right, bias_left, bias_rest = attend(
+    qa_own, qa_away, kv_right, kv_left, kv_rest, bias_grads = attend(
         places, qd_mine, swapped(qd_away), blocks, bias_pair, chips, row_count
     )
 
-    kv_parts = lax.all_to_all(
-        kv_grads.reshape((devices,) + kv_grads.shape[2:]), "col", 0, 0, tiled=True
-    )
-    key_gradient, value_gradient = total(kv_parts.reshape(kv_grads.shape), key_vectors)
+    bias_parts = lax.all_to_all(bias_grads, "row", 0, 0, tiled=True)
+
+    def added(*parts):
+        return sum(part.astype(jnp.float32) for part in parts)
+
+    def both(*parts):
+        return lax.optimization_barrier(parts)
+
+    def low(*parts):
+        return added(*parts).astype(jnp.bfloat16)
+
+    home, near, far, behind = kv_rest[:2], kv_rest[2:4], kv_rest[4:6], kv_rest[6:8]
+    home_across, near_across, behind_across = kv_rest[8:10], kv_rest[10:12], kv_rest[12:]
+    from_left, from_right = both(along(kv_right, 1, 0), along(kv_left, -1, 0))
+    onward = jnp.concatenate([low(near_across[:1], from_left[None]), near_across[1:], far[:1]])
+    backward = jnp.concatenate([behind_across[:1], low(behind_across[1:], from_right[None]), far[1:]])
+    from_left, from_right = both(along(onward, 1, 0), along(backward, -1, 0))
+    from_across = along(low(home_across, from_left[:2], from_right[:2]), 0, 1)
+    onward = jnp.concatenate([low(near[:1], from_left[2:]), near[1:]])
+    backward = jnp.concatenate([behind[:1], low(behind[1:], from_right[2:])])
+    kv_sum = low(home, along(onward, 1, 0), along(backward, -1, 0), from_across)
+    kv_back = swapped(kv_sum[1])
+    key_gradient = in_order(kv_sum[0, ..., :half], kv_back[..., :half], 2)
+    key_gradient = (key_gradient.astype(jnp.float32) * scaling).astype(jnp.bfloat16)
+    value_gradient = in_order(kv_sum[0, ..., half:], kv_back[..., half:], 2)
 
     qa_back = swapped(qa_away)
     query_gradient = in_order(qa_own[..., :half], qa_back[..., :half], 2)
     attended = in_order(qa_own[..., half:], qa_back[..., half:], 2).astype(jnp.float32)
     gate_gradient = (gate_slope * attended).astype(jnp.bfloat16)
 
-    def along_row(array, turn, side):
-        pairs = []
-        for index in range(row_count):
-            high, low = index // row_ring, index % row_ring
-            pairs.append((index, ((high + side) % 2) * row_ring + (low + turn) % row_ring))
-        return lax.ppermute(array, "row", pairs)
-
-    def added(*parts):
-        return sum(part.astype(jnp.float32) for part in parts)
-
-    from_left = along_row(bias_right, 1, 0)
-    from_right = along_row(bias_left, -1, 0)
-    onward = jnp.concatenate([added(bias_rest[4:6], from_left).astype(jnp.bfloat16), bias_rest[6:8]])
-    backward = jnp.concatenate([bias_rest[8:10], added(bias_rest[10:], from_right).astype(jnp.bfloat16)])
-    sums = added(bias_rest[:4], along_row(onward, 1, 0), along_row(backward, -1, 0))
-    low_sums = sums.astype(jnp.bfloat16)
-    diagonal = []
-    for index in range(row_count * devices):
-        up = (index // devices + row_ring) % row_count
-        diagonal.append((index, up * devices + (index % devices ^ 1)))
-    bias_own = added(sums[0], along_row(low_sums[2], 0, 1))
-    bias_away = added(swapped(low_sums[1]), lax.ppermute(low_sums[3], ("row", "col"), diagonal))
-    bias_gradient = in_order(bias_own, bias_away, 0)
+    bias_sum = jnp.sum(bias_parts.astype(jnp.float32), axis=0)
+    bias_gradient = in_order(
+        bias_sum[0], swapped(bias_sum[1].astype(jnp.bfloat16)).astype(jnp.float32), 0
+    )
     return (query_gradient, key_gradient, value_gradient, gate_gradient, bias_gradient)
 
 

time: 97.2 us -> 97.9 us (level)
  waiting for transfers between devices: 37 us -> 25.3 us
  blocking collectives: 0 us -> 11.6 us
  other arithmetic: 5.82 us -> 9.17 us
  Pallas kernels: 19.7 us -> 17.7 us
    ppermute x6 -> x0, waiting for transfers between devices: 19.7 us -> none  [the longest x5 18.1 us: along_row(): return lax.ppermute(array, 'row', pairs)]
    all_to_all x0 -> x1, blocking collectives: none -> 11.6 us  [local(): regrouped = lax.all_to_all(packed, 'col', 0, 0, tiled=True)]
    ppermute x7 -> x14, waiting for transfers between devices: 11.2 us -> 22.3 us  [along(): return lax.ppermute(array, 'col', pairs)]
    ppermute x6 -> x0, starting transfers between devices: 11 us -> none  [the longest x1 5.56 us: local(): lax.ppermute(low_sums[3], ('row', 'col'), diagonal)]
    ppermute x7 -> x14, starting transfers between devices: 7.68 us -> 16.7 us  [along(): return lax.ppermute(array, 'col', pairs)]
    all_to_all x2 -> x1, waiting for transfers between devices: 4.88 us -> 0.01 us  [local(): bias_parts = lax.all_to_all(bias_grads, 'row', 0, 0, tiled=True)]
    ppermute x5 -> x6, starting transfers between devices: 4.38 us -> 8.41 us  [swapped(): return lax.ppermute(array, 'col', swap)]
    pallas_call x1 -> x0, Pallas kernels: 2.32 us -> none  [total(): pl.pallas_call(total_kernel, out_shape=[out, out], name='total_key_value')]
  transfers between devices with their start and end apart: 20 -> 21, of which waited for: 12 -> 10; matrix products, arithmetic and copies ran while one was open for 5% -> 5% of each run, Pallas kernels for 4% -> 4%
where the time goes in v5:
time: 97.9 us; the launch traced here: 97.5 us
  starting transfers between devices  32.3 us (33%)
  waiting for transfers between devices  25.3 us (26%)
  Pallas kernels  17.7 us (18%)
  blocking collectives  11.6 us (12%)
  other arithmetic  9.17 us (9%)
    ppermute x14, waiting for transfers between devices, along(): return lax.ppermute(array, 'col', pairs)  22.3 us
    ppermute x14, starting transfers between devices, along(): return lax.ppermute(array, 'col', pairs)  16.7 us
    pallas_call x1, Pallas kernels, attend(): pl.pallas_call(attention_kernel, grid_spec=pltpu.PrefetchScalarGridSpec(n...  12.1 us
    all_to_all x1, blocking collectives, local(): regrouped = lax.all_to_all(packed, 'col', 0, 0, tiled=True)  11.6 us
    ppermute x6, starting transfers between devices, swapped(): return lax.ppermute(array, 'col', swap)  8.41 us
    all_to_all x1, starting transfers between devices, local(): bias_parts = lax.all_to_all(bias_grads, 'row', 0, 0, tiled=True)  7.21 us
    select_n x5, other arithmetic, in_order(): jnp.where(core == 0, jnp.concatenate([mine, other], axis=axis), jnp.conca...  3.69 us
    ppermute x6, waiting for transfers between devices, swapped(): return lax.ppermute(array, 'col', swap)  2.94 us
  transfers between devices with their start and end apart: 21, of which 10 were waited for; matrix products, arithmetic and copies ran while one was open for 5% of the time, Pallas kernels for 4%

profile of v5, /device:TPU:1, one launch (start us, length us, event | category | flops | bytes accessed | tf_op | source)
XLA Modules:
  0.0 97.5 jit_solution(11068933134680403512)
XLA Ops:
  0.7 1.8 %prepare_key_value.1 = (bf16[400,128]{1,0:T(8,128)(2,1)}, bf16[400,128]{1,0:T(8,128)(2,1)}) custom-call(s32[1]{0:T(128)} %bitcast.16.core_ref, bf16[4,96,128]{2,1,0:T(8,128)(2,1)} %key_ref.1, bf16[4,96,128]{2,1,0:T(8,128)(2,1)} %value_ref.1, s32[4,96]{1,0:T(4,128)} %mask_ref.1), custom_call_target="tpu_custom_call" | custom-call | tf_op jit(solution)/shard_map/prepare_key_value/pallas_call | solution.py:218
  2.5 1.4 %collective-permute-start = (bf16[400,128]{1,0:T(8,128)(2,1)}, bf16[400,128]{1,0:T(8,128)(2,1)S(1)}, u32[]{:S(2)}, u32[]{:S(2)}) collective-permute-start(bf16[400,128]{1,0:T(8,128)(2,1)} %get-tuple-element.28), channel_id=1, source_target_pairs={{0,1},{1,0},{2,3},{3,2},{4,5},{5,4},{6,7},{7,6},{8,9},{9,8},{10,11... | collective-permute-start | bytes 307208 | tf_op jit(solution)/shard_map/ppermute | solution.py:366
  3.9 1.2 %collective-permute-done = bf16[400,128]{1,0:T(8,128)(2,1)S(1)} collective-permute-done((bf16[400,128]{1,0:T(8,128)(2,1)}, bf16[400,128]{1,0:T(8,128)(2,1)S(1)}, u32[]{:S(2)}, u32[]{:S(2)}) %collective-permute-start) | collective-permute-done | bytes 102432 | tf_op jit(solution)/shard_map/ppermute | solution.py:366
  5.1 1.0 %maximum_select_fusion.2.own_ref = bf16[2,400,128]{2,1,0:T(8,128)(2,1)S(1)} fusion(bf16[1,400,128]{2,1,0:T(8,128)(2,1)S(1)} %bitcast.42, bf16[1,400,128]{2,1,0:T(8,128)(2,1)} %bitcast.41, pred[]{:T(512)S(6)} %eq.61), kind=kLoop, calls=%fused_computation.11 | loop fusion | flops 307200 | bytes 409601 | tf_op jit(solution)/shard_map/jit(_where)/select_n | solution.py:359
  6.1 1.8 %collective-permute-start.3 = (bf16[2,400,128]{2,1,0:T(8,128)(2,1)S(1)}, bf16[2,400,128]{2,1,0:T(8,128)(2,1)S(1)}, u32[]{:S(2)}, u32[]{:S(2)}) collective-permute-start(bf16[2,400,128]{2,1,0:T(8,128)(2,1)S(1)} %maximum_select_fusion.2.own_ref), channel_id=1, source_target_pairs={{0,8},{1,9},{2,10},{3,11},{4,12},{5,13},{6,14},{7,15},{8,0},{9,1},... | collective-permute-start | bytes 614408 | tf_op jit(solution)/shard_map/ppermute | solution.py:384
  7.9 2.5 %collective-permute-start.2 = (bf16[2,400,128]{2,1,0:T(8,128)(2,1)S(1)}, bf16[2,400,128]{2,1,0:T(8,128)(2,1)S(1)}, u32[]{:S(2)}, u32[]{:S(2)}) collective-permute-start(bf16[2,400,128]{2,1,0:T(8,128)(2,1)S(1)} %maximum_select_fusion.2.own_ref), channel_id=1, source_target_pairs={{0,6},{1,7},{2,0},{3,1},{4,2},{5,3},{6,4},{7,5},{8,14},{9,15},{10,... | collective-permute-start | bytes 614408 | tf_op jit(solution)/shard_map/ppermute | solution.py:384
  10.4 1.7 %pack_cotangent.1 = bf16[16,32,128]{2,1,0:T(8,128)(2,1)} custom-call(bf16[4,8,1536]{2,1,0:T(8,128)(2,1)} %cotangent_ref), custom_call_target="tpu_custom_call" | custom-call | tf_op jit(solution)/shard_map/pack_cotangent/pallas_call | solution.py:237
  12.0 11.6 %all_to_all.10.packed_ref = bf16[16,32,128]{2,1,0:T(8,128)(2,1)} all-to-all(bf16[16,32,128]{2,1,0:T(8,128)(2,1)} %pack_cotangent.1), channel_id=1, replica_groups=mesh['row'=8,'col'=16] {'col'}, dimensions={0} | all-to-all | bytes 262144 | tf_op jit(solution)/shard_map/all_to_all | solution.py:387
  23.7 0.9 pad_maximum_fusion
  24.6 1.1 %collective-permute-start.6 = (bf16[3,400,128]{2,1,0:T(8,128)(2,1)}, bf16[3,400,128]{2,1,0:T(8,128)(2,1)S(1)}, u32[]{:S(2)}, u32[]{:S(2)}) collective-permute-start(bf16[3,400,128]{2,1,0:T(8,128)(2,1)} %get-tuple-element.59), channel_id=1, source_target_pairs={{0,6},{1,7},{2,0},{3,1},{4,2},{5,3},{6,4},{7,5},{8,14},{9,15},{10,... | collective-permute-start | bytes 921608 | tf_op jit(solution)/shard_map/ppermute | solution.py:384
  25.6 0.9 broadcast_select_fusion.1
  26.5 0.6 collective-permute-start.9
  27.1 0.5 collective-permute-start.5
  27.7 0.1 stack.71.place_ref
  27.8 2.1 %project_cotangent.1 = (bf16[4,96,128]{2,1,0:T(8,128)(2,1)}, bf16[4,96,128]{2,1,0:T(8,128)(2,1)}, f32[4,96,128]{2,1,0:T(8,128)}) custom-call(s32[1]{0:T(128)} %bitcast.16.core_ref, bf16[16,32,128]{2,1,0:T(8,128)(2,1)} %all_to_all.10.packed_ref, bf16[128,128]{1,0:T(8,128)(2,1)} %weight_ref.1, bf16[4,96,128]{2,1,0:T(8,128)(2,1)} %gate_ref.1, ...), custom_call_target="tpu_custom_call" | custom-call | tf_op jit(solution)/shard_map/project_cotangent/pallas_call | solution.py:266
  29.9 0.3 collective-permute-start.4
  30.2 3.0 %collective-permute-done.6.right_pair_ref = bf16[3,400,128]{2,1,0:T(8,128)(2,1)S(1)} collective-permute-done((bf16[3,400,128]{2,1,0:T(8,128)(2,1)}, bf16[3,400,128]{2,1,0:T(8,128)(2,1)S(1)}, u32[]{:S(2)}, u32[]{:S(2)}) %collective-permute-start.6) | collective-permute-done | bytes 307232 | tf_op jit(solution)/shard_map/ppermute | solution.py:384
  33.1 2.5 %collective-permute-start.8 = (bf16[400,128]{1,0:T(8,128)(2,1)S(1)}, bf16[400,128]{1,0:T(8,128)(2,1)S(1)}, u32[]{:S(2)}, u32[]{:S(2)}) collective-permute-start(bf16[400,128]{1,0:T(8,128)(2,1)S(1)} %slice_bitcast_fusion.1), channel_id=1, source_target_pairs={{0,6},{1,7},{2,0},{3,1},{4,2},{5,3},{6,4},{7,5},{8,14},{9,15},{10,... | collective-permute-start | bytes 307208 | tf_op jit(solution)/shard_map/ppermute | solution.py:384
  35.7 1.8 %collective-permute-done.5.left_pair_ref = bf16[3,400,128]{2,1,0:T(8,128)(2,1)S(1)} collective-permute-done((bf16[3,400,128]{2,1,0:T(8,128)(2,1)}, bf16[3,400,128]{2,1,0:T(8,128)(2,1)S(1)}, u32[]{:S(2)}, u32[]{:S(2)}) %collective-permute-start.5) | collective-permute-done | bytes 307232 | tf_op jit(solution)/shard_map/ppermute | solution.py:384
  37.6 0.4 maximum_select_fusion
  38.0 4.3 %collective-permute-done.7.left_far_ref = bf16[400,128]{1,0:T(8,128)(2,1)S(1)} collective-permute-done((bf16[400,128]{1,0:T(8,128)(2,1)S(1)}, bf16[400,128]{1,0:T(8,128)(2,1)S(1)}, u32[]{:S(2)}, u32[]{:S(2)}) %collective-permute-start.7) | collective-permute-done | bytes 102432 | tf_op jit(solution)/shard_map/ppermute | solution.py:384
  42.3 12.1 %attention_both.1 = (bf16[4,96,128]{2,1,0:T(8,128)(2,1)S(1)}, bf16[4,96,128]{2,1,0:T(8,128)(2,1)S(1)}, bf16[4,96,128]{2,1,0:T(8,128)(2,1)S(1)}, bf16[4,96,128]{2...) custom-call(s32[17]{0:T(128)S(1)} %stack.71.place_ref, ...), custom_call_target="tpu_custom_call" | custom-call | flops 3623878656 | bytes 16777216 | tf_op jit(solution)/shard_map/attention_both/pallas_call | solution.py:289
  54.4 7.2 %all-to-all-start.1 = ((bf16[8,2,2,96,192]{4,3,2,1,0:T(8,128)(2,1)}), bf16[8,2,2,96,192]{4,3,2,1,0:T(8,128)(2,1)}, u32[]{:S(2)}, u32[]{:S(2)}) async-start(bf16[8,2,2,96,192]{4,3,2,1,0:T(8,128)(2,1)} %get-tuple-element.46), calls=%async_computation.1 | async-start | bytes 3145728 | tf_op jit(solution)/shard_map/all_to_all | solution.py:412
  61.6 0.1 fusion.4
  61.7 2.3 %collective-permute-start.10 = (bf16[4,96,128]{2,1,0:T(8,128)(2,1)S(1)}, bf16[4,96,128]{2,1,0:T(8,128)(2,1)S(1)}, u32[]{:S(2)}, u32[]{:S(2)}) collective-permute-start(bf16[4,96,128]{2,1,0:T(8,128)(2,1)S(1)} %get-tuple-element.37), channel_id=1, source_target_pairs={{0,1},{1,0},{2,3},{3,2},{4,5},{5,4},{6,7},{7,6},{8,9},{9,8},{10,11... | collective-permute-start | bytes 294920 | tf_op jit(solution)/shard_map/ppermute | solution.py:366
  64.0 2.7 %collective-permute-start.12 = (bf16[4,96,128]{2,1,0:T(8,128)(2,1)S(1)}, bf16[4,96,128]{2,1,0:T(8,128)(2,1)S(1)}, u32[]{:S(2)}, u32[]{:S(2)}) collective-permute-start(bf16[4,96,128]{2,1,0:T(8,128)(2,1)S(1)} %get-tuple-element.40), channel_id=1, source_target_pairs={{0,6},{1,7},{2,0},{3,1},{4,2},{5,3},{6,4},{7,5},{8,14},{9,15},{10,... | collective-permute-start | bytes 294920 | tf_op jit(solution)/shard_map/ppermute | solution.py:384
  66.7 2.9 %collective-permute-done.11 = bf16[4,96,128]{2,1,0:T(8,128)(2,1)S(1)} collective-permute-done((bf16[4,96,128]{2,1,0:T(8,128)(2,1)S(1)}, bf16[4,96,128]{2,1,0:T(8,128)(2,1)S(1)}, u32[]{:S(2)}, u32[]{:S(2)}) %collective-permute-start.11) | collective-permute-done | bytes 98336 | tf_op jit(solution)/shard_map/ppermute | solution.py:384
  69.9 2.7 %collective-permute-start.14 = (bf16[3,4,96,128]{3,2,1,0:T(8,128)(2,1)S(1)}, bf16[3,4,96,128]{3,2,1,0:T(8,128)(2,1)S(1)}, u32[]{:S(2)}, u32[]{:S(2)}) collective-permute-start(bf16[3,4,96,128]{3,2,1,0:T(8,128)(2,1)S(1)} %pad_maximum_fusion.3), channel_id=1, source_target_pairs={{0,6},{1,7},{2,0},{3,1},{4,2},{5,3},{6,4},{7,5},{8,14},{9,15},{10,... | collective-permute-start | bytes 884744 | tf_op jit(solution)/shard_map/ppermute | solution.py:384
  72.6 0.1 fusion.5
  72.7 0.8 maximum_select_fusion.3
  73.5 5.4 %collective-permute-done.13 = bf16[3,4,96,128]{3,2,1,0:T(8,128)(2,1)S(1)} collective-permute-done((bf16[3,4,96,128]{3,2,1,0:T(8,128)(2,1)S(1)}, bf16[3,4,96,128]{3,2,1,0:T(8,128)(2,1)S(1)}, u32[]{:S(2)}, u32[]{:S(2)}) %collective-permute-start.13) | collective-permute-done | bytes 294944 | tf_op jit(solution)/shard_map/ppermute | solution.py:384
  78.9 0.1 add_convert_fusion.1
  79.1 2.5 %collective-permute-start.16 = (bf16[2,4,96,128]{3,2,1,0:T(8,128)(2,1)S(1)}, bf16[2,4,96,128]{3,2,1,0:T(8,128)(2,1)S(1)}, u32[]{:S(2)}, u32[]{:S(2)}) collective-permute-start(bf16[2,4,96,128]{3,2,1,0:T(8,128)(2,1)S(1)} %pad_maximum_fusion.5), channel_id=1, source_target_pairs={{0,6},{1,7},{2,0},{3,1},{4,2},{5,3},{6,4},{7,5},{8,14},{9,15},{10,... | collective-permute-start | bytes 589832 | tf_op jit(solution)/shard_map/ppermute | solution.py:384
  81.8 0.1 collective-permute-start.17
  81.9 0.8 multiply_convert_fusion
  82.6 1.6 %collective-permute-done.16 = bf16[2,4,96,128]{3,2,1,0:T(8,128)(2,1)S(1)} collective-permute-done((bf16[2,4,96,128]{3,2,1,0:T(8,128)(2,1)S(1)}, bf16[2,4,96,128]{3,2,1,0:T(8,128)(2,1)S(1)}, u32[]{:S(2)}, u32[]{:S(2)}) %collective-permute-start.16) | collective-permute-done | bytes 196640 | tf_op jit(solution)/shard_map/ppermute | solution.py:384
  84.3 3.2 %collective-permute-done.15 = bf16[2,4,96,128]{3,2,1,0:T(8,128)(2,1)S(1)} collective-permute-done((bf16[2,4,96,128]{3,2,1,0:T(8,128)(2,1)S(1)}, bf16[2,4,96,128]{3,2,1,0:T(8,128)(2,1)S(1)}, u32[]{:S(2)}, u32[]{:S(2)}) %collective-permute-start.15) | collective-permute-done | bytes 196640 | tf_op jit(solution)/shard_map/ppermute | solution.py:384
  87.5 0.1 add_convert_fusion
  87.6 3.4 %collective-permute-start.18 = (bf16[4,96,128]{2,1,0:T(8,128)(2,1)S(1)}, bf16[4,96,128]{2,1,0:T(8,128)(2,1)S(1)}, u32[]{:S(2)}, u32[]{:S(2)}) collective-permute-start(bf16[4,96,128]{2,1,0:T(8,128)(2,1)S(1)} %slice_bitcast_fusion.4), channel_id=1, source_target_pairs={{0,1},{1,0},{2,3},{3,2},{4,5},{5,4},{6,7},{7,6},{8,9},{9,8},{10,11... | collective-permute-start | bytes 294920 | tf_op jit(solution)/shard_map/ppermute | solution.py:366
  91.0 0.1 slice_bitcast_fusion.3
  91.1 0.8 collective-permute-done.18
  91.9 0.1 fusion.6
  92.0 0.8 maximum_select_fusion.5
  92.8 0.8 multiply_convert_fusion.1
  93.6 1.7 %convert_reduce_fusion = f32[2,2,96,192]{3,2,1,0:T(8,128)S(1)} fusion(bf16[8,2,2,96,192]{4,3,2,1,0:T(8,128)(2,1)} %all-to-all-done.1), kind=kLoop, calls=%fused_computation | loop fusion | flops 1105920 | bytes 1474560 | tf_op jit(solution)/shard_map/reduce_sum | solution.py:443
  95.3 0.4 collective-permute-start.19
  95.7 0.9 collective-permute-done.19
  96.7 0.8 maximum_select_fusion.1
  (37 shorter events, 0.6 us)
Async XLA Ops:
  0.6 25.0 %copy-start.1 = (bf16[4,96,1536]{2,1,0:T(8,128)(2,1)S(1)}, bf16[4,96,1536]{2,1,0:T(8,128)(2,1)}, u32[]{:S(2)}) copy-start(bf16[4,96,1536]{2,1,0:T(8,128)(2,1)} %param.12) | copy-start | bytes 3538948
  2.5 2.6 %collective-permute-start = (bf16[400,128]{1,0:T(8,128)(2,1)}, bf16[400,128]{1,0:T(8,128)(2,1)S(1)}, u32[]{:S(2)}, u32[]{:S(2)}) collective-permute-start(bf16[400,128]{1,0:T(8,128)(2,1)} %get-tuple-element.28), channel_id=1, source_target_pairs={{0,1},{1,0},{2,3},{3,2},{4,5},{5,4},{6,7},{7,6},{8,9},{9,8},{10,11... | collective-permute-start | bytes 307208 | tf_op jit(solution)/shard_map/ppermute | solution.py:366
  6.1 17.6 %collective-permute-start.3 = (bf16[2,400,128]{2,1,0:T(8,128)(2,1)S(1)}, bf16[2,400,128]{2,1,0:T(8,128)(2,1)S(1)}, u32[]{:S(2)}, u32[]{:S(2)}) collective-permute-start(bf16[2,400,128]{2,1,0:T(8,128)(2,1)S(1)} %maximum_select_fusion.2.own_ref), channel_id=1, source_target_pairs={{0,8},{1,9},{2,10},{3,11},{4,12},{5,13},{6,14},{7,15},{8,0},{9,1},... | collective-permute-start | bytes 614408 | tf_op jit(solution)/shard_map/ppermute | solution.py:384
  7.9 15.8 %collective-permute-start.2 = (bf16[2,400,128]{2,1,0:T(8,128)(2,1)S(1)}, bf16[2,400,128]{2,1,0:T(8,128)(2,1)S(1)}, u32[]{:S(2)}, u32[]{:S(2)}) collective-permute-start(bf16[2,400,128]{2,1,0:T(8,128)(2,1)S(1)} %maximum_select_fusion.2.own_ref), channel_id=1, source_target_pairs={{0,6},{1,7},{2,0},{3,1},{4,2},{5,3},{6,4},{7,5},{8,14},{9,15},{10,... | collective-permute-start | bytes 614408 | tf_op jit(solution)/shard_map/ppermute | solution.py:384
  10.4 13.3 %collective-permute-start.1 = (bf16[2,400,128]{2,1,0:T(8,128)(2,1)S(1)}, bf16[2,400,128]{2,1,0:T(8,128)(2,1)S(1)}, u32[]{:S(2)}, u32[]{:S(2)}) collective-permute-start(bf16[2,400,128]{2,1,0:T(8,128)(2,1)S(1)} %maximum_select_fusion.2.own_ref), channel_id=1, source_target_pairs={{0,2},{1,3},{2,4},{3,5},{4,6},{5,7},{6,0},{7,1},{8,10},{9,11},{10,... | collective-permute-start | bytes 614408 | tf_op jit(solution)/shard_map/ppermute | solution.py:384
  24.6 8.6 %collective-permute-start.6 = (bf16[3,400,128]{2,1,0:T(8,128)(2,1)}, bf16[3,400,128]{2,1,0:T(8,128)(2,1)S(1)}, u32[]{:S(2)}, u32[]{:S(2)}) collective-permute-start(bf16[3,400,128]{2,1,0:T(8,128)(2,1)} %get-tuple-element.59), channel_id=1, source_target_pairs={{0,6},{1,7},{2,0},{3,1},{4,2},{5,3},{6,4},{7,5},{8,14},{9,15},{10,... | collective-permute-start | bytes 921608 | tf_op jit(solution)/shard_map/ppermute | solution.py:384
  26.5 11.0 %collective-permute-start.9 = (bf16[2,96,1536]{2,1,0:T(8,128)(2,1)}, bf16[2,96,1536]{2,1,0:T(8,128)(2,1)S(1)}, u32[]{:S(2)}, u32[]{:S(2)}) collective-permute-start(bf16[2,96,1536]{2,1,0:T(8,128)(2,1)} %get-tuple-element.58), channel_id=1, source_target_pairs={{0,1},{1,0},{2,3},{3,2},{4,5},{5,4},{6,7},{7,6},{8,9},{9,8},{10,11... | collective-permute-start | bytes 1769480 | tf_op jit(solution)/shard_map/ppermute | solution.py:366
  27.1 10.3 %collective-permute-start.5 = (bf16[3,400,128]{2,1,0:T(8,128)(2,1)}, bf16[3,400,128]{2,1,0:T(8,128)(2,1)S(1)}, u32[]{:S(2)}, u32[]{:S(2)}) collective-permute-start(bf16[3,400,128]{2,1,0:T(8,128)(2,1)} %get-tuple-element.60), channel_id=1, source_target_pairs={{0,2},{1,3},{2,4},{3,5},{4,6},{5,7},{6,0},{7,1},{8,10},{9,11},{10,... | collective-permute-start | bytes 921608 | tf_op jit(solution)/shard_map/ppermute | solution.py:384
  29.9 12.4 %copy-start = (bf16[4,96,128]{2,1,0:T(8,128)(2,1)S(1)}, bf16[4,96,128]{2,1,0:T(8,128)(2,1)}, u32[]{:S(2)}) copy-start(bf16[4,96,128]{2,1,0:T(8,128)(2,1)} %get-tuple-element.31.qd_mine_ref) | copy-start | bytes 294916
  29.9 8.1 %collective-permute-start.4 = (bf16[4,96,128]{2,1,0:T(8,128)(2,1)}, bf16[4,96,128]{2,1,0:T(8,128)(2,1)S(1)}, u32[]{:S(2)}, u32[]{:S(2)}) collective-permute-start(bf16[4,96,128]{2,1,0:T(8,128)(2,1)} %get-tuple-element.32), channel_id=1, source_target_pairs={{0,1},{1,0},{2,3},{3,2},{4,5},{5,4},{6,7},{7,6},{8,9},{9,8},{10,11... | collective-permute-start | bytes 294920 | tf_op jit(solution)/shard_map/ppermute | solution.py:366
  33.1 4.8 %collective-permute-start.8 = (bf16[400,128]{1,0:T(8,128)(2,1)S(1)}, bf16[400,128]{1,0:T(8,128)(2,1)S(1)}, u32[]{:S(2)}, u32[]{:S(2)}) collective-permute-start(bf16[400,128]{1,0:T(8,128)(2,1)S(1)} %slice_bitcast_fusion.1), channel_id=1, source_target_pairs={{0,6},{1,7},{2,0},{3,1},{4,2},{5,3},{6,4},{7,5},{8,14},{9,15},{10,... | collective-permute-start | bytes 307208 | tf_op jit(solution)/shard_map/ppermute | solution.py:384
  37.5 4.8 %collective-permute-start.7 = (bf16[400,128]{1,0:T(8,128)(2,1)S(1)}, bf16[400,128]{1,0:T(8,128)(2,1)S(1)}, u32[]{:S(2)}, u32[]{:S(2)}) collective-permute-start(bf16[400,128]{1,0:T(8,128)(2,1)S(1)} %slice_bitcast_fusion.2), channel_id=1, source_target_pairs={{0,2},{1,3},{2,4},{3,5},{4,6},{5,7},{6,0},{7,1},{8,10},{9,11},{10,... | collective-permute-start | bytes 307208 | tf_op jit(solution)/shard_map/ppermute | solution.py:384
  54.4 39.2 %all-to-all-start.1 = ((bf16[8,2,2,96,192]{4,3,2,1,0:T(8,128)(2,1)}), bf16[8,2,2,96,192]{4,3,2,1,0:T(8,128)(2,1)}, u32[]{:S(2)}, u32[]{:S(2)}) async-start(bf16[8,2,2,96,192]{4,3,2,1,0:T(8,128)(2,1)} %get-tuple-element.46), calls=%async_computation.1 | async-start | bytes 3145728 | tf_op jit(solution)/shard_map/all_to_all | solution.py:412
  61.7 10.9 %collective-permute-start.10 = (bf16[4,96,128]{2,1,0:T(8,128)(2,1)S(1)}, bf16[4,96,128]{2,1,0:T(8,128)(2,1)S(1)}, u32[]{:S(2)}, u32[]{:S(2)}) collective-permute-start(bf16[4,96,128]{2,1,0:T(8,128)(2,1)S(1)} %get-tuple-element.37), channel_id=1, source_target_pairs={{0,1},{1,0},{2,3},{3,2},{4,5},{5,4},{6,7},{7,6},{8,9},{9,8},{10,11... | collective-permute-start | bytes 294920 | tf_op jit(solution)/shard_map/ppermute | solution.py:366
  64.0 5.7 %collective-permute-start.11 = (bf16[4,96,128]{2,1,0:T(8,128)(2,1)S(1)}, bf16[4,96,128]{2,1,0:T(8,128)(2,1)S(1)}, u32[]{:S(2)}, u32[]{:S(2)}) collective-permute-start(bf16[4,96,128]{2,1,0:T(8,128)(2,1)S(1)} %get-tuple-element.39), channel_id=1, source_target_pairs={{0,2},{1,3},{2,4},{3,5},{4,6},{5,7},{6,0},{7,1},{8,10},{9,11},{10,... | collective-permute-start | bytes 294920 | tf_op jit(solution)/shard_map/ppermute | solution.py:384
  64.0 5.7 %collective-permute-start.12 = (bf16[4,96,128]{2,1,0:T(8,128)(2,1)S(1)}, bf16[4,96,128]{2,1,0:T(8,128)(2,1)S(1)}, u32[]{:S(2)}, u32[]{:S(2)}) collective-permute-start(bf16[4,96,128]{2,1,0:T(8,128)(2,1)S(1)} %get-tuple-element.40), channel_id=1, source_target_pairs={{0,6},{1,7},{2,0},{3,1},{4,2},{5,3},{6,4},{7,5},{8,14},{9,15},{10,... | collective-permute-start | bytes 294920 | tf_op jit(solution)/shard_map/ppermute | solution.py:384
  69.7 9.2 %collective-permute-start.13 = (bf16[3,4,96,128]{3,2,1,0:T(8,128)(2,1)S(1)}, bf16[3,4,96,128]{3,2,1,0:T(8,128)(2,1)S(1)}, u32[]{:S(2)}, u32[]{:S(2)}) collective-permute-start(bf16[3,4,96,128]{3,2,1,0:T(8,128)(2,1)S(1)} %pad_maximum_fusion.2), channel_id=1, source_target_pairs={{0,2},{1,3},{2,4},{3,5},{4,6},{5,7},{6,0},{7,1},{8,10},{9,11},{10,... | collective-permute-start | bytes 884744 | tf_op jit(solution)/shard_map/ppermute | solution.py:384
  69.9 12.0 %copy-start.2 = (f32[4,96,128]{2,1,0:T(8,128)S(1)}, f32[4,96,128]{2,1,0:T(8,128)}, u32[]{:S(2)}) copy-start(f32[4,96,128]{2,1,0:T(8,128)} %get-tuple-element.45) | copy-start | bytes 589828
  69.9 9.0 %collective-permute-start.14 = (bf16[3,4,96,128]{3,2,1,0:T(8,128)(2,1)S(1)}, bf16[3,4,96,128]{3,2,1,0:T(8,128)(2,1)S(1)}, u32[]{:S(2)}, u32[]{:S(2)}) collective-permute-start(bf16[3,4,96,128]{3,2,1,0:T(8,128)(2,1)S(1)} %pad_maximum_fusion.3), channel_id=1, source_target_pairs={{0,6},{1,7},{2,0},{3,1},{4,2},{5,3},{6,4},{7,5},{8,14},{9,15},{10,... | collective-permute-start | bytes 884744 | tf_op jit(solution)/shard_map/ppermute | solution.py:384
  79.1 5.2 %collective-permute-start.16 = (bf16[2,4,96,128]{3,2,1,0:T(8,128)(2,1)S(1)}, bf16[2,4,96,128]{3,2,1,0:T(8,128)(2,1)S(1)}, u32[]{:S(2)}, u32[]{:S(2)}) collective-permute-start(bf16[2,4,96,128]{3,2,1,0:T(8,128)(2,1)S(1)} %pad_maximum_fusion.5), channel_id=1, source_target_pairs={{0,6},{1,7},{2,0},{3,1},{4,2},{5,3},{6,4},{7,5},{8,14},{9,15},{10,... | collective-permute-start | bytes 589832 | tf_op jit(solution)/shard_map/ppermute | solution.py:384
  81.7 5.8 %collective-permute-start.15 = (bf16[2,4,96,128]{3,2,1,0:T(8,128)(2,1)S(1)}, bf16[2,4,96,128]{3,2,1,0:T(8,128)(2,1)S(1)}, u32[]{:S(2)}, u32[]{:S(2)}) collective-permute-start(bf16[2,4,96,128]{3,2,1,0:T(8,128)(2,1)S(1)} %pad_maximum_fusion.4), channel_id=1, source_target_pairs={{0,2},{1,3},{2,4},{3,5},{4,6},{5,7},{6,0},{7,1},{8,10},{9,11},{10,... | collective-permute-start | bytes 589832 | tf_op jit(solution)/shard_map/ppermute | solution.py:384
  81.8 5.7 %collective-permute-start.17 = (bf16[2,4,96,128]{3,2,1,0:T(8,128)(2,1)S(1)}, bf16[2,4,96,128]{3,2,1,0:T(8,128)(2,1)S(1)}, u32[]{:S(2)}, u32[]{:S(2)}) collective-permute-start(bf16[2,4,96,128]{3,2,1,0:T(8,128)(2,1)S(1)} %add_convert_fusion.1), channel_id=1, source_target_pairs={{0,8},{1,9},{2,10},{3,11},{4,12},{5,13},{6,14},{7,15},{8,0},{9,1},... | collective-permute-start | bytes 589832 | tf_op jit(solution)/shard_map/ppermute | solution.py:384
  87.6 4.3 %collective-permute-start.18 = (bf16[4,96,128]{2,1,0:T(8,128)(2,1)S(1)}, bf16[4,96,128]{2,1,0:T(8,128)(2,1)S(1)}, u32[]{:S(2)}, u32[]{:S(2)}) collective-permute-start(bf16[4,96,128]{2,1,0:T(8,128)(2,1)S(1)} %slice_bitcast_fusion.4), channel_id=1, source_target_pairs={{0,1},{1,0},{2,3},{3,2},{4,5},{5,4},{6,7},{7,6},{8,9},{9,8},{10,11... | collective-permute-start | bytes 294920 | tf_op jit(solution)/shard_map/ppermute | solution.py:366
  95.3 1.4 %collective-permute-start.19 = (bf16[2,96,192]{2,1,0:T(8,128)(2,1)S(1)}, bf16[2,96,192]{2,1,0:T(8,128)(2,1)S(1)}, u32[]{:S(2)}, u32[]{:S(2)}) collective-permute-start(bf16[2,96,192]{2,1,0:T(8,128)(2,1)S(1)} %fusion.2), channel_id=1, source_target_pairs={{0,1},{1,0},{2,3},{3,2},{4,5},{5,4},{6,7},{7,6},{8,9},{9,8},{10,11... | collective-permute-start | bytes 221192 | tf_op jit(solution)/shard_map/ppermute | solution.py:366

commit v6 on v5

--- a/solution.py
+++ b/solution.py
@@ -20,14 +20,8 @@
     place_ref,
     qd_mine_ref,
     qd_other_ref,
-    own_ref,
-    left_ref,
-    right_ref,
-    across_ref,
-    left_pair_ref,
-    right_pair_ref,
-    left_far_ref,
-    right_far_ref,
+    kv_ref,
+    mask_ref,
     bias_ref,
     qa_own_ref,
     qa_away_ref,
@@ -35,7 +29,6 @@
     left_out_ref,
     rest_out_ref,
     dbias_ref,
-    kv_ref,
     cap_ref,
     s_ref,
     b2_ref,
@@ -51,7 +44,7 @@
     queries = rows // 2
     keys = bias_ref.shape[1]
     head_width = qd_mine_ref.shape[2] // 4
-    core = place_ref[8 + PIECES]
+    core = place_ref[PIECES]
     scaling = 1.0 / math.sqrt(head_width)
 
     @pl.when(step == 0)
@@ -63,29 +56,17 @@
             return carry
 
         lax.fori_loop(0, rows // CHUNK, fill, 0)
-        kv_ref[place_ref[0]] = own_ref[...]
-        kv_ref[place_ref[1]] = left_ref[...]
-        kv_ref[place_ref[2]] = right_ref[...]
-        kv_ref[place_ref[3], 0] = left_pair_ref[2]
-        kv_ref[place_ref[3], 1] = right_pair_ref[2]
-        kv_ref[place_ref[4]] = across_ref[...]
-        kv_ref[place_ref[5]] = left_pair_ref[:2]
-        kv_ref[place_ref[6]] = right_pair_ref[:2]
-        kv_ref[place_ref[7], 0] = left_far_ref[...]
-        kv_ref[place_ref[7], 1] = right_far_ref[...]
-        first = own_ref.shape[1] - MASK_ROWS
-        masks = kv_ref[:, :, first:, :].astype(jnp.float32)
+        masks = mask_ref[...].astype(jnp.float32)
         for column in range(cap_ref.shape[0]):
-            pieces = []
-            for group in range(masks.shape[0]):
-                for side in range(2):
-                    pieces.append(masks[group, side, column : column + 1, : queries // 2])
+            pieces = [
+                masks[source, column : column + 1, : queries // 2] for source in range(masks.shape[0])
+            ]
             cap_ref[column] = jnp.where(
                 jnp.concatenate(pieces, axis=1) > 0.5, 1e30, NEG_FILL * LOG2E
             )
 
     half = queries // 2
-    kv = kv_ref[:, :, pl.ds(step * half, half), :].reshape(keys, 4 * head_width)
+    kv = kv_ref[...].reshape(keys, 4 * head_width)
     qd_mine = qd_mine_ref[0]
     qd_other = qd_other_ref[0]
     qd = jnp.concatenate(
@@ -173,7 +154,7 @@
     for group in range(PIECES):
         for side in range(2):
             start = group * queries + side * half
-            target = 2 * place_ref[8 + group] + (side + core) % 2
+            target = 2 * place_ref[group] + (side + core) % 2
             dkv_ref[target, step] = key_value[start : start + half]
 
     @pl.when(step == last)
@@ -191,54 +172,43 @@
         rest_out_ref[12:] = dkv_ref[14:]
 
 
-def prepare_kernel(core_ref, key_ref, value_ref, mask_ref, mine_ref, other_ref):
+def prepare_kernel(key_ref, value_ref, mask_ref, cotangent_ref, packed_ref):
     columns, tokens, channels = key_ref.shape
     half = channels // 2
-    core = core_ref[0]
-    filler = jnp.zeros((MASK_ROWS - columns, channels), jnp.float32)
+    devices = packed_ref.shape[0]
+    pairs = columns * tokens
+    rows = cotangent_ref.shape[0] * cotangent_ref.shape[1]
     mask = mask_ref[...].astype(jnp.float32)
     mask = jnp.concatenate([mask, jnp.zeros((columns, channels - tokens), jnp.float32)], axis=1)
+    filler = jnp.zeros((MASK_ROWS - columns, channels), jnp.float32)
     mask = jnp.concatenate([mask, filler], axis=0).astype(jnp.bfloat16)
     for column in range(columns):
         key = key_ref[column]
         value = value_ref[column]
-        low = jnp.concatenate([key[:, :half], value[:, :half]], axis=1)
-        high = jnp.concatenate([key[:, half:], value[:, half:]], axis=1)
-        part = slice(column * tokens, (column + 1) * tokens)
-        mine_ref[part, :] = jnp.where(core == 0, low, high)
-        other_ref[part, :] = jnp.where(core == 0, high, low)
-    mine_ref[columns * tokens :, :] = mask
-    other_ref[columns * tokens :, :] = mask
-
-
-def prepare(core, key, value, mask):
+        sides = [
+            jnp.concatenate([key[:, :half], value[:, :half]], axis=1),
+            jnp.concatenate([key[:, half:], value[:, half:]], axis=1),
+        ]
+        for device in range(devices):
+            packed_ref[device, column * tokens : (column + 1) * tokens, :] = sides[device % 2]
+    cotangent = cotangent_ref[...].astype(jnp.float32).reshape(rows, cotangent_ref.shape[2])
+    filler = jnp.zeros((rows, channels - tokens), jnp.float32)
+    for device in range(devices):
+        part = cotangent[:, device * tokens : (device + 1) * tokens]
+        part = jnp.concatenate([part, filler], axis=1).astype(jnp.bfloat16)
+        packed_ref[device, pairs : pairs + rows, :] = part
+        packed_ref[device, pairs + rows :, :] = mask
+
+
+def prepare(key, value, mask, cotangent, devices):
     columns, tokens, channels = key.shape
-    out = jax.ShapeDtypeStruct((columns * tokens + MASK_ROWS, channels), jnp.bfloat16)
-    vmem = pl.BlockSpec(memory_space=pltpu.VMEM)
+    rows = columns * tokens + cotangent.shape[0] * cotangent.shape[1] + MASK_ROWS
     return pl.pallas_call(
         prepare_kernel,
-        in_specs=[pl.BlockSpec(memory_space=pltpu.SMEM), vmem, vmem, vmem],
-        out_shape=[out, out],
-        name="prepare_key_value",
-    )(core, key, value, mask)
-
-
-def pack_kernel(cotangent_ref, packed_ref):
-    width = cotangent_ref.shape[2] // packed_ref.shape[0]
-    rows = packed_ref.shape[1]
-    whole = cotangent_ref[...].astype(jnp.float32).reshape(rows, cotangent_ref.shape[2])
-    filler = jnp.zeros((rows, packed_ref.shape[2] - width), jnp.float32)
-    for piece in range(packed_ref.shape[0]):
-        part = whole[:, piece * width : (piece + 1) * width]
-        packed_ref[piece] = jnp.concatenate([part, filler], axis=1).astype(jnp.bfloat16)
-
-
-def pack(cotangent, pieces):
-    return pl.pallas_call(
-        pack_kernel,
-        out_shape=jax.ShapeDtypeStruct((pieces, cotangent.shape[0] * cotangent.shape[1], 128), jnp.bfloat16),
-        name="pack_cotangent",
-    )(cotangent)
+        out_shape=jax.ShapeDtypeStruct((devices, rows, channels), jnp.bfloat16),
+        compiler_params=pltpu.CompilerParams(vmem_limit_bytes=32 * 1024 * 1024),
+        name="prepare_exchange",
+    )(key, value, mask, cotangent)
 
 
 def project_kernel(core_ref, packed_ref, weight_ref, gate_ref, query_ref, mine_ref, other_ref, slope_ref):
@@ -262,10 +232,23 @@
 
 
 def project(core, packed, weight, gate, query):
-    vmem = pl.BlockSpec(memory_space=pltpu.VMEM)
+    columns, tokens, channels = gate.shape
+    rows = weight.shape[0] // packed.shape[0] * columns
+
+    def whole(array):
+        return pl.BlockSpec(array.shape, lambda i: (0,) * array.ndim)
+
     return pl.pallas_call(
         project_kernel,
-        in_specs=[pl.BlockSpec(memory_space=pltpu.SMEM)] + [vmem] * 4,
+        grid=(1,),
+        in_specs=[
+            pl.BlockSpec(memory_space=pltpu.SMEM),
+            pl.BlockSpec((packed.shape[0], rows, channels), lambda i: (0, columns * tokens // rows, 0)),
+            whole(weight),
+            whole(gate),
+            whole(query),
+        ],
+        out_specs=[whole(gate)] * 3,
         out_shape=[
             jax.ShapeDtypeStruct(gate.shape, jnp.bfloat16),
             jax.ShapeDtypeStruct(gate.shape, jnp.bfloat16),
@@ -275,10 +258,12 @@
     )(core, packed, weight, gate, query)
 
 
-def attend(places, mine, other, blocks, bias, chips, row_count):
+def attend(places, mine, other, received, bias, row_count):
     columns, tokens, lanes = mine.shape
     rows, keys = bias.shape
     width = keys // row_count
+    devices = received.shape[0]
+    mask_place = received.shape[1] // MASK_ROWS - 1
     work = columns * rows * keys
 
     def whole(shape):
@@ -292,8 +277,11 @@
             num_scalar_prefetch=1,
             grid=(columns,),
             in_specs=[column_spec, column_spec]
-            + [whole(block.shape) for block in blocks]
-            + [whole(bias.shape)],
+            + [
+                pl.BlockSpec((devices, tokens, lanes), lambda j, places: (0, j, 0)),
+                pl.BlockSpec((devices, MASK_ROWS, lanes), lambda j, places: (0, mask_place, 0)),
+                whole(bias.shape),
+            ],
             out_specs=[
                 column_spec,
                 column_spec,
@@ -303,7 +291,6 @@
                 whole((row_count, 2) + piece),
             ],
             scratch_shapes=[
-                pltpu.VMEM((chips,) + blocks[0].shape, jnp.bfloat16),
                 pltpu.VMEM((columns, 1, keys), jnp.float32),
                 pltpu.VMEM((rows, keys), jnp.float32),
                 pltpu.VMEM((rows, keys), jnp.float32),
@@ -325,7 +312,7 @@
         compiler_params=pltpu.CompilerParams(vmem_limit_bytes=48 * 1024 * 1024),
         cost_estimate=pl.CostEstimate(flops=12 * 128 * work, bytes_accessed=16 * 2**20, transcendentals=work),
         name="attention_both",
-    )(places, mine, other, *blocks, bias)
+    )(places, mine, other, received, received, bias)
 
 
 def local(
@@ -369,10 +356,6 @@
     bias_pair = in_order(bias_mine, swapped(bias_other), 1).reshape(-1, keys)
 
     core_word = core.astype(jnp.int32).reshape(1)
-    kv_mine, kv_away = prepare(core_word, key_vectors, value_vectors, pair_mask)
-    kv_away, output_cotangent = lax.optimization_barrier((kv_away, output_cotangent))
-    packed = pack(output_cotangent, devices)
-    block = in_order(kv_mine[None], swapped(kv_away)[None], 0)
     ring = chips // 2
 
     def along(array, turn, side):
@@ -383,33 +366,22 @@
             pairs.append((index, 2 * target + index % 2))
         return lax.ppermute(array, "col", pairs)
 
-    left, right, across = along(block, 1, 0), along(block, -1, 0), along(block, 0, 1)
-    regrouped = lax.all_to_all(packed, "col", 0, 0, tiled=True)
-    left, right, across, regrouped = lax.optimization_barrier((left, right, across, regrouped))
-    left_pair = along(jnp.concatenate([across, left[:1]], axis=0), 1, 0)
-    right_pair = along(jnp.concatenate([across, right[1:]], axis=0), -1, 0)
-    left_far = along(left_pair[0], 1, 0)
-    right_far = along(right_pair[1], -1, 0)
-    blocks = [block, left, right, across, left_pair, right_pair, left_far, right_far]
+    packed = prepare(key_vectors, value_vectors, pair_mask, output_cotangent, devices)
+    received = lax.all_to_all(packed, "col", 0, 0, tiled=True)
     chip = lax.axis_index("col") // 2
     places = [
-        ((chip // ring + side) % 2) * ring + (chip % ring + turn) % ring
-        for side in range(2)
-        for turn in (0, ring - 1, 1, 2)
-    ] + [
         ring * ((index // ring - chip // ring) % 2) + (index % ring - chip % ring) % ring
         for index in range(chips)
     ]
     places.append(core)
     places = jnp.stack(places).astype(jnp.int32)
 
-    qd_mine, qd_away, gate_slope = project(core_word, regrouped, output_weight, gate_logits, query_vectors)
+    qd_mine, qd_away, gate_slope = project(core_word, received, output_weight, gate_logits, query_vectors)
 
     qa_own, qa_away, kv_right, kv_left, kv_rest, bias_grads = attend(
-        places, qd_mine, swapped(qd_away), blocks, bias_pair, chips, row_count
-    )
-
-    bias_parts = lax.all_to_all(bias_grads, "row", 0, 0, tiled=True)
+        places, qd_mine, swapped(qd_away), received, bias_pair, row_count
+    )
+
 
     def added(*parts):
         return sum(part.astype(jnp.float32) for part in parts)
@@ -425,6 +397,8 @@
     from_left, from_right = both(along(kv_right, 1, 0), along(kv_left, -1, 0))
     onward = jnp.concatenate([low(near_across[:1], from_left[None]), near_across[1:], far[:1]])
     backward = jnp.concatenate([behind_across[:1], low(behind_across[1:], from_right[None]), far[1:]])
+    onward, backward, bias_grads = both(onward, backward, bias_grads)
+    bias_parts = lax.all_to_all(bias_grads, "row", 0, 0, tiled=True)
     from_left, from_right = both(along(onward, 1, 0), along(backward, -1, 0))
     from_across = along(low(home_across, from_left[:2], from_right[:2]), 0, 1)
     onward = jnp.concatenate([low(near[:1], from_left[2:]), near[1:]])

time: 97.9 us -> 97.6 us (level)
  blocking collectives: 11.6 us -> 0 us
  waiting for transfers between devices: 25.3 us -> 36.8 us
  local copies, waits for them, and re-layouts: 0.6 us -> 5.14 us
  starting transfers between devices: 32.3 us -> 30.2 us
  other arithmetic: 9.17 us -> 7.87 us
  Pallas kernels: 17.7 us -> 16.5 us
    all_to_all x0 -> x1, waiting for transfers between devices: none -> 21.2 us  [local(): received = lax.all_to_all(packed, 'col', 0, 0, tiled=True)]
    all_to_all x1 -> x0, blocking collectives: 11.6 us -> none  [local(): regrouped = lax.all_to_all(packed, 'col', 0, 0, tiled=True)]
    ppermute x14 -> x7, waiting for transfers between devices: 22.3 us -> 13 us  [along(): return lax.ppermute(array, 'col', pairs)]
    ppermute x14 -> x7, starting transfers between devices: 16.7 us -> 8.04 us  [along(): return lax.ppermute(array, 'col', pairs)]
    all_to_all x0 -> x1, starting transfers between devices: none -> 7.17 us  [local(): received = lax.all_to_all(packed, 'col', 0, 0, tiled=True)]
    unnamed x6 -> x14, local copies, waits for them, and re-layouts: 0.01 us -> 4.59 us
    pallas_call x3 -> x2, Pallas kernels: 5.6 us -> 3.64 us  [the longest x1 2.1 us: project(): pl.pallas_call(project_kernel, grid=(1,), in_specs=[pl.BlockSpec(memory_s...]
    reduce_sum x1, other arithmetic: 1.71 us -> 0.27 us  [local(): bias_sum = jnp.sum(bias_parts.astype(jnp.float32), axis=0)]
  transfers between devices with their start and end apart: 21 -> 14, of which waited for: 10 -> 9; matrix products, arithmetic and copies ran while one was open for 5% -> 7% of each run, Pallas kernels for 4% -> 2%
where the time goes in v6:
time: 97.6 us; the launch traced here: 97.2 us
  waiting for transfers between devices  36.8 us (38%)
  starting transfers between devices  30.2 us (31%)
  Pallas kernels  16.5 us (17%)
  other arithmetic  7.87 us (8%)
  local copies, waits for them, and re-layouts  5.14 us (5%)
    all_to_all x1, waiting for transfers between devices, local(): received = lax.all_to_all(packed, 'col', 0, 0, tiled=True)  21.2 us
    ppermute x7, waiting for transfers between devices, along(): return lax.ppermute(array, 'col', pairs)  13 us
    pallas_call x1, Pallas kernels, attend(): pl.pallas_call(attention_kernel, grid_spec=pltpu.PrefetchScalarGridSpec(n...  12.8 us
    ppermute x7, starting transfers between devices, along(): return lax.ppermute(array, 'col', pairs)  8.04 us
    ppermute x5, starting transfers between devices, swapped(): return lax.ppermute(array, 'col', swap)  7.74 us
    all_to_all x1, starting transfers between devices, local(): bias_parts = lax.all_to_all(bias_grads, 'row', 0, 0, tiled=True)  7.21 us
    all_to_all x1, starting transfers between devices, local(): received = lax.all_to_all(packed, 'col', 0, 0, tiled=True)  7.17 us
    unnamed x14, local copies, waits for them, and re-layouts  4.59 us
  transfers between devices with their start and end apart: 14, of which 9 were waited for; matrix products, arithmetic and copies ran while one was open for 7% of the time, Pallas kernels for 2%

profile of v6, /device:TPU:1, one launch (start us, length us, event | category | flops | bytes accessed | tf_op | source)
XLA Modules:
  0.0 97.2 jit_solution(10365946599611994665)
XLA Ops:
  0.6 0.9 copy-done
  1.5 0.9 copy-done.1
  2.4 0.9 copy-done.2
  3.3 0.7 copy-done.3
  4.0 1.5 %prepare_exchange.1 = bf16[16,432,128]{2,1,0:T(8,128)(2,1)} custom-call(bf16[4,96,128]{2,1,0:T(8,128)(2,1)S(1)} %copy-done, bf16[4,96,128]{2,1,0:T(8,128)(2,1)S(1)} %copy-done.1, s32[4,96]{1,0:T(4,128)S(1)} %copy-done.3, bf16[4,8,1536]{2,1,0:T(8,128)(2,1)S(1)} %copy-done.2), custom_call_target="tpu_custom_call" | custom-call | tf_op jit(solution)/shard_map/prepare_exchange/pallas_call | solution.py:206
  5.5 7.2 %all-to-all-start = ((bf16[16,432,128]{2,1,0:T(8,128)(2,1)}), bf16[16,432,128]{2,1,0:T(8,128)(2,1)S(1)}, u32[]{:S(2)}, u32[]{:S(2)}) async-start(bf16[16,432,128]{2,1,0:T(8,128)(2,1)} %prepare_exchange.1), calls=%async_computation | async-start | bytes 3538944 | tf_op jit(solution)/shard_map/all_to_all | solution.py:370
  12.7 2.2 %broadcast_select_fusion.1 = (bf16[2,96,1536]{2,1,0:T(8,128)(2,1)S(1)}, bf16[2,96,1536]{2,1,0:T(8,128)(2,1)}) fusion(pred[]{:T(512)S(6)} %eq.36, bf16[4,96,1536]{2,1,0:T(8,128)(2,1)} %param.12), kind=kLoop, calls=%fused_computation.3 | loop fusion | flops 589824 | bytes 2359297 | tf_op jit(solution)/shard_map/jit(_where)/select_n | solution.py:343
  14.9 0.1 collective-permute-start.1
  15.0 0.1 stack.39.place_ref
  15.1 21.2 %all-to-all-done.packed_ref.kv_ref.mask_ref = bf16[16,432,128]{2,1,0:T(8,128)(2,1)S(1)} async-done(((bf16[16,432,128]{2,1,0:T(8,128)(2,1)}), bf16[16,432,128]{2,1,0:T(8,128)(2,1)S(1)}, u32[]{:S(2)}, u32[]{:S(2)}) %all-to-all-start) | async-done | bytes 1769504 | tf_op jit(solution)/shard_map/all_to_all | solution.py:370
  36.3 1.2 %copy-done.5 = bf16[16,432,128]{2,1,0:T(8,128)(2,1)} copy-done((bf16[16,432,128]{2,1,0:T(8,128)(2,1)}, bf16[16,432,128]{2,1,0:T(8,128)(2,1)S(1)}, u32[]{:S(2)}) %copy-start.5) | copy-done | bytes 1769496
  37.5 2.1 %project_cotangent.1 = (bf16[4,96,128]{2,1,0:T(8,128)(2,1)}, bf16[4,96,128]{2,1,0:T(8,128)(2,1)}, f32[4,96,128]{2,1,0:T(8,128)}) custom-call(s32[1]{0:T(128)} %bitcast.8.core_ref, bf16[16,432,128]{2,1,0:T(8,128)(2,1)} %copy-done.5, bf16[128,128]{1,0:T(8,128)(2,1)} %weight_ref.1, bf16[4,96,128]{2,1,0:T(8,128)(2,1)} %gate_ref.1, bf16[4,96,128]{2,1,0:T(8,128)(2,1)} %query_ref.1), custom_call_target="tpu_custom_call" | custom-call | tf_op jit(solution)/shard_map/project_cotangent/pallas_call | solution.py:241
  39.6 0.7 collective-permute-start
  40.3 0.4 maximum_select_fusion
  40.7 0.8 collective-permute-done.qd_other_ref
  41.5 12.8 %attention_both.1 = (bf16[4,96,128]{2,1,0:T(8,128)(2,1)S(1)}, bf16[4,96,128]{2,1,0:T(8,128)(2,1)S(1)}, bf16[4,96,128]{2,1,0:T(8,128)(2,1)S(1)}, bf16[4,96,128]{2...) custom-call(s32[9]{0:T(128)S(1)} %stack.39.place_ref, ...), custom_call_target="tpu_custom_call" | custom-call | flops 3623878656 | bytes 16777216 | tf_op jit(solution)/shard_map/attention_both/pallas_call | solution.py:274
  54.3 0.1 fusion.4
  54.4 0.4 collective-permute-start.2
  54.9 1.9 %collective-permute-start.3 = (bf16[4,96,128]{2,1,0:T(8,128)(2,1)S(1)}, bf16[4,96,128]{2,1,0:T(8,128)(2,1)S(1)}, u32[]{:S(2)}, u32[]{:S(2)}) collective-permute-start(bf16[4,96,128]{2,1,0:T(8,128)(2,1)S(1)} %get-tuple-element.26), channel_id=1, source_target_pairs={{0,2},{1,3},{2,4},{3,5},{4,6},{5,7},{6,0},{7,1},{8,10},{9,11},{10,... | collective-permute-start | bytes 294920 | tf_op jit(solution)/shard_map/ppermute | solution.py:367
  56.7 0.8 collective-permute-start.4
  57.6 2.7 %collective-permute-done.3 = bf16[4,96,128]{2,1,0:T(8,128)(2,1)S(1)} collective-permute-done((bf16[4,96,128]{2,1,0:T(8,128)(2,1)S(1)}, bf16[4,96,128]{2,1,0:T(8,128)(2,1)S(1)}, u32[]{:S(2)}, u32[]{:S(2)}) %collective-permute-start.3) | collective-permute-done | bytes 98336 | tf_op jit(solution)/shard_map/ppermute | solution.py:367
  60.3 0.3 collective-permute-done.4
  60.7 0.9 pad_maximum_fusion
  61.6 7.2 %all-to-all-start.1 = ((bf16[8,2,2,96,192]{4,3,2,1,0:T(8,128)(2,1)}), bf16[8,2,2,96,192]{4,3,2,1,0:T(8,128)(2,1)S(1)}, u32[]{:S(2)}, u32[]{:S(2)}) async-start(bf16[8,2,2,96,192]{4,3,2,1,0:T(8,128)(2,1)} %get-tuple-element.36), calls=%async_computation.1 | async-start | bytes 3145728 | tf_op jit(solution)/shard_map/all_to_all | solution.py:401
  68.8 0.4 collective-permute-start.5
  69.2 2.4 %collective-permute-start.6 = (bf16[3,4,96,128]{3,2,1,0:T(8,128)(2,1)}, bf16[3,4,96,128]{3,2,1,0:T(8,128)(2,1)S(1)}, u32[]{:S(2)}, u32[]{:S(2)}) collective-permute-start(bf16[3,4,96,128]{3,2,1,0:T(8,128)(2,1)} %get-tuple-element.32), channel_id=1, source_target_pairs={{0,6},{1,7},{2,0},{3,1},{4,2},{5,3},{6,4},{7,5},{8,14},{9,15},{10,... | collective-permute-start | bytes 884744 | tf_op jit(solution)/shard_map/ppermute | solution.py:367
  71.6 0.1 fusion.5
  71.7 0.8 maximum_select_fusion.2
  72.4 4.8 %collective-permute-done.5 = bf16[3,4,96,128]{3,2,1,0:T(8,128)(2,1)S(1)} collective-permute-done((bf16[3,4,96,128]{3,2,1,0:T(8,128)(2,1)}, bf16[3,4,96,128]{3,2,1,0:T(8,128)(2,1)S(1)}, u32[]{:S(2)}, u32[]{:S(2)}) %collective-permute-start.5) | collective-permute-done | bytes 294944 | tf_op jit(solution)/shard_map/ppermute | solution.py:367
  77.3 0.1 add_convert_fusion.1
  77.3 0.1 add_convert_fusion.3
  77.4 2.5 %collective-permute-start.8 = (bf16[2,4,96,128]{3,2,1,0:T(8,128)(2,1)S(1)}, bf16[2,4,96,128]{3,2,1,0:T(8,128)(2,1)S(1)}, u32[]{:S(2)}, u32[]{:S(2)}) collective-permute-start(bf16[2,4,96,128]{3,2,1,0:T(8,128)(2,1)S(1)} %pad_maximum_fusion.3), channel_id=1, source_target_pairs={{0,6},{1,7},{2,0},{3,1},{4,2},{5,3},{6,4},{7,5},{8,14},{9,15},{10,... | collective-permute-start | bytes 589832 | tf_op jit(solution)/shard_map/ppermute | solution.py:367
  79.9 0.1 collective-permute-start.7
  80.0 0.1 collective-permute-start.9
  80.1 0.8 multiply_convert_fusion
  80.9 1.6 %collective-permute-done.8 = bf16[2,4,96,128]{3,2,1,0:T(8,128)(2,1)S(1)} collective-permute-done((bf16[2,4,96,128]{3,2,1,0:T(8,128)(2,1)S(1)}, bf16[2,4,96,128]{3,2,1,0:T(8,128)(2,1)S(1)}, u32[]{:S(2)}, u32[]{:S(2)}) %collective-permute-start.8) | collective-permute-done | bytes 196640 | tf_op jit(solution)/shard_map/ppermute | solution.py:367
  82.5 3.5 %collective-permute-done.7 = bf16[2,4,96,128]{3,2,1,0:T(8,128)(2,1)S(1)} collective-permute-done((bf16[2,4,96,128]{3,2,1,0:T(8,128)(2,1)S(1)}, bf16[2,4,96,128]{3,2,1,0:T(8,128)(2,1)S(1)}, u32[]{:S(2)}, u32[]{:S(2)}) %collective-permute-start.7) | collective-permute-done | bytes 196640 | tf_op jit(solution)/shard_map/ppermute | solution.py:367
  86.0 0.1 add_convert_fusion
  86.1 6.0 %collective-permute-start.10 = (bf16[4,96,128]{2,1,0:T(8,128)(2,1)S(1)}, bf16[4,96,128]{2,1,0:T(8,128)(2,1)S(1)}, u32[]{:S(2)}, u32[]{:S(2)}) collective-permute-start(bf16[4,96,128]{2,1,0:T(8,128)(2,1)S(1)} %slice_bitcast_fusion.2), channel_id=1, source_target_pairs={{0,1},{1,0},{2,3},{3,2},{4,5},{5,4},{6,7},{7,6},{8,9},{9,8},{10,11... | collective-permute-start | bytes 294920 | tf_op jit(solution)/shard_map/ppermute | solution.py:353
  92.2 0.1 slice_bitcast_fusion.1
  92.3 0.8 collective-permute-done.10
  93.1 0.1 fusion.6
  93.2 0.8 maximum_select_fusion.4
  94.0 0.8 multiply_convert_fusion.1
  94.8 0.3 convert_reduce_fusion
  95.0 0.4 collective-permute-start.11
  95.5 0.9 collective-permute-done.11
  96.4 0.8 maximum_select_fusion.1
  (22 shorter events, 0.2 us)
Async XLA Ops:
  0.6 0.9 copy-start
  1.5 0.9 copy-start.1
  2.4 0.9 copy-start.2
  3.3 0.7 copy-start.3
  5.5 30.7 %all-to-all-start = ((bf16[16,432,128]{2,1,0:T(8,128)(2,1)}), bf16[16,432,128]{2,1,0:T(8,128)(2,1)S(1)}, u32[]{:S(2)}, u32[]{:S(2)}) async-start(bf16[16,432,128]{2,1,0:T(8,128)(2,1)} %prepare_exchange.1), calls=%async_computation | async-start | bytes 3538944 | tf_op jit(solution)/shard_map/all_to_all | solution.py:370
  14.9 25.5 %collective-permute-start.1 = (bf16[2,96,1536]{2,1,0:T(8,128)(2,1)}, bf16[2,96,1536]{2,1,0:T(8,128)(2,1)S(1)}, u32[]{:S(2)}, u32[]{:S(2)}) collective-permute-start(bf16[2,96,1536]{2,1,0:T(8,128)(2,1)} %get-tuple-element.48), channel_id=1, source_target_pairs={{0,1},{1,0},{2,3},{3,2},{4,5},{5,4},{6,7},{7,6},{8,9},{9,8},{10,11... | collective-permute-start | bytes 1769480 | tf_op jit(solution)/shard_map/ppermute | solution.py:353
  36.3 1.2 %copy-start.5 = (bf16[16,432,128]{2,1,0:T(8,128)(2,1)}, bf16[16,432,128]{2,1,0:T(8,128)(2,1)S(1)}, u32[]{:S(2)}) copy-start(bf16[16,432,128]{2,1,0:T(8,128)(2,1)S(1)} %all-to-all-done.packed_ref.kv_ref.mask_ref) | copy-start | bytes 5308420
  39.6 1.9 %copy-start.4 = (bf16[4,96,128]{2,1,0:T(8,128)(2,1)S(1)}, bf16[4,96,128]{2,1,0:T(8,128)(2,1)}, u32[]{:S(2)}) copy-start(bf16[4,96,128]{2,1,0:T(8,128)(2,1)} %get-tuple-element.21.qd_mine_ref) | copy-start | bytes 294916
  39.6 1.9 %collective-permute-start = (bf16[4,96,128]{2,1,0:T(8,128)(2,1)}, bf16[4,96,128]{2,1,0:T(8,128)(2,1)S(1)}, u32[]{:S(2)}, u32[]{:S(2)}) collective-permute-start(bf16[4,96,128]{2,1,0:T(8,128)(2,1)} %get-tuple-element.22), channel_id=1, source_target_pairs={{0,1},{1,0},{2,3},{3,2},{4,5},{5,4},{6,7},{7,6},{8,9},{9,8},{10,11... | collective-permute-start | bytes 294920 | tf_op jit(solution)/shard_map/ppermute | solution.py:353
  54.4 17.1 %collective-permute-start.2 = (bf16[4,96,128]{2,1,0:T(8,128)(2,1)S(1)}, bf16[4,96,128]{2,1,0:T(8,128)(2,1)S(1)}, u32[]{:S(2)}, u32[]{:S(2)}) collective-permute-start(bf16[4,96,128]{2,1,0:T(8,128)(2,1)S(1)} %get-tuple-element.24), channel_id=1, source_target_pairs={{0,1},{1,0},{2,3},{3,2},{4,5},{5,4},{6,7},{7,6},{8,9},{9,8},{10,11... | collective-permute-start | bytes 294920 | tf_op jit(solution)/shard_map/ppermute | solution.py:353
  54.9 5.5 %collective-permute-start.3 = (bf16[4,96,128]{2,1,0:T(8,128)(2,1)S(1)}, bf16[4,96,128]{2,1,0:T(8,128)(2,1)S(1)}, u32[]{:S(2)}, u32[]{:S(2)}) collective-permute-start(bf16[4,96,128]{2,1,0:T(8,128)(2,1)S(1)} %get-tuple-element.26), channel_id=1, source_target_pairs={{0,2},{1,3},{2,4},{3,5},{4,6},{5,7},{6,0},{7,1},{8,10},{9,11},{10,... | collective-permute-start | bytes 294920 | tf_op jit(solution)/shard_map/ppermute | solution.py:367
  56.7 3.9 %collective-permute-start.4 = (bf16[4,96,128]{2,1,0:T(8,128)(2,1)S(1)}, bf16[4,96,128]{2,1,0:T(8,128)(2,1)S(1)}, u32[]{:S(2)}, u32[]{:S(2)}) collective-permute-start(bf16[4,96,128]{2,1,0:T(8,128)(2,1)S(1)} %get-tuple-element.27), channel_id=1, source_target_pairs={{0,6},{1,7},{2,0},{3,1},{4,2},{5,3},{6,4},{7,5},{8,14},{9,15},{10,... | collective-permute-start | bytes 294920 | tf_op jit(solution)/shard_map/ppermute | solution.py:367
  61.6 33.2 %all-to-all-start.1 = ((bf16[8,2,2,96,192]{4,3,2,1,0:T(8,128)(2,1)}), bf16[8,2,2,96,192]{4,3,2,1,0:T(8,128)(2,1)S(1)}, u32[]{:S(2)}, u32[]{:S(2)}) async-start(bf16[8,2,2,96,192]{4,3,2,1,0:T(8,128)(2,1)} %get-tuple-element.36), calls=%async_computation.1 | async-start | bytes 3145728 | tf_op jit(solution)/shard_map/all_to_all | solution.py:401
  68.8 11.3 %copy-start.6 = (f32[4,96,128]{2,1,0:T(8,128)S(1)}, f32[4,96,128]{2,1,0:T(8,128)}, u32[]{:S(2)}) copy-start(f32[4,96,128]{2,1,0:T(8,128)} %get-tuple-element.35) | copy-start | bytes 589828
  68.8 8.4 %collective-permute-start.5 = (bf16[3,4,96,128]{3,2,1,0:T(8,128)(2,1)}, bf16[3,4,96,128]{3,2,1,0:T(8,128)(2,1)S(1)}, u32[]{:S(2)}, u32[]{:S(2)}) collective-permute-start(bf16[3,4,96,128]{3,2,1,0:T(8,128)(2,1)} %get-tuple-element.31), channel_id=1, source_target_pairs={{0,2},{1,3},{2,4},{3,5},{4,6},{5,7},{6,0},{7,1},{8,10},{9,11},{10,... | collective-permute-start | bytes 884744 | tf_op jit(solution)/shard_map/ppermute | solution.py:367
  69.2 8.0 %collective-permute-start.6 = (bf16[3,4,96,128]{3,2,1,0:T(8,128)(2,1)}, bf16[3,4,96,128]{3,2,1,0:T(8,128)(2,1)S(1)}, u32[]{:S(2)}, u32[]{:S(2)}) collective-permute-start(bf16[3,4,96,128]{3,2,1,0:T(8,128)(2,1)} %get-tuple-element.32), channel_id=1, source_target_pairs={{0,6},{1,7},{2,0},{3,1},{4,2},{5,3},{6,4},{7,5},{8,14},{9,15},{10,... | collective-permute-start | bytes 884744 | tf_op jit(solution)/shard_map/ppermute | solution.py:367
  77.4 5.1 %collective-permute-start.8 = (bf16[2,4,96,128]{3,2,1,0:T(8,128)(2,1)S(1)}, bf16[2,4,96,128]{3,2,1,0:T(8,128)(2,1)S(1)}, u32[]{:S(2)}, u32[]{:S(2)}) collective-permute-start(bf16[2,4,96,128]{3,2,1,0:T(8,128)(2,1)S(1)} %pad_maximum_fusion.3), channel_id=1, source_target_pairs={{0,6},{1,7},{2,0},{3,1},{4,2},{5,3},{6,4},{7,5},{8,14},{9,15},{10,... | collective-permute-start | bytes 589832 | tf_op jit(solution)/shard_map/ppermute | solution.py:367
  79.9 6.1 %collective-permute-start.7 = (bf16[2,4,96,128]{3,2,1,0:T(8,128)(2,1)S(1)}, bf16[2,4,96,128]{3,2,1,0:T(8,128)(2,1)S(1)}, u32[]{:S(2)}, u32[]{:S(2)}) collective-permute-start(bf16[2,4,96,128]{3,2,1,0:T(8,128)(2,1)S(1)} %pad_maximum_fusion.2), channel_id=1, source_target_pairs={{0,2},{1,3},{2,4},{3,5},{4,6},{5,7},{6,0},{7,1},{8,10},{9,11},{10,... | collective-permute-start | bytes 589832 | tf_op jit(solution)/shard_map/ppermute | solution.py:367
  80.0 6.0 %collective-permute-start.9 = (bf16[2,4,96,128]{3,2,1,0:T(8,128)(2,1)S(1)}, bf16[2,4,96,128]{3,2,1,0:T(8,128)(2,1)S(1)}, u32[]{:S(2)}, u32[]{:S(2)}) collective-permute-start(bf16[2,4,96,128]{3,2,1,0:T(8,128)(2,1)S(1)} %add_convert_fusion.1), channel_id=1, source_target_pairs={{0,8},{1,9},{2,10},{3,11},{4,12},{5,13},{6,14},{7,15},{8,0},{9,1},... | collective-permute-start | bytes 589832 | tf_op jit(solution)/shard_map/ppermute | solution.py:367
  86.1 7.0 %collective-permute-start.10 = (bf16[4,96,128]{2,1,0:T(8,128)(2,1)S(1)}, bf16[4,96,128]{2,1,0:T(8,128)(2,1)S(1)}, u32[]{:S(2)}, u32[]{:S(2)}) collective-permute-start(bf16[4,96,128]{2,1,0:T(8,128)(2,1)S(1)} %slice_bitcast_fusion.2), channel_id=1, source_target_pairs={{0,1},{1,0},{2,3},{3,2},{4,5},{5,4},{6,7},{7,6},{8,9},{9,8},{10,11... | collective-permute-start | bytes 294920 | tf_op jit(solution)/shard_map/ppermute | solution.py:353
  95.0 1.4 %collective-permute-start.11 = (bf16[2,96,192]{2,1,0:T(8,128)(2,1)S(1)}, bf16[2,96,192]{2,1,0:T(8,128)(2,1)S(1)}, u32[]{:S(2)}, u32[]{:S(2)}) collective-permute-start(bf16[2,96,192]{2,1,0:T(8,128)(2,1)S(1)} %fusion.2), channel_id=1, source_target_pairs={{0,1},{1,0},{2,3},{3,2},{4,5},{5,4},{6,7},{7,6},{8,9},{9,8},{10,11... | collective-permute-start | bytes 221192 | tf_op jit(solution)/shard_map/ppermute | solution.py:353

commit v7 on v6

--- a/solution.py
+++ b/solution.py
@@ -14,6 +14,7 @@
 UNROLL = 12
 MASK_ROWS = 16
 PIECES = 8
+VMEM_WIDE = 60 * 1024 * 1024
 
 
 def attention_kernel(
@@ -25,10 +26,10 @@
     bias_ref,
     qa_own_ref,
     qa_away_ref,
+    dkv_ref,
     right_out_ref,
     left_out_ref,
     rest_out_ref,
-    dbias_ref,
     cap_ref,
     s_ref,
     b2_ref,
@@ -36,7 +37,7 @@
     dp_ref,
     de_ref,
     row_ref,
-    dkv_ref,
+    dbias_ref,
 ):
     step = pl.program_id(0)
     last = pl.num_programs(0) - 1
@@ -150,26 +151,22 @@
     key_value = lax.dot_general(
         sides, de_ref[...], (((0,), (0,)), ((), ())), preferred_element_type=jnp.float32
     )
-    key_value = key_value.T.astype(jnp.bfloat16)
-    for group in range(PIECES):
-        for side in range(2):
-            start = group * queries + side * half
-            target = 2 * place_ref[group] + (side + core) % 2
-            dkv_ref[target, step] = key_value[start : start + half]
+    dkv_ref[...] = key_value.T.astype(jnp.bfloat16).reshape(dkv_ref.shape)
 
     @pl.when(step == last)
     def _():
-        width = dbias_ref.shape[4]
+        width = dbias_ref.shape[3]
         for piece in range(PIECES):
             for head in range(2):
                 for side in range(2):
                     start = head * queries + side * half
                     part = acc_ref[start : start + half, piece * width : (piece + 1) * width]
-                    dbias_ref[piece, (side + core) % 2, head] = part.astype(jnp.bfloat16)
-        right_out_ref[...] = dkv_ref[12]
-        left_out_ref[...] = dkv_ref[13]
-        rest_out_ref[:12] = dkv_ref[:12]
-        rest_out_ref[12:] = dkv_ref[14:]
+                    target = 2 * place_ref[piece] + (side + core) % 2
+                    dbias_ref[target, head] = part.astype(jnp.bfloat16)
+        right_out_ref[...] = dbias_ref[8:10]
+        left_out_ref[...] = dbias_ref[10:12]
+        rest_out_ref[:8] = dbias_ref[:8]
+        rest_out_ref[8:] = dbias_ref[12:]
 
 
 def prepare_kernel(key_ref, value_ref, mask_ref, cotangent_ref, packed_ref):
@@ -203,10 +200,18 @@
 def prepare(key, value, mask, cotangent, devices):
     columns, tokens, channels = key.shape
     rows = columns * tokens + cotangent.shape[0] * cotangent.shape[1] + MASK_ROWS
+
+    def whole(shape):
+        return pl.BlockSpec(shape, lambda i: (0,) * len(shape))
+
+    out = (devices, rows, channels)
     return pl.pallas_call(
         prepare_kernel,
-        out_shape=jax.ShapeDtypeStruct((devices, rows, channels), jnp.bfloat16),
-        compiler_params=pltpu.CompilerParams(vmem_limit_bytes=32 * 1024 * 1024),
+        grid=(1,),
+        in_specs=[whole(key.shape), whole(value.shape), whole(mask.shape), whole(cotangent.shape)],
+        out_specs=whole(out),
+        out_shape=jax.ShapeDtypeStruct(out, jnp.bfloat16),
+        compiler_params=pltpu.CompilerParams(vmem_limit_bytes=VMEM_WIDE),
         name="prepare_exchange",
     )(key, value, mask, cotangent)
 
@@ -254,8 +259,27 @@
             jax.ShapeDtypeStruct(gate.shape, jnp.bfloat16),
             jax.ShapeDtypeStruct(gate.shape, jnp.float32),
         ],
+        compiler_params=pltpu.CompilerParams(vmem_limit_bytes=VMEM_WIDE),
         name="project_cotangent",
     )(core, packed, weight, gate, query)
+
+
+def total_kernel(parts_ref, key_ref, value_ref):
+    half = key_ref.shape[2] // 2
+    scaling = 1.0 / math.sqrt(key_ref.shape[2] // HEADS)
+    for column in range(key_ref.shape[0]):
+        sums = [
+            jnp.sum(parts_ref[:, side, column].astype(jnp.float32), axis=0) for side in range(2)
+        ]
+        key = jnp.concatenate([part[:, :half] for part in sums], axis=1) * scaling
+        key_ref[column] = key.astype(jnp.bfloat16)
+        value = jnp.concatenate([part[:, half:] for part in sums], axis=1)
+        value_ref[column] = value.astype(jnp.bfloat16)
+
+
+def total(parts, like):
+    out = jax.ShapeDtypeStruct(like.shape, jnp.bfloat16)
+    return pl.pallas_call(total_kernel, out_shape=[out, out], compiler_params=pltpu.CompilerParams(vmem_limit_bytes=VMEM_WIDE), name="total_key_value")(parts)
 
 
 def attend(places, mine, other, received, bias, row_count):
@@ -285,10 +309,10 @@
             out_specs=[
                 column_spec,
                 column_spec,
-                whole(mine.shape),
-                whole(mine.shape),
-                whole((14,) + mine.shape),
-                whole((row_count, 2) + piece),
+                pl.BlockSpec((devices, 1, tokens, lanes), lambda j, places: (0, j, 0, 0)),
+                whole((2,) + piece),
+                whole((2,) + piece),
+                whole((12,) + piece),
             ],
             scratch_shapes=[
                 pltpu.VMEM((columns, 1, keys), jnp.float32),
@@ -298,16 +322,16 @@
                 pltpu.VMEM((rows, keys), jnp.float32),
                 pltpu.VMEM((2 * rows, keys), jnp.bfloat16),
                 pltpu.VMEM((rows, 128), jnp.float32),
-                pltpu.VMEM((16,) + mine.shape, jnp.bfloat16),
+                pltpu.VMEM((16,) + piece, jnp.bfloat16),
             ],
         ),
         out_shape=[
             jax.ShapeDtypeStruct(mine.shape, jnp.bfloat16),
             jax.ShapeDtypeStruct(mine.shape, jnp.bfloat16),
-            jax.ShapeDtypeStruct(mine.shape, jnp.bfloat16),
-            jax.ShapeDtypeStruct(mine.shape, jnp.bfloat16),
-            jax.ShapeDtypeStruct((14,) + mine.shape, jnp.bfloat16),
-            jax.ShapeDtypeStruct((row_count, 2) + piece, jnp.bfloat16),
+            jax.ShapeDtypeStruct((devices,) + mine.shape, jnp.bfloat16),
+            jax.ShapeDtypeStruct((2,) + piece, jnp.bfloat16),
+            jax.ShapeDtypeStruct((2,) + piece, jnp.bfloat16),
+            jax.ShapeDtypeStruct((12,) + piece, jnp.bfloat16),
         ],
         compiler_params=pltpu.CompilerParams(vmem_limit_bytes=48 * 1024 * 1024),
         cost_estimate=pl.CostEstimate(flops=12 * 128 * work, bytes_accessed=16 * 2**20, transcendentals=work),
@@ -329,11 +353,9 @@
     half = channels // 2
     devices = lax.axis_size("col")
     row_count = lax.axis_size("row")
-    chips = devices // 2
     core = lax.axis_index("col") % 2
     scaling = 1.0 / math.sqrt(channels // HEADS)
     swap = [(index, index ^ 1) for index in range(devices)]
-    chip_groups = [[2 * chip + side for chip in range(chips)] for side in range(2)]
     keys = pair_bias.shape[2]
 
     def mine_other(array, axis):
@@ -356,68 +378,55 @@
     bias_pair = in_order(bias_mine, swapped(bias_other), 1).reshape(-1, keys)
 
     core_word = core.astype(jnp.int32).reshape(1)
-    ring = chips // 2
-
-    def along(array, turn, side):
-        pairs = []
-        for index in range(devices):
-            high, low = index // (2 * ring), index // 2 % ring
-            target = ((high + side) % 2) * ring + (low + turn) % ring
-            pairs.append((index, 2 * target + index % 2))
-        return lax.ppermute(array, "col", pairs)
-
     packed = prepare(key_vectors, value_vectors, pair_mask, output_cotangent, devices)
     received = lax.all_to_all(packed, "col", 0, 0, tiled=True)
-    chip = lax.axis_index("col") // 2
+    place = lax.axis_index("row")
+    row_ring = row_count // 2
     places = [
-        ring * ((index // ring - chip // ring) % 2) + (index % ring - chip % ring) % ring
-        for index in range(chips)
+        2 * ((index % row_ring - place) % row_ring) + (index // row_ring - place // row_ring) % 2
+        for index in range(row_count)
     ]
     places.append(core)
     places = jnp.stack(places).astype(jnp.int32)
 
     qd_mine, qd_away, gate_slope = project(core_word, received, output_weight, gate_logits, query_vectors)
 
-    qa_own, qa_away, kv_right, kv_left, kv_rest, bias_grads = attend(
+    qa_own, qa_away, kv_grads, bias_right, bias_left, bias_rest = attend(
         places, qd_mine, swapped(qd_away), received, bias_pair, row_count
     )
-
-
-    def added(*parts):
-        return sum(part.astype(jnp.float32) for part in parts)
-
-    def both(*parts):
-        return lax.optimization_barrier(parts)
-
-    def low(*parts):
-        return added(*parts).astype(jnp.bfloat16)
-
-    home, near, far, behind = kv_rest[:2], kv_rest[2:4], kv_rest[4:6], kv_rest[6:8]
-    home_across, near_across, behind_across = kv_rest[8:10], kv_rest[10:12], kv_rest[12:]
-    from_left, from_right = both(along(kv_right, 1, 0), along(kv_left, -1, 0))
-    onward = jnp.concatenate([low(near_across[:1], from_left[None]), near_across[1:], far[:1]])
-    backward = jnp.concatenate([behind_across[:1], low(behind_across[1:], from_right[None]), far[1:]])
-    onward, backward, bias_grads = both(onward, backward, bias_grads)
-    bias_parts = lax.all_to_all(bias_grads, "row", 0, 0, tiled=True)
-    from_left, from_right = both(along(onward, 1, 0), along(backward, -1, 0))
-    from_across = along(low(home_across, from_left[:2], from_right[:2]), 0, 1)
-    onward = jnp.concatenate([low(near[:1], from_left[2:]), near[1:]])
-    backward = jnp.concatenate([behind[:1], low(behind[1:], from_right[2:])])
-    kv_sum = low(home, along(onward, 1, 0), along(backward, -1, 0), from_across)
-    kv_back = swapped(kv_sum[1])
-    key_gradient = in_order(kv_sum[0, ..., :half], kv_back[..., :half], 2)
-    key_gradient = (key_gradient.astype(jnp.float32) * scaling).astype(jnp.bfloat16)
-    value_gradient = in_order(kv_sum[0, ..., half:], kv_back[..., half:], 2)
 
     qa_back = swapped(qa_away)
     query_gradient = in_order(qa_own[..., :half], qa_back[..., :half], 2)
     attended = in_order(qa_own[..., half:], qa_back[..., half:], 2).astype(jnp.float32)
     gate_gradient = (gate_slope * attended).astype(jnp.bfloat16)
 
-    bias_sum = jnp.sum(bias_parts.astype(jnp.float32), axis=0)
-    bias_gradient = in_order(
-        bias_sum[0], swapped(bias_sum[1].astype(jnp.bfloat16)).astype(jnp.float32), 0
-    )
+    def along_row(array, turn, side):
+        pairs = []
+        for index in range(row_count):
+            high, low = index // row_ring, index % row_ring
+            pairs.append((index, ((high + side) % 2) * row_ring + (low + turn) % row_ring))
+        return lax.ppermute(array, "row", pairs)
+
+    def added(*parts):
+        return sum(part.astype(jnp.float32) for part in parts)
+
+    from_left = along_row(bias_right, 1, 0)
+    from_right = along_row(bias_left, -1, 0)
+    from_left, from_right, kv_grads = lax.optimization_barrier((from_left, from_right, kv_grads))
+    kv_parts = lax.all_to_all(kv_grads, "col", 0, 0, tiled=True)
+    kv_parts = kv_parts.reshape((devices // 2, 2) + kv_parts.shape[1:])
+    key_gradient, value_gradient = total(kv_parts, key_vectors)
+    onward = jnp.concatenate([added(bias_rest[4:6], from_left).astype(jnp.bfloat16), bias_rest[6:8]])
+    backward = jnp.concatenate([bias_rest[8:10], added(bias_rest[10:], from_right).astype(jnp.bfloat16)])
+    sums = added(bias_rest[:4], along_row(onward, 1, 0), along_row(backward, -1, 0))
+    low_sums = sums.astype(jnp.bfloat16)
+    diagonal = []
+    for index in range(row_count * devices):
+        up = (index // devices + row_ring) % row_count
+        diagonal.append((index, up * devices + (index % devices ^ 1)))
+    bias_own = added(sums[0], along_row(low_sums[2], 0, 1))
+    bias_away = added(swapped(low_sums[1]), lax.ppermute(low_sums[3], ("row", "col"), diagonal))
+    bias_gradient = in_order(bias_own, bias_away, 0)
     return (query_gradient, key_gradient, value_gradient, gate_gradient, bias_gradient)
 
 

time: 97.6 us -> 95.8 us (0.982)
  starting transfers between devices: 30.2 us -> 23.3 us
  waiting for transfers between devices: 36.8 us -> 41.6 us
  Pallas kernels: 16.5 us -> 19.5 us
  other arithmetic: 7.87 us -> 5.09 us
    ppermute x5 -> x4, starting transfers between devices: 7.74 us -> 1.2 us  [swapped(): return lax.ppermute(array, 'col', swap)]
    ppermute x7 -> x6, waiting for transfers between devices: 13 us -> 18.4 us  [the longest x5 15.1 us: along_row(): return lax.ppermute(array, 'row', pairs)]
    pallas_call x1 -> x2, Pallas kernels: 1.54 us -> 4.86 us  [the longest x1 2.54 us: prepare(): pl.pallas_call(prepare_kernel, grid=(1,), in_specs=[whole(key.shape), who...]
    all_to_all x1, starting transfers between devices: 7.21 us -> 4.61 us  [local(): kv_parts = lax.all_to_all(kv_grads, 'col', 0, 0, tiled=True)]
    ppermute x7 -> x6, starting transfers between devices: 8.04 us -> 10.2 us  [the longest x5 5.75 us: along_row(): return lax.ppermute(array, 'row', pairs)]
    unnamed x14 -> x16, local copies, waits for them, and re-layouts: 4.59 us -> 2.45 us
    ppermute x5 -> x4, waiting for transfers between devices: 2.56 us -> 0.78 us  [swapped(): return lax.ppermute(array, 'col', swap)]
    select_n x1, other arithmetic: 2.15 us -> 0.91 us  [mine_other(): return (jnp.where(core == 0, low, high), jnp.where(core == 0, high, low))]
  transfers between devices with their start and end apart: 14 -> 12, of which waited for: 9 -> 7; matrix products, arithmetic and copies ran while one was open for 7% -> 8% of each run, Pallas kernels for 2% -> 2%
where the time goes in v7:
time: 95.8 us; the launch traced here: 95.3 us
  waiting for transfers between devices  41.6 us (43%)
  starting transfers between devices  23.3 us (24%)
  Pallas kernels  19.5 us (20%)
  other arithmetic  5.09 us (5%)
  local copies, waits for them, and re-layouts  5.07 us (5%)
    all_to_all x1, waiting for transfers between devices, local(): received = lax.all_to_all(packed, 'col', 0, 0, tiled=True)  22.5 us
    ppermute x5, waiting for transfers between devices, along_row(): return lax.ppermute(array, 'row', pairs)  15.1 us
    pallas_call x1, Pallas kernels, attend(): pl.pallas_call(attention_kernel, grid_spec=pltpu.PrefetchScalarGridSpec(n...  12.5 us
    all_to_all x1, starting transfers between devices, local(): received = lax.all_to_all(packed, 'col', 0, 0, tiled=True)  7.3 us
    ppermute x5, starting transfers between devices, along_row(): return lax.ppermute(array, 'row', pairs)  5.75 us
    all_to_all x1, starting transfers between devices, local(): kv_parts = lax.all_to_all(kv_grads, 'col', 0, 0, tiled=True)  4.61 us
    ppermute x1, starting transfers between devices, local(): lax.ppermute(low_sums[3], ('row', 'col'), diagonal)  4.46 us
    ppermute x1, waiting for transfers between devices, local(): lax.ppermute(low_sums[3], ('row', 'col'), diagonal)  3.28 us
  transfers between devices with their start and end apart: 12, of which 7 were waited for; matrix products, arithmetic and copies ran while one was open for 8% of the time, Pallas kernels for 2%

profile of v7, /device:TPU:1, one launch (start us, length us, event | category | flops | bytes accessed | tf_op | source)
XLA Modules:
  0.0 95.3 jit_solution(10903903269477987819)
XLA Ops:
  0.6 2.5 %prepare_exchange.1 = bf16[16,432,128]{2,1,0:T(8,128)(2,1)} custom-call(bf16[4,96,128]{2,1,0:T(8,128)(2,1)} %key_ref.1, bf16[4,96,128]{2,1,0:T(8,128)(2,1)} %value_ref.1, s32[4,96]{1,0:T(4,128)} %mask_ref.1, bf16[4,8,1536]{2,1,0:T(8,128)(2,1)} %cotangent_ref.1), custom_call_target="tpu_custom_call" | custom-call | tf_op jit(solution)/shard_map/prepare_exchange/pallas_call | solution.py:208
  3.2 7.3 %all-to-all-start = ((bf16[16,432,128]{2,1,0:T(8,128)(2,1)}), bf16[16,432,128]{2,1,0:T(8,128)(2,1)S(1)}, u32[]{:S(2)}, u32[]{:S(2)}) async-start(bf16[16,432,128]{2,1,0:T(8,128)(2,1)} %prepare_exchange.1), calls=%async_computation | async-start | bytes 3538944 | tf_op jit(solution)/shard_map/all_to_all | solution.py:382
  10.5 0.0 copy-done.3
  10.5 0.9 broadcast_select_fusion.1
  11.4 0.1 collective-permute-start.1
  11.5 0.1 stack.39.place_ref
  11.6 22.5 %all-to-all-done.packed_ref.kv_ref.mask_ref = bf16[16,432,128]{2,1,0:T(8,128)(2,1)S(1)} async-done(((bf16[16,432,128]{2,1,0:T(8,128)(2,1)}), bf16[16,432,128]{2,1,0:T(8,128)(2,1)S(1)}, u32[]{:S(2)}, u32[]{:S(2)}) %all-to-all-start) | async-done | bytes 1769504 | tf_op jit(solution)/shard_map/all_to_all | solution.py:382
  34.1 1.2 %copy-done.1 = bf16[16,432,128]{2,1,0:T(8,128)(2,1)} copy-done((bf16[16,432,128]{2,1,0:T(8,128)(2,1)}, bf16[16,432,128]{2,1,0:T(8,128)(2,1)S(1)}, u32[]{:S(2)}) %copy-start.1) | copy-done | bytes 1769496
  35.3 2.1 %project_cotangent.1 = (bf16[4,96,128]{2,1,0:T(8,128)(2,1)}, bf16[4,96,128]{2,1,0:T(8,128)(2,1)}, f32[4,96,128]{2,1,0:T(8,128)}) custom-call(s32[1]{0:T(128)} %bitcast.8.core_ref, bf16[16,432,128]{2,1,0:T(8,128)(2,1)} %copy-done.1, bf16[128,128]{1,0:T(8,128)(2,1)} %weight_ref.1, bf16[4,96,128]{2,1,0:T(8,128)(2,1)} %gate_ref.1, bf16[4,96,128]{2,1,0:T(8,128)(2,1)} %query_ref.1), custom_call_target="tpu_custom_call" | custom-call | tf_op jit(solution)/shard_map/project_cotangent/pallas_call | solution.py:246
  37.4 0.7 collective-permute-start
  38.1 0.0 collective-permute-done.1
  38.1 0.4 maximum_select_fusion
  38.5 0.8 collective-permute-done.qd_other_ref
  39.3 0.0 copy-done
  39.3 12.5 %attention_both.1 = (bf16[4,96,128]{2,1,0:T(8,128)(2,1)S(1)}, bf16[4,96,128]{2,1,0:T(8,128)(2,1)S(1)}, bf16[16,4,96,128]{3,2,1,0:T(8,128)(2,1)}, bf16[2,2,96,192...) custom-call(s32[9]{0:T(128)S(1)} %stack.39.place_ref, ...), custom_call_target="tpu_custom_call" | custom-call | flops 3623878656 | bytes 16777216 | tf_op jit(solution)/shard_map/attention_both/pallas_call | solution.py:298
  51.8 0.4 collective-permute-start.2
  52.1 1.3 %collective-permute-start.3 = (bf16[2,2,96,192]{3,2,1,0:T(8,128)(2,1)S(1)}, bf16[2,2,96,192]{3,2,1,0:T(8,128)(2,1)}, u32[]{:S(2)}, u32[]{:S(2)}) collective-permute-start(bf16[2,2,96,192]{3,2,1,0:T(8,128)(2,1)S(1)} %get-tuple-element.23), channel_id=1, source_target_pairs={{0,16},{16,32},{32,48},{48,0},{64,80},{80,96},{96,112},{112,64},{1... | collective-permute-start | bytes 442376 | tf_op jit(solution)/shard_map/ppermute | solution.py:408
  53.4 1.4 %collective-permute-start.4 = (bf16[2,2,96,192]{3,2,1,0:T(8,128)(2,1)S(1)}, bf16[2,2,96,192]{3,2,1,0:T(8,128)(2,1)}, u32[]{:S(2)}, u32[]{:S(2)}) collective-permute-start(bf16[2,2,96,192]{3,2,1,0:T(8,128)(2,1)S(1)} %get-tuple-element.24), channel_id=1, source_target_pairs={{0,48},{16,0},{32,16},{48,32},{64,112},{80,64},{96,80},{112,96},{1... | collective-permute-start | bytes 442376 | tf_op jit(solution)/shard_map/ppermute | solution.py:408
  54.9 0.7 fusion.2
  55.6 0.7 fusion.3
  56.3 3.6 %collective-permute-done.3 = bf16[2,2,96,192]{3,2,1,0:T(8,128)(2,1)} collective-permute-done((bf16[2,2,96,192]{3,2,1,0:T(8,128)(2,1)S(1)}, bf16[2,2,96,192]{3,2,1,0:T(8,128)(2,1)}, u32[]{:S(2)}, u32[]{:S(2)}) %collective-permute-start.3) | collective-permute-done | bytes 147488 | tf_op jit(solution)/shard_map/ppermute | solution.py:408
  59.9 0.0 collective-permute-done.4
  59.9 4.6 %all-to-all-start.1 = ((bf16[16,4,96,128]{3,2,1,0:T(8,128)(2,1)}), bf16[16,4,96,128]{3,2,1,0:T(8,128)(2,1)S(1)}, u32[]{:S(2)}, u32[]{:S(2)}) async-start(bf16[16,4,96,128]{3,2,1,0:T(8,128)(2,1)} %get-tuple-element.26), calls=%async_computation.1 | async-start | bytes 3145728 | tf_op jit(solution)/shard_map/all_to_all | solution.py:416
  64.6 1.2 %add_convert_fusion.1 = (bf16[2,2,96,192]{3,2,1,0:T(8,128)(2,1)S(1)}, bf16[2,2,96,192]{3,2,1,0:T(8,128)(2,1)S(1)}) fusion(bf16[2,2,96,192]{3,2,1,0:T(8,128)(2,1)} %collective-permute-done.3, bf16[12,2,96,192]{3,2,1,0:T(8,128)(2,1)S(1)} %get-tuple-element.30, bf16[2,2,96,192]{3,2,1,0:T(8,128)(2,1)} %collective-permute-done.4), kind=kLoop, calls=%fused_computation.8 | loop fusion | flops 589824 | bytes 884736 | tf_op jit(solution)/shard_map/convert_element_type | solution.py:419
  65.7 0.0 copy-start.6
  65.7 0.0 copy-start.7
  65.7 0.1 pad_maximum_fusion.1
  65.8 2.7 %collective-permute-start.6 = (bf16[4,2,96,192]{3,2,1,0:T(8,128)(2,1)S(1)}, bf16[4,2,96,192]{3,2,1,0:T(8,128)(2,1)S(1)}, u32[]{:S(2)}, u32[]{:S(2)}) collective-permute-start(bf16[4,2,96,192]{3,2,1,0:T(8,128)(2,1)S(1)} %pad_maximum_fusion.1), channel_id=1, source_target_pairs={{0,48},{16,0},{32,16},{48,32},{64,112},{80,64},{96,80},{112,96},{1... | collective-permute-start | bytes 884744 | tf_op jit(solution)/shard_map/ppermute | solution.py:408
  68.6 0.1 pad_maximum_fusion
  68.6 0.1 collective-permute-start.5
  68.7 0.0 collective-permute-done.2
  68.7 1.1 %fusion.4 = (bf16[4,96,64]{2,1,0:T(8,128)(2,1)S(1)}, bf16[4,96,64]{2,1,0:T(8,128)(2,1)S(1)}) fusion(bf16[4,96,128]{2,1,0:T(8,128)(2,1)} %collective-permute-done.2), kind=kLoop, calls=%fused_computation.21 | loop fusion | bytes 196608 | tf_op jit(solution)/shard_map/slice | solution.py:400
  69.8 0.8 multiply_convert_fusion
  70.6 6.4 %collective-permute-done.6 = bf16[4,2,96,192]{3,2,1,0:T(8,128)(2,1)S(1)} collective-permute-done((bf16[4,2,96,192]{3,2,1,0:T(8,128)(2,1)S(1)}, bf16[4,2,96,192]{3,2,1,0:T(8,128)(2,1)S(1)}, u32[]{:S(2)}, u32[]{:S(2)}) %collective-permute-start.6) | collective-permute-done | bytes 294944 | tf_op jit(solution)/shard_map/ppermute | solution.py:408
  77.0 3.2 %collective-permute-done.5 = bf16[4,2,96,192]{3,2,1,0:T(8,128)(2,1)S(1)} collective-permute-done((bf16[4,2,96,192]{3,2,1,0:T(8,128)(2,1)S(1)}, bf16[4,2,96,192]{3,2,1,0:T(8,128)(2,1)S(1)}, u32[]{:S(2)}, u32[]{:S(2)}) %collective-permute-start.5) | collective-permute-done | bytes 294944 | tf_op jit(solution)/shard_map/ppermute | solution.py:408
  80.3 0.1 fusion.1
  80.4 4.5 %collective-permute-start.9 = (bf16[2,96,192]{2,1,0:T(8,128)(2,1)S(1)}, bf16[2,96,192]{2,1,0:T(8,128)(2,1)S(1)}, u32[]{:S(2)}, u32[]{:S(2)}) collective-permute-start(bf16[2,96,192]{2,1,0:T(8,128)(2,1)S(1)} %get-tuple-element.42), channel_id=1, source_target_pairs={{0,65},{1,64},{2,67},{3,66},{4,69},{5,68},{6,71},{7,70},{8,73},{9,... | collective-permute-start | bytes 221192 | tf_op jit(solution)/shard_map/ppermute | solution.py:428
  84.9 0.0 collective-permute-start.8
  84.9 0.0 copy-done.5
  84.9 0.8 maximum_select_fusion.2
  85.7 0.2 collective-permute-start.7
  85.9 3.3 %collective-permute-done.9 = bf16[2,96,192]{2,1,0:T(8,128)(2,1)S(1)} collective-permute-done((bf16[2,96,192]{2,1,0:T(8,128)(2,1)S(1)}, bf16[2,96,192]{2,1,0:T(8,128)(2,1)S(1)}, u32[]{:S(2)}, u32[]{:S(2)}) %collective-permute-start.9) | collective-permute-done | bytes 73760 | tf_op jit(solution)/shard_map/ppermute | solution.py:428
  89.2 0.0 collective-permute-done.8
  89.2 1.8 %collective-permute-done.7 = bf16[2,96,192]{2,1,0:T(8,128)(2,1)S(1)} collective-permute-done((bf16[2,96,192]{2,1,0:T(8,128)(2,1)S(1)}, bf16[2,96,192]{2,1,0:T(8,128)(2,1)S(1)}, u32[]{:S(2)}, u32[]{:S(2)}) %collective-permute-start.7) | collective-permute-done | bytes 73760 | tf_op jit(solution)/shard_map/ppermute | solution.py:408
  91.0 0.8 maximum_select_fusion.1
  91.8 0.0 all-to-all-done.1
  91.8 1.2 %copy-done.2 = bf16[16,4,96,128]{3,2,1,0:T(8,128)(2,1)} copy-done((bf16[16,4,96,128]{3,2,1,0:T(8,128)(2,1)}, bf16[16,4,96,128]{3,2,1,0:T(8,128)(2,1)S(1)}, u32[]{:S(2)}) %copy-start.2) | copy-done | bytes 1572888
  93.0 2.3 %total_key_value.1 = (bf16[4,96,128]{2,1,0:T(8,128)(2,1)}, bf16[4,96,128]{2,1,0:T(8,128)(2,1)}) custom-call(bf16[8,2,4,96,128]{4,3,2,1,0:T(8,128)(2,1)} %bitcast.22), custom_call_target="tpu_custom_call" | custom-call | tf_op jit(solution)/shard_map/total_key_value/pallas_call | solution.py:282
  (12 shorter events, 0.1 us)
Async XLA Ops:
  3.2 7.3 %copy-start.3 = (bf16[4,96,1536]{2,1,0:T(8,128)(2,1)S(1)}, bf16[4,96,1536]{2,1,0:T(8,128)(2,1)}, u32[]{:S(2)}) copy-start(bf16[4,96,1536]{2,1,0:T(8,128)(2,1)} %param.12) | copy-start | bytes 3538948
  3.2 30.9 %all-to-all-start = ((bf16[16,432,128]{2,1,0:T(8,128)(2,1)}), bf16[16,432,128]{2,1,0:T(8,128)(2,1)S(1)}, u32[]{:S(2)}, u32[]{:S(2)}) async-start(bf16[16,432,128]{2,1,0:T(8,128)(2,1)} %prepare_exchange.1), calls=%async_computation | async-start | bytes 3538944 | tf_op jit(solution)/shard_map/all_to_all | solution.py:382
  11.4 26.7 %collective-permute-start.1 = (bf16[2,96,1536]{2,1,0:T(8,128)(2,1)}, bf16[2,96,1536]{2,1,0:T(8,128)(2,1)S(1)}, u32[]{:S(2)}, u32[]{:S(2)}) collective-permute-start(bf16[2,96,1536]{2,1,0:T(8,128)(2,1)} %get-tuple-element.40), channel_id=1, source_target_pairs={{0,1},{1,0},{2,3},{3,2},{4,5},{5,4},{6,7},{7,6},{8,9},{9,8},{10,11... | collective-permute-start | bytes 1769480 | tf_op jit(solution)/shard_map/ppermute | solution.py:375
  34.1 1.2 %copy-start.1 = (bf16[16,432,128]{2,1,0:T(8,128)(2,1)}, bf16[16,432,128]{2,1,0:T(8,128)(2,1)S(1)}, u32[]{:S(2)}) copy-start(bf16[16,432,128]{2,1,0:T(8,128)(2,1)S(1)} %all-to-all-done.packed_ref.kv_ref.mask_ref) | copy-start | bytes 5308420
  37.4 1.9 %collective-permute-start = (bf16[4,96,128]{2,1,0:T(8,128)(2,1)}, bf16[4,96,128]{2,1,0:T(8,128)(2,1)S(1)}, u32[]{:S(2)}, u32[]{:S(2)}) collective-permute-start(bf16[4,96,128]{2,1,0:T(8,128)(2,1)} %get-tuple-element.20), channel_id=1, source_target_pairs={{0,1},{1,0},{2,3},{3,2},{4,5},{5,4},{6,7},{7,6},{8,9},{9,8},{10,11... | collective-permute-start | bytes 294920 | tf_op jit(solution)/shard_map/ppermute | solution.py:375
  38.1 1.2 %copy-start = (bf16[4,96,128]{2,1,0:T(8,128)(2,1)S(1)}, bf16[4,96,128]{2,1,0:T(8,128)(2,1)}, u32[]{:S(2)}) copy-start(bf16[4,96,128]{2,1,0:T(8,128)(2,1)} %get-tuple-element.19.qd_mine_ref) | copy-start | bytes 294916
  51.8 16.9 %collective-permute-start.2 = (bf16[4,96,128]{2,1,0:T(8,128)(2,1)S(1)}, bf16[4,96,128]{2,1,0:T(8,128)(2,1)}, u32[]{:S(2)}, u32[]{:S(2)}) collective-permute-start(bf16[4,96,128]{2,1,0:T(8,128)(2,1)S(1)} %get-tuple-element.22), channel_id=1, source_target_pairs={{0,1},{1,0},{2,3},{3,2},{4,5},{5,4},{6,7},{7,6},{8,9},{9,8},{10,11... | collective-permute-start | bytes 294920 | tf_op jit(solution)/shard_map/ppermute | solution.py:375
  52.1 7.8 %collective-permute-start.3 = (bf16[2,2,96,192]{3,2,1,0:T(8,128)(2,1)S(1)}, bf16[2,2,96,192]{3,2,1,0:T(8,128)(2,1)}, u32[]{:S(2)}, u32[]{:S(2)}) collective-permute-start(bf16[2,2,96,192]{3,2,1,0:T(8,128)(2,1)S(1)} %get-tuple-element.23), channel_id=1, source_target_pairs={{0,16},{16,32},{32,48},{48,0},{64,80},{80,96},{96,112},{112,64},{1... | collective-permute-start | bytes 442376 | tf_op jit(solution)/shard_map/ppermute | solution.py:408
  53.4 6.5 %collective-permute-start.4 = (bf16[2,2,96,192]{3,2,1,0:T(8,128)(2,1)S(1)}, bf16[2,2,96,192]{3,2,1,0:T(8,128)(2,1)}, u32[]{:S(2)}, u32[]{:S(2)}) collective-permute-start(bf16[2,2,96,192]{3,2,1,0:T(8,128)(2,1)S(1)} %get-tuple-element.24), channel_id=1, source_target_pairs={{0,48},{16,0},{32,16},{48,32},{64,112},{80,64},{96,80},{112,96},{1... | collective-permute-start | bytes 442376 | tf_op jit(solution)/shard_map/ppermute | solution.py:408
  59.9 31.9 %all-to-all-start.1 = ((bf16[16,4,96,128]{3,2,1,0:T(8,128)(2,1)}), bf16[16,4,96,128]{3,2,1,0:T(8,128)(2,1)S(1)}, u32[]{:S(2)}, u32[]{:S(2)}) async-start(bf16[16,4,96,128]{3,2,1,0:T(8,128)(2,1)} %get-tuple-element.26), calls=%async_computation.1 | async-start | bytes 3145728 | tf_op jit(solution)/shard_map/all_to_all | solution.py:416
  64.5 1.2 %copy-start.4 = (bf16[2,2,96,192]{3,2,1,0:T(8,128)(2,1)S(1)}, bf16[2,2,96,192]{3,2,1,0:T(8,128)(2,1)}, u32[]{:S(2)}) copy-start(bf16[2,2,96,192]{3,2,1,0:T(8,128)(2,1)} %get-tuple-element.38) | copy-start | bytes 442372
  65.7 4.1 %copy-start.6 = (bf16[4,96,64]{2,1,0:T(8,128)(2,1)S(1)}, bf16[4,96,64]{2,1,0:T(8,128)(2,1)}, u32[]{:S(2)}) copy-start(bf16[4,96,64]{2,1,0:T(8,128)(2,1)} %get-tuple-element.44) | copy-start | bytes 147460
  65.7 4.1 %copy-start.7 = (f32[4,96,128]{2,1,0:T(8,128)S(1)}, f32[4,96,128]{2,1,0:T(8,128)}, u32[]{:S(2)}) copy-start(f32[4,96,128]{2,1,0:T(8,128)} %get-tuple-element.29) | copy-start | bytes 589828
  65.8 11.2 %collective-permute-start.6 = (bf16[4,2,96,192]{3,2,1,0:T(8,128)(2,1)S(1)}, bf16[4,2,96,192]{3,2,1,0:T(8,128)(2,1)S(1)}, u32[]{:S(2)}, u32[]{:S(2)}) collective-permute-start(bf16[4,2,96,192]{3,2,1,0:T(8,128)(2,1)S(1)} %pad_maximum_fusion.1), channel_id=1, source_target_pairs={{0,48},{16,0},{32,16},{48,32},{64,112},{80,64},{96,80},{112,96},{1... | collective-permute-start | bytes 884744 | tf_op jit(solution)/shard_map/ppermute | solution.py:408
  68.6 11.6 %collective-permute-start.5 = (bf16[4,2,96,192]{3,2,1,0:T(8,128)(2,1)S(1)}, bf16[4,2,96,192]{3,2,1,0:T(8,128)(2,1)S(1)}, u32[]{:S(2)}, u32[]{:S(2)}) collective-permute-start(bf16[4,2,96,192]{3,2,1,0:T(8,128)(2,1)S(1)} %pad_maximum_fusion), channel_id=1, source_target_pairs={{0,16},{16,32},{32,48},{48,0},{64,80},{80,96},{96,112},{112,64},{1... | collective-permute-start | bytes 884744 | tf_op jit(solution)/shard_map/ppermute | solution.py:408
  70.6 14.3 %copy-start.5 = (bf16[4,96,64]{2,1,0:T(8,128)(2,1)S(1)}, bf16[4,96,64]{2,1,0:T(8,128)(2,1)}, u32[]{:S(2)}) copy-start(bf16[4,96,64]{2,1,0:T(8,128)(2,1)} %get-tuple-element.45) | copy-start | bytes 147460
  80.4 8.7 %collective-permute-start.9 = (bf16[2,96,192]{2,1,0:T(8,128)(2,1)S(1)}, bf16[2,96,192]{2,1,0:T(8,128)(2,1)S(1)}, u32[]{:S(2)}, u32[]{:S(2)}) collective-permute-start(bf16[2,96,192]{2,1,0:T(8,128)(2,1)S(1)} %get-tuple-element.42), channel_id=1, source_target_pairs={{0,65},{1,64},{2,67},{3,66},{4,69},{5,68},{6,71},{7,70},{8,73},{9,... | collective-permute-start | bytes 221192 | tf_op jit(solution)/shard_map/ppermute | solution.py:428
  84.9 4.3 %collective-permute-start.8 = (bf16[2,96,192]{2,1,0:T(8,128)(2,1)S(1)}, bf16[2,96,192]{2,1,0:T(8,128)(2,1)S(1)}, u32[]{:S(2)}, u32[]{:S(2)}) collective-permute-start(bf16[2,96,192]{2,1,0:T(8,128)(2,1)S(1)} %get-tuple-element.43), channel_id=1, source_target_pairs={{0,1},{1,0},{2,3},{3,2},{4,5},{5,4},{6,7},{7,6},{8,9},{9,8},{10,11... | collective-permute-start | bytes 221192 | tf_op jit(solution)/shard_map/ppermute | solution.py:375
  85.7 5.4 %collective-permute-start.7 = (bf16[2,96,192]{2,1,0:T(8,128)(2,1)S(1)}, bf16[2,96,192]{2,1,0:T(8,128)(2,1)S(1)}, u32[]{:S(2)}, u32[]{:S(2)}) collective-permute-start(bf16[2,96,192]{2,1,0:T(8,128)(2,1)S(1)} %get-tuple-element.41), channel_id=1, source_target_pairs={{0,64},{16,80},{32,96},{48,112},{64,0},{80,16},{96,32},{112,48},{1... | collective-permute-start | bytes 221192 | tf_op jit(solution)/shard_map/ppermute | solution.py:408
  91.8 1.2 %copy-start.2 = (bf16[16,4,96,128]{3,2,1,0:T(8,128)(2,1)}, bf16[16,4,96,128]{3,2,1,0:T(8,128)(2,1)S(1)}, u32[]{:S(2)}) copy-start(bf16[16,4,96,128]{3,2,1,0:T(8,128)(2,1)S(1)} %all-to-all-done.1) | copy-start | bytes 4718596

commit v8 on v7

--- a/solution.py
+++ b/solution.py
@@ -19,10 +19,12 @@
 
 def attention_kernel(
     place_ref,
-    qd_mine_ref,
-    qd_other_ref,
+    qg_mine_ref,
+    qg_other_ref,
     kv_ref,
     mask_ref,
+    cotangent_ref,
+    weight_ref,
     bias_ref,
     qa_own_ref,
     qa_away_ref,
@@ -30,6 +32,7 @@
     right_out_ref,
     left_out_ref,
     rest_out_ref,
+    gated_ref,
     cap_ref,
     s_ref,
     b2_ref,
@@ -44,7 +47,7 @@
     rows = bias_ref.shape[0]
     queries = rows // 2
     keys = bias_ref.shape[1]
-    head_width = qd_mine_ref.shape[2] // 4
+    head_width = qg_mine_ref.shape[2] // 4
     core = place_ref[PIECES]
     scaling = 1.0 / math.sqrt(head_width)
 
@@ -57,6 +60,14 @@
             return carry
 
         lax.fori_loop(0, rows // CHUNK, fill, 0)
+        sources, _, lanes = cotangent_ref.shape
+        cotangent = cotangent_ref[...].astype(jnp.float32)
+        cotangent = cotangent.reshape(sources, 2, cap_ref.shape[0], lanes // sources, lanes)
+        for column in range(cotangent.shape[2]):
+            for side in range(2):
+                part = cotangent[:, side, column].reshape(lanes, lanes).astype(jnp.bfloat16)
+                gated = jnp.dot(weight_ref[...], part, preferred_element_type=jnp.float32)
+                gated_ref[column, side * queries // 2 : (side + 1) * queries // 2] = gated.T[: queries // 2]
         masks = mask_ref[...].astype(jnp.float32)
         for column in range(cap_ref.shape[0]):
             pieces = [
@@ -68,12 +79,16 @@
 
     half = queries // 2
     kv = kv_ref[...].reshape(keys, 4 * head_width)
-    qd_mine = qd_mine_ref[0]
-    qd_other = qd_other_ref[0]
-    qd = jnp.concatenate(
-        [jnp.where(core == 0, qd_mine, qd_other), jnp.where(core == 0, qd_other, qd_mine)], axis=0
-    )
+    qg_mine = qg_mine_ref[0]
+    qg_other = qg_other_ref[0]
+    query_gate = jnp.concatenate(
+        [jnp.where(core == 0, qg_mine, qg_other), jnp.where(core == 0, qg_other, qg_mine)], axis=0
+    )
+    sigma = jax.nn.sigmoid(query_gate.astype(jnp.float32))
+    gated_grad = gated_ref[step] * sigma
+    gate_slope = gated_grad * (1.0 - sigma)
     lane = lax.broadcasted_iota(jnp.int32, (queries, 4 * head_width), 1)
+    qd = jnp.where(lane < 2 * head_width, query_gate, gated_grad.astype(jnp.bfloat16))
     zero = jnp.zeros_like(qd)
 
     def only(part):
@@ -143,7 +158,7 @@
     merged = jnp.where(
         lane < 2 * head_width,
         jnp.where(lane < head_width, q0, q1),
-        jnp.where(lane < 3 * head_width, att0, att1),
+        jnp.where(lane < 3 * head_width, att0, att1) * gate_slope,
     )
     qa_own_ref[0] = jnp.where(core == 0, merged[:half], merged[half:]).astype(jnp.bfloat16)
     qa_away_ref[0] = jnp.where(core == 0, merged[half:], merged[:half]).astype(jnp.bfloat16)
@@ -191,15 +206,17 @@
     cotangent = cotangent_ref[...].astype(jnp.float32).reshape(rows, cotangent_ref.shape[2])
     filler = jnp.zeros((rows, channels - tokens), jnp.float32)
     for device in range(devices):
+        packed_ref[device, pairs + 2 * rows :, :] = mask
         part = cotangent[:, device * tokens : (device + 1) * tokens]
         part = jnp.concatenate([part, filler], axis=1).astype(jnp.bfloat16)
-        packed_ref[device, pairs : pairs + rows, :] = part
-        packed_ref[device, pairs + rows :, :] = mask
+        start = pairs + device % 2 * rows
+        packed_ref[device, start : start + rows, :] = part
+        packed_ref[device ^ 1, start : start + rows, :] = part
 
 
 def prepare(key, value, mask, cotangent, devices):
     columns, tokens, channels = key.shape
-    rows = columns * tokens + cotangent.shape[0] * cotangent.shape[1] + MASK_ROWS
+    rows = columns * tokens + 2 * cotangent.shape[0] * cotangent.shape[1] + MASK_ROWS
 
     def whole(shape):
         return pl.BlockSpec(shape, lambda i: (0,) * len(shape))
@@ -216,78 +233,14 @@
     )(key, value, mask, cotangent)
 
 
-def project_kernel(core_ref, packed_ref, weight_ref, gate_ref, query_ref, mine_ref, other_ref, slope_ref):
-    pieces, rows, lanes = packed_ref.shape
-    columns, tokens, channels = gate_ref.shape
-    half = channels // 2
-    core = core_ref[0]
-    whole = packed_ref[...].astype(jnp.float32).reshape(pieces, columns, rows // columns, lanes)
-    for column in range(columns):
-        part = whole[:, column].reshape(channels, lanes).astype(jnp.bfloat16)
-        gated = jnp.dot(weight_ref[...], part, preferred_element_type=jnp.float32).T[:tokens]
-        sigma = jax.nn.sigmoid(gate_ref[column].astype(jnp.float32))
-        grad = gated * sigma
-        slope_ref[column] = grad * (1.0 - sigma)
-        grad = grad.astype(jnp.bfloat16)
-        query = query_ref[column]
-        low = jnp.concatenate([query[:, :half], grad[:, :half]], axis=1)
-        high = jnp.concatenate([query[:, half:], grad[:, half:]], axis=1)
-        mine_ref[column] = jnp.where(core == 0, low, high)
-        other_ref[column] = jnp.where(core == 0, high, low)
-
-
-def project(core, packed, weight, gate, query):
-    columns, tokens, channels = gate.shape
-    rows = weight.shape[0] // packed.shape[0] * columns
-
-    def whole(array):
-        return pl.BlockSpec(array.shape, lambda i: (0,) * array.ndim)
-
-    return pl.pallas_call(
-        project_kernel,
-        grid=(1,),
-        in_specs=[
-            pl.BlockSpec(memory_space=pltpu.SMEM),
-            pl.BlockSpec((packed.shape[0], rows, channels), lambda i: (0, columns * tokens // rows, 0)),
-            whole(weight),
-            whole(gate),
-            whole(query),
-        ],
-        out_specs=[whole(gate)] * 3,
-        out_shape=[
-            jax.ShapeDtypeStruct(gate.shape, jnp.bfloat16),
-            jax.ShapeDtypeStruct(gate.shape, jnp.bfloat16),
-            jax.ShapeDtypeStruct(gate.shape, jnp.float32),
-        ],
-        compiler_params=pltpu.CompilerParams(vmem_limit_bytes=VMEM_WIDE),
-        name="project_cotangent",
-    )(core, packed, weight, gate, query)
-
-
-def total_kernel(parts_ref, key_ref, value_ref):
-    half = key_ref.shape[2] // 2
-    scaling = 1.0 / math.sqrt(key_ref.shape[2] // HEADS)
-    for column in range(key_ref.shape[0]):
-        sums = [
-            jnp.sum(parts_ref[:, side, column].astype(jnp.float32), axis=0) for side in range(2)
-        ]
-        key = jnp.concatenate([part[:, :half] for part in sums], axis=1) * scaling
-        key_ref[column] = key.astype(jnp.bfloat16)
-        value = jnp.concatenate([part[:, half:] for part in sums], axis=1)
-        value_ref[column] = value.astype(jnp.bfloat16)
-
-
-def total(parts, like):
-    out = jax.ShapeDtypeStruct(like.shape, jnp.bfloat16)
-    return pl.pallas_call(total_kernel, out_shape=[out, out], compiler_params=pltpu.CompilerParams(vmem_limit_bytes=VMEM_WIDE), name="total_key_value")(parts)
-
-
-def attend(places, mine, other, received, bias, row_count):
+def attend(places, mine, other, received, weight, bias, row_count):
     columns, tokens, lanes = mine.shape
     rows, keys = bias.shape
     width = keys // row_count
     devices = received.shape[0]
     mask_place = received.shape[1] // MASK_ROWS - 1
+    cotangent_rows = 2 * columns * lanes // devices
+    cotangent_place = columns * tokens // cotangent_rows
     work = columns * rows * keys
 
     def whole(shape):
@@ -304,6 +257,10 @@
             + [
                 pl.BlockSpec((devices, tokens, lanes), lambda j, places: (0, j, 0)),
                 pl.BlockSpec((devices, MASK_ROWS, lanes), lambda j, places: (0, mask_place, 0)),
+                pl.BlockSpec(
+                    (devices, cotangent_rows, lanes), lambda j, places: (0, cotangent_place, 0)
+                ),
+                whole(weight.shape),
                 whole(bias.shape),
             ],
             out_specs=[
@@ -315,6 +272,7 @@
                 whole((12,) + piece),
             ],
             scratch_shapes=[
+                pltpu.VMEM((columns, rows // 2, lanes), jnp.float32),
                 pltpu.VMEM((columns, 1, keys), jnp.float32),
                 pltpu.VMEM((rows, keys), jnp.float32),
                 pltpu.VMEM((rows, keys), jnp.float32),
@@ -336,7 +294,7 @@
         compiler_params=pltpu.CompilerParams(vmem_limit_bytes=48 * 1024 * 1024),
         cost_estimate=pl.CostEstimate(flops=12 * 128 * work, bytes_accessed=16 * 2**20, transcendentals=work),
         name="attention_both",
-    )(places, mine, other, received, received, bias)
+    )(places, mine, other, received, received, received, weight, bias)
 
 
 def local(
@@ -377,7 +335,6 @@
     bias_mine, bias_other = mine_other(pair_bias, 0)
     bias_pair = in_order(bias_mine, swapped(bias_other), 1).reshape(-1, keys)
 
-    core_word = core.astype(jnp.int32).reshape(1)
     packed = prepare(key_vectors, value_vectors, pair_mask, output_cotangent, devices)
     received = lax.all_to_all(packed, "col", 0, 0, tiled=True)
     place = lax.axis_index("row")
@@ -389,16 +346,20 @@
     places.append(core)
     places = jnp.stack(places).astype(jnp.int32)
 
-    qd_mine, qd_away, gate_slope = project(core_word, received, output_weight, gate_logits, query_vectors)
+    query_mine, query_other = mine_other(query_vectors, 2)
+    gate_mine, gate_other = mine_other(gate_logits, 2)
+    qg_mine = jnp.concatenate([query_mine, gate_mine], axis=2)
+    qg_other = swapped(jnp.concatenate([query_other, gate_other], axis=2))
+    weight_mine, _ = mine_other(output_weight, 0)
+    weight_mine = jnp.pad(weight_mine, ((half, 0), (0, 0)))
 
     qa_own, qa_away, kv_grads, bias_right, bias_left, bias_rest = attend(
-        places, qd_mine, swapped(qd_away), received, bias_pair, row_count
+        places, qg_mine, qg_other, received, weight_mine, bias_pair, row_count
     )
 
     qa_back = swapped(qa_away)
     query_gradient = in_order(qa_own[..., :half], qa_back[..., :half], 2)
-    attended = in_order(qa_own[..., half:], qa_back[..., half:], 2).astype(jnp.float32)
-    gate_gradient = (gate_slope * attended).astype(jnp.bfloat16)
+    gate_gradient = in_order(qa_own[..., half:], qa_back[..., half:], 2)
 
     def along_row(array, turn, side):
         pairs = []
@@ -415,7 +376,11 @@
     from_left, from_right, kv_grads = lax.optimization_barrier((from_left, from_right, kv_grads))
     kv_parts = lax.all_to_all(kv_grads, "col", 0, 0, tiled=True)
     kv_parts = kv_parts.reshape((devices // 2, 2) + kv_parts.shape[1:])
-    key_gradient, value_gradient = total(kv_parts, key_vectors)
+    kv_sum = jnp.sum(kv_parts.astype(jnp.float32), axis=0)
+    key_gradient = jnp.concatenate([kv_sum[0, ..., :half], kv_sum[1, ..., :half]], axis=2) * scaling
+    key_gradient = key_gradient.astype(jnp.bfloat16)
+    value_gradient = jnp.concatenate([kv_sum[0, ..., half:], kv_sum[1, ..., half:]], axis=2)
+    value_gradient = value_gradient.astype(jnp.bfloat16)
     onward = jnp.concatenate([added(bias_rest[4:6], from_left).astype(jnp.bfloat16), bias_rest[6:8]])
     backward = jnp.concatenate([bias_rest[8:10], added(bias_rest[10:], from_right).astype(jnp.bfloat16)])
     sums = added(bias_rest[:4], along_row(onward, 1, 0), along_row(backward, -1, 0))
@@ -424,8 +389,15 @@
     for index in range(row_count * devices):
         up = (index // devices + row_ring) % row_count
         diagonal.append((index, up * devices + (index % devices ^ 1)))
-    bias_own = added(sums[0], along_row(low_sums[2], 0, 1))
-    bias_away = added(swapped(low_sums[1]), lax.ppermute(low_sums[3], ("row", "col"), diagonal))
+    from_high, from_core, from_diagonal, key_gradient, value_gradient = lax.optimization_barrier((
+        along_row(low_sums[2], 0, 1),
+        swapped(low_sums[1]),
+        lax.ppermute(low_sums[3], ("row", "col"), diagonal),
+        key_gradient,
+        value_gradient,
+    ))
+    bias_own = added(sums[0], from_high)
+    bias_away = added(from_core, from_diagonal)
     bias_gradient = in_order(bias_own, bias_away, 0)
     return (query_gradient, key_gradient, value_gradient, gate_gradient, bias_gradient)
 

time: 95.8 us -> 90.3 us (0.943)
  local copies, waits for them, and re-layouts: 5.07 us -> 1.03 us
  Pallas kernels: 19.5 us -> 15.5 us
  other arithmetic: 5.09 us -> 6.51 us
  waiting for transfers between devices: 41.6 us -> 42.6 us
    pallas_call x2 -> x0, Pallas kernels: 4.43 us -> none  [the longest x1 2.32 us: total(): pl.pallas_call(total_kernel, out_shape=[out, out], compiler_params=pltpu....]
    ppermute x1, waiting for transfers between devices: 3.28 us -> 1.29 us  [local(): lax.ppermute(low_sums[3], ('row', 'col'), diagonal)]
    ppermute x5, waiting for transfers between devices: 15.1 us -> 17.1 us  [along_row(): return lax.ppermute(array, 'row', pairs)]
    unnamed x16 -> x8, local copies, waits for them, and re-layouts: 2.45 us -> 0.55 us
    slice x2, local copies, waits for them, and re-layouts: 1.81 us -> 0.2 us  [local(): gate_gradient = in_order(qa_own[..., half:], qa_back[..., half:], 2)]
    all_to_all x1, waiting for transfers between devices: 0.01 us -> 1.09 us  [local(): kv_parts = lax.all_to_all(kv_grads, 'col', 0, 0, tiled=True)]
    convert_element_type x1, other arithmetic: 1.16 us -> 0.1 us  [local(): added(bias_rest[4:6], from_left).astype(jnp.bfloat16)]
  transfers between devices with their start and end apart: 12 -> 12, of which waited for: 7 -> 8; matrix products, arithmetic and copies ran while one was open for 8% -> 6% of each run, Pallas kernels for 2% -> 0%
where the time goes in v8:
time: 90.3 us; the launch traced here: 90 us
  waiting for transfers between devices  42.6 us (47%)
  starting transfers between devices  23.6 us (26%)
  Pallas kernels  15.5 us (17%)
  other arithmetic  6.51 us (7%)
  local copies, waits for them, and re-layouts  1.03 us (1%)
    all_to_all x1, waiting for transfers between devices, local(): received = lax.all_to_all(packed, 'col', 0, 0, tiled=True)  22.6 us
    ppermute x5, waiting for transfers between devices, along_row(): return lax.ppermute(array, 'row', pairs)  17.1 us
    pallas_call x1, Pallas kernels, attend(): pl.pallas_call(attention_kernel, grid_spec=pltpu.PrefetchScalarGridSpec(n...  12.9 us
    all_to_all x1, starting transfers between devices, local(): received = lax.all_to_all(packed, 'col', 0, 0, tiled=True)  7.3 us
    ppermute x5, starting transfers between devices, along_row(): return lax.ppermute(array, 'row', pairs)  5.76 us
    all_to_all x1, starting transfers between devices, local(): kv_parts = lax.all_to_all(kv_grads, 'col', 0, 0, tiled=True)  4.95 us
    ppermute x1, starting transfers between devices, local(): lax.ppermute(low_sums[3], ('row', 'col'), diagonal)  4.46 us
    pallas_call x1, Pallas kernels, prepare(): pl.pallas_call(prepare_kernel, grid=(1,), in_specs=[whole(key.shape), who...  2.54 us
  transfers between devices with their start and end apart: 12, of which 8 were waited for; matrix products, arithmetic and copies ran while one was open for 6% of the time, Pallas kernels for 0%

profile of v8, /device:TPU:1, one launch (start us, length us, event | category | flops | bytes accessed | tf_op | source)
XLA Modules:
  0.0 90.0 jit_solution(3277853492723505539)
XLA Ops:
  0.6 2.5 %prepare_exchange.1 = bf16[16,464,128]{2,1,0:T(8,128)(2,1)} custom-call(bf16[4,96,128]{2,1,0:T(8,128)(2,1)} %key_ref.1, bf16[4,96,128]{2,1,0:T(8,128)(2,1)} %value_ref.1, s32[4,96]{1,0:T(4,128)} %mask_ref.1, bf16[4,8,1536]{2,1,0:T(8,128)(2,1)} %cotangent_ref.1), custom_call_target="tpu_custom_call" | custom-call | tf_op jit(solution)/shard_map/prepare_exchange/pallas_call | solution.py:225
  3.2 7.3 %all-to-all-start = ((bf16[16,464,128]{2,1,0:T(8,128)(2,1)}), bf16[16,464,128]{2,1,0:T(8,128)(2,1)}, u32[]{:S(2)}, u32[]{:S(2)}) async-start(bf16[16,464,128]{2,1,0:T(8,128)(2,1)} %prepare_exchange.1), calls=%async_computation | async-start | bytes 3801088 | tf_op jit(solution)/shard_map/all_to_all | solution.py:339
  10.5 0.0 copy-start.1
  10.5 0.0 copy-start.2
  10.5 0.1 broadcast_select_fusion.1
  10.6 0.0 copy-start.3
  10.6 0.2 collective-permute-start.1
  10.9 0.5 copy-done.1
  11.4 0.1 broadcast_select_fusion.3
  11.5 0.1 broadcast_select_fusion.2
  11.6 0.1 pad_maximum_fusion.3
  11.7 0.2 collective-permute-start
  12.0 0.1 stack.39.place_ref
  12.1 0.1 pad_maximum_fusion.2.qg_mine_ref
  12.2 0.5 collective-permute-done.1
  12.7 0.4 maximum_select_fusion
  13.1 0.0 collective-permute-done.qg_other_ref
  13.1 22.6 %all-to-all-done.kv_ref.mask_ref.cotangent_ref = bf16[16,464,128]{2,1,0:T(8,128)(2,1)} async-done(((bf16[16,464,128]{2,1,0:T(8,128)(2,1)}), bf16[16,464,128]{2,1,0:T(8,128)(2,1)}, u32[]{:S(2)}, u32[]{:S(2)}) %all-to-all-start) | async-done | bytes 1900576 | tf_op jit(solution)/shard_map/all_to_all | solution.py:339
  35.7 12.9 %attention_both.1 = (bf16[4,96,128]{2,1,0:T(8,128)(2,1)S(1)}, bf16[4,96,128]{2,1,0:T(8,128)(2,1)S(1)}, bf16[16,4,96,128]{3,2,1,0:T(8,128)(2,1)}, bf16[2,2,96,192...) custom-call(s32[9]{0:T(128)S(1)} %stack.39.place_ref, ...), custom_call_target="tpu_custom_call" | custom-call | flops 3623878656 | bytes 16777216 | tf_op jit(solution)/shard_map/attention_both/pallas_call | solution.py:251
  48.6 0.6 collective-permute-start.2
  49.2 1.3 %collective-permute-start.3 = (bf16[2,2,96,192]{3,2,1,0:T(8,128)(2,1)S(1)}, bf16[2,2,96,192]{3,2,1,0:T(8,128)(2,1)S(1)}, u32[]{:S(2)}, u32[]{:S(2)}) collective-permute-start(bf16[2,2,96,192]{3,2,1,0:T(8,128)(2,1)S(1)} %get-tuple-element.22), channel_id=1, source_target_pairs={{0,16},{16,32},{32,48},{48,0},{64,80},{80,96},{96,112},{112,64},{1... | collective-permute-start | bytes 442376 | tf_op jit(solution)/shard_map/ppermute | solution.py:369
  50.5 1.4 %collective-permute-start.4 = (bf16[2,2,96,192]{3,2,1,0:T(8,128)(2,1)S(1)}, bf16[2,2,96,192]{3,2,1,0:T(8,128)(2,1)S(1)}, u32[]{:S(2)}, u32[]{:S(2)}) collective-permute-start(bf16[2,2,96,192]{3,2,1,0:T(8,128)(2,1)S(1)} %get-tuple-element.23), channel_id=1, source_target_pairs={{0,48},{16,0},{32,16},{48,32},{64,112},{80,64},{96,80},{112,96},{1... | collective-permute-start | bytes 442376 | tf_op jit(solution)/shard_map/ppermute | solution.py:369
  52.0 0.1 fusion.4
  52.1 5.0 %collective-permute-done.3 = bf16[2,2,96,192]{3,2,1,0:T(8,128)(2,1)S(1)} collective-permute-done((bf16[2,2,96,192]{3,2,1,0:T(8,128)(2,1)S(1)}, bf16[2,2,96,192]{3,2,1,0:T(8,128)(2,1)S(1)}, u32[]{:S(2)}, u32[]{:S(2)}) %collective-permute-start.3) | collective-permute-done | bytes 147488 | tf_op jit(solution)/shard_map/ppermute | solution.py:369
  57.1 0.0 collective-permute-done.4
  57.1 5.0 %all-to-all-start.1 = ((bf16[16,4,96,128]{3,2,1,0:T(8,128)(2,1)}), bf16[16,4,96,128]{3,2,1,0:T(8,128)(2,1)S(1)}, u32[]{:S(2)}, u32[]{:S(2)}) async-start(bf16[16,4,96,128]{3,2,1,0:T(8,128)(2,1)} %get-tuple-element.27), calls=%async_computation.1 | async-start | bytes 3145728 | tf_op jit(solution)/shard_map/all_to_all | solution.py:377
  62.1 0.1 add_convert_fusion.1
  62.2 0.1 pad_maximum_fusion.1
  62.3 2.7 %collective-permute-start.6 = (bf16[4,2,96,192]{3,2,1,0:T(8,128)(2,1)S(1)}, bf16[4,2,96,192]{3,2,1,0:T(8,128)(2,1)S(1)}, u32[]{:S(2)}, u32[]{:S(2)}) collective-permute-start(bf16[4,2,96,192]{3,2,1,0:T(8,128)(2,1)S(1)} %pad_maximum_fusion.1), channel_id=1, source_target_pairs={{0,48},{16,0},{32,16},{48,32},{64,112},{80,64},{96,80},{112,96},{1... | collective-permute-start | bytes 884744 | tf_op jit(solution)/shard_map/ppermute | solution.py:369
  65.0 0.1 pad_maximum_fusion
  65.1 0.1 collective-permute-start.5
  65.2 0.0 collective-permute-done.2
  65.2 0.1 fusion.5
  65.3 0.9 maximum_select_fusion.2
  66.2 7.3 %collective-permute-done.6 = bf16[4,2,96,192]{3,2,1,0:T(8,128)(2,1)S(1)} collective-permute-done((bf16[4,2,96,192]{3,2,1,0:T(8,128)(2,1)S(1)}, bf16[4,2,96,192]{3,2,1,0:T(8,128)(2,1)S(1)}, u32[]{:S(2)}, u32[]{:S(2)}) %collective-permute-start.6) | collective-permute-done | bytes 294944 | tf_op jit(solution)/shard_map/ppermute | solution.py:369
  73.5 3.2 %collective-permute-done.5 = bf16[4,2,96,192]{3,2,1,0:T(8,128)(2,1)S(1)} collective-permute-done((bf16[4,2,96,192]{3,2,1,0:T(8,128)(2,1)S(1)}, bf16[4,2,96,192]{3,2,1,0:T(8,128)(2,1)S(1)}, u32[]{:S(2)}, u32[]{:S(2)}) %collective-permute-start.5) | collective-permute-done | bytes 294944 | tf_op jit(solution)/shard_map/ppermute | solution.py:369
  76.7 1.0 %fusion.2 = (bf16[4,2,96,192]{3,2,1,0:T(8,128)(2,1)S(1)}, f32[4,2,96,192]{3,2,1,0:T(8,128)}) fusion(bf16[4,2,96,192]{3,2,1,0:T(8,128)(2,1)S(1)} %collective-permute-done.6, bf16[4,2,96,192]{3,2,1,0:T(8,128)(2,1)S(1)} %collective-permute-done.5, bf16[12,2,96,192]{3,2,1,0:T(8,128)(2,1)S(1)} %get-tuple-element.21), kind=kLoop, calls=%fused_computation.32 | loop fusion | flops 884736 | bytes 1769472 | tf_op jit(solution)/shard_map/convert_element_type | solution.py:387
  77.8 4.5 %collective-permute-start.9 = (bf16[2,96,192]{2,1,0:T(8,128)(2,1)S(1)}, bf16[2,96,192]{2,1,0:T(8,128)(2,1)S(1)}, u32[]{:S(2)}, u32[]{:S(2)}) collective-permute-start(bf16[2,96,192]{2,1,0:T(8,128)(2,1)S(1)} %get-tuple-element.43), channel_id=1, source_target_pairs={{0,65},{1,64},{2,67},{3,66},{4,69},{5,68},{6,71},{7,70},{8,73},{9,... | collective-permute-start | bytes 221192 | tf_op jit(solution)/shard_map/ppermute | solution.py:395
  82.2 0.2 collective-permute-start.7
  82.4 1.1 %all-to-all-done.1 = bf16[16,4,96,128]{3,2,1,0:T(8,128)(2,1)S(1)} async-done(((bf16[16,4,96,128]{3,2,1,0:T(8,128)(2,1)}), bf16[16,4,96,128]{3,2,1,0:T(8,128)(2,1)S(1)}, u32[]{:S(2)}, u32[]{:S(2)}) %all-to-all-start.1) | async-done | bytes 1572896 | tf_op jit(solution)/shard_map/all_to_all | solution.py:377
  83.5 0.2 convert_reduce_fusion
  83.8 0.1 slice_bitcast_fusion.4
  83.9 0.8 fusion.1
  84.7 0.7 pad_maximum_fusion.4
  85.4 1.3 %collective-permute-done.9 = bf16[2,96,192]{2,1,0:T(8,128)(2,1)S(1)} collective-permute-done((bf16[2,96,192]{2,1,0:T(8,128)(2,1)S(1)}, bf16[2,96,192]{2,1,0:T(8,128)(2,1)S(1)}, u32[]{:S(2)}, u32[]{:S(2)}) %collective-permute-start.9) | collective-permute-done | bytes 73760 | tf_op jit(solution)/shard_map/ppermute | solution.py:395
  86.7 1.5 %collective-permute-done.7 = bf16[2,96,192]{2,1,0:T(8,128)(2,1)S(1)} collective-permute-done((bf16[2,96,192]{2,1,0:T(8,128)(2,1)S(1)}, bf16[2,96,192]{2,1,0:T(8,128)(2,1)S(1)}, u32[]{:S(2)}, u32[]{:S(2)}) %collective-permute-start.7) | collective-permute-done | bytes 73760 | tf_op jit(solution)/shard_map/ppermute | solution.py:369
  88.2 1.0 %fusion = (f32[2,96,192]{2,1,0:T(8,128)S(1)}, f32[2,96,192]{2,1,0:T(8,128)S(1)}) fusion(f32[4,2,96,192]{3,2,1,0:T(8,128)} %get-tuple-element.34, bf16[2,96,192]{2,1,0:T(8,128)(2,1)S(1)} %collective-permute-done.7, bf16[2,96,192]{2,1,0:T(8,128)(2,1)S(1)} %collective-permute-done.9, bf16[2,96,192]{2,1,0:T(8,128)(2,1)S(1)} %collective-permute-done.8), kind=kLoop, calls=%fused_computation.11 | loop fusion | flops 184320 | bytes 663552 | tf_op jit(solution)/shard_map/add | solution.py:372
  89.2 0.8 maximum_select_fusion.1
  (12 shorter events, 0.1 us)
Async XLA Ops:
  3.2 7.3 %copy-start = (bf16[4,96,1536]{2,1,0:T(8,128)(2,1)S(1)}, bf16[4,96,1536]{2,1,0:T(8,128)(2,1)}, u32[]{:S(2)}) copy-start(bf16[4,96,1536]{2,1,0:T(8,128)(2,1)} %param.12) | copy-start | bytes 3538948
  3.2 32.5 %all-to-all-start = ((bf16[16,464,128]{2,1,0:T(8,128)(2,1)}), bf16[16,464,128]{2,1,0:T(8,128)(2,1)}, u32[]{:S(2)}, u32[]{:S(2)}) async-start(bf16[16,464,128]{2,1,0:T(8,128)(2,1)} %prepare_exchange.1), calls=%async_computation | async-start | bytes 3801088 | tf_op jit(solution)/shard_map/all_to_all | solution.py:339
  10.5 0.9 copy-start.1
  10.5 1.0 %copy-start.2 = (bf16[4,96,128]{2,1,0:T(8,128)(2,1)S(1)}, bf16[4,96,128]{2,1,0:T(8,128)(2,1)}, u32[]{:S(2)}) copy-start(bf16[4,96,128]{2,1,0:T(8,128)(2,1)} %param.11) | copy-start | bytes 294916
  10.6 1.3 %copy-start.3 = (bf16[128,128]{1,0:T(8,128)(2,1)S(1)}, bf16[128,128]{1,0:T(8,128)(2,1)}, u32[]{:S(2)}) copy-start(bf16[128,128]{1,0:T(8,128)(2,1)} %param.14) | copy-start | bytes 98308
  10.6 2.1 %collective-permute-start.1 = (bf16[2,96,1536]{2,1,0:T(8,128)(2,1)S(1)}, bf16[2,96,1536]{2,1,0:T(8,128)(2,1)S(1)}, u32[]{:S(2)}, u32[]{:S(2)}) collective-permute-start(bf16[2,96,1536]{2,1,0:T(8,128)(2,1)S(1)} %get-tuple-element.40), channel_id=1, source_target_pairs={{0,1},{1,0},{2,3},{3,2},{4,5},{5,4},{6,7},{7,6},{8,9},{9,8},{10,11... | collective-permute-start | bytes 1769480 | tf_op jit(solution)/shard_map/ppermute | solution.py:333
  11.7 1.4 %collective-permute-start = (bf16[4,96,128]{2,1,0:T(8,128)(2,1)S(1)}, bf16[4,96,128]{2,1,0:T(8,128)(2,1)S(1)}, u32[]{:S(2)}, u32[]{:S(2)}) collective-permute-start(bf16[4,96,128]{2,1,0:T(8,128)(2,1)S(1)} %pad_maximum_fusion.3), channel_id=1, source_target_pairs={{0,1},{1,0},{2,3},{3,2},{4,5},{5,4},{6,7},{7,6},{8,9},{9,8},{10,11... | collective-permute-start | bytes 294920 | tf_op jit(solution)/shard_map/ppermute | solution.py:333
  48.6 16.6 %collective-permute-start.2 = (bf16[4,96,128]{2,1,0:T(8,128)(2,1)S(1)}, bf16[4,96,128]{2,1,0:T(8,128)(2,1)S(1)}, u32[]{:S(2)}, u32[]{:S(2)}) collective-permute-start(bf16[4,96,128]{2,1,0:T(8,128)(2,1)S(1)} %get-tuple-element.20), channel_id=1, source_target_pairs={{0,1},{1,0},{2,3},{3,2},{4,5},{5,4},{6,7},{7,6},{8,9},{9,8},{10,11... | collective-permute-start | bytes 294920 | tf_op jit(solution)/shard_map/ppermute | solution.py:333
  49.2 7.9 %collective-permute-start.3 = (bf16[2,2,96,192]{3,2,1,0:T(8,128)(2,1)S(1)}, bf16[2,2,96,192]{3,2,1,0:T(8,128)(2,1)S(1)}, u32[]{:S(2)}, u32[]{:S(2)}) collective-permute-start(bf16[2,2,96,192]{3,2,1,0:T(8,128)(2,1)S(1)} %get-tuple-element.22), channel_id=1, source_target_pairs={{0,16},{16,32},{32,48},{48,0},{64,80},{80,96},{96,112},{112,64},{1... | collective-permute-start | bytes 442376 | tf_op jit(solution)/shard_map/ppermute | solution.py:369
  50.5 6.6 %collective-permute-start.4 = (bf16[2,2,96,192]{3,2,1,0:T(8,128)(2,1)S(1)}, bf16[2,2,96,192]{3,2,1,0:T(8,128)(2,1)S(1)}, u32[]{:S(2)}, u32[]{:S(2)}) collective-permute-start(bf16[2,2,96,192]{3,2,1,0:T(8,128)(2,1)S(1)} %get-tuple-element.23), channel_id=1, source_target_pairs={{0,48},{16,0},{32,16},{48,32},{64,112},{80,64},{96,80},{112,96},{1... | collective-permute-start | bytes 442376 | tf_op jit(solution)/shard_map/ppermute | solution.py:369
  57.1 26.4 %all-to-all-start.1 = ((bf16[16,4,96,128]{3,2,1,0:T(8,128)(2,1)}), bf16[16,4,96,128]{3,2,1,0:T(8,128)(2,1)S(1)}, u32[]{:S(2)}, u32[]{:S(2)}) async-start(bf16[16,4,96,128]{3,2,1,0:T(8,128)(2,1)} %get-tuple-element.27), calls=%async_computation.1 | async-start | bytes 3145728 | tf_op jit(solution)/shard_map/all_to_all | solution.py:377
  62.3 11.2 %collective-permute-start.6 = (bf16[4,2,96,192]{3,2,1,0:T(8,128)(2,1)S(1)}, bf16[4,2,96,192]{3,2,1,0:T(8,128)(2,1)S(1)}, u32[]{:S(2)}, u32[]{:S(2)}) collective-permute-start(bf16[4,2,96,192]{3,2,1,0:T(8,128)(2,1)S(1)} %pad_maximum_fusion.1), channel_id=1, source_target_pairs={{0,48},{16,0},{32,16},{48,32},{64,112},{80,64},{96,80},{112,96},{1... | collective-permute-start | bytes 884744 | tf_op jit(solution)/shard_map/ppermute | solution.py:369
  65.1 11.6 %collective-permute-start.5 = (bf16[4,2,96,192]{3,2,1,0:T(8,128)(2,1)S(1)}, bf16[4,2,96,192]{3,2,1,0:T(8,128)(2,1)S(1)}, u32[]{:S(2)}, u32[]{:S(2)}) collective-permute-start(bf16[4,2,96,192]{3,2,1,0:T(8,128)(2,1)S(1)} %pad_maximum_fusion), channel_id=1, source_target_pairs={{0,16},{16,32},{32,48},{48,0},{64,80},{80,96},{96,112},{112,64},{1... | collective-permute-start | bytes 884744 | tf_op jit(solution)/shard_map/ppermute | solution.py:369
  77.8 9.0 %collective-permute-start.9 = (bf16[2,96,192]{2,1,0:T(8,128)(2,1)S(1)}, bf16[2,96,192]{2,1,0:T(8,128)(2,1)S(1)}, u32[]{:S(2)}, u32[]{:S(2)}) collective-permute-start(bf16[2,96,192]{2,1,0:T(8,128)(2,1)S(1)} %get-tuple-element.43), channel_id=1, source_target_pairs={{0,65},{1,64},{2,67},{3,66},{4,69},{5,68},{6,71},{7,70},{8,73},{9,... | collective-permute-start | bytes 221192 | tf_op jit(solution)/shard_map/ppermute | solution.py:395
  82.2 4.5 %collective-permute-start.8 = (bf16[2,96,192]{2,1,0:T(8,128)(2,1)S(1)}, bf16[2,96,192]{2,1,0:T(8,128)(2,1)S(1)}, u32[]{:S(2)}, u32[]{:S(2)}) collective-permute-start(bf16[2,96,192]{2,1,0:T(8,128)(2,1)S(1)} %get-tuple-element.44), channel_id=1, source_target_pairs={{0,1},{1,0},{2,3},{3,2},{4,5},{5,4},{6,7},{7,6},{8,9},{9,8},{10,11... | collective-permute-start | bytes 221192 | tf_op jit(solution)/shard_map/ppermute | solution.py:333
  82.2 6.0 %collective-permute-start.7 = (bf16[2,96,192]{2,1,0:T(8,128)(2,1)S(1)}, bf16[2,96,192]{2,1,0:T(8,128)(2,1)S(1)}, u32[]{:S(2)}, u32[]{:S(2)}) collective-permute-start(bf16[2,96,192]{2,1,0:T(8,128)(2,1)S(1)} %get-tuple-element.45), channel_id=1, source_target_pairs={{0,64},{16,80},{32,96},{48,112},{64,0},{80,16},{96,32},{112,48},{1... | collective-permute-start | bytes 221192 | tf_op jit(solution)/shard_map/ppermute | solution.py:369

commit v9 on v8

--- a/solution.py
+++ b/solution.py
@@ -1,3 +1,4 @@
+import functools
 import math
 
 import jax
@@ -17,36 +18,15 @@
 VMEM_WIDE = 60 * 1024 * 1024
 
 
-def attention_kernel(
-    place_ref,
-    qg_mine_ref,
-    qg_other_ref,
-    kv_ref,
-    mask_ref,
-    cotangent_ref,
-    weight_ref,
-    bias_ref,
-    qa_own_ref,
-    qa_away_ref,
-    dkv_ref,
-    right_out_ref,
-    left_out_ref,
-    rest_out_ref,
-    gated_ref,
-    cap_ref,
-    s_ref,
-    b2_ref,
-    acc_ref,
-    dp_ref,
-    de_ref,
-    row_ref,
-    dbias_ref,
-):
+def attention_kernel(head, *refs):
+    place_ref, qg_mine_ref, qg_other_ref, kv_ref, mask_ref, cotangent_ref, weight_ref, bias_ref = refs[:8]
+    earlier = refs[8 : 8 + 3 * head]
+    qa_own_ref, qa_away_ref, dkv_ref, right_out_ref, left_out_ref, rest_out_ref = refs[8 + 3 * head :][:6]
+    gated_ref, cap_ref, s_ref, b2_ref, acc_ref, dp_ref, de_ref, row_ref, dbias_ref = refs[14 + 3 * head :]
     step = pl.program_id(0)
     last = pl.num_programs(0) - 1
-    rows = bias_ref.shape[0]
-    queries = rows // 2
-    keys = bias_ref.shape[1]
+    queries, keys = bias_ref.shape
+    half = queries // 2
     head_width = qg_mine_ref.shape[2] // 4
     core = place_ref[PIECES]
     scaling = 1.0 / math.sqrt(head_width)
@@ -59,7 +39,7 @@
             acc_ref[part, :] = jnp.zeros((CHUNK, keys), jnp.float32)
             return carry
 
-        lax.fori_loop(0, rows // CHUNK, fill, 0)
+        lax.fori_loop(0, queries // CHUNK, fill, 0)
         sources, _, lanes = cotangent_ref.shape
         cotangent = cotangent_ref[...].astype(jnp.float32)
         cotangent = cotangent.reshape(sources, 2, cap_ref.shape[0], lanes // sources, lanes)
@@ -67,117 +47,121 @@
             for side in range(2):
                 part = cotangent[:, side, column].reshape(lanes, lanes).astype(jnp.bfloat16)
                 gated = jnp.dot(weight_ref[...], part, preferred_element_type=jnp.float32)
-                gated_ref[column, side * queries // 2 : (side + 1) * queries // 2] = gated.T[: queries // 2]
+                gated_ref[column, side * half : (side + 1) * half] = gated.T[:half]
         masks = mask_ref[...].astype(jnp.float32)
         for column in range(cap_ref.shape[0]):
             pieces = [
-                masks[source, column : column + 1, : queries // 2] for source in range(masks.shape[0])
+                masks[source, column : column + 1, :half] for source in range(masks.shape[0])
             ]
             cap_ref[column] = jnp.where(
                 jnp.concatenate(pieces, axis=1) > 0.5, 1e30, NEG_FILL * LOG2E
             )
 
-    half = queries // 2
-    kv = kv_ref[...].reshape(keys, 4 * head_width)
-    qg_mine = qg_mine_ref[0]
-    qg_other = qg_other_ref[0]
-    query_gate = jnp.concatenate(
-        [jnp.where(core == 0, qg_mine, qg_other), jnp.where(core == 0, qg_other, qg_mine)], axis=0
-    )
-    sigma = jax.nn.sigmoid(query_gate.astype(jnp.float32))
-    gated_grad = gated_ref[step] * sigma
-    gate_slope = gated_grad * (1.0 - sigma)
     lane = lax.broadcasted_iota(jnp.int32, (queries, 4 * head_width), 1)
-    qd = jnp.where(lane < 2 * head_width, query_gate, gated_grad.astype(jnp.bfloat16))
-    zero = jnp.zeros_like(qd)
-
-    def only(part):
-        return jnp.where((lane >= part * head_width) & (lane < (part + 1) * head_width), qd, zero)
-
     transposed = (((1,), (1,)), ((), ()))
-    cap = cap_ref[step]
-    query_rows = [only(0), only(1)]
-    grad_rows = [only(2), only(3)]
-
-    def scores_of(head):
-        s_ref[head * queries : (head + 1) * queries, :] = lax.dot_general(
-            query_rows[head], kv, transposed, preferred_element_type=jnp.float32
+    is_query = (lane >= head * head_width) & (lane < (head + 1) * head_width)
+    is_gate = (lane >= (head + 2) * head_width) & (lane < (head + 3) * head_width)
+    kvs, query_rows, grad_rows, slopes = [], [], [], []
+    for unit in range(2):
+        kvs.append(kv_ref[:, unit * half : (unit + 1) * half, :].reshape(keys, 4 * head_width))
+        mine = qg_mine_ref[unit]
+        other = qg_other_ref[unit]
+        query_gate = jnp.concatenate(
+            [jnp.where(core == 0, mine, other), jnp.where(core == 0, other, mine)], axis=0
         )
-
-    def soften(head):
+        sigma = jax.nn.sigmoid(query_gate.astype(jnp.float32))
+        gated_grad = gated_ref[2 * step + unit] * sigma
+        slopes.append(gated_grad * (1.0 - sigma))
+        zero = jnp.zeros_like(query_gate)
+        query_rows.append(jnp.where(is_query, query_gate, zero))
+        grad_rows.append(jnp.where(is_gate, gated_grad.astype(jnp.bfloat16), zero))
+
+    def scores_of(unit):
+        s_ref[unit * queries : (unit + 1) * queries, :] = lax.dot_general(
+            query_rows[unit], kvs[unit], transposed, preferred_element_type=jnp.float32
+        )
+
+    def soften(unit):
+        cap = cap_ref[2 * step + unit]
+
         def one(index, carry):
-            start = head * queries + index * CHUNK
-            part = pl.ds(start, CHUNK)
-            scores = jnp.minimum(s_ref[part, :] * (scaling * LOG2E) + b2_ref[part, :], cap)
+            inner = index * CHUNK
+            part = pl.ds(unit * queries + inner, CHUNK)
+            scores = s_ref[part, :] * (scaling * LOG2E) + b2_ref[pl.ds(inner, CHUNK), :]
+            scores = jnp.minimum(scores, cap)
             weights = jnp.exp2(scores - jnp.max(scores, axis=1, keepdims=True))
             row_ref[part, :] = jnp.broadcast_to(jnp.sum(weights, axis=1, keepdims=True), (CHUNK, 128))
-            de_ref[pl.ds(rows + start, CHUNK), :] = weights.astype(jnp.bfloat16)
+            de_ref[pl.ds((2 * unit + 1) * queries + inner, CHUNK), :] = weights.astype(jnp.bfloat16)
             return carry
 
         lax.fori_loop(0, queries // CHUNK, one, 0, unroll=UNROLL)
 
-    def cotangents(head):
-        part = slice(head * queries, (head + 1) * queries)
-        weights_low = de_ref[rows + head * queries : rows + (head + 1) * queries, :]
+    def cotangents(unit):
+        part = slice(unit * queries, (unit + 1) * queries)
+        weights_low = de_ref[(2 * unit + 1) * queries : (2 * unit + 2) * queries, :]
         inverse = 1.0 / row_ref[part, :]
-        attended = jnp.dot(weights_low, kv, preferred_element_type=jnp.float32) * inverse
-        grad_wide = grad_rows[head].astype(jnp.float32)
+        attended = jnp.dot(weights_low, kvs[unit], preferred_element_type=jnp.float32) * inverse
+        grad_wide = grad_rows[unit].astype(jnp.float32)
         delta = jnp.sum(grad_wide * attended, axis=1, keepdims=True)
         row_ref[part, :] = delta * inverse
         grad_scaled = (grad_wide * inverse).astype(jnp.bfloat16)
-        dp_ref[part, :] = lax.dot_general(grad_scaled, kv, transposed, preferred_element_type=jnp.float32)
+        dp_ref[part, :] = lax.dot_general(
+            grad_scaled, kvs[unit], transposed, preferred_element_type=jnp.float32
+        )
         return attended, grad_scaled
 
-    def backward(head):
+    def backward(unit):
         def one(index, carry):
-            start = head * queries + index * CHUNK
-            part = pl.ds(start, CHUNK)
-            weights = de_ref[pl.ds(rows + start, CHUNK), :].astype(jnp.float32)
+            inner = index * CHUNK
+            part = pl.ds(unit * queries + inner, CHUNK)
+            weights = de_ref[pl.ds((2 * unit + 1) * queries + inner, CHUNK), :].astype(jnp.float32)
             score_grad = weights * (dp_ref[part, :] - row_ref[part, :1])
-            acc_ref[part, :] += score_grad
-            de_ref[part, :] = score_grad.astype(jnp.bfloat16)
+            acc_ref[pl.ds(inner, CHUNK), :] += score_grad
+            de_ref[pl.ds(2 * unit * queries + inner, CHUNK), :] = score_grad.astype(jnp.bfloat16)
             return carry
 
         lax.fori_loop(0, queries // CHUNK, one, 0, unroll=UNROLL)
 
-    def query_of(head):
-        return jnp.dot(
-            de_ref[head * queries : (head + 1) * queries, :], kv, preferred_element_type=jnp.float32
-        ) * scaling
+    def finish(unit, attended, grad_scaled):
+        low = de_ref[2 * unit * queries : (2 * unit + 1) * queries, :]
+        query = jnp.dot(low, kvs[unit], preferred_element_type=jnp.float32) * scaling
+        merged = jnp.where(is_query, query, jnp.where(is_gate, attended * slopes[unit], 0.0))
+        own = jnp.where(core == 0, merged[:half], merged[half:])
+        away = jnp.where(core == 0, merged[half:], merged[:half])
+        sides = jnp.concatenate([query_rows[unit], grad_scaled], axis=0)
+        key_value = lax.dot_general(
+            sides,
+            de_ref[2 * unit * queries : (2 * unit + 2) * queries, :],
+            (((0,), (0,)), ((), ())),
+            preferred_element_type=jnp.float32,
+        ).T.reshape(dkv_ref.shape[0], half, 4 * head_width)
+        if earlier:
+            own = own + earlier[0][unit].astype(jnp.float32)
+            away = away + earlier[1][unit].astype(jnp.float32)
+            key_value = key_value + earlier[2][:, unit].astype(jnp.float32)
+        qa_own_ref[unit] = own.astype(jnp.bfloat16)
+        qa_away_ref[unit] = away.astype(jnp.bfloat16)
+        dkv_ref[:, unit] = key_value.astype(jnp.bfloat16)
 
     scores_of(0)
     scores_of(1)
     soften(0)
-    att0, sc0 = cotangents(0)
+    first = cotangents(0)
     soften(1)
-    att1, sc1 = cotangents(1)
+    second = cotangents(1)
     backward(0)
-    q0 = query_of(0)
+    finish(0, *first)
     backward(1)
-    q1 = query_of(1)
-    merged = jnp.where(
-        lane < 2 * head_width,
-        jnp.where(lane < head_width, q0, q1),
-        jnp.where(lane < 3 * head_width, att0, att1) * gate_slope,
-    )
-    qa_own_ref[0] = jnp.where(core == 0, merged[:half], merged[half:]).astype(jnp.bfloat16)
-    qa_away_ref[0] = jnp.where(core == 0, merged[half:], merged[:half]).astype(jnp.bfloat16)
-    sides = jnp.concatenate(query_rows + [sc0, sc1], axis=0)
-    key_value = lax.dot_general(
-        sides, de_ref[...], (((0,), (0,)), ((), ())), preferred_element_type=jnp.float32
-    )
-    dkv_ref[...] = key_value.T.astype(jnp.bfloat16).reshape(dkv_ref.shape)
+    finish(1, *second)
 
     @pl.when(step == last)
     def _():
-        width = dbias_ref.shape[3]
+        width = dbias_ref.shape[2]
         for piece in range(PIECES):
-            for head in range(2):
-                for side in range(2):
-                    start = head * queries + side * half
-                    part = acc_ref[start : start + half, piece * width : (piece + 1) * width]
-                    target = 2 * place_ref[piece] + (side + core) % 2
-                    dbias_ref[target, head] = part.astype(jnp.bfloat16)
+            for side in range(2):
+                part = acc_ref[side * half : (side + 1) * half, piece * width : (piece + 1) * width]
+                target = 2 * place_ref[piece] + (side + core) % 2
+                dbias_ref[target] = part.astype(jnp.bfloat16)
         right_out_ref[...] = dbias_ref[8:10]
         left_out_ref[...] = dbias_ref[10:12]
         rest_out_ref[:8] = dbias_ref[:8]
@@ -233,53 +217,56 @@
     )(key, value, mask, cotangent)
 
 
-def attend(places, mine, other, received, weight, bias, row_count):
+def attend(head, places, mine, other, received, weight, bias, row_count, earlier):
     columns, tokens, lanes = mine.shape
-    rows, keys = bias.shape
+    queries, keys = bias.shape[0] // 2, bias.shape[1]
     width = keys // row_count
     devices = received.shape[0]
     mask_place = received.shape[1] // MASK_ROWS - 1
     cotangent_rows = 2 * columns * lanes // devices
     cotangent_place = columns * tokens // cotangent_rows
-    work = columns * rows * keys
+    work = columns * queries * keys
 
     def whole(shape):
         return pl.BlockSpec(shape, lambda j, places: (0,) * len(shape))
 
-    column_spec = pl.BlockSpec((1, tokens, lanes), lambda j, places: (j, 0, 0))
-    piece = (2, tokens, width)
+    column_spec = pl.BlockSpec((2, tokens, lanes), lambda j, places: (j, 0, 0))
+    grad_spec = pl.BlockSpec((devices, 2, tokens, lanes), lambda j, places: (0, j, 0, 0))
+    piece = (tokens, width)
     return pl.pallas_call(
-        attention_kernel,
+        functools.partial(attention_kernel, head),
         grid_spec=pltpu.PrefetchScalarGridSpec(
             num_scalar_prefetch=1,
-            grid=(columns,),
-            in_specs=[column_spec, column_spec]
-            + [
-                pl.BlockSpec((devices, tokens, lanes), lambda j, places: (0, j, 0)),
+            grid=(columns // 2,),
+            in_specs=[
+                column_spec,
+                column_spec,
+                pl.BlockSpec((devices, 2 * tokens, lanes), lambda j, places: (0, j, 0)),
                 pl.BlockSpec((devices, MASK_ROWS, lanes), lambda j, places: (0, mask_place, 0)),
                 pl.BlockSpec(
                     (devices, cotangent_rows, lanes), lambda j, places: (0, cotangent_place, 0)
                 ),
                 whole(weight.shape),
-                whole(bias.shape),
-            ],
+                pl.BlockSpec((queries, keys), lambda j, places: (head, 0)),
+            ]
+            + [column_spec, column_spec, grad_spec][: len(earlier)],
             out_specs=[
                 column_spec,
                 column_spec,
-                pl.BlockSpec((devices, 1, tokens, lanes), lambda j, places: (0, j, 0, 0)),
+                grad_spec,
                 whole((2,) + piece),
                 whole((2,) + piece),
                 whole((12,) + piece),
             ],
             scratch_shapes=[
-                pltpu.VMEM((columns, rows // 2, lanes), jnp.float32),
+                pltpu.VMEM((columns, queries, lanes), jnp.float32),
                 pltpu.VMEM((columns, 1, keys), jnp.float32),
-                pltpu.VMEM((rows, keys), jnp.float32),
-                pltpu.VMEM((rows, keys), jnp.float32),
-                pltpu.VMEM((rows, keys), jnp.float32),
-                pltpu.VMEM((rows, keys), jnp.float32),
-                pltpu.VMEM((2 * rows, keys), jnp.bfloat16),
-                pltpu.VMEM((rows, 128), jnp.float32),
+                pltpu.VMEM((2 * queries, keys), jnp.float32),
+                pltpu.VMEM((queries, keys), jnp.float32),
+                pltpu.VMEM((queries, keys), jnp.float32),
+                pltpu.VMEM((2 * queries, keys), jnp.float32),
+                pltpu.VMEM((4 * queries, keys), jnp.bfloat16),
+                pltpu.VMEM((2 * queries, 128), jnp.float32),
                 pltpu.VMEM((16,) + piece, jnp.bfloat16),
             ],
         ),
@@ -293,8 +280,8 @@
         ],
         compiler_params=pltpu.CompilerParams(vmem_limit_bytes=48 * 1024 * 1024),
         cost_estimate=pl.CostEstimate(flops=12 * 128 * work, bytes_accessed=16 * 2**20, transcendentals=work),
-        name="attention_both",
-    )(places, mine, other, received, received, received, weight, bias)
+        name="attention_head",
+    )(places, mine, other, received, received, received, weight, bias, *earlier)
 
 
 def local(
@@ -353,13 +340,9 @@
     weight_mine, _ = mine_other(output_weight, 0)
     weight_mine = jnp.pad(weight_mine, ((half, 0), (0, 0)))
 
-    qa_own, qa_away, kv_grads, bias_right, bias_left, bias_rest = attend(
-        places, qg_mine, qg_other, received, weight_mine, bias_pair, row_count
-    )
-
-    qa_back = swapped(qa_away)
-    query_gradient = in_order(qa_own[..., :half], qa_back[..., :half], 2)
-    gate_gradient = in_order(qa_own[..., half:], qa_back[..., half:], 2)
+    shared = (places, qg_mine, qg_other, received, weight_mine, bias_pair, row_count)
+    *earlier, bias_right, bias_left, bias_rest = attend(0, *shared, ())
+    (qa_own, qa_away, kv_grads, bias_right_2, bias_left_2, bias_rest_2) = attend(1, *shared, tuple(earlier))
 
     def along_row(array, turn, side):
         pairs = []
@@ -371,8 +354,20 @@
     def added(*parts):
         return sum(part.astype(jnp.float32) for part in parts)
 
-    from_left = along_row(bias_right, 1, 0)
-    from_right = along_row(bias_left, -1, 0)
+    def ring_onward(rest, from_left, from_right):
+        onward = jnp.concatenate([added(rest[4:6], from_left).astype(jnp.bfloat16), rest[6:8]])
+        backward = jnp.concatenate([rest[8:10], added(rest[10:], from_right).astype(jnp.bfloat16)])
+        return along_row(onward, 1, 0), along_row(backward, -1, 0)
+
+    from_left, from_right = along_row(bias_right, 1, 0), along_row(bias_left, -1, 0)
+    second = (bias_right_2, bias_left_2, bias_rest_2, kv_grads, qa_own, qa_away)
+    from_left, from_right, bias_rest, second = lax.optimization_barrier(
+        (from_left, from_right, bias_rest, second)
+    )
+    bias_right_2, bias_left_2, bias_rest_2, kv_grads, qa_own, qa_away = second
+    from_left, from_right = ring_onward(bias_rest, from_left, from_right)
+    sums = added(bias_rest[:4], from_left, from_right)
+    from_left, from_right = along_row(bias_right_2, 1, 0), along_row(bias_left_2, -1, 0)
     from_left, from_right, kv_grads = lax.optimization_barrier((from_left, from_right, kv_grads))
     kv_parts = lax.all_to_all(kv_grads, "col", 0, 0, tiled=True)
     kv_parts = kv_parts.reshape((devices // 2, 2) + kv_parts.shape[1:])
@@ -381,9 +376,11 @@
     key_gradient = key_gradient.astype(jnp.bfloat16)
     value_gradient = jnp.concatenate([kv_sum[0, ..., half:], kv_sum[1, ..., half:]], axis=2)
     value_gradient = value_gradient.astype(jnp.bfloat16)
-    onward = jnp.concatenate([added(bias_rest[4:6], from_left).astype(jnp.bfloat16), bias_rest[6:8]])
-    backward = jnp.concatenate([bias_rest[8:10], added(bias_rest[10:], from_right).astype(jnp.bfloat16)])
-    sums = added(bias_rest[:4], along_row(onward, 1, 0), along_row(backward, -1, 0))
+    from_left, from_right = ring_onward(bias_rest_2, from_left, from_right)
+    sums = jnp.stack([sums, added(bias_rest_2[:4], from_left, from_right)], axis=1)
+    qa_back = swapped(qa_away)
+    query_gradient = in_order(qa_own[..., :half], qa_back[..., :half], 2)
+    gate_gradient = in_order(qa_own[..., half:], qa_back[..., half:], 2)
     low_sums = sums.astype(jnp.bfloat16)
     diagonal = []
     for index in range(row_count * devices):

time: 90.3 us -> 92.7 us (1.027)
  waiting for transfers between devices: 42.6 us -> 35.1 us
  starting transfers between devices: 23.6 us -> 27.9 us
  other arithmetic: 6.51 us -> 9.65 us
  Pallas kernels: 15.5 us -> 17.5 us
    ppermute x5 -> x9, waiting for transfers between devices: 17.1 us -> 9.5 us  [along_row(): return lax.ppermute(array, 'row', pairs)]
    ppermute x5 -> x9, starting transfers between devices: 5.76 us -> 13 us  [along_row(): return lax.ppermute(array, 'row', pairs)]
    ppermute x1, starting transfers between devices: 4.46 us -> 0.01 us  [local(): lax.ppermute(low_sums[3], ('row', 'col'), diagonal)]
    all_to_all x1, waiting for transfers between devices: 22.6 us -> 19.1 us  [local(): received = lax.all_to_all(packed, 'col', 0, 0, tiled=True)]
    all_to_all x1, waiting for transfers between devices: 1.09 us -> 4.33 us  [local(): kv_parts = lax.all_to_all(kv_grads, 'col', 0, 0, tiled=True)]
    pallas_call x1 -> x2, Pallas kernels: 12.9 us -> 14.9 us  [attend(): pl.pallas_call(functools.partial(attention_kernel, head), grid_spec=pltpu...]
    select_n x3, other arithmetic: 2.04 us -> 3.55 us  [in_order(): jnp.where(core == 0, jnp.concatenate([mine, other], axis=axis), jnp.conca...]
    ppermute x4, starting transfers between devices: 1.13 us -> 2.62 us  [swapped(): return lax.ppermute(array, 'col', swap)]
  transfers between devices with their start and end apart: 12 -> 16, of which waited for: 8 -> 7; matrix products, arithmetic and copies ran while one was open for 6% -> 10% of each run, Pallas kernels for 0% -> 9%
where the time goes in v9:
time: 92.7 us; the launch traced here: 92.4 us
  waiting for transfers between devices  35.1 us (38%)
  starting transfers between devices  27.9 us (30%)
  Pallas kernels  17.5 us (19%)
  other arithmetic  9.65 us (10%)
  local copies, waits for them, and re-layouts  1.32 us (1%)
    all_to_all x1, waiting for transfers between devices, local(): received = lax.all_to_all(packed, 'col', 0, 0, tiled=True)  19.1 us
    pallas_call x2, Pallas kernels, attend(): pl.pallas_call(functools.partial(attention_kernel, head), grid_spec=pltpu...  14.9 us
    ppermute x9, starting transfers between devices, along_row(): return lax.ppermute(array, 'row', pairs)  13 us
    ppermute x9, waiting for transfers between devices, along_row(): return lax.ppermute(array, 'row', pairs)  9.5 us
    all_to_all x1, starting transfers between devices, local(): received = lax.all_to_all(packed, 'col', 0, 0, tiled=True)  7.3 us
    all_to_all x1, starting transfers between devices, local(): kv_parts = lax.all_to_all(kv_grads, 'col', 0, 0, tiled=True)  4.93 us
    all_to_all x1, waiting for transfers between devices, local(): kv_parts = lax.all_to_all(kv_grads, 'col', 0, 0, tiled=True)  4.33 us
    select_n x3, other arithmetic, in_order(): jnp.where(core == 0, jnp.concatenate([mine, other], axis=axis), jnp.conca...  3.55 us
  transfers between devices with their start and end apart: 16, of which 7 were waited for; matrix products, arithmetic and copies ran while one was open for 10% of the time, Pallas kernels for 9%

profile of v9, /device:TPU:1, one launch (start us, length us, event | category | flops | bytes accessed | tf_op | source)
XLA Modules:
  0.0 92.4 jit_solution(11924424862485885783)
XLA Ops:
  0.6 2.6 %prepare_exchange.1 = bf16[16,464,128]{2,1,0:T(8,128)(2,1)} custom-call(bf16[4,96,128]{2,1,0:T(8,128)(2,1)} %key_ref.1, bf16[4,96,128]{2,1,0:T(8,128)(2,1)} %value_ref.1, s32[4,96]{1,0:T(4,128)} %mask_ref.1, bf16[4,8,1536]{2,1,0:T(8,128)(2,1)} %cotangent_ref.1), custom_call_target="tpu_custom_call" | custom-call | tf_op jit(solution)/shard_map/prepare_exchange/pallas_call | solution.py:209
  3.2 7.3 %all-to-all-start = ((bf16[16,464,128]{2,1,0:T(8,128)(2,1)}), bf16[16,464,128]{2,1,0:T(8,128)(2,1)S(1)}, u32[]{:S(2)}, u32[]{:S(2)}) async-start(bf16[16,464,128]{2,1,0:T(8,128)(2,1)} %prepare_exchange.1), calls=%async_computation | async-start | bytes 3801088 | tf_op jit(solution)/shard_map/all_to_all | solution.py:326
  10.5 0.0 copy-start.5
  10.6 0.0 copy-start.6
  10.6 1.1 %broadcast_select_fusion.1 = (bf16[2,96,1536]{2,1,0:T(8,128)(2,1)}, bf16[2,96,1536]{2,1,0:T(8,128)(2,1)}) fusion(pred[]{:T(512)S(6)} %eq.31, bf16[4,96,1536]{2,1,0:T(8,128)(2,1)S(1)} %copy-done.2), kind=kLoop, calls=%fused_computation.7 | loop fusion | flops 589824 | bytes 2359297 | tf_op jit(solution)/shard_map/jit(_where)/select_n | solution.py:310
  11.7 0.1 collective-permute-start.1
  11.8 0.1 broadcast_select_fusion.2
  11.9 0.1 broadcast_select_fusion.3
  12.0 0.1 pad_maximum_fusion.6
  12.1 0.5 collective-permute-start
  12.6 0.1 stack.48.refs_0_
  12.7 0.1 pad_maximum_fusion.5.refs_1_
  12.8 1.1 %collective-permute-done.1 = bf16[2,96,1536]{2,1,0:T(8,128)(2,1)S(1)} collective-permute-done((bf16[2,96,1536]{2,1,0:T(8,128)(2,1)}, bf16[2,96,1536]{2,1,0:T(8,128)(2,1)S(1)}, u32[]{:S(2)}, u32[]{:S(2)}) %collective-permute-start.1) | collective-permute-done | bytes 589856 | tf_op jit(solution)/shard_map/ppermute | solution.py:320
  13.9 0.8 copy-done.3
  14.7 1.9 %maximum_select_fusion = bf16[2,192,1536]{2,1,0:T(8,128)(2,1)S(1)} fusion(bf16[2,96,1536]{2,1,0:T(8,128)(2,1)} %copy-done.3, bf16[2,96,1536]{2,1,0:T(8,128)(2,1)} %get-tuple-element.63, pred[]{:T(512)S(6)} %eq.31), kind=kLoop, calls=%fused_computation.1 | loop fusion | flops 5308416 | bytes 2359297 | tf_op jit(solution)/shard_map/jit(_where)/select_n | solution.py:313
  16.6 0.0 collective-permute-done.refs_2_
  16.6 19.1 %all-to-all-done.refs_3_.refs_4_.refs_5_ = bf16[16,464,128]{2,1,0:T(8,128)(2,1)S(1)} async-done(((bf16[16,464,128]{2,1,0:T(8,128)(2,1)}), bf16[16,464,128]{2,1,0:T(8,128)(2,1)S(1)}, u32[]{:S(2)}, u32[]{:S(2)}) %all-to-all-start) | async-done | bytes 1900576 | tf_op jit(solution)/shard_map/all_to_all | solution.py:326
  35.7 6.6 %attention_head.2 = (bf16[4,96,128]{2,1,0:T(8,128)(2,1)S(1)}, bf16[4,96,128]{2,1,0:T(8,128)(2,1)S(1)}, bf16[16,4,96,128]{3,2,1,0:T(8,128)(2,1)S(1)}, bf16[2,96,1...) custom-call(s32[9]{0:T(128)S(1)} %stack.48.refs_0_, ...), custom_call_target="tpu_custom_call" | custom-call | flops 1811939328 | bytes 16777216 | tf_op jit(solution)/shard_map/attention_head/pallas_call | solution.py:236
  42.4 1.4 %collective-permute-start.2 = (bf16[2,96,192]{2,1,0:T(8,128)(2,1)S(1)}, bf16[2,96,192]{2,1,0:T(8,128)(2,1)S(1)}, u32[]{:S(2)}, u32[]{:S(2)}) collective-permute-start(bf16[2,96,192]{2,1,0:T(8,128)(2,1)S(1)} %get-tuple-element.34), channel_id=1, source_target_pairs={{0,16},{16,32},{32,48},{48,0},{64,80},{80,96},{96,112},{112,64},{1... | collective-permute-start | bytes 221192 | tf_op jit(solution)/shard_map/ppermute | solution.py:352
  43.7 1.5 %collective-permute-start.3 = (bf16[2,96,192]{2,1,0:T(8,128)(2,1)S(1)}, bf16[2,96,192]{2,1,0:T(8,128)(2,1)S(1)}, u32[]{:S(2)}, u32[]{:S(2)}) collective-permute-start(bf16[2,96,192]{2,1,0:T(8,128)(2,1)S(1)} %get-tuple-element.35), channel_id=1, source_target_pairs={{0,48},{16,0},{32,16},{48,32},{64,112},{80,64},{96,80},{112,96},{1... | collective-permute-start | bytes 221192 | tf_op jit(solution)/shard_map/ppermute | solution.py:352
  45.2 8.3 %attention_head.3 = (bf16[4,96,128]{2,1,0:T(8,128)(2,1)S(1)}, bf16[4,96,128]{2,1,0:T(8,128)(2,1)S(1)}, bf16[16,4,96,128]{3,2,1,0:T(8,128)(2,1)}, bf16[2,96,192]{...) custom-call(s32[9]{0:T(128)S(1)} %stack.48.refs_0_, ...), custom_call_target="tpu_custom_call" | custom-call | flops 1811939328 | bytes 16777216 | tf_op jit(solution)/shard_map/attention_head/pallas_call | solution.py:236
  53.5 0.0 collective-permute-done.2
  53.5 0.0 collective-permute-done.3
  53.6 1.1 %collective-permute-start.4 = (bf16[4,96,128]{2,1,0:T(8,128)(2,1)S(1)}, bf16[4,96,128]{2,1,0:T(8,128)(2,1)S(1)}, u32[]{:S(2)}, u32[]{:S(2)}) collective-permute-start(bf16[4,96,128]{2,1,0:T(8,128)(2,1)S(1)} %get-tuple-element.47), channel_id=1, source_target_pairs={{0,1},{1,0},{2,3},{3,2},{4,5},{5,4},{6,7},{7,6},{8,9},{9,8},{10,11... | collective-permute-start | bytes 294920 | tf_op jit(solution)/shard_map/ppermute | solution.py:320
  54.6 0.1 fusion.6
  54.7 0.2 collective-permute-start.7
  54.9 2.6 %collective-permute-start.8 = (bf16[2,96,192]{2,1,0:T(8,128)(2,1)S(1)}, bf16[2,96,192]{2,1,0:T(8,128)(2,1)S(1)}, u32[]{:S(2)}, u32[]{:S(2)}) collective-permute-start(bf16[2,96,192]{2,1,0:T(8,128)(2,1)S(1)} %get-tuple-element.53), channel_id=1, source_target_pairs={{0,48},{16,0},{32,16},{48,32},{64,112},{80,64},{96,80},{112,96},{1... | collective-permute-start | bytes 221192 | tf_op jit(solution)/shard_map/ppermute | solution.py:352
  57.6 0.4 collective-permute-start.6
  58.0 2.4 %collective-permute-done.7 = bf16[2,96,192]{2,1,0:T(8,128)(2,1)S(1)} collective-permute-done((bf16[2,96,192]{2,1,0:T(8,128)(2,1)S(1)}, bf16[2,96,192]{2,1,0:T(8,128)(2,1)S(1)}, u32[]{:S(2)}, u32[]{:S(2)}) %collective-permute-start.7) | collective-permute-done | bytes 73760 | tf_op jit(solution)/shard_map/ppermute | solution.py:352
  60.4 4.9 %all-to-all-start.1 = ((bf16[16,4,96,128]{3,2,1,0:T(8,128)(2,1)}), bf16[16,4,96,128]{3,2,1,0:T(8,128)(2,1)}, u32[]{:S(2)}, u32[]{:S(2)}) async-start(bf16[16,4,96,128]{3,2,1,0:T(8,128)(2,1)} %get-tuple-element.57), calls=%async_computation.1 | async-start | bytes 3145728 | tf_op jit(solution)/shard_map/all_to_all | solution.py:372
  65.4 1.0 %collective-permute-start.5 = (bf16[4,96,192]{2,1,0:T(8,128)(2,1)S(1)}, bf16[4,96,192]{2,1,0:T(8,128)(2,1)S(1)}, u32[]{:S(2)}, u32[]{:S(2)}) collective-permute-start(bf16[4,96,192]{2,1,0:T(8,128)(2,1)S(1)} %pad_maximum_fusion.1), channel_id=1, source_target_pairs={{0,16},{16,32},{32,48},{48,0},{64,80},{80,96},{96,112},{112,64},{1... | collective-permute-start | bytes 442376 | tf_op jit(solution)/shard_map/ppermute | solution.py:352
  66.5 2.6 %collective-permute-start.10 = (bf16[4,96,192]{2,1,0:T(8,128)(2,1)S(1)}, bf16[4,96,192]{2,1,0:T(8,128)(2,1)S(1)}, u32[]{:S(2)}, u32[]{:S(2)}) collective-permute-start(bf16[4,96,192]{2,1,0:T(8,128)(2,1)S(1)} %pad_maximum_fusion.4), channel_id=1, source_target_pairs={{0,48},{16,0},{32,16},{48,32},{64,112},{80,64},{96,80},{112,96},{1... | collective-permute-start | bytes 442376 | tf_op jit(solution)/shard_map/ppermute | solution.py:352
  69.1 0.1 collective-permute-start.9
  69.2 0.1 fusion.7
  69.3 0.9 maximum_select_fusion.2
  70.2 3.9 %collective-permute-done.5 = bf16[4,96,192]{2,1,0:T(8,128)(2,1)S(1)} collective-permute-done((bf16[4,96,192]{2,1,0:T(8,128)(2,1)S(1)}, bf16[4,96,192]{2,1,0:T(8,128)(2,1)S(1)}, u32[]{:S(2)}, u32[]{:S(2)}) %collective-permute-start.5) | collective-permute-done | bytes 147488 | tf_op jit(solution)/shard_map/ppermute | solution.py:352
  74.0 1.0 %add_bitcast_fusion.1 = f32[4,1,96,192]{3,2,0,1:T(8,128)S(1)} fusion(bf16[4,96,192]{2,1,0:T(8,128)(2,1)S(1)} %collective-permute-done.6, bf16[4,96,192]{2,1,0:T(8,128)(2,1)S(1)} %collective-permute-done.5, bf16[12,96,192]{2,1,0:T(8,128)(2,1)} %copy-done.1), kind=kLoop, calls=%fused_computation.10 | loop fusion | flops 368640 | bytes 737280 | tf_op jit(solution)/shard_map/stack | solution.py:380
  75.0 3.2 %collective-permute-done.9 = bf16[4,96,192]{2,1,0:T(8,128)(2,1)S(1)} collective-permute-done((bf16[4,96,192]{2,1,0:T(8,128)(2,1)S(1)}, bf16[4,96,192]{2,1,0:T(8,128)(2,1)S(1)}, u32[]{:S(2)}, u32[]{:S(2)}) %collective-permute-start.9) | collective-permute-done | bytes 147488 | tf_op jit(solution)/shard_map/ppermute | solution.py:352
  78.3 0.1 add_bitcast_fusion
  78.4 3.4 %collective-permute-start.11 = (bf16[2,96,192]{2,1,0:T(8,128)(2,1)S(1)}, bf16[2,96,192]{2,1,0:T(8,128)(2,1)S(1)}, u32[]{:S(2)}, u32[]{:S(2)}) collective-permute-start(bf16[2,96,192]{2,1,0:T(8,128)(2,1)S(1)} %get-tuple-element.77), channel_id=1, source_target_pairs={{0,64},{16,80},{32,96},{48,112},{64,0},{80,16},{96,32},{112,48},{1... | collective-permute-start | bytes 221192 | tf_op jit(solution)/shard_map/ppermute | solution.py:352
  81.8 1.0 %collective-permute-start.12 = (bf16[2,96,192]{2,1,0:T(8,128)(2,1)S(1)}, bf16[2,96,192]{2,1,0:T(8,128)(2,1)S(1)}, u32[]{:S(2)}, u32[]{:S(2)}) collective-permute-start(bf16[2,96,192]{2,1,0:T(8,128)(2,1)S(1)} %get-tuple-element.76), channel_id=1, source_target_pairs={{0,1},{1,0},{2,3},{3,2},{4,5},{5,4},{6,7},{7,6},{8,9},{9,8},{10,11... | collective-permute-start | bytes 221192 | tf_op jit(solution)/shard_map/ppermute | solution.py:320
  82.7 4.3 %all-to-all-done.1 = bf16[16,4,96,128]{3,2,1,0:T(8,128)(2,1)} async-done(((bf16[16,4,96,128]{3,2,1,0:T(8,128)(2,1)}), bf16[16,4,96,128]{3,2,1,0:T(8,128)(2,1)}, u32[]{:S(2)}, u32[]{:S(2)}) %all-to-all-start.1) | async-done | bytes 1572896 | tf_op jit(solution)/shard_map/all_to_all | solution.py:372
  87.0 1.7 %convert_reduce_fusion = f32[2,4,96,128]{3,2,1,0:T(8,128)S(1)} fusion(bf16[8,2,4,96,128]{4,3,2,1,0:T(8,128)(2,1)} %bitcast.21), kind=kLoop, calls=%fused_computation | loop fusion | flops 1474560 | bytes 1966080 | tf_op jit(solution)/shard_map/reduce_sum | solution.py:374
  88.8 0.1 slice_bitcast_fusion.3
  88.9 0.8 fusion.3
  89.7 0.7 pad_maximum_fusion.7
  90.4 1.1 %collective-permute-done.13 = bf16[2,96,192]{2,1,0:T(8,128)(2,1)S(1)} collective-permute-done((bf16[2,96,192]{2,1,0:T(8,128)(2,1)S(1)}, bf16[2,96,192]{2,1,0:T(8,128)(2,1)S(1)}, u32[]{:S(2)}, u32[]{:S(2)}) %collective-permute-start.13) | collective-permute-done | bytes 73760 | tf_op jit(solution)/shard_map/ppermute | solution.py:392
  91.6 0.8 maximum_select_fusion.1
  (32 shorter events, 0.5 us)
Async XLA Ops:
  3.2 7.3 %copy-start.2 = (bf16[4,96,1536]{2,1,0:T(8,128)(2,1)S(1)}, bf16[4,96,1536]{2,1,0:T(8,128)(2,1)}, u32[]{:S(2)}) copy-start(bf16[4,96,1536]{2,1,0:T(8,128)(2,1)} %param.12) | copy-start | bytes 3538948
  3.2 32.5 %all-to-all-start = ((bf16[16,464,128]{2,1,0:T(8,128)(2,1)}), bf16[16,464,128]{2,1,0:T(8,128)(2,1)S(1)}, u32[]{:S(2)}, u32[]{:S(2)}) async-start(bf16[16,464,128]{2,1,0:T(8,128)(2,1)} %prepare_exchange.1), calls=%async_computation | async-start | bytes 3801088 | tf_op jit(solution)/shard_map/all_to_all | solution.py:326
  10.5 1.3 %copy-start.4 = (bf16[4,96,128]{2,1,0:T(8,128)(2,1)S(1)}, bf16[4,96,128]{2,1,0:T(8,128)(2,1)}, u32[]{:S(2)}) copy-start(bf16[4,96,128]{2,1,0:T(8,128)(2,1)} %param.11) | copy-start | bytes 294916
  10.5 1.4 %copy-start.5 = (bf16[4,96,128]{2,1,0:T(8,128)(2,1)S(1)}, bf16[4,96,128]{2,1,0:T(8,128)(2,1)}, u32[]{:S(2)}) copy-start(bf16[4,96,128]{2,1,0:T(8,128)(2,1)} %param.8) | copy-start | bytes 294916
  10.6 2.0 %copy-start.6 = (bf16[128,128]{1,0:T(8,128)(2,1)S(1)}, bf16[128,128]{1,0:T(8,128)(2,1)}, u32[]{:S(2)}) copy-start(bf16[128,128]{1,0:T(8,128)(2,1)} %param.14) | copy-start | bytes 98308
  11.7 2.2 %collective-permute-start.1 = (bf16[2,96,1536]{2,1,0:T(8,128)(2,1)}, bf16[2,96,1536]{2,1,0:T(8,128)(2,1)S(1)}, u32[]{:S(2)}, u32[]{:S(2)}) collective-permute-start(bf16[2,96,1536]{2,1,0:T(8,128)(2,1)} %get-tuple-element.64), channel_id=1, source_target_pairs={{0,1},{1,0},{2,3},{3,2},{4,5},{5,4},{6,7},{7,6},{8,9},{9,8},{10,11... | collective-permute-start | bytes 1769480 | tf_op jit(solution)/shard_map/ppermute | solution.py:320
  12.1 4.5 %collective-permute-start = (bf16[4,96,128]{2,1,0:T(8,128)(2,1)S(1)}, bf16[4,96,128]{2,1,0:T(8,128)(2,1)S(1)}, u32[]{:S(2)}, u32[]{:S(2)}) collective-permute-start(bf16[4,96,128]{2,1,0:T(8,128)(2,1)S(1)} %pad_maximum_fusion.6), channel_id=1, source_target_pairs={{0,1},{1,0},{2,3},{3,2},{4,5},{5,4},{6,7},{7,6},{8,9},{9,8},{10,11... | collective-permute-start | bytes 294920 | tf_op jit(solution)/shard_map/ppermute | solution.py:320
  13.9 0.8 copy-start.3
  35.7 6.6 %copy-start = (bf16[16,464,128]{2,1,0:T(8,128)(2,1)}, bf16[16,464,128]{2,1,0:T(8,128)(2,1)S(1)}, u32[]{:S(2)}) copy-start(bf16[16,464,128]{2,1,0:T(8,128)(2,1)S(1)} %all-to-all-done.refs_3_.refs_4_.refs_5_) | copy-start | bytes 5701636
  42.4 15.2 %copy-start.1 = (bf16[12,96,192]{2,1,0:T(8,128)(2,1)}, bf16[12,96,192]{2,1,0:T(8,128)(2,1)S(1)}, u32[]{:S(2)}) copy-start(bf16[12,96,192]{2,1,0:T(8,128)(2,1)S(1)} %get-tuple-element.48) | copy-start | bytes 1327108
  42.4 11.2 %collective-permute-start.2 = (bf16[2,96,192]{2,1,0:T(8,128)(2,1)S(1)}, bf16[2,96,192]{2,1,0:T(8,128)(2,1)S(1)}, u32[]{:S(2)}, u32[]{:S(2)}) collective-permute-start(bf16[2,96,192]{2,1,0:T(8,128)(2,1)S(1)} %get-tuple-element.34), channel_id=1, source_target_pairs={{0,16},{16,32},{32,48},{48,0},{64,80},{80,96},{96,112},{112,64},{1... | collective-permute-start | bytes 221192 | tf_op jit(solution)/shard_map/ppermute | solution.py:352
  43.7 9.8 %collective-permute-start.3 = (bf16[2,96,192]{2,1,0:T(8,128)(2,1)S(1)}, bf16[2,96,192]{2,1,0:T(8,128)(2,1)S(1)}, u32[]{:S(2)}, u32[]{:S(2)}) collective-permute-start(bf16[2,96,192]{2,1,0:T(8,128)(2,1)S(1)} %get-tuple-element.35), channel_id=1, source_target_pairs={{0,48},{16,0},{32,16},{48,32},{64,112},{80,64},{96,80},{112,96},{1... | collective-permute-start | bytes 221192 | tf_op jit(solution)/shard_map/ppermute | solution.py:352
  53.6 15.6 %collective-permute-start.4 = (bf16[4,96,128]{2,1,0:T(8,128)(2,1)S(1)}, bf16[4,96,128]{2,1,0:T(8,128)(2,1)S(1)}, u32[]{:S(2)}, u32[]{:S(2)}) collective-permute-start(bf16[4,96,128]{2,1,0:T(8,128)(2,1)S(1)} %get-tuple-element.47), channel_id=1, source_target_pairs={{0,1},{1,0},{2,3},{3,2},{4,5},{5,4},{6,7},{7,6},{8,9},{9,8},{10,11... | collective-permute-start | bytes 294920 | tf_op jit(solution)/shard_map/ppermute | solution.py:320
  54.7 5.7 %collective-permute-start.7 = (bf16[2,96,192]{2,1,0:T(8,128)(2,1)S(1)}, bf16[2,96,192]{2,1,0:T(8,128)(2,1)S(1)}, u32[]{:S(2)}, u32[]{:S(2)}) collective-permute-start(bf16[2,96,192]{2,1,0:T(8,128)(2,1)S(1)} %get-tuple-element.52), channel_id=1, source_target_pairs={{0,16},{16,32},{32,48},{48,0},{64,80},{80,96},{96,112},{112,64},{1... | collective-permute-start | bytes 221192 | tf_op jit(solution)/shard_map/ppermute | solution.py:352
  54.9 5.5 %collective-permute-start.8 = (bf16[2,96,192]{2,1,0:T(8,128)(2,1)S(1)}, bf16[2,96,192]{2,1,0:T(8,128)(2,1)S(1)}, u32[]{:S(2)}, u32[]{:S(2)}) collective-permute-start(bf16[2,96,192]{2,1,0:T(8,128)(2,1)S(1)} %get-tuple-element.53), channel_id=1, source_target_pairs={{0,48},{16,0},{32,16},{48,32},{64,112},{80,64},{96,80},{112,96},{1... | collective-permute-start | bytes 221192 | tf_op jit(solution)/shard_map/ppermute | solution.py:352
  57.6 12.6 %collective-permute-start.6 = (bf16[4,96,192]{2,1,0:T(8,128)(2,1)S(1)}, bf16[4,96,192]{2,1,0:T(8,128)(2,1)S(1)}, u32[]{:S(2)}, u32[]{:S(2)}) collective-permute-start(bf16[4,96,192]{2,1,0:T(8,128)(2,1)S(1)} %pad_maximum_fusion.2), channel_id=1, source_target_pairs={{0,48},{16,0},{32,16},{48,32},{64,112},{80,64},{96,80},{112,96},{1... | collective-permute-start | bytes 442376 | tf_op jit(solution)/shard_map/ppermute | solution.py:352
  60.4 26.6 %all-to-all-start.1 = ((bf16[16,4,96,128]{3,2,1,0:T(8,128)(2,1)}), bf16[16,4,96,128]{3,2,1,0:T(8,128)(2,1)}, u32[]{:S(2)}, u32[]{:S(2)}) async-start(bf16[16,4,96,128]{3,2,1,0:T(8,128)(2,1)} %get-tuple-element.57), calls=%async_computation.1 | async-start | bytes 3145728 | tf_op jit(solution)/shard_map/all_to_all | solution.py:372
  65.4 8.6 %collective-permute-start.5 = (bf16[4,96,192]{2,1,0:T(8,128)(2,1)S(1)}, bf16[4,96,192]{2,1,0:T(8,128)(2,1)S(1)}, u32[]{:S(2)}, u32[]{:S(2)}) collective-permute-start(bf16[4,96,192]{2,1,0:T(8,128)(2,1)S(1)} %pad_maximum_fusion.1), channel_id=1, source_target_pairs={{0,16},{16,32},{32,48},{48,0},{64,80},{80,96},{96,112},{112,64},{1... | collective-permute-start | bytes 442376 | tf_op jit(solution)/shard_map/ppermute | solution.py:352
  66.5 8.6 %collective-permute-start.10 = (bf16[4,96,192]{2,1,0:T(8,128)(2,1)S(1)}, bf16[4,96,192]{2,1,0:T(8,128)(2,1)S(1)}, u32[]{:S(2)}, u32[]{:S(2)}) collective-permute-start(bf16[4,96,192]{2,1,0:T(8,128)(2,1)S(1)} %pad_maximum_fusion.4), channel_id=1, source_target_pairs={{0,48},{16,0},{32,16},{48,32},{64,112},{80,64},{96,80},{112,96},{1... | collective-permute-start | bytes 442376 | tf_op jit(solution)/shard_map/ppermute | solution.py:352
  69.1 9.2 %collective-permute-start.9 = (bf16[4,96,192]{2,1,0:T(8,128)(2,1)S(1)}, bf16[4,96,192]{2,1,0:T(8,128)(2,1)S(1)}, u32[]{:S(2)}, u32[]{:S(2)}) collective-permute-start(bf16[4,96,192]{2,1,0:T(8,128)(2,1)S(1)} %pad_maximum_fusion.3), channel_id=1, source_target_pairs={{0,16},{16,32},{32,48},{48,0},{64,80},{80,96},{96,112},{112,64},{1... | collective-permute-start | bytes 442376 | tf_op jit(solution)/shard_map/ppermute | solution.py:352
  78.4 12.0 %collective-permute-start.11 = (bf16[2,96,192]{2,1,0:T(8,128)(2,1)S(1)}, bf16[2,96,192]{2,1,0:T(8,128)(2,1)S(1)}, u32[]{:S(2)}, u32[]{:S(2)}) collective-permute-start(bf16[2,96,192]{2,1,0:T(8,128)(2,1)S(1)} %get-tuple-element.77), channel_id=1, source_target_pairs={{0,64},{16,80},{32,96},{48,112},{64,0},{80,16},{96,32},{112,48},{1... | collective-permute-start | bytes 221192 | tf_op jit(solution)/shard_map/ppermute | solution.py:352
  81.8 8.7 %collective-permute-start.12 = (bf16[2,96,192]{2,1,0:T(8,128)(2,1)S(1)}, bf16[2,96,192]{2,1,0:T(8,128)(2,1)S(1)}, u32[]{:S(2)}, u32[]{:S(2)}) collective-permute-start(bf16[2,96,192]{2,1,0:T(8,128)(2,1)S(1)} %get-tuple-element.76), channel_id=1, source_target_pairs={{0,1},{1,0},{2,3},{3,2},{4,5},{5,4},{6,7},{7,6},{8,9},{9,8},{10,11... | collective-permute-start | bytes 221192 | tf_op jit(solution)/shard_map/ppermute | solution.py:320
  82.7 8.8 %collective-permute-start.13 = (bf16[2,96,192]{2,1,0:T(8,128)(2,1)S(1)}, bf16[2,96,192]{2,1,0:T(8,128)(2,1)S(1)}, u32[]{:S(2)}, u32[]{:S(2)}) collective-permute-start(bf16[2,96,192]{2,1,0:T(8,128)(2,1)S(1)} %get-tuple-element.75), channel_id=1, source_target_pairs={{0,65},{1,64},{2,67},{3,66},{4,69},{5,68},{6,71},{7,70},{8,73},{9,... | collective-permute-start | bytes 221192 | tf_op jit(solution)/shard_map/ppermute | solution.py:392

commit v10 on v9

--- a/solution.py
+++ b/solution.py
@@ -368,7 +368,6 @@
     from_left, from_right = ring_onward(bias_rest, from_left, from_right)
     sums = added(bias_rest[:4], from_left, from_right)
     from_left, from_right = along_row(bias_right_2, 1, 0), along_row(bias_left_2, -1, 0)
-    from_left, from_right, kv_grads = lax.optimization_barrier((from_left, from_right, kv_grads))
     kv_parts = lax.all_to_all(kv_grads, "col", 0, 0, tiled=True)
     kv_parts = kv_parts.reshape((devices // 2, 2) + kv_parts.shape[1:])
     kv_sum = jnp.sum(kv_parts.astype(jnp.float32), axis=0)
@@ -386,13 +385,9 @@
     for index in range(row_count * devices):
         up = (index // devices + row_ring) % row_count
         diagonal.append((index, up * devices + (index % devices ^ 1)))
-    from_high, from_core, from_diagonal, key_gradient, value_gradient = lax.optimization_barrier((
-        along_row(low_sums[2], 0, 1),
-        swapped(low_sums[1]),
-        lax.ppermute(low_sums[3], ("row", "col"), diagonal),
-        key_gradient,
-        value_gradient,
-    ))
+    from_high = along_row(low_sums[2], 0, 1)
+    from_core = swapped(low_sums[1])
+    from_diagonal = lax.ppermute(low_sums[3], ("row", "col"), diagonal)
     bias_own = added(sums[0], from_high)
     bias_away = added(from_core, from_diagonal)
     bias_gradient = in_order(bias_own, bias_away, 0)

time: 92.7 us -> 91.5 us (0.987); the launches traced: 92.4 us -> 89.6 us
  waiting for transfers between devices: 35.1 us -> 30.5 us
  starting transfers between devices: 27.9 us -> 29.9 us
    all_to_all x1, waiting for transfers between devices: 4.33 us -> 0.01 us  [local(): kv_parts = lax.all_to_all(kv_grads, 'col', 0, 0, tiled=True)]
    ppermute x1, starting transfers between devices: 0.01 us -> 2.96 us  [local(): from_diagonal = lax.ppermute(low_sums[3], ('row', 'col'), diagonal)]
    ppermute x9, waiting for transfers between devices: 9.5 us -> 6.96 us  [along_row(): return lax.ppermute(array, 'row', pairs)]
    ppermute x1, waiting for transfers between devices: 1.1 us -> 3.3 us  [local(): from_diagonal = lax.ppermute(low_sums[3], ('row', 'col'), diagonal)]
  transfers between devices with their start and end apart: 16 -> 16, of which waited for: 7 -> 8; matrix products, arithmetic and copies ran while one was open for 10% -> 7% of each run, Pallas kernels for 9% -> 9%
where the time goes in v10:
time: 91.5 us; the launch traced here: 89.6 us
  waiting for transfers between devices  30.5 us (33%)
  starting transfers between devices  29.9 us (33%)
  Pallas kernels  17.5 us (19%)
  other arithmetic  8.75 us (10%)
  local copies, waits for them, and re-layouts  2.13 us (2%)
    all_to_all x1, waiting for transfers between devices, local(): received = lax.all_to_all(packed, 'col', 0, 0, tiled=True)  19.1 us
    pallas_call x2, Pallas kernels, attend(): pl.pallas_call(functools.partial(attention_kernel, head), grid_spec=pltpu...  14.9 us
    ppermute x9, starting transfers between devices, along_row(): return lax.ppermute(array, 'row', pairs)  13.1 us
    all_to_all x1, starting transfers between devices, local(): received = lax.all_to_all(packed, 'col', 0, 0, tiled=True)  7.3 us
    ppermute x9, waiting for transfers between devices, along_row(): return lax.ppermute(array, 'row', pairs)  6.96 us
    all_to_all x1, starting transfers between devices, local(): kv_parts = lax.all_to_all(kv_grads, 'col', 0, 0, tiled=True)  4.43 us
    select_n x3, other arithmetic, in_order(): jnp.where(core == 0, jnp.concatenate([mine, other], axis=axis), jnp.conca...  3.55 us
    ppermute x1, waiting for transfers between devices, local(): from_diagonal = lax.ppermute(low_sums[3], ('row', 'col'), diagonal)  3.3 us
  transfers between devices with their start and end apart: 16, of which 8 were waited for; matrix products, arithmetic and copies ran while one was open for 7% of the time, Pallas kernels for 9%

profile of v10, /device:TPU:1, one launch (start us, length us, event | category | flops | bytes accessed | tf_op | source)
XLA Modules:
  0.0 89.6 jit_solution(6596310439407522133)
XLA Ops:
  0.6 2.6 %prepare_exchange.1 = bf16[16,464,128]{2,1,0:T(8,128)(2,1)} custom-call(bf16[4,96,128]{2,1,0:T(8,128)(2,1)} %key_ref.1, bf16[4,96,128]{2,1,0:T(8,128)(2,1)} %value_ref.1, s32[4,96]{1,0:T(4,128)} %mask_ref.1, bf16[4,8,1536]{2,1,0:T(8,128)(2,1)} %cotangent_ref.1), custom_call_target="tpu_custom_call" | custom-call | tf_op jit(solution)/shard_map/prepare_exchange/pallas_call | solution.py:209
  3.2 7.3 %all-to-all-start = ((bf16[16,464,128]{2,1,0:T(8,128)(2,1)}), bf16[16,464,128]{2,1,0:T(8,128)(2,1)S(1)}, u32[]{:S(2)}, u32[]{:S(2)}) async-start(bf16[16,464,128]{2,1,0:T(8,128)(2,1)} %prepare_exchange.1), calls=%async_computation | async-start | bytes 3801088 | tf_op jit(solution)/shard_map/all_to_all | solution.py:326
  10.6 1.1 %broadcast_select_fusion.1 = (bf16[2,96,1536]{2,1,0:T(8,128)(2,1)}, bf16[2,96,1536]{2,1,0:T(8,128)(2,1)}) fusion(pred[]{:T(512)S(6)} %eq.31, bf16[4,96,1536]{2,1,0:T(8,128)(2,1)S(1)} %copy-done.3), kind=kLoop, calls=%fused_computation.7 | loop fusion | flops 589824 | bytes 2359297 | tf_op jit(solution)/shard_map/jit(_where)/select_n | solution.py:310
  11.7 0.1 collective-permute-start.1
  11.8 0.1 broadcast_select_fusion.2
  11.9 0.1 broadcast_select_fusion.3
  12.0 0.1 pad_maximum_fusion.6
  12.1 0.5 collective-permute-start
  12.6 0.1 stack.48.refs_0_
  12.7 0.1 pad_maximum_fusion.5.refs_1_
  12.8 1.1 %collective-permute-done.1 = bf16[2,96,1536]{2,1,0:T(8,128)(2,1)S(1)} collective-permute-done((bf16[2,96,1536]{2,1,0:T(8,128)(2,1)}, bf16[2,96,1536]{2,1,0:T(8,128)(2,1)S(1)}, u32[]{:S(2)}, u32[]{:S(2)}) %collective-permute-start.1) | collective-permute-done | bytes 589856 | tf_op jit(solution)/shard_map/ppermute | solution.py:320
  13.9 0.8 copy-done.4
  14.7 1.9 %maximum_select_fusion = bf16[2,192,1536]{2,1,0:T(8,128)(2,1)S(1)} fusion(bf16[2,96,1536]{2,1,0:T(8,128)(2,1)} %copy-done.4, bf16[2,96,1536]{2,1,0:T(8,128)(2,1)} %get-tuple-element.47, pred[]{:T(512)S(6)} %eq.31), kind=kLoop, calls=%fused_computation.1 | loop fusion | flops 5308416 | bytes 2359297 | tf_op jit(solution)/shard_map/jit(_where)/select_n | solution.py:313
  16.6 19.1 %all-to-all-done.refs_3_.refs_4_.refs_5_ = bf16[16,464,128]{2,1,0:T(8,128)(2,1)S(1)} async-done(((bf16[16,464,128]{2,1,0:T(8,128)(2,1)}), bf16[16,464,128]{2,1,0:T(8,128)(2,1)S(1)}, u32[]{:S(2)}, u32[]{:S(2)}) %all-to-all-start) | async-done | bytes 1900576 | tf_op jit(solution)/shard_map/all_to_all | solution.py:326
  35.7 6.6 %attention_head.2 = (bf16[4,96,128]{2,1,0:T(8,128)(2,1)S(1)}, bf16[4,96,128]{2,1,0:T(8,128)(2,1)S(1)}, bf16[16,4,96,128]{3,2,1,0:T(8,128)(2,1)S(1)}, bf16[2,96,1...) custom-call(s32[9]{0:T(128)S(1)} %stack.48.refs_0_, ...), custom_call_target="tpu_custom_call" | custom-call | flops 1811939328 | bytes 16777216 | tf_op jit(solution)/shard_map/attention_head/pallas_call | solution.py:236
  42.4 0.8 copy-done.1
  43.2 1.3 %collective-permute-start.2 = (bf16[2,96,192]{2,1,0:T(8,128)(2,1)S(1)}, bf16[2,96,192]{2,1,0:T(8,128)(2,1)S(1)}, u32[]{:S(2)}, u32[]{:S(2)}) collective-permute-start(bf16[2,96,192]{2,1,0:T(8,128)(2,1)S(1)} %get-tuple-element.26), channel_id=1, source_target_pairs={{0,16},{16,32},{32,48},{48,0},{64,80},{80,96},{96,112},{112,64},{1... | collective-permute-start | bytes 221192 | tf_op jit(solution)/shard_map/ppermute | solution.py:352
  44.5 1.4 %collective-permute-start.3 = (bf16[2,96,192]{2,1,0:T(8,128)(2,1)S(1)}, bf16[2,96,192]{2,1,0:T(8,128)(2,1)S(1)}, u32[]{:S(2)}, u32[]{:S(2)}) collective-permute-start(bf16[2,96,192]{2,1,0:T(8,128)(2,1)S(1)} %get-tuple-element.27), channel_id=1, source_target_pairs={{0,48},{16,0},{32,16},{48,32},{64,112},{80,64},{96,80},{112,96},{1... | collective-permute-start | bytes 221192 | tf_op jit(solution)/shard_map/ppermute | solution.py:352
  45.9 8.3 %attention_head.3 = (bf16[4,96,128]{2,1,0:T(8,128)(2,1)S(1)}, bf16[4,96,128]{2,1,0:T(8,128)(2,1)S(1)}, bf16[16,4,96,128]{3,2,1,0:T(8,128)(2,1)}, bf16[2,96,192]{...) custom-call(s32[9]{0:T(128)S(1)} %stack.48.refs_0_, ...), custom_call_target="tpu_custom_call" | custom-call | flops 1811939328 | bytes 16777216 | tf_op jit(solution)/shard_map/attention_head/pallas_call | solution.py:236
  54.2 1.2 %collective-permute-start.4 = (bf16[4,96,128]{2,1,0:T(8,128)(2,1)S(1)}, bf16[4,96,128]{2,1,0:T(8,128)(2,1)S(1)}, u32[]{:S(2)}, u32[]{:S(2)}) collective-permute-start(bf16[4,96,128]{2,1,0:T(8,128)(2,1)S(1)} %get-tuple-element.39), channel_id=1, source_target_pairs={{0,1},{1,0},{2,3},{3,2},{4,5},{5,4},{6,7},{7,6},{8,9},{9,8},{10,11... | collective-permute-start | bytes 294920 | tf_op jit(solution)/shard_map/ppermute | solution.py:320
  55.4 0.1 fusion.7
  55.5 4.4 %all-to-all-start.1 = ((bf16[16,4,96,128]{3,2,1,0:T(8,128)(2,1)}), bf16[16,4,96,128]{3,2,1,0:T(8,128)(2,1)}, u32[]{:S(2)}, u32[]{:S(2)}) async-start(bf16[16,4,96,128]{3,2,1,0:T(8,128)(2,1)} %get-tuple-element.40), calls=%async_computation.1 | async-start | bytes 3145728 | tf_op jit(solution)/shard_map/all_to_all | solution.py:371
  59.9 0.1 collective-permute-start.7
  60.1 2.6 %collective-permute-start.9 = (bf16[2,96,192]{2,1,0:T(8,128)(2,1)S(1)}, bf16[2,96,192]{2,1,0:T(8,128)(2,1)S(1)}, u32[]{:S(2)}, u32[]{:S(2)}) collective-permute-start(bf16[2,96,192]{2,1,0:T(8,128)(2,1)S(1)} %get-tuple-element.46), channel_id=1, source_target_pairs={{0,48},{16,0},{32,16},{48,32},{64,112},{80,64},{96,80},{112,96},{1... | collective-permute-start | bytes 221192 | tf_op jit(solution)/shard_map/ppermute | solution.py:352
  62.7 0.1 add_convert_fusion.3
  62.8 0.4 collective-permute-start.6
  63.2 1.2 %collective-permute-start.5 = (bf16[4,96,192]{2,1,0:T(8,128)(2,1)S(1)}, bf16[4,96,192]{2,1,0:T(8,128)(2,1)S(1)}, u32[]{:S(2)}, u32[]{:S(2)}) collective-permute-start(bf16[4,96,192]{2,1,0:T(8,128)(2,1)S(1)} %pad_maximum_fusion.1), channel_id=1, source_target_pairs={{0,16},{16,32},{32,48},{48,0},{64,80},{80,96},{96,112},{112,64},{1... | collective-permute-start | bytes 442376 | tf_op jit(solution)/shard_map/ppermute | solution.py:352
  64.5 1.0 %collective-permute-done.7 = bf16[2,96,192]{2,1,0:T(8,128)(2,1)S(1)} collective-permute-done((bf16[2,96,192]{2,1,0:T(8,128)(2,1)S(1)}, bf16[2,96,192]{2,1,0:T(8,128)(2,1)S(1)}, u32[]{:S(2)}, u32[]{:S(2)}) %collective-permute-start.7) | collective-permute-done | bytes 73760 | tf_op jit(solution)/shard_map/ppermute | solution.py:352
  65.6 2.5 %collective-permute-start.10 = (bf16[4,96,192]{2,1,0:T(8,128)(2,1)S(1)}, bf16[4,96,192]{2,1,0:T(8,128)(2,1)S(1)}, u32[]{:S(2)}, u32[]{:S(2)}) collective-permute-start(bf16[4,96,192]{2,1,0:T(8,128)(2,1)S(1)} %pad_maximum_fusion.4), channel_id=1, source_target_pairs={{0,48},{16,0},{32,16},{48,32},{64,112},{80,64},{96,80},{112,96},{1... | collective-permute-start | bytes 442376 | tf_op jit(solution)/shard_map/ppermute | solution.py:352
  68.1 0.1 collective-permute-start.8
  68.2 0.1 fusion.8
  68.3 0.4 collective-permute-done.6
  68.7 1.3 %collective-permute-done.5 = bf16[4,96,192]{2,1,0:T(8,128)(2,1)S(1)} collective-permute-done((bf16[4,96,192]{2,1,0:T(8,128)(2,1)S(1)}, bf16[4,96,192]{2,1,0:T(8,128)(2,1)S(1)}, u32[]{:S(2)}, u32[]{:S(2)}) %collective-permute-start.5) | collective-permute-done | bytes 147488 | tf_op jit(solution)/shard_map/ppermute | solution.py:352
  70.0 0.1 add_bitcast_fusion.1
  70.1 2.8 %collective-permute-done.10 = bf16[4,96,192]{2,1,0:T(8,128)(2,1)S(1)} collective-permute-done((bf16[4,96,192]{2,1,0:T(8,128)(2,1)S(1)}, bf16[4,96,192]{2,1,0:T(8,128)(2,1)S(1)}, u32[]{:S(2)}, u32[]{:S(2)}) %collective-permute-start.10) | collective-permute-done | bytes 147488 | tf_op jit(solution)/shard_map/ppermute | solution.py:352
  72.9 1.4 %collective-permute-done.8 = bf16[4,96,192]{2,1,0:T(8,128)(2,1)S(1)} collective-permute-done((bf16[4,96,192]{2,1,0:T(8,128)(2,1)S(1)}, bf16[4,96,192]{2,1,0:T(8,128)(2,1)S(1)}, u32[]{:S(2)}, u32[]{:S(2)}) %collective-permute-start.8) | collective-permute-done | bytes 147488 | tf_op jit(solution)/shard_map/ppermute | solution.py:352
  74.3 0.1 add_bitcast_fusion
  74.4 0.1 fusion
  74.5 3.4 %collective-permute-start.11 = (bf16[2,96,192]{2,1,0:T(8,128)(2,1)S(1)}, bf16[2,96,192]{2,1,0:T(8,128)(2,1)S(1)}, u32[]{:S(2)}, u32[]{:S(2)}) collective-permute-start(bf16[2,96,192]{2,1,0:T(8,128)(2,1)S(1)} %get-tuple-element.57), channel_id=1, source_target_pairs={{0,64},{16,80},{32,96},{48,112},{64,0},{80,16},{96,32},{112,48},{1... | collective-permute-start | bytes 221192 | tf_op jit(solution)/shard_map/ppermute | solution.py:352
  77.9 0.9 maximum_select_fusion.2
  78.8 3.0 %collective-permute-start.13 = (bf16[2,96,192]{2,1,0:T(8,128)(2,1)S(1)}, bf16[2,96,192]{2,1,0:T(8,128)(2,1)S(1)}, u32[]{:S(2)}, u32[]{:S(2)}) collective-permute-start(bf16[2,96,192]{2,1,0:T(8,128)(2,1)S(1)} %get-tuple-element.58), channel_id=1, source_target_pairs={{0,65},{1,64},{2,67},{3,66},{4,69},{5,68},{6,71},{7,70},{8,73},{9,... | collective-permute-start | bytes 221192 | tf_op jit(solution)/shard_map/ppermute | solution.py:390
  81.7 0.4 collective-permute-start.12
  82.2 3.3 %collective-permute-done.13 = bf16[2,96,192]{2,1,0:T(8,128)(2,1)S(1)} collective-permute-done((bf16[2,96,192]{2,1,0:T(8,128)(2,1)S(1)}, bf16[2,96,192]{2,1,0:T(8,128)(2,1)S(1)}, u32[]{:S(2)}, u32[]{:S(2)}) %collective-permute-start.13) | collective-permute-done | bytes 73760 | tf_op jit(solution)/shard_map/ppermute | solution.py:390
  85.5 0.8 maximum_select_fusion.1
  86.3 1.7 %convert_reduce_fusion = f32[2,4,96,128]{3,2,1,0:T(8,128)S(1)} fusion(bf16[8,2,4,96,128]{4,3,2,1,0:T(8,128)(2,1)} %bitcast.21), kind=kLoop, calls=%fused_computation | loop fusion | flops 1474560 | bytes 1966080 | tf_op jit(solution)/shard_map/reduce_sum | solution.py:373
  88.0 0.1 slice_bitcast_fusion.6
  88.1 0.8 fusion.4
  88.9 0.7 pad_maximum_fusion.7
  (35 shorter events, 0.4 us)
Async XLA Ops:
  3.2 7.3 %copy-start.3 = (bf16[4,96,1536]{2,1,0:T(8,128)(2,1)S(1)}, bf16[4,96,1536]{2,1,0:T(8,128)(2,1)}, u32[]{:S(2)}) copy-start(bf16[4,96,1536]{2,1,0:T(8,128)(2,1)} %param.12) | copy-start | bytes 3538948
  3.2 32.5 %all-to-all-start = ((bf16[16,464,128]{2,1,0:T(8,128)(2,1)}), bf16[16,464,128]{2,1,0:T(8,128)(2,1)S(1)}, u32[]{:S(2)}, u32[]{:S(2)}) async-start(bf16[16,464,128]{2,1,0:T(8,128)(2,1)} %prepare_exchange.1), calls=%async_computation | async-start | bytes 3801088 | tf_op jit(solution)/shard_map/all_to_all | solution.py:326
  10.5 1.3 %copy-start.5 = (bf16[4,96,128]{2,1,0:T(8,128)(2,1)S(1)}, bf16[4,96,128]{2,1,0:T(8,128)(2,1)}, u32[]{:S(2)}) copy-start(bf16[4,96,128]{2,1,0:T(8,128)(2,1)} %param.11) | copy-start | bytes 294916
  10.5 1.4 %copy-start.6 = (bf16[4,96,128]{2,1,0:T(8,128)(2,1)S(1)}, bf16[4,96,128]{2,1,0:T(8,128)(2,1)}, u32[]{:S(2)}) copy-start(bf16[4,96,128]{2,1,0:T(8,128)(2,1)} %param.8) | copy-start | bytes 294916
  10.6 2.0 %copy-start.7 = (bf16[128,128]{1,0:T(8,128)(2,1)S(1)}, bf16[128,128]{1,0:T(8,128)(2,1)}, u32[]{:S(2)}) copy-start(bf16[128,128]{1,0:T(8,128)(2,1)} %param.14) | copy-start | bytes 98308
  11.7 2.2 %collective-permute-start.1 = (bf16[2,96,1536]{2,1,0:T(8,128)(2,1)}, bf16[2,96,1536]{2,1,0:T(8,128)(2,1)S(1)}, u32[]{:S(2)}, u32[]{:S(2)}) collective-permute-start(bf16[2,96,1536]{2,1,0:T(8,128)(2,1)} %get-tuple-element.48), channel_id=1, source_target_pairs={{0,1},{1,0},{2,3},{3,2},{4,5},{5,4},{6,7},{7,6},{8,9},{9,8},{10,11... | collective-permute-start | bytes 1769480 | tf_op jit(solution)/shard_map/ppermute | solution.py:320
  12.1 4.5 %collective-permute-start = (bf16[4,96,128]{2,1,0:T(8,128)(2,1)S(1)}, bf16[4,96,128]{2,1,0:T(8,128)(2,1)S(1)}, u32[]{:S(2)}, u32[]{:S(2)}) collective-permute-start(bf16[4,96,128]{2,1,0:T(8,128)(2,1)S(1)} %pad_maximum_fusion.6), channel_id=1, source_target_pairs={{0,1},{1,0},{2,3},{3,2},{4,5},{5,4},{6,7},{7,6},{8,9},{9,8},{10,11... | collective-permute-start | bytes 294920 | tf_op jit(solution)/shard_map/ppermute | solution.py:320
  13.9 0.8 copy-start.4
  35.7 6.6 %copy-start = (bf16[16,464,128]{2,1,0:T(8,128)(2,1)}, bf16[16,464,128]{2,1,0:T(8,128)(2,1)S(1)}, u32[]{:S(2)}) copy-start(bf16[16,464,128]{2,1,0:T(8,128)(2,1)S(1)} %all-to-all-done.refs_3_.refs_4_.refs_5_) | copy-start | bytes 5701636
  42.3 0.8 copy-start.1
  43.2 11.1 %collective-permute-start.2 = (bf16[2,96,192]{2,1,0:T(8,128)(2,1)S(1)}, bf16[2,96,192]{2,1,0:T(8,128)(2,1)S(1)}, u32[]{:S(2)}, u32[]{:S(2)}) collective-permute-start(bf16[2,96,192]{2,1,0:T(8,128)(2,1)S(1)} %get-tuple-element.26), channel_id=1, source_target_pairs={{0,16},{16,32},{32,48},{48,0},{64,80},{80,96},{96,112},{112,64},{1... | collective-permute-start | bytes 221192 | tf_op jit(solution)/shard_map/ppermute | solution.py:352
  44.5 9.8 %collective-permute-start.3 = (bf16[2,96,192]{2,1,0:T(8,128)(2,1)S(1)}, bf16[2,96,192]{2,1,0:T(8,128)(2,1)S(1)}, u32[]{:S(2)}, u32[]{:S(2)}) collective-permute-start(bf16[2,96,192]{2,1,0:T(8,128)(2,1)S(1)} %get-tuple-element.27), channel_id=1, source_target_pairs={{0,48},{16,0},{32,16},{48,32},{64,112},{80,64},{96,80},{112,96},{1... | collective-permute-start | bytes 221192 | tf_op jit(solution)/shard_map/ppermute | solution.py:352
  54.2 14.0 %collective-permute-start.4 = (bf16[4,96,128]{2,1,0:T(8,128)(2,1)S(1)}, bf16[4,96,128]{2,1,0:T(8,128)(2,1)S(1)}, u32[]{:S(2)}, u32[]{:S(2)}) collective-permute-start(bf16[4,96,128]{2,1,0:T(8,128)(2,1)S(1)} %get-tuple-element.39), channel_id=1, source_target_pairs={{0,1},{1,0},{2,3},{3,2},{4,5},{5,4},{6,7},{7,6},{8,9},{9,8},{10,11... | collective-permute-start | bytes 294920 | tf_op jit(solution)/shard_map/ppermute | solution.py:320
  55.5 7.2 %copy-start.2 = (bf16[12,96,192]{2,1,0:T(8,128)(2,1)S(1)}, bf16[12,96,192]{2,1,0:T(8,128)(2,1)}, u32[]{:S(2)}) copy-start(bf16[12,96,192]{2,1,0:T(8,128)(2,1)} %copy-done.1) | copy-start | bytes 1327108
  55.5 30.8 %all-to-all-start.1 = ((bf16[16,4,96,128]{3,2,1,0:T(8,128)(2,1)}), bf16[16,4,96,128]{3,2,1,0:T(8,128)(2,1)}, u32[]{:S(2)}, u32[]{:S(2)}) async-start(bf16[16,4,96,128]{3,2,1,0:T(8,128)(2,1)} %get-tuple-element.40), calls=%async_computation.1 | async-start | bytes 3145728 | tf_op jit(solution)/shard_map/all_to_all | solution.py:371
  59.9 5.5 %collective-permute-start.7 = (bf16[2,96,192]{2,1,0:T(8,128)(2,1)S(1)}, bf16[2,96,192]{2,1,0:T(8,128)(2,1)S(1)}, u32[]{:S(2)}, u32[]{:S(2)}) collective-permute-start(bf16[2,96,192]{2,1,0:T(8,128)(2,1)S(1)} %get-tuple-element.45), channel_id=1, source_target_pairs={{0,16},{16,32},{32,48},{48,0},{64,80},{80,96},{96,112},{112,64},{1... | collective-permute-start | bytes 221192 | tf_op jit(solution)/shard_map/ppermute | solution.py:352
  60.1 5.4 %collective-permute-start.9 = (bf16[2,96,192]{2,1,0:T(8,128)(2,1)S(1)}, bf16[2,96,192]{2,1,0:T(8,128)(2,1)S(1)}, u32[]{:S(2)}, u32[]{:S(2)}) collective-permute-start(bf16[2,96,192]{2,1,0:T(8,128)(2,1)S(1)} %get-tuple-element.46), channel_id=1, source_target_pairs={{0,48},{16,0},{32,16},{48,32},{64,112},{80,64},{96,80},{112,96},{1... | collective-permute-start | bytes 221192 | tf_op jit(solution)/shard_map/ppermute | solution.py:352
  62.8 5.9 %collective-permute-start.6 = (bf16[4,96,192]{2,1,0:T(8,128)(2,1)S(1)}, bf16[4,96,192]{2,1,0:T(8,128)(2,1)S(1)}, u32[]{:S(2)}, u32[]{:S(2)}) collective-permute-start(bf16[4,96,192]{2,1,0:T(8,128)(2,1)S(1)} %pad_maximum_fusion.2), channel_id=1, source_target_pairs={{0,48},{16,0},{32,16},{48,32},{64,112},{80,64},{96,80},{112,96},{1... | collective-permute-start | bytes 442376 | tf_op jit(solution)/shard_map/ppermute | solution.py:352
  63.2 6.8 %collective-permute-start.5 = (bf16[4,96,192]{2,1,0:T(8,128)(2,1)S(1)}, bf16[4,96,192]{2,1,0:T(8,128)(2,1)S(1)}, u32[]{:S(2)}, u32[]{:S(2)}) collective-permute-start(bf16[4,96,192]{2,1,0:T(8,128)(2,1)S(1)} %pad_maximum_fusion.1), channel_id=1, source_target_pairs={{0,16},{16,32},{32,48},{48,0},{64,80},{80,96},{96,112},{112,64},{1... | collective-permute-start | bytes 442376 | tf_op jit(solution)/shard_map/ppermute | solution.py:352
  65.6 7.4 %collective-permute-start.10 = (bf16[4,96,192]{2,1,0:T(8,128)(2,1)S(1)}, bf16[4,96,192]{2,1,0:T(8,128)(2,1)S(1)}, u32[]{:S(2)}, u32[]{:S(2)}) collective-permute-start(bf16[4,96,192]{2,1,0:T(8,128)(2,1)S(1)} %pad_maximum_fusion.4), channel_id=1, source_target_pairs={{0,48},{16,0},{32,16},{48,32},{64,112},{80,64},{96,80},{112,96},{1... | collective-permute-start | bytes 442376 | tf_op jit(solution)/shard_map/ppermute | solution.py:352
  68.1 6.2 %collective-permute-start.8 = (bf16[4,96,192]{2,1,0:T(8,128)(2,1)S(1)}, bf16[4,96,192]{2,1,0:T(8,128)(2,1)S(1)}, u32[]{:S(2)}, u32[]{:S(2)}) collective-permute-start(bf16[4,96,192]{2,1,0:T(8,128)(2,1)S(1)} %pad_maximum_fusion.3), channel_id=1, source_target_pairs={{0,16},{16,32},{32,48},{48,0},{64,80},{80,96},{96,112},{112,64},{1... | collective-permute-start | bytes 442376 | tf_op jit(solution)/shard_map/ppermute | solution.py:352
  74.5 7.6 %collective-permute-start.11 = (bf16[2,96,192]{2,1,0:T(8,128)(2,1)S(1)}, bf16[2,96,192]{2,1,0:T(8,128)(2,1)S(1)}, u32[]{:S(2)}, u32[]{:S(2)}) collective-permute-start(bf16[2,96,192]{2,1,0:T(8,128)(2,1)S(1)} %get-tuple-element.57), channel_id=1, source_target_pairs={{0,64},{16,80},{32,96},{48,112},{64,0},{80,16},{96,32},{112,48},{1... | collective-permute-start | bytes 221192 | tf_op jit(solution)/shard_map/ppermute | solution.py:352
  78.8 6.7 %collective-permute-start.13 = (bf16[2,96,192]{2,1,0:T(8,128)(2,1)S(1)}, bf16[2,96,192]{2,1,0:T(8,128)(2,1)S(1)}, u32[]{:S(2)}, u32[]{:S(2)}) collective-permute-start(bf16[2,96,192]{2,1,0:T(8,128)(2,1)S(1)} %get-tuple-element.58), channel_id=1, source_target_pairs={{0,65},{1,64},{2,67},{3,66},{4,69},{5,68},{6,71},{7,70},{8,73},{9,... | collective-permute-start | bytes 221192 | tf_op jit(solution)/shard_map/ppermute | solution.py:390
  81.7 3.7 %collective-permute-start.12 = (bf16[2,96,192]{2,1,0:T(8,128)(2,1)S(1)}, bf16[2,96,192]{2,1,0:T(8,128)(2,1)S(1)}, u32[]{:S(2)}, u32[]{:S(2)}) collective-permute-start(bf16[2,96,192]{2,1,0:T(8,128)(2,1)S(1)} %get-tuple-element.59), channel_id=1, source_target_pairs={{0,1},{1,0},{2,3},{3,2},{4,5},{5,4},{6,7},{7,6},{8,9},{9,8},{10,11... | collective-permute-start | bytes 221192 | tf_op jit(solution)/shard_map/ppermute | solution.py:320

commit v11 on v9

--- a/solution.py
+++ b/solution.py
@@ -365,10 +365,13 @@
         (from_left, from_right, bias_rest, second)
     )
     bias_right_2, bias_left_2, bias_rest_2, kv_grads, qa_own, qa_away = second
+    qa_back = swapped(qa_away)
+    from_left, from_right, bias_right_2, bias_left_2, qa_back = lax.optimization_barrier(
+        (from_left, from_right, bias_right_2, bias_left_2, qa_back)
+    )
     from_left, from_right = ring_onward(bias_rest, from_left, from_right)
     sums = added(bias_rest[:4], from_left, from_right)
     from_left, from_right = along_row(bias_right_2, 1, 0), along_row(bias_left_2, -1, 0)
-    from_left, from_right, kv_grads = lax.optimization_barrier((from_left, from_right, kv_grads))
     kv_parts = lax.all_to_all(kv_grads, "col", 0, 0, tiled=True)
     kv_parts = kv_parts.reshape((devices // 2, 2) + kv_parts.shape[1:])
     kv_sum = jnp.sum(kv_parts.astype(jnp.float32), axis=0)
@@ -378,7 +381,6 @@
     value_gradient = value_gradient.astype(jnp.bfloat16)
     from_left, from_right = ring_onward(bias_rest_2, from_left, from_right)
     sums = jnp.stack([sums, added(bias_rest_2[:4], from_left, from_right)], axis=1)
-    qa_back = swapped(qa_away)
     query_gradient = in_order(qa_own[..., :half], qa_back[..., :half], 2)
     gate_gradient = in_order(qa_own[..., half:], qa_back[..., half:], 2)
     low_sums = sums.astype(jnp.bfloat16)

time: 92.7 us -> 87.6 us (0.945)
  waiting for transfers between devices: 35.1 us -> 28.8 us
  starting transfers between devices: 27.9 us -> 30 us
    all_to_all x1, waiting for transfers between devices: 4.33 us -> 0.26 us  [local(): kv_parts = lax.all_to_all(kv_grads, 'col', 0, 0, tiled=True)]
    ppermute x9, waiting for transfers between devices: 9.5 us -> 6.11 us  [along_row(): return lax.ppermute(array, 'row', pairs)]
    ppermute x4, starting transfers between devices: 2.62 us -> 5.01 us  [swapped(): return lax.ppermute(array, 'col', swap)]
    ppermute x1, waiting for transfers between devices: 1.1 us -> 2.27 us  [local(): lax.ppermute(low_sums[3], ('row', 'col'), diagonal)]
  transfers between devices with their start and end apart: 16 -> 16, of which waited for: 7 -> 9; matrix products, arithmetic and copies ran while one was open for 10% -> 10% of each run, Pallas kernels for 9% -> 10%
where the time goes in v11:
time: 87.6 us; the launch traced here: 87.2 us
  starting transfers between devices  30 us (34%)
  waiting for transfers between devices  28.8 us (33%)
  Pallas kernels  17.5 us (20%)
  other arithmetic  8.73 us (10%)
  local copies, waits for them, and re-layouts  1.31 us (1%)
  between operations  0.91 us (1%)
    all_to_all x1, waiting for transfers between devices, local(): received = lax.all_to_all(packed, 'col', 0, 0, tiled=True)  19.1 us
    pallas_call x2, Pallas kernels, attend(): pl.pallas_call(functools.partial(attention_kernel, head), grid_spec=pltpu...  14.9 us
    ppermute x9, starting transfers between devices, along_row(): return lax.ppermute(array, 'row', pairs)  13.2 us
    all_to_all x1, starting transfers between devices, local(): received = lax.all_to_all(packed, 'col', 0, 0, tiled=True)  7.3 us
    ppermute x9, waiting for transfers between devices, along_row(): return lax.ppermute(array, 'row', pairs)  6.11 us
    ppermute x4, starting transfers between devices, swapped(): return lax.ppermute(array, 'col', swap)  5.01 us
    all_to_all x1, starting transfers between devices, local(): kv_parts = lax.all_to_all(kv_grads, 'col', 0, 0, tiled=True)  4.44 us
    select_n x3, other arithmetic, in_order(): jnp.where(core == 0, jnp.concatenate([mine, other], axis=axis), jnp.conca...  3.55 us
  transfers between devices with their start and end apart: 16, of which 9 were waited for; matrix products, arithmetic and copies ran while one was open for 10% of the time, Pallas kernels for 10%

profile of v11, /device:TPU:1, one launch (start us, length us, event | category | flops | bytes accessed | tf_op | source)
XLA Modules:
  0.0 87.2 jit_solution(5048956441736307070)
XLA Ops:
  0.6 2.6 %prepare_exchange.1 = bf16[16,464,128]{2,1,0:T(8,128)(2,1)} custom-call(bf16[4,96,128]{2,1,0:T(8,128)(2,1)} %key_ref.1, bf16[4,96,128]{2,1,0:T(8,128)(2,1)} %value_ref.1, s32[4,96]{1,0:T(4,128)} %mask_ref.1, bf16[4,8,1536]{2,1,0:T(8,128)(2,1)} %cotangent_ref.1), custom_call_target="tpu_custom_call" | custom-call | tf_op jit(solution)/shard_map/prepare_exchange/pallas_call | solution.py:209
  3.2 7.3 %all-to-all-start = ((bf16[16,464,128]{2,1,0:T(8,128)(2,1)}), bf16[16,464,128]{2,1,0:T(8,128)(2,1)S(1)}, u32[]{:S(2)}, u32[]{:S(2)}) async-start(bf16[16,464,128]{2,1,0:T(8,128)(2,1)} %prepare_exchange.1), calls=%async_computation | async-start | bytes 3801088 | tf_op jit(solution)/shard_map/all_to_all | solution.py:326
  10.5 0.0 copy-start.6
  10.6 1.1 %broadcast_select_fusion.1 = (bf16[2,96,1536]{2,1,0:T(8,128)(2,1)}, bf16[2,96,1536]{2,1,0:T(8,128)(2,1)}) fusion(pred[]{:T(512)S(6)} %eq.31, bf16[4,96,1536]{2,1,0:T(8,128)(2,1)S(1)} %copy-done.3), kind=kLoop, calls=%fused_computation.7 | loop fusion | flops 589824 | bytes 2359297 | tf_op jit(solution)/shard_map/jit(_where)/select_n | solution.py:310
  11.7 0.1 collective-permute-start.1
  11.8 0.1 broadcast_select_fusion.2
  11.9 0.1 broadcast_select_fusion.3
  12.0 0.1 pad_maximum_fusion.6
  12.1 0.5 collective-permute-start
  12.6 0.1 stack.48.refs_0_
  12.7 0.1 pad_maximum_fusion.5.refs_1_
  12.8 1.1 %collective-permute-done.1 = bf16[2,96,1536]{2,1,0:T(8,128)(2,1)S(1)} collective-permute-done((bf16[2,96,1536]{2,1,0:T(8,128)(2,1)}, bf16[2,96,1536]{2,1,0:T(8,128)(2,1)S(1)}, u32[]{:S(2)}, u32[]{:S(2)}) %collective-permute-start.1) | collective-permute-done | bytes 589856 | tf_op jit(solution)/shard_map/ppermute | solution.py:320
  13.9 0.8 copy-done.4
  14.7 1.9 %maximum_select_fusion = bf16[2,192,1536]{2,1,0:T(8,128)(2,1)S(1)} fusion(bf16[2,96,1536]{2,1,0:T(8,128)(2,1)} %copy-done.4, bf16[2,96,1536]{2,1,0:T(8,128)(2,1)} %get-tuple-element.67, pred[]{:T(512)S(6)} %eq.31), kind=kLoop, calls=%fused_computation.1 | loop fusion | flops 5308416 | bytes 2359297 | tf_op jit(solution)/shard_map/jit(_where)/select_n | solution.py:313
  16.6 19.1 %all-to-all-done.refs_3_.refs_4_.refs_5_ = bf16[16,464,128]{2,1,0:T(8,128)(2,1)S(1)} async-done(((bf16[16,464,128]{2,1,0:T(8,128)(2,1)}), bf16[16,464,128]{2,1,0:T(8,128)(2,1)S(1)}, u32[]{:S(2)}, u32[]{:S(2)}) %all-to-all-start) | async-done | bytes 1900576 | tf_op jit(solution)/shard_map/all_to_all | solution.py:326
  35.7 6.6 %attention_head.2 = (bf16[4,96,128]{2,1,0:T(8,128)(2,1)S(1)}, bf16[4,96,128]{2,1,0:T(8,128)(2,1)S(1)}, bf16[16,4,96,128]{3,2,1,0:T(8,128)(2,1)S(1)}, bf16[2,96,1...) custom-call(s32[9]{0:T(128)S(1)} %stack.48.refs_0_, ...), custom_call_target="tpu_custom_call" | custom-call | flops 1811939328 | bytes 16777216 | tf_op jit(solution)/shard_map/attention_head/pallas_call | solution.py:236
  42.4 1.4 %collective-permute-start.2 = (bf16[2,96,192]{2,1,0:T(8,128)(2,1)S(1)}, bf16[2,96,192]{2,1,0:T(8,128)(2,1)S(1)}, u32[]{:S(2)}, u32[]{:S(2)}) collective-permute-start(bf16[2,96,192]{2,1,0:T(8,128)(2,1)S(1)} %get-tuple-element.36), channel_id=1, source_target_pairs={{0,16},{16,32},{32,48},{48,0},{64,80},{80,96},{96,112},{112,64},{1... | collective-permute-start | bytes 221192 | tf_op jit(solution)/shard_map/ppermute | solution.py:352
  43.7 1.5 %collective-permute-start.3 = (bf16[2,96,192]{2,1,0:T(8,128)(2,1)S(1)}, bf16[2,96,192]{2,1,0:T(8,128)(2,1)S(1)}, u32[]{:S(2)}, u32[]{:S(2)}) collective-permute-start(bf16[2,96,192]{2,1,0:T(8,128)(2,1)S(1)} %get-tuple-element.37), channel_id=1, source_target_pairs={{0,48},{16,0},{32,16},{48,32},{64,112},{80,64},{96,80},{112,96},{1... | collective-permute-start | bytes 221192 | tf_op jit(solution)/shard_map/ppermute | solution.py:352
  45.2 8.3 %attention_head.3 = (bf16[4,96,128]{2,1,0:T(8,128)(2,1)S(1)}, bf16[4,96,128]{2,1,0:T(8,128)(2,1)S(1)}, bf16[16,4,96,128]{3,2,1,0:T(8,128)(2,1)}, bf16[2,96,192]{...) custom-call(s32[9]{0:T(128)S(1)} %stack.48.refs_0_, ...), custom_call_target="tpu_custom_call" | custom-call | flops 1811939328 | bytes 16777216 | tf_op jit(solution)/shard_map/attention_head/pallas_call | solution.py:236
  53.5 1.1 %collective-permute-start.4 = (bf16[4,96,128]{2,1,0:T(8,128)(2,1)S(1)}, bf16[4,96,128]{2,1,0:T(8,128)(2,1)S(1)}, u32[]{:S(2)}, u32[]{:S(2)}) collective-permute-start(bf16[4,96,128]{2,1,0:T(8,128)(2,1)S(1)} %get-tuple-element.53), channel_id=1, source_target_pairs={{0,1},{1,0},{2,3},{3,2},{4,5},{5,4},{6,7},{7,6},{8,9},{9,8},{10,11... | collective-permute-start | bytes 294920 | tf_op jit(solution)/shard_map/ppermute | solution.py:320
  54.6 0.1 fusion.6
  54.8 4.4 %all-to-all-start.1 = ((bf16[16,4,96,128]{3,2,1,0:T(8,128)(2,1)}), bf16[16,4,96,128]{3,2,1,0:T(8,128)(2,1)}, u32[]{:S(2)}, u32[]{:S(2)}) async-start(bf16[16,4,96,128]{3,2,1,0:T(8,128)(2,1)} %get-tuple-element.61), calls=%async_computation.1 | async-start | bytes 3145728 | tf_op jit(solution)/shard_map/all_to_all | solution.py:375
  59.3 0.2 collective-permute-start.7
  59.4 2.6 %collective-permute-start.9 = (bf16[2,96,192]{2,1,0:T(8,128)(2,1)S(1)}, bf16[2,96,192]{2,1,0:T(8,128)(2,1)S(1)}, u32[]{:S(2)}, u32[]{:S(2)}) collective-permute-start(bf16[2,96,192]{2,1,0:T(8,128)(2,1)S(1)} %get-tuple-element.60), channel_id=1, source_target_pairs={{0,48},{16,0},{32,16},{48,32},{64,112},{80,64},{96,80},{112,96},{1... | collective-permute-start | bytes 221192 | tf_op jit(solution)/shard_map/ppermute | solution.py:352
  62.0 0.1 add_convert_fusion.3
  62.1 0.4 collective-permute-start.6
  62.5 1.2 %collective-permute-start.5 = (bf16[4,96,192]{2,1,0:T(8,128)(2,1)S(1)}, bf16[4,96,192]{2,1,0:T(8,128)(2,1)S(1)}, u32[]{:S(2)}, u32[]{:S(2)}) collective-permute-start(bf16[4,96,192]{2,1,0:T(8,128)(2,1)S(1)} %pad_maximum_fusion.1), channel_id=1, source_target_pairs={{0,16},{16,32},{32,48},{48,0},{64,80},{80,96},{96,112},{112,64},{1... | collective-permute-start | bytes 442376 | tf_op jit(solution)/shard_map/ppermute | solution.py:352
  63.7 0.1 fusion.7
  63.8 0.9 %maximum_select_fusion.2 = (bf16[4,96,128]{2,1,0:T(8,128)(2,1)}, bf16[4,96,128]{2,1,0:T(8,128)(2,1)}) fusion(bf16[4,96,64]{2,1,0:T(8,128)(2,1)S(1)} %get-tuple-element.87, bf16[4,96,64]{2,1,0:T(8,128)(2,1)S(1)} %get-tuple-element.85, pred[]{:T(512)S(6)} %eq.31, bf16[4,96,64]{2,1,0:T(8,128)(2,1)S(1)} %get-tuple-element.84, ...), kind=kLoop, calls=%fused_computation.34 | loop fusion | flops 884736 | bytes 393217 | tf_op jit(solution)/shard_map/jit(_where)/select_n | solution.py:313
  64.7 0.1 collective-permute-done.7
  64.8 0.1 add_convert_fusion.1
  64.9 2.5 %collective-permute-start.10 = (bf16[4,96,192]{2,1,0:T(8,128)(2,1)S(1)}, bf16[4,96,192]{2,1,0:T(8,128)(2,1)S(1)}, u32[]{:S(2)}, u32[]{:S(2)}) collective-permute-start(bf16[4,96,192]{2,1,0:T(8,128)(2,1)S(1)} %pad_maximum_fusion.4), channel_id=1, source_target_pairs={{0,48},{16,0},{32,16},{48,32},{64,112},{80,64},{96,80},{112,96},{1... | collective-permute-start | bytes 442376 | tf_op jit(solution)/shard_map/ppermute | solution.py:352
  67.5 0.1 collective-permute-start.8
  67.5 0.5 collective-permute-done.6
  68.0 1.3 %collective-permute-done.5 = bf16[4,96,192]{2,1,0:T(8,128)(2,1)S(1)} collective-permute-done((bf16[4,96,192]{2,1,0:T(8,128)(2,1)S(1)}, bf16[4,96,192]{2,1,0:T(8,128)(2,1)S(1)}, u32[]{:S(2)}, u32[]{:S(2)}) %collective-permute-start.5) | collective-permute-done | bytes 147488 | tf_op jit(solution)/shard_map/ppermute | solution.py:352
  69.3 0.1 add_bitcast_fusion.1
  69.4 2.8 %collective-permute-done.10 = bf16[4,96,192]{2,1,0:T(8,128)(2,1)S(1)} collective-permute-done((bf16[4,96,192]{2,1,0:T(8,128)(2,1)S(1)}, bf16[4,96,192]{2,1,0:T(8,128)(2,1)S(1)}, u32[]{:S(2)}, u32[]{:S(2)}) %collective-permute-start.10) | collective-permute-done | bytes 147488 | tf_op jit(solution)/shard_map/ppermute | solution.py:352
  72.2 1.4 %collective-permute-done.8 = bf16[4,96,192]{2,1,0:T(8,128)(2,1)S(1)} collective-permute-done((bf16[4,96,192]{2,1,0:T(8,128)(2,1)S(1)}, bf16[4,96,192]{2,1,0:T(8,128)(2,1)S(1)}, u32[]{:S(2)}, u32[]{:S(2)}) %collective-permute-start.8) | collective-permute-done | bytes 147488 | tf_op jit(solution)/shard_map/ppermute | solution.py:352
  73.7 0.1 add_bitcast_fusion
  73.8 3.4 %collective-permute-start.11 = (bf16[2,96,192]{2,1,0:T(8,128)(2,1)S(1)}, bf16[2,96,192]{2,1,0:T(8,128)(2,1)S(1)}, u32[]{:S(2)}, u32[]{:S(2)}) collective-permute-start(bf16[2,96,192]{2,1,0:T(8,128)(2,1)S(1)} %get-tuple-element.81), channel_id=1, source_target_pairs={{0,64},{16,80},{32,96},{48,112},{64,0},{80,16},{96,32},{112,48},{1... | collective-permute-start | bytes 221192 | tf_op jit(solution)/shard_map/ppermute | solution.py:352
  77.2 3.3 %collective-permute-start.12 = (bf16[2,96,192]{2,1,0:T(8,128)(2,1)S(1)}, bf16[2,96,192]{2,1,0:T(8,128)(2,1)S(1)}, u32[]{:S(2)}, u32[]{:S(2)}) collective-permute-start(bf16[2,96,192]{2,1,0:T(8,128)(2,1)S(1)} %get-tuple-element.80), channel_id=1, source_target_pairs={{0,1},{1,0},{2,3},{3,2},{4,5},{5,4},{6,7},{7,6},{8,9},{9,8},{10,11... | collective-permute-start | bytes 221192 | tf_op jit(solution)/shard_map/ppermute | solution.py:320
  80.5 0.3 all-to-all-done.1
  80.8 1.7 %convert_reduce_fusion = f32[2,4,96,128]{3,2,1,0:T(8,128)S(1)} fusion(bf16[8,2,4,96,128]{4,3,2,1,0:T(8,128)(2,1)} %bitcast.21), kind=kLoop, calls=%fused_computation | loop fusion | flops 1474560 | bytes 1966080 | tf_op jit(solution)/shard_map/reduce_sum | solution.py:377
  82.5 0.1 slice_bitcast_fusion.3
  82.6 0.8 fusion.3
  83.4 0.7 pad_maximum_fusion.7
  84.1 2.3 %collective-permute-done.13 = bf16[2,96,192]{2,1,0:T(8,128)(2,1)S(1)} collective-permute-done((bf16[2,96,192]{2,1,0:T(8,128)(2,1)S(1)}, bf16[2,96,192]{2,1,0:T(8,128)(2,1)S(1)}, u32[]{:S(2)}, u32[]{:S(2)}) %collective-permute-start.13) | collective-permute-done | bytes 73760 | tf_op jit(solution)/shard_map/ppermute | solution.py:394
  86.5 0.8 maximum_select_fusion.1
  (34 shorter events, 0.4 us)
Async XLA Ops:
  3.2 7.3 %copy-start.3 = (bf16[4,96,1536]{2,1,0:T(8,128)(2,1)S(1)}, bf16[4,96,1536]{2,1,0:T(8,128)(2,1)}, u32[]{:S(2)}) copy-start(bf16[4,96,1536]{2,1,0:T(8,128)(2,1)} %param.12) | copy-start | bytes 3538948
  3.2 32.5 %all-to-all-start = ((bf16[16,464,128]{2,1,0:T(8,128)(2,1)}), bf16[16,464,128]{2,1,0:T(8,128)(2,1)S(1)}, u32[]{:S(2)}, u32[]{:S(2)}) async-start(bf16[16,464,128]{2,1,0:T(8,128)(2,1)} %prepare_exchange.1), calls=%async_computation | async-start | bytes 3801088 | tf_op jit(solution)/shard_map/all_to_all | solution.py:326
  10.5 1.3 %copy-start.5 = (bf16[4,96,128]{2,1,0:T(8,128)(2,1)S(1)}, bf16[4,96,128]{2,1,0:T(8,128)(2,1)}, u32[]{:S(2)}) copy-start(bf16[4,96,128]{2,1,0:T(8,128)(2,1)} %param.11) | copy-start | bytes 294916
  10.5 1.4 %copy-start.6 = (bf16[4,96,128]{2,1,0:T(8,128)(2,1)S(1)}, bf16[4,96,128]{2,1,0:T(8,128)(2,1)}, u32[]{:S(2)}) copy-start(bf16[4,96,128]{2,1,0:T(8,128)(2,1)} %param.8) | copy-start | bytes 294916
  10.6 2.0 %copy-start.7 = (bf16[128,128]{1,0:T(8,128)(2,1)S(1)}, bf16[128,128]{1,0:T(8,128)(2,1)}, u32[]{:S(2)}) copy-start(bf16[128,128]{1,0:T(8,128)(2,1)} %param.14) | copy-start | bytes 98308
  11.7 2.2 %collective-permute-start.1 = (bf16[2,96,1536]{2,1,0:T(8,128)(2,1)}, bf16[2,96,1536]{2,1,0:T(8,128)(2,1)S(1)}, u32[]{:S(2)}, u32[]{:S(2)}) collective-permute-start(bf16[2,96,1536]{2,1,0:T(8,128)(2,1)} %get-tuple-element.68), channel_id=1, source_target_pairs={{0,1},{1,0},{2,3},{3,2},{4,5},{5,4},{6,7},{7,6},{8,9},{9,8},{10,11... | collective-permute-start | bytes 1769480 | tf_op jit(solution)/shard_map/ppermute | solution.py:320
  12.1 4.5 %collective-permute-start = (bf16[4,96,128]{2,1,0:T(8,128)(2,1)S(1)}, bf16[4,96,128]{2,1,0:T(8,128)(2,1)S(1)}, u32[]{:S(2)}, u32[]{:S(2)}) collective-permute-start(bf16[4,96,128]{2,1,0:T(8,128)(2,1)S(1)} %pad_maximum_fusion.6), channel_id=1, source_target_pairs={{0,1},{1,0},{2,3},{3,2},{4,5},{5,4},{6,7},{7,6},{8,9},{9,8},{10,11... | collective-permute-start | bytes 294920 | tf_op jit(solution)/shard_map/ppermute | solution.py:320
  13.9 0.8 copy-start.4
  35.7 6.6 %copy-start = (bf16[16,464,128]{2,1,0:T(8,128)(2,1)}, bf16[16,464,128]{2,1,0:T(8,128)(2,1)S(1)}, u32[]{:S(2)}) copy-start(bf16[16,464,128]{2,1,0:T(8,128)(2,1)S(1)} %all-to-all-done.refs_3_.refs_4_.refs_5_) | copy-start | bytes 5701636
  42.3 12.4 %copy-start.1 = (bf16[12,96,192]{2,1,0:T(8,128)(2,1)}, bf16[12,96,192]{2,1,0:T(8,128)(2,1)S(1)}, u32[]{:S(2)}) copy-start(bf16[12,96,192]{2,1,0:T(8,128)(2,1)S(1)} %get-tuple-element.55) | copy-start | bytes 1327108
  42.4 11.2 %collective-permute-start.2 = (bf16[2,96,192]{2,1,0:T(8,128)(2,1)S(1)}, bf16[2,96,192]{2,1,0:T(8,128)(2,1)S(1)}, u32[]{:S(2)}, u32[]{:S(2)}) collective-permute-start(bf16[2,96,192]{2,1,0:T(8,128)(2,1)S(1)} %get-tuple-element.36), channel_id=1, source_target_pairs={{0,16},{16,32},{32,48},{48,0},{64,80},{80,96},{96,112},{112,64},{1... | collective-permute-start | bytes 221192 | tf_op jit(solution)/shard_map/ppermute | solution.py:352
  43.7 9.8 %collective-permute-start.3 = (bf16[2,96,192]{2,1,0:T(8,128)(2,1)S(1)}, bf16[2,96,192]{2,1,0:T(8,128)(2,1)S(1)}, u32[]{:S(2)}, u32[]{:S(2)}) collective-permute-start(bf16[2,96,192]{2,1,0:T(8,128)(2,1)S(1)} %get-tuple-element.37), channel_id=1, source_target_pairs={{0,48},{16,0},{32,16},{48,32},{64,112},{80,64},{96,80},{112,96},{1... | collective-permute-start | bytes 221192 | tf_op jit(solution)/shard_map/ppermute | solution.py:352
  53.5 5.7 %collective-permute-start.4 = (bf16[4,96,128]{2,1,0:T(8,128)(2,1)S(1)}, bf16[4,96,128]{2,1,0:T(8,128)(2,1)S(1)}, u32[]{:S(2)}, u32[]{:S(2)}) collective-permute-start(bf16[4,96,128]{2,1,0:T(8,128)(2,1)S(1)} %get-tuple-element.53), channel_id=1, source_target_pairs={{0,1},{1,0},{2,3},{3,2},{4,5},{5,4},{6,7},{7,6},{8,9},{9,8},{10,11... | collective-permute-start | bytes 294920 | tf_op jit(solution)/shard_map/ppermute | solution.py:320
  54.8 7.2 %copy-start.2 = (bf16[12,96,192]{2,1,0:T(8,128)(2,1)S(1)}, bf16[12,96,192]{2,1,0:T(8,128)(2,1)}, u32[]{:S(2)}) copy-start(bf16[12,96,192]{2,1,0:T(8,128)(2,1)} %copy-done.1) | copy-start | bytes 1327108
  54.8 26.0 %all-to-all-start.1 = ((bf16[16,4,96,128]{3,2,1,0:T(8,128)(2,1)}), bf16[16,4,96,128]{3,2,1,0:T(8,128)(2,1)}, u32[]{:S(2)}, u32[]{:S(2)}) async-start(bf16[16,4,96,128]{3,2,1,0:T(8,128)(2,1)} %get-tuple-element.61), calls=%async_computation.1 | async-start | bytes 3145728 | tf_op jit(solution)/shard_map/all_to_all | solution.py:375
  59.3 5.5 %collective-permute-start.7 = (bf16[2,96,192]{2,1,0:T(8,128)(2,1)S(1)}, bf16[2,96,192]{2,1,0:T(8,128)(2,1)S(1)}, u32[]{:S(2)}, u32[]{:S(2)}) collective-permute-start(bf16[2,96,192]{2,1,0:T(8,128)(2,1)S(1)} %get-tuple-element.59), channel_id=1, source_target_pairs={{0,16},{16,32},{32,48},{48,0},{64,80},{80,96},{96,112},{112,64},{1... | collective-permute-start | bytes 221192 | tf_op jit(solution)/shard_map/ppermute | solution.py:352
  59.4 5.4 %collective-permute-start.9 = (bf16[2,96,192]{2,1,0:T(8,128)(2,1)S(1)}, bf16[2,96,192]{2,1,0:T(8,128)(2,1)S(1)}, u32[]{:S(2)}, u32[]{:S(2)}) collective-permute-start(bf16[2,96,192]{2,1,0:T(8,128)(2,1)S(1)} %get-tuple-element.60), channel_id=1, source_target_pairs={{0,48},{16,0},{32,16},{48,32},{64,112},{80,64},{96,80},{112,96},{1... | collective-permute-start | bytes 221192 | tf_op jit(solution)/shard_map/ppermute | solution.py:352
  62.1 5.9 %collective-permute-start.6 = (bf16[4,96,192]{2,1,0:T(8,128)(2,1)S(1)}, bf16[4,96,192]{2,1,0:T(8,128)(2,1)S(1)}, u32[]{:S(2)}, u32[]{:S(2)}) collective-permute-start(bf16[4,96,192]{2,1,0:T(8,128)(2,1)S(1)} %pad_maximum_fusion.2), channel_id=1, source_target_pairs={{0,48},{16,0},{32,16},{48,32},{64,112},{80,64},{96,80},{112,96},{1... | collective-permute-start | bytes 442376 | tf_op jit(solution)/shard_map/ppermute | solution.py:352
  62.5 6.8 %collective-permute-start.5 = (bf16[4,96,192]{2,1,0:T(8,128)(2,1)S(1)}, bf16[4,96,192]{2,1,0:T(8,128)(2,1)S(1)}, u32[]{:S(2)}, u32[]{:S(2)}) collective-permute-start(bf16[4,96,192]{2,1,0:T(8,128)(2,1)S(1)} %pad_maximum_fusion.1), channel_id=1, source_target_pairs={{0,16},{16,32},{32,48},{48,0},{64,80},{80,96},{96,112},{112,64},{1... | collective-permute-start | bytes 442376 | tf_op jit(solution)/shard_map/ppermute | solution.py:352
  64.9 7.3 %collective-permute-start.10 = (bf16[4,96,192]{2,1,0:T(8,128)(2,1)S(1)}, bf16[4,96,192]{2,1,0:T(8,128)(2,1)S(1)}, u32[]{:S(2)}, u32[]{:S(2)}) collective-permute-start(bf16[4,96,192]{2,1,0:T(8,128)(2,1)S(1)} %pad_maximum_fusion.4), channel_id=1, source_target_pairs={{0,48},{16,0},{32,16},{48,32},{64,112},{80,64},{96,80},{112,96},{1... | collective-permute-start | bytes 442376 | tf_op jit(solution)/shard_map/ppermute | solution.py:352
  67.5 6.2 %collective-permute-start.8 = (bf16[4,96,192]{2,1,0:T(8,128)(2,1)S(1)}, bf16[4,96,192]{2,1,0:T(8,128)(2,1)S(1)}, u32[]{:S(2)}, u32[]{:S(2)}) collective-permute-start(bf16[4,96,192]{2,1,0:T(8,128)(2,1)S(1)} %pad_maximum_fusion.3), channel_id=1, source_target_pairs={{0,16},{16,32},{32,48},{48,0},{64,80},{80,96},{96,112},{112,64},{1... | collective-permute-start | bytes 442376 | tf_op jit(solution)/shard_map/ppermute | solution.py:352
  73.8 10.4 %collective-permute-start.11 = (bf16[2,96,192]{2,1,0:T(8,128)(2,1)S(1)}, bf16[2,96,192]{2,1,0:T(8,128)(2,1)S(1)}, u32[]{:S(2)}, u32[]{:S(2)}) collective-permute-start(bf16[2,96,192]{2,1,0:T(8,128)(2,1)S(1)} %get-tuple-element.81), channel_id=1, source_target_pairs={{0,64},{16,80},{32,96},{48,112},{64,0},{80,16},{96,32},{112,48},{1... | collective-permute-start | bytes 221192 | tf_op jit(solution)/shard_map/ppermute | solution.py:352
  77.2 7.0 %collective-permute-start.12 = (bf16[2,96,192]{2,1,0:T(8,128)(2,1)S(1)}, bf16[2,96,192]{2,1,0:T(8,128)(2,1)S(1)}, u32[]{:S(2)}, u32[]{:S(2)}) collective-permute-start(bf16[2,96,192]{2,1,0:T(8,128)(2,1)S(1)} %get-tuple-element.80), channel_id=1, source_target_pairs={{0,1},{1,0},{2,3},{3,2},{4,5},{5,4},{6,7},{7,6},{8,9},{9,8},{10,11... | collective-permute-start | bytes 221192 | tf_op jit(solution)/shard_map/ppermute | solution.py:320
  80.5 5.9 %collective-permute-start.13 = (bf16[2,96,192]{2,1,0:T(8,128)(2,1)S(1)}, bf16[2,96,192]{2,1,0:T(8,128)(2,1)S(1)}, u32[]{:S(2)}, u32[]{:S(2)}) collective-permute-start(bf16[2,96,192]{2,1,0:T(8,128)(2,1)S(1)} %get-tuple-element.79), channel_id=1, source_target_pairs={{0,65},{1,64},{2,67},{3,66},{4,69},{5,68},{6,71},{7,70},{8,73},{9,... | collective-permute-start | bytes 221192 | tf_op jit(solution)/shard_map/ppermute | solution.py:394

commit v12 on v11

--- a/solution.py
+++ b/solution.py
@@ -134,14 +134,22 @@
             de_ref[2 * unit * queries : (2 * unit + 2) * queries, :],
             (((0,), (0,)), ((), ())),
             preferred_element_type=jnp.float32,
-        ).T.reshape(dkv_ref.shape[0], half, 4 * head_width)
+        )
+        keys_here = key_value[head * head_width : (head + 1) * head_width]
+        values_here = key_value[(head + 2) * head_width : (head + 3) * head_width]
         if earlier:
             own = own + earlier[0][unit].astype(jnp.float32)
             away = away + earlier[1][unit].astype(jnp.float32)
-            key_value = key_value + earlier[2][:, unit].astype(jnp.float32)
+            passed = earlier[2][unit].astype(jnp.float32)
+            key_value = jnp.concatenate(
+                [passed[:head_width], keys_here, passed[head_width:], values_here], axis=0
+            )
+            key_value = key_value.T.reshape(dkv_ref.shape[0], half, 4 * head_width)
+            dkv_ref[:, unit] = key_value.astype(jnp.bfloat16)
+        else:
+            dkv_ref[unit] = jnp.concatenate([keys_here, values_here], axis=0).astype(jnp.bfloat16)
         qa_own_ref[unit] = own.astype(jnp.bfloat16)
         qa_away_ref[unit] = away.astype(jnp.bfloat16)
-        dkv_ref[:, unit] = key_value.astype(jnp.bfloat16)
 
     scores_of(0)
     scores_of(1)
@@ -231,7 +239,13 @@
         return pl.BlockSpec(shape, lambda j, places: (0,) * len(shape))
 
     column_spec = pl.BlockSpec((2, tokens, lanes), lambda j, places: (j, 0, 0))
-    grad_spec = pl.BlockSpec((devices, 2, tokens, lanes), lambda j, places: (0, j, 0, 0))
+    part_spec = pl.BlockSpec((2, lanes // 2, keys), lambda j, places: (j, 0, 0))
+    part_shape = (columns, lanes // 2, keys)
+    if earlier:
+        grad_spec = pl.BlockSpec((devices, 2, tokens, lanes), lambda j, places: (0, j, 0, 0))
+        grad_shape = (devices,) + mine.shape
+    else:
+        grad_spec, grad_shape = part_spec, part_shape
     piece = (tokens, width)
     return pl.pallas_call(
         functools.partial(attention_kernel, head),
@@ -249,7 +263,7 @@
                 whole(weight.shape),
                 pl.BlockSpec((queries, keys), lambda j, places: (head, 0)),
             ]
-            + [column_spec, column_spec, grad_spec][: len(earlier)],
+            + [column_spec, column_spec, part_spec][: len(earlier)],
             out_specs=[
                 column_spec,
                 column_spec,
@@ -273,7 +287,7 @@
         out_shape=[
             jax.ShapeDtypeStruct(mine.shape, jnp.bfloat16),
             jax.ShapeDtypeStruct(mine.shape, jnp.bfloat16),
-            jax.ShapeDtypeStruct((devices,) + mine.shape, jnp.bfloat16),
+            jax.ShapeDtypeStruct(grad_shape, jnp.bfloat16),
             jax.ShapeDtypeStruct((2,) + piece, jnp.bfloat16),
             jax.ShapeDtypeStruct((2,) + piece, jnp.bfloat16),
             jax.ShapeDtypeStruct((12,) + piece, jnp.bfloat16),

time: 87.6 us -> 87.2 us (level)
  transfers between devices with their start and end apart: 16 -> 16, of which waited for: 9 -> 9; matrix products, arithmetic and copies ran while one was open for 10% -> 10% of each run, Pallas kernels for 10% -> 9%
where the time goes in v12:
time: 87.2 us; the launch traced here: 86.9 us
  starting transfers between devices  30 us (34%)
  waiting for transfers between devices  28.8 us (33%)
  Pallas kernels  17.1 us (20%)
  other arithmetic  8.73 us (10%)
  local copies, waits for them, and re-layouts  1.31 us (2%)
  between operations  0.91 us (1%)
    all_to_all x1, waiting for transfers between devices, local(): received = lax.all_to_all(packed, 'col', 0, 0, tiled=True)  19.1 us
    pallas_call x2, Pallas kernels, attend(): pl.pallas_call(functools.partial(attention_kernel, head), grid_spec=pltpu...  14.5 us
    ppermute x9, starting transfers between devices, along_row(): return lax.ppermute(array, 'row', pairs)  13.2 us
    all_to_all x1, starting transfers between devices, local(): received = lax.all_to_all(packed, 'col', 0, 0, tiled=True)  7.3 us
    ppermute x9, waiting for transfers between devices, along_row(): return lax.ppermute(array, 'row', pairs)  6.11 us
    ppermute x4, starting transfers between devices, swapped(): return lax.ppermute(array, 'col', swap)  5 us
    all_to_all x1, starting transfers between devices, local(): kv_parts = lax.all_to_all(kv_grads, 'col', 0, 0, tiled=True)  4.44 us
    select_n x3, other arithmetic, in_order(): jnp.where(core == 0, jnp.concatenate([mine, other], axis=axis), jnp.conca...  3.55 us
  transfers between devices with their start and end apart: 16, of which 9 were waited for; matrix products, arithmetic and copies ran while one was open for 10% of the time, Pallas kernels for 9%

profile of v12, /device:TPU:1, one launch (start us, length us, event | category | flops | bytes accessed | tf_op | source)
XLA Modules:
  0.0 86.9 jit_solution(2575893629789872926)
XLA Ops:
  0.6 2.6 %prepare_exchange.1 = bf16[16,464,128]{2,1,0:T(8,128)(2,1)} custom-call(bf16[4,96,128]{2,1,0:T(8,128)(2,1)} %key_ref.1, bf16[4,96,128]{2,1,0:T(8,128)(2,1)} %value_ref.1, s32[4,96]{1,0:T(4,128)} %mask_ref.1, bf16[4,8,1536]{2,1,0:T(8,128)(2,1)} %cotangent_ref.1), custom_call_target="tpu_custom_call" | custom-call | tf_op jit(solution)/shard_map/prepare_exchange/pallas_call | solution.py:217
  3.2 7.3 %all-to-all-start = ((bf16[16,464,128]{2,1,0:T(8,128)(2,1)}), bf16[16,464,128]{2,1,0:T(8,128)(2,1)S(1)}, u32[]{:S(2)}, u32[]{:S(2)}) async-start(bf16[16,464,128]{2,1,0:T(8,128)(2,1)} %prepare_exchange.1), calls=%async_computation | async-start | bytes 3801088 | tf_op jit(solution)/shard_map/all_to_all | solution.py:340
  10.5 0.0 copy-start.6
  10.6 1.1 %broadcast_select_fusion.1 = (bf16[2,96,1536]{2,1,0:T(8,128)(2,1)}, bf16[2,96,1536]{2,1,0:T(8,128)(2,1)}) fusion(pred[]{:T(512)S(6)} %eq.31, bf16[4,96,1536]{2,1,0:T(8,128)(2,1)S(1)} %copy-done.3), kind=kLoop, calls=%fused_computation.7 | loop fusion | flops 589824 | bytes 2359297 | tf_op jit(solution)/shard_map/jit(_where)/select_n | solution.py:324
  11.7 0.1 collective-permute-start.1
  11.8 0.1 broadcast_select_fusion.2
  11.9 0.1 broadcast_select_fusion.3
  12.0 0.1 pad_maximum_fusion.6
  12.1 0.5 collective-permute-start
  12.6 0.1 stack.48.refs_0_
  12.7 0.1 pad_maximum_fusion.5.refs_1_
  12.8 1.1 %collective-permute-done.1 = bf16[2,96,1536]{2,1,0:T(8,128)(2,1)S(1)} collective-permute-done((bf16[2,96,1536]{2,1,0:T(8,128)(2,1)}, bf16[2,96,1536]{2,1,0:T(8,128)(2,1)S(1)}, u32[]{:S(2)}, u32[]{:S(2)}) %collective-permute-start.1) | collective-permute-done | bytes 589856 | tf_op jit(solution)/shard_map/ppermute | solution.py:334
  13.9 0.8 copy-done.4
  14.7 1.9 %maximum_select_fusion = bf16[2,192,1536]{2,1,0:T(8,128)(2,1)S(1)} fusion(bf16[2,96,1536]{2,1,0:T(8,128)(2,1)} %copy-done.4, bf16[2,96,1536]{2,1,0:T(8,128)(2,1)} %get-tuple-element.67, pred[]{:T(512)S(6)} %eq.31), kind=kLoop, calls=%fused_computation.1 | loop fusion | flops 5308416 | bytes 2359297 | tf_op jit(solution)/shard_map/jit(_where)/select_n | solution.py:327
  16.6 19.1 %all-to-all-done.refs_3_.refs_4_.refs_5_ = bf16[16,464,128]{2,1,0:T(8,128)(2,1)S(1)} async-done(((bf16[16,464,128]{2,1,0:T(8,128)(2,1)}), bf16[16,464,128]{2,1,0:T(8,128)(2,1)S(1)}, u32[]{:S(2)}, u32[]{:S(2)}) %all-to-all-start) | async-done | bytes 1900576 | tf_op jit(solution)/shard_map/all_to_all | solution.py:340
  35.7 6.3 %attention_head.2 = (bf16[4,96,128]{2,1,0:T(8,128)(2,1)S(1)}, bf16[4,96,128]{2,1,0:T(8,128)(2,1)S(1)}, bf16[4,64,1536]{2,1,0:T(8,128)(2,1)S(1)}, bf16[2,96,192]{...) custom-call(s32[9]{0:T(128)S(1)} %stack.48.refs_0_, ...), custom_call_target="tpu_custom_call" | custom-call | flops 1811939328 | bytes 16777216 | tf_op jit(solution)/shard_map/attention_head/pallas_call | solution.py:250
  42.1 1.4 %collective-permute-start.2 = (bf16[2,96,192]{2,1,0:T(8,128)(2,1)S(1)}, bf16[2,96,192]{2,1,0:T(8,128)(2,1)S(1)}, u32[]{:S(2)}, u32[]{:S(2)}) collective-permute-start(bf16[2,96,192]{2,1,0:T(8,128)(2,1)S(1)} %get-tuple-element.36), channel_id=1, source_target_pairs={{0,16},{16,32},{32,48},{48,0},{64,80},{80,96},{96,112},{112,64},{1... | collective-permute-start | bytes 221192 | tf_op jit(solution)/shard_map/ppermute | solution.py:366
  43.4 1.5 %collective-permute-start.3 = (bf16[2,96,192]{2,1,0:T(8,128)(2,1)S(1)}, bf16[2,96,192]{2,1,0:T(8,128)(2,1)S(1)}, u32[]{:S(2)}, u32[]{:S(2)}) collective-permute-start(bf16[2,96,192]{2,1,0:T(8,128)(2,1)S(1)} %get-tuple-element.37), channel_id=1, source_target_pairs={{0,48},{16,0},{32,16},{48,32},{64,112},{80,64},{96,80},{112,96},{1... | collective-permute-start | bytes 221192 | tf_op jit(solution)/shard_map/ppermute | solution.py:366
  45.0 8.2 %attention_head.3 = (bf16[4,96,128]{2,1,0:T(8,128)(2,1)S(1)}, bf16[4,96,128]{2,1,0:T(8,128)(2,1)S(1)}, bf16[16,4,96,128]{3,2,1,0:T(8,128)(2,1)}, bf16[2,96,192]{...) custom-call(s32[9]{0:T(128)S(1)} %stack.48.refs_0_, ...), custom_call_target="tpu_custom_call" | custom-call | flops 1811939328 | bytes 16777216 | tf_op jit(solution)/shard_map/attention_head/pallas_call | solution.py:250
  53.2 1.1 %collective-permute-start.4 = (bf16[4,96,128]{2,1,0:T(8,128)(2,1)S(1)}, bf16[4,96,128]{2,1,0:T(8,128)(2,1)S(1)}, u32[]{:S(2)}, u32[]{:S(2)}) collective-permute-start(bf16[4,96,128]{2,1,0:T(8,128)(2,1)S(1)} %get-tuple-element.53), channel_id=1, source_target_pairs={{0,1},{1,0},{2,3},{3,2},{4,5},{5,4},{6,7},{7,6},{8,9},{9,8},{10,11... | collective-permute-start | bytes 294920 | tf_op jit(solution)/shard_map/ppermute | solution.py:334
  54.3 0.1 fusion.6
  54.4 4.4 %all-to-all-start.1 = ((bf16[16,4,96,128]{3,2,1,0:T(8,128)(2,1)}), bf16[16,4,96,128]{3,2,1,0:T(8,128)(2,1)}, u32[]{:S(2)}, u32[]{:S(2)}) async-start(bf16[16,4,96,128]{3,2,1,0:T(8,128)(2,1)} %get-tuple-element.61), calls=%async_computation.1 | async-start | bytes 3145728 | tf_op jit(solution)/shard_map/all_to_all | solution.py:389
  58.9 0.2 collective-permute-start.7
  59.0 2.6 %collective-permute-start.9 = (bf16[2,96,192]{2,1,0:T(8,128)(2,1)S(1)}, bf16[2,96,192]{2,1,0:T(8,128)(2,1)S(1)}, u32[]{:S(2)}, u32[]{:S(2)}) collective-permute-start(bf16[2,96,192]{2,1,0:T(8,128)(2,1)S(1)} %get-tuple-element.60), channel_id=1, source_target_pairs={{0,48},{16,0},{32,16},{48,32},{64,112},{80,64},{96,80},{112,96},{1... | collective-permute-start | bytes 221192 | tf_op jit(solution)/shard_map/ppermute | solution.py:366
  61.6 0.1 add_convert_fusion.3
  61.7 0.4 collective-permute-start.6
  62.2 1.2 %collective-permute-start.5 = (bf16[4,96,192]{2,1,0:T(8,128)(2,1)S(1)}, bf16[4,96,192]{2,1,0:T(8,128)(2,1)S(1)}, u32[]{:S(2)}, u32[]{:S(2)}) collective-permute-start(bf16[4,96,192]{2,1,0:T(8,128)(2,1)S(1)} %pad_maximum_fusion.1), channel_id=1, source_target_pairs={{0,16},{16,32},{32,48},{48,0},{64,80},{80,96},{96,112},{112,64},{1... | collective-permute-start | bytes 442376 | tf_op jit(solution)/shard_map/ppermute | solution.py:366
  63.4 0.1 fusion.7
  63.5 0.9 %maximum_select_fusion.2 = (bf16[4,96,128]{2,1,0:T(8,128)(2,1)}, bf16[4,96,128]{2,1,0:T(8,128)(2,1)}) fusion(bf16[4,96,64]{2,1,0:T(8,128)(2,1)S(1)} %get-tuple-element.87, bf16[4,96,64]{2,1,0:T(8,128)(2,1)S(1)} %get-tuple-element.85, pred[]{:T(512)S(6)} %eq.31, bf16[4,96,64]{2,1,0:T(8,128)(2,1)S(1)} %get-tuple-element.84, ...), kind=kLoop, calls=%fused_computation.34 | loop fusion | flops 884736 | bytes 393217 | tf_op jit(solution)/shard_map/jit(_where)/select_n | solution.py:327
  64.4 0.1 collective-permute-done.7
  64.4 0.1 add_convert_fusion.1
  64.5 2.5 %collective-permute-start.10 = (bf16[4,96,192]{2,1,0:T(8,128)(2,1)S(1)}, bf16[4,96,192]{2,1,0:T(8,128)(2,1)S(1)}, u32[]{:S(2)}, u32[]{:S(2)}) collective-permute-start(bf16[4,96,192]{2,1,0:T(8,128)(2,1)S(1)} %pad_maximum_fusion.4), channel_id=1, source_target_pairs={{0,48},{16,0},{32,16},{48,32},{64,112},{80,64},{96,80},{112,96},{1... | collective-permute-start | bytes 442376 | tf_op jit(solution)/shard_map/ppermute | solution.py:366
  67.1 0.1 collective-permute-start.8
  67.2 0.5 collective-permute-done.6
  67.6 1.3 %collective-permute-done.5 = bf16[4,96,192]{2,1,0:T(8,128)(2,1)S(1)} collective-permute-done((bf16[4,96,192]{2,1,0:T(8,128)(2,1)S(1)}, bf16[4,96,192]{2,1,0:T(8,128)(2,1)S(1)}, u32[]{:S(2)}, u32[]{:S(2)}) %collective-permute-start.5) | collective-permute-done | bytes 147488 | tf_op jit(solution)/shard_map/ppermute | solution.py:366
  68.9 0.1 add_bitcast_fusion.1
  69.0 2.8 %collective-permute-done.10 = bf16[4,96,192]{2,1,0:T(8,128)(2,1)S(1)} collective-permute-done((bf16[4,96,192]{2,1,0:T(8,128)(2,1)S(1)}, bf16[4,96,192]{2,1,0:T(8,128)(2,1)S(1)}, u32[]{:S(2)}, u32[]{:S(2)}) %collective-permute-start.10) | collective-permute-done | bytes 147488 | tf_op jit(solution)/shard_map/ppermute | solution.py:366
  71.8 1.4 %collective-permute-done.8 = bf16[4,96,192]{2,1,0:T(8,128)(2,1)S(1)} collective-permute-done((bf16[4,96,192]{2,1,0:T(8,128)(2,1)S(1)}, bf16[4,96,192]{2,1,0:T(8,128)(2,1)S(1)}, u32[]{:S(2)}, u32[]{:S(2)}) %collective-permute-start.8) | collective-permute-done | bytes 147488 | tf_op jit(solution)/shard_map/ppermute | solution.py:366
  73.3 0.1 add_bitcast_fusion
  73.4 3.4 %collective-permute-start.11 = (bf16[2,96,192]{2,1,0:T(8,128)(2,1)S(1)}, bf16[2,96,192]{2,1,0:T(8,128)(2,1)S(1)}, u32[]{:S(2)}, u32[]{:S(2)}) collective-permute-start(bf16[2,96,192]{2,1,0:T(8,128)(2,1)S(1)} %get-tuple-element.81), channel_id=1, source_target_pairs={{0,64},{16,80},{32,96},{48,112},{64,0},{80,16},{96,32},{112,48},{1... | collective-permute-start | bytes 221192 | tf_op jit(solution)/shard_map/ppermute | solution.py:366
  76.8 3.3 %collective-permute-start.12 = (bf16[2,96,192]{2,1,0:T(8,128)(2,1)S(1)}, bf16[2,96,192]{2,1,0:T(8,128)(2,1)S(1)}, u32[]{:S(2)}, u32[]{:S(2)}) collective-permute-start(bf16[2,96,192]{2,1,0:T(8,128)(2,1)S(1)} %get-tuple-element.80), channel_id=1, source_target_pairs={{0,1},{1,0},{2,3},{3,2},{4,5},{5,4},{6,7},{7,6},{8,9},{9,8},{10,11... | collective-permute-start | bytes 221192 | tf_op jit(solution)/shard_map/ppermute | solution.py:334
  80.1 0.3 all-to-all-done.1
  80.4 1.7 %convert_reduce_fusion = f32[2,4,96,128]{3,2,1,0:T(8,128)S(1)} fusion(bf16[8,2,4,96,128]{4,3,2,1,0:T(8,128)(2,1)} %bitcast.21), kind=kLoop, calls=%fused_computation | loop fusion | flops 1474560 | bytes 1966080 | tf_op jit(solution)/shard_map/reduce_sum | solution.py:391
  82.1 0.1 slice_bitcast_fusion.3
  82.3 0.8 fusion.3
  83.0 0.7 pad_maximum_fusion.7
  83.8 2.3 %collective-permute-done.13 = bf16[2,96,192]{2,1,0:T(8,128)(2,1)S(1)} collective-permute-done((bf16[2,96,192]{2,1,0:T(8,128)(2,1)S(1)}, bf16[2,96,192]{2,1,0:T(8,128)(2,1)S(1)}, u32[]{:S(2)}, u32[]{:S(2)}) %collective-permute-start.13) | collective-permute-done | bytes 73760 | tf_op jit(solution)/shard_map/ppermute | solution.py:408
  86.1 0.8 maximum_select_fusion.1
  (34 shorter events, 0.4 us)
Async XLA Ops:
  3.2 7.3 %copy-start.3 = (bf16[4,96,1536]{2,1,0:T(8,128)(2,1)S(1)}, bf16[4,96,1536]{2,1,0:T(8,128)(2,1)}, u32[]{:S(2)}) copy-start(bf16[4,96,1536]{2,1,0:T(8,128)(2,1)} %param.12) | copy-start | bytes 3538948
  3.2 32.5 %all-to-all-start = ((bf16[16,464,128]{2,1,0:T(8,128)(2,1)}), bf16[16,464,128]{2,1,0:T(8,128)(2,1)S(1)}, u32[]{:S(2)}, u32[]{:S(2)}) async-start(bf16[16,464,128]{2,1,0:T(8,128)(2,1)} %prepare_exchange.1), calls=%async_computation | async-start | bytes 3801088 | tf_op jit(solution)/shard_map/all_to_all | solution.py:340
  10.5 1.3 %copy-start.5 = (bf16[4,96,128]{2,1,0:T(8,128)(2,1)S(1)}, bf16[4,96,128]{2,1,0:T(8,128)(2,1)}, u32[]{:S(2)}) copy-start(bf16[4,96,128]{2,1,0:T(8,128)(2,1)} %param.11) | copy-start | bytes 294916
  10.5 1.4 %copy-start.6 = (bf16[4,96,128]{2,1,0:T(8,128)(2,1)S(1)}, bf16[4,96,128]{2,1,0:T(8,128)(2,1)}, u32[]{:S(2)}) copy-start(bf16[4,96,128]{2,1,0:T(8,128)(2,1)} %param.8) | copy-start | bytes 294916
  10.6 2.0 %copy-start.7 = (bf16[128,128]{1,0:T(8,128)(2,1)S(1)}, bf16[128,128]{1,0:T(8,128)(2,1)}, u32[]{:S(2)}) copy-start(bf16[128,128]{1,0:T(8,128)(2,1)} %param.14) | copy-start | bytes 98308
  11.7 2.2 %collective-permute-start.1 = (bf16[2,96,1536]{2,1,0:T(8,128)(2,1)}, bf16[2,96,1536]{2,1,0:T(8,128)(2,1)S(1)}, u32[]{:S(2)}, u32[]{:S(2)}) collective-permute-start(bf16[2,96,1536]{2,1,0:T(8,128)(2,1)} %get-tuple-element.68), channel_id=1, source_target_pairs={{0,1},{1,0},{2,3},{3,2},{4,5},{5,4},{6,7},{7,6},{8,9},{9,8},{10,11... | collective-permute-start | bytes 1769480 | tf_op jit(solution)/shard_map/ppermute | solution.py:334
  12.1 4.5 %collective-permute-start = (bf16[4,96,128]{2,1,0:T(8,128)(2,1)S(1)}, bf16[4,96,128]{2,1,0:T(8,128)(2,1)S(1)}, u32[]{:S(2)}, u32[]{:S(2)}) collective-permute-start(bf16[4,96,128]{2,1,0:T(8,128)(2,1)S(1)} %pad_maximum_fusion.6), channel_id=1, source_target_pairs={{0,1},{1,0},{2,3},{3,2},{4,5},{5,4},{6,7},{7,6},{8,9},{9,8},{10,11... | collective-permute-start | bytes 294920 | tf_op jit(solution)/shard_map/ppermute | solution.py:334
  13.9 0.8 copy-start.4
  35.7 6.3 %copy-start = (bf16[16,464,128]{2,1,0:T(8,128)(2,1)}, bf16[16,464,128]{2,1,0:T(8,128)(2,1)S(1)}, u32[]{:S(2)}) copy-start(bf16[16,464,128]{2,1,0:T(8,128)(2,1)S(1)} %all-to-all-done.refs_3_.refs_4_.refs_5_) | copy-start | bytes 5701636
  42.1 12.3 %copy-start.1 = (bf16[12,96,192]{2,1,0:T(8,128)(2,1)}, bf16[12,96,192]{2,1,0:T(8,128)(2,1)S(1)}, u32[]{:S(2)}) copy-start(bf16[12,96,192]{2,1,0:T(8,128)(2,1)S(1)} %get-tuple-element.55) | copy-start | bytes 1327108
  42.1 11.1 %collective-permute-start.2 = (bf16[2,96,192]{2,1,0:T(8,128)(2,1)S(1)}, bf16[2,96,192]{2,1,0:T(8,128)(2,1)S(1)}, u32[]{:S(2)}, u32[]{:S(2)}) collective-permute-start(bf16[2,96,192]{2,1,0:T(8,128)(2,1)S(1)} %get-tuple-element.36), channel_id=1, source_target_pairs={{0,16},{16,32},{32,48},{48,0},{64,80},{80,96},{96,112},{112,64},{1... | collective-permute-start | bytes 221192 | tf_op jit(solution)/shard_map/ppermute | solution.py:366
  43.4 9.7 %collective-permute-start.3 = (bf16[2,96,192]{2,1,0:T(8,128)(2,1)S(1)}, bf16[2,96,192]{2,1,0:T(8,128)(2,1)S(1)}, u32[]{:S(2)}, u32[]{:S(2)}) collective-permute-start(bf16[2,96,192]{2,1,0:T(8,128)(2,1)S(1)} %get-tuple-element.37), channel_id=1, source_target_pairs={{0,48},{16,0},{32,16},{48,32},{64,112},{80,64},{96,80},{112,96},{1... | collective-permute-start | bytes 221192 | tf_op jit(solution)/shard_map/ppermute | solution.py:366
  53.2 5.7 %collective-permute-start.4 = (bf16[4,96,128]{2,1,0:T(8,128)(2,1)S(1)}, bf16[4,96,128]{2,1,0:T(8,128)(2,1)S(1)}, u32[]{:S(2)}, u32[]{:S(2)}) collective-permute-start(bf16[4,96,128]{2,1,0:T(8,128)(2,1)S(1)} %get-tuple-element.53), channel_id=1, source_target_pairs={{0,1},{1,0},{2,3},{3,2},{4,5},{5,4},{6,7},{7,6},{8,9},{9,8},{10,11... | collective-permute-start | bytes 294920 | tf_op jit(solution)/shard_map/ppermute | solution.py:334
  54.4 7.2 %copy-start.2 = (bf16[12,96,192]{2,1,0:T(8,128)(2,1)S(1)}, bf16[12,96,192]{2,1,0:T(8,128)(2,1)}, u32[]{:S(2)}) copy-start(bf16[12,96,192]{2,1,0:T(8,128)(2,1)} %copy-done.1) | copy-start | bytes 1327108
  54.4 26.0 %all-to-all-start.1 = ((bf16[16,4,96,128]{3,2,1,0:T(8,128)(2,1)}), bf16[16,4,96,128]{3,2,1,0:T(8,128)(2,1)}, u32[]{:S(2)}, u32[]{:S(2)}) async-start(bf16[16,4,96,128]{3,2,1,0:T(8,128)(2,1)} %get-tuple-element.61), calls=%async_computation.1 | async-start | bytes 3145728 | tf_op jit(solution)/shard_map/all_to_all | solution.py:389
  58.9 5.5 %collective-permute-start.7 = (bf16[2,96,192]{2,1,0:T(8,128)(2,1)S(1)}, bf16[2,96,192]{2,1,0:T(8,128)(2,1)S(1)}, u32[]{:S(2)}, u32[]{:S(2)}) collective-permute-start(bf16[2,96,192]{2,1,0:T(8,128)(2,1)S(1)} %get-tuple-element.59), channel_id=1, source_target_pairs={{0,16},{16,32},{32,48},{48,0},{64,80},{80,96},{96,112},{112,64},{1... | collective-permute-start | bytes 221192 | tf_op jit(solution)/shard_map/ppermute | solution.py:366
  59.0 5.4 %collective-permute-start.9 = (bf16[2,96,192]{2,1,0:T(8,128)(2,1)S(1)}, bf16[2,96,192]{2,1,0:T(8,128)(2,1)S(1)}, u32[]{:S(2)}, u32[]{:S(2)}) collective-permute-start(bf16[2,96,192]{2,1,0:T(8,128)(2,1)S(1)} %get-tuple-element.60), channel_id=1, source_target_pairs={{0,48},{16,0},{32,16},{48,32},{64,112},{80,64},{96,80},{112,96},{1... | collective-permute-start | bytes 221192 | tf_op jit(solution)/shard_map/ppermute | solution.py:366
  61.7 5.9 %collective-permute-start.6 = (bf16[4,96,192]{2,1,0:T(8,128)(2,1)S(1)}, bf16[4,96,192]{2,1,0:T(8,128)(2,1)S(1)}, u32[]{:S(2)}, u32[]{:S(2)}) collective-permute-start(bf16[4,96,192]{2,1,0:T(8,128)(2,1)S(1)} %pad_maximum_fusion.2), channel_id=1, source_target_pairs={{0,48},{16,0},{32,16},{48,32},{64,112},{80,64},{96,80},{112,96},{1... | collective-permute-start | bytes 442376 | tf_op jit(solution)/shard_map/ppermute | solution.py:366
  62.2 6.8 %collective-permute-start.5 = (bf16[4,96,192]{2,1,0:T(8,128)(2,1)S(1)}, bf16[4,96,192]{2,1,0:T(8,128)(2,1)S(1)}, u32[]{:S(2)}, u32[]{:S(2)}) collective-permute-start(bf16[4,96,192]{2,1,0:T(8,128)(2,1)S(1)} %pad_maximum_fusion.1), channel_id=1, source_target_pairs={{0,16},{16,32},{32,48},{48,0},{64,80},{80,96},{96,112},{112,64},{1... | collective-permute-start | bytes 442376 | tf_op jit(solution)/shard_map/ppermute | solution.py:366
  64.5 7.3 %collective-permute-start.10 = (bf16[4,96,192]{2,1,0:T(8,128)(2,1)S(1)}, bf16[4,96,192]{2,1,0:T(8,128)(2,1)S(1)}, u32[]{:S(2)}, u32[]{:S(2)}) collective-permute-start(bf16[4,96,192]{2,1,0:T(8,128)(2,1)S(1)} %pad_maximum_fusion.4), channel_id=1, source_target_pairs={{0,48},{16,0},{32,16},{48,32},{64,112},{80,64},{96,80},{112,96},{1... | collective-permute-start | bytes 442376 | tf_op jit(solution)/shard_map/ppermute | solution.py:366
  67.1 6.2 %collective-permute-start.8 = (bf16[4,96,192]{2,1,0:T(8,128)(2,1)S(1)}, bf16[4,96,192]{2,1,0:T(8,128)(2,1)S(1)}, u32[]{:S(2)}, u32[]{:S(2)}) collective-permute-start(bf16[4,96,192]{2,1,0:T(8,128)(2,1)S(1)} %pad_maximum_fusion.3), channel_id=1, source_target_pairs={{0,16},{16,32},{32,48},{48,0},{64,80},{80,96},{96,112},{112,64},{1... | collective-permute-start | bytes 442376 | tf_op jit(solution)/shard_map/ppermute | solution.py:366
  73.4 10.4 %collective-permute-start.11 = (bf16[2,96,192]{2,1,0:T(8,128)(2,1)S(1)}, bf16[2,96,192]{2,1,0:T(8,128)(2,1)S(1)}, u32[]{:S(2)}, u32[]{:S(2)}) collective-permute-start(bf16[2,96,192]{2,1,0:T(8,128)(2,1)S(1)} %get-tuple-element.81), channel_id=1, source_target_pairs={{0,64},{16,80},{32,96},{48,112},{64,0},{80,16},{96,32},{112,48},{1... | collective-permute-start | bytes 221192 | tf_op jit(solution)/shard_map/ppermute | solution.py:366
  76.8 7.0 %collective-permute-start.12 = (bf16[2,96,192]{2,1,0:T(8,128)(2,1)S(1)}, bf16[2,96,192]{2,1,0:T(8,128)(2,1)S(1)}, u32[]{:S(2)}, u32[]{:S(2)}) collective-permute-start(bf16[2,96,192]{2,1,0:T(8,128)(2,1)S(1)} %get-tuple-element.80), channel_id=1, source_target_pairs={{0,1},{1,0},{2,3},{3,2},{4,5},{5,4},{6,7},{7,6},{8,9},{9,8},{10,11... | collective-permute-start | bytes 221192 | tf_op jit(solution)/shard_map/ppermute | solution.py:334
  80.1 5.9 %collective-permute-start.13 = (bf16[2,96,192]{2,1,0:T(8,128)(2,1)S(1)}, bf16[2,96,192]{2,1,0:T(8,128)(2,1)S(1)}, u32[]{:S(2)}, u32[]{:S(2)}) collective-permute-start(bf16[2,96,192]{2,1,0:T(8,128)(2,1)S(1)} %get-tuple-element.79), channel_id=1, source_target_pairs={{0,65},{1,64},{2,67},{3,66},{4,69},{5,68},{6,71},{7,70},{8,73},{9,... | collective-permute-start | bytes 221192 | tf_op jit(solution)/shard_map/ppermute | solution.py:408

commit v13 on v12

--- a/solution.py
+++ b/solution.py
@@ -170,7 +170,7 @@
                 part = acc_ref[side * half : (side + 1) * half, piece * width : (piece + 1) * width]
                 target = 2 * place_ref[piece] + (side + core) % 2
                 dbias_ref[target] = part.astype(jnp.bfloat16)
-        right_out_ref[...] = dbias_ref[8:10]
+        right_out_ref[...] = dbias_ref[8 : 8 + right_out_ref.shape[0]]
         left_out_ref[...] = dbias_ref[10:12]
         rest_out_ref[:8] = dbias_ref[:8]
         rest_out_ref[8:] = dbias_ref[12:]
@@ -268,7 +268,7 @@
                 column_spec,
                 column_spec,
                 grad_spec,
-                whole((2,) + piece),
+                whole((2 if earlier else 4,) + piece),
                 whole((2,) + piece),
                 whole((12,) + piece),
             ],
@@ -288,7 +288,7 @@
             jax.ShapeDtypeStruct(mine.shape, jnp.bfloat16),
             jax.ShapeDtypeStruct(mine.shape, jnp.bfloat16),
             jax.ShapeDtypeStruct(grad_shape, jnp.bfloat16),
-            jax.ShapeDtypeStruct((2,) + piece, jnp.bfloat16),
+            jax.ShapeDtypeStruct((2 if earlier else 4,) + piece, jnp.bfloat16),
             jax.ShapeDtypeStruct((2,) + piece, jnp.bfloat16),
             jax.ShapeDtypeStruct((12,) + piece, jnp.bfloat16),
         ],
@@ -355,7 +355,7 @@
     weight_mine = jnp.pad(weight_mine, ((half, 0), (0, 0)))
 
     shared = (places, qg_mine, qg_other, received, weight_mine, bias_pair, row_count)
-    *earlier, bias_right, bias_left, bias_rest = attend(0, *shared, ())
+    *earlier, bias_right, _, bias_rest = attend(0, *shared, ())
     (qa_own, qa_away, kv_grads, bias_right_2, bias_left_2, bias_rest_2) = attend(1, *shared, tuple(earlier))
 
     def along_row(array, turn, side):
@@ -373,17 +373,16 @@
         backward = jnp.concatenate([rest[8:10], added(rest[10:], from_right).astype(jnp.bfloat16)])
         return along_row(onward, 1, 0), along_row(backward, -1, 0)
 
-    from_left, from_right = along_row(bias_right, 1, 0), along_row(bias_left, -1, 0)
+    from_left = along_row(bias_right, 1, 0)
     second = (bias_right_2, bias_left_2, bias_rest_2, kv_grads, qa_own, qa_away)
-    from_left, from_right, bias_rest, second = lax.optimization_barrier(
-        (from_left, from_right, bias_rest, second)
-    )
+    from_left, bias_rest, second = lax.optimization_barrier((from_left, bias_rest, second))
     bias_right_2, bias_left_2, bias_rest_2, kv_grads, qa_own, qa_away = second
     qa_back = swapped(qa_away)
-    from_left, from_right, bias_right_2, bias_left_2, qa_back = lax.optimization_barrier(
-        (from_left, from_right, bias_right_2, bias_left_2, qa_back)
+    from_left, bias_right_2, bias_left_2, qa_back = lax.optimization_barrier(
+        (from_left, bias_right_2, bias_left_2, qa_back)
     )
-    from_left, from_right = ring_onward(bias_rest, from_left, from_right)
+    onward = added(bias_rest[4:8], from_left).astype(jnp.bfloat16)
+    from_left, from_right = along_row(onward, 1, 0), along_row(bias_rest[8:], -1, 0)
     sums = added(bias_rest[:4], from_left, from_right)
     from_left, from_right = along_row(bias_right_2, 1, 0), along_row(bias_left_2, -1, 0)
     kv_parts = lax.all_to_all(kv_grads, "col", 0, 0, tiled=True)

time: 87.2 us -> 86.6 us (level)
  starting transfers between devices: 30 us -> 27.4 us
  waiting for transfers between devices: 28.8 us -> 30.3 us
    ppermute x9 -> x8, starting transfers between devices: 13.2 us -> 11.5 us  [along_row(): return lax.ppermute(array, 'row', pairs)]
    ppermute x9 -> x8, waiting for transfers between devices: 6.11 us -> 7.56 us  [along_row(): return lax.ppermute(array, 'row', pairs)]
    all_to_all x1, waiting for transfers between devices: 0.26 us -> 1.22 us  [local(): kv_parts = lax.all_to_all(kv_grads, 'col', 0, 0, tiled=True)]
    ppermute x1, waiting for transfers between devices: 2.28 us -> 1.31 us  [local(): lax.ppermute(low_sums[3], ('row', 'col'), diagonal)]
    ppermute x4, starting transfers between devices: 5 us -> 4.13 us  [swapped(): return lax.ppermute(array, 'col', swap)]
  transfers between devices with their start and end apart: 16 -> 15, of which waited for: 9 -> 8; matrix products, arithmetic and copies ran while one was open for 10% -> 10% of each run, Pallas kernels for 9% -> 10%
where the time goes in v13:
time: 86.6 us; the launch traced here: 86.3 us
  waiting for transfers between devices  30.3 us (35%)
  starting transfers between devices  27.4 us (32%)
  Pallas kernels  17.8 us (21%)
  other arithmetic  8.65 us (10%)
  local copies, waits for them, and re-layouts  1.33 us (2%)
  between operations  0.88 us (1%)
    all_to_all x1, waiting for transfers between devices, local(): received = lax.all_to_all(packed, 'col', 0, 0, tiled=True)  19.1 us
    pallas_call x2, Pallas kernels, attend(): pl.pallas_call(functools.partial(attention_kernel, head), grid_spec=pltpu...  15.2 us
    ppermute x8, starting transfers between devices, along_row(): return lax.ppermute(array, 'row', pairs)  11.5 us
    ppermute x8, waiting for transfers between devices, along_row(): return lax.ppermute(array, 'row', pairs)  7.56 us
    all_to_all x1, starting transfers between devices, local(): received = lax.all_to_all(packed, 'col', 0, 0, tiled=True)  7.3 us
    all_to_all x1, starting transfers between devices, local(): kv_parts = lax.all_to_all(kv_grads, 'col', 0, 0, tiled=True)  4.42 us
    ppermute x4, starting transfers between devices, swapped(): return lax.ppermute(array, 'col', swap)  4.13 us
    select_n x3, other arithmetic, in_order(): jnp.where(core == 0, jnp.concatenate([mine, other], axis=axis), jnp.conca...  3.55 us
  transfers between devices with their start and end apart: 15, of which 8 were waited for; matrix products, arithmetic and copies ran while one was open for 10% of the time, Pallas kernels for 10%

profile of v13, /device:TPU:1, one launch (start us, length us, event | category | flops | bytes accessed | tf_op | source)
XLA Modules:
  0.0 86.3 jit_solution(11385174312460868470)
XLA Ops:
  0.6 2.6 %prepare_exchange.1 = bf16[16,464,128]{2,1,0:T(8,128)(2,1)} custom-call(bf16[4,96,128]{2,1,0:T(8,128)(2,1)} %key_ref.1, bf16[4,96,128]{2,1,0:T(8,128)(2,1)} %value_ref.1, s32[4,96]{1,0:T(4,128)} %mask_ref.1, bf16[4,8,1536]{2,1,0:T(8,128)(2,1)} %cotangent_ref.1), custom_call_target="tpu_custom_call" | custom-call | tf_op jit(solution)/shard_map/prepare_exchange/pallas_call | solution.py:217
  3.2 7.3 %all-to-all-start = ((bf16[16,464,128]{2,1,0:T(8,128)(2,1)}), bf16[16,464,128]{2,1,0:T(8,128)(2,1)S(1)}, u32[]{:S(2)}, u32[]{:S(2)}) async-start(bf16[16,464,128]{2,1,0:T(8,128)(2,1)} %prepare_exchange.1), calls=%async_computation | async-start | bytes 3801088 | tf_op jit(solution)/shard_map/all_to_all | solution.py:340
  10.5 0.0 copy-start.6
  10.6 0.0 copy-start.7
  10.6 1.1 %broadcast_select_fusion.1 = (bf16[2,96,1536]{2,1,0:T(8,128)(2,1)}, bf16[2,96,1536]{2,1,0:T(8,128)(2,1)}) fusion(pred[]{:T(512)S(6)} %eq.31, bf16[4,96,1536]{2,1,0:T(8,128)(2,1)S(1)} %copy-done.3), kind=kLoop, calls=%fused_computation.7 | loop fusion | flops 589824 | bytes 2359297 | tf_op jit(solution)/shard_map/jit(_where)/select_n | solution.py:324
  11.7 0.1 collective-permute-start.1
  11.8 0.1 broadcast_select_fusion.2
  11.9 0.1 broadcast_select_fusion.3
  12.0 0.1 pad_maximum_fusion.4
  12.1 0.5 collective-permute-start
  12.6 0.1 stack.48.refs_0_
  12.7 0.1 pad_maximum_fusion.3.refs_1_
  12.8 1.1 %collective-permute-done.1 = bf16[2,96,1536]{2,1,0:T(8,128)(2,1)S(1)} collective-permute-done((bf16[2,96,1536]{2,1,0:T(8,128)(2,1)}, bf16[2,96,1536]{2,1,0:T(8,128)(2,1)S(1)}, u32[]{:S(2)}, u32[]{:S(2)}) %collective-permute-start.1) | collective-permute-done | bytes 589856 | tf_op jit(solution)/shard_map/ppermute | solution.py:334
  13.9 0.8 copy-done.4
  14.7 1.9 %maximum_select_fusion = bf16[2,192,1536]{2,1,0:T(8,128)(2,1)S(1)} fusion(bf16[2,96,1536]{2,1,0:T(8,128)(2,1)} %copy-done.4, bf16[2,96,1536]{2,1,0:T(8,128)(2,1)} %get-tuple-element.61, pred[]{:T(512)S(6)} %eq.31), kind=kLoop, calls=%fused_computation.1 | loop fusion | flops 5308416 | bytes 2359297 | tf_op jit(solution)/shard_map/jit(_where)/select_n | solution.py:327
  16.6 19.1 %all-to-all-done.refs_3_.refs_4_.refs_5_ = bf16[16,464,128]{2,1,0:T(8,128)(2,1)S(1)} async-done(((bf16[16,464,128]{2,1,0:T(8,128)(2,1)}), bf16[16,464,128]{2,1,0:T(8,128)(2,1)S(1)}, u32[]{:S(2)}, u32[]{:S(2)}) %all-to-all-start) | async-done | bytes 1900576 | tf_op jit(solution)/shard_map/all_to_all | solution.py:340
  35.7 7.0 %attention_head.2 = (bf16[4,96,128]{2,1,0:T(8,128)(2,1)S(1)}, bf16[4,96,128]{2,1,0:T(8,128)(2,1)S(1)}, bf16[4,64,1536]{2,1,0:T(8,128)(2,1)S(1)}, bf16[4,96,192]{...) custom-call(s32[9]{0:T(128)S(1)} %stack.48.refs_0_, ...), custom_call_target="tpu_custom_call" | custom-call | flops 1811939328 | bytes 16777216 | tf_op jit(solution)/shard_map/attention_head/pallas_call | solution.py:250
  42.7 1.3 %collective-permute-start.2 = (bf16[4,96,192]{2,1,0:T(8,128)(2,1)S(1)}, bf16[4,96,192]{2,1,0:T(8,128)(2,1)S(1)}, u32[]{:S(2)}, u32[]{:S(2)}) collective-permute-start(bf16[4,96,192]{2,1,0:T(8,128)(2,1)S(1)} %get-tuple-element.33), channel_id=1, source_target_pairs={{0,16},{16,32},{32,48},{48,0},{64,80},{80,96},{96,112},{112,64},{1... | collective-permute-start | bytes 442376 | tf_op jit(solution)/shard_map/ppermute | solution.py:366
  44.0 8.2 %attention_head.3 = (bf16[4,96,128]{2,1,0:T(8,128)(2,1)S(1)}, bf16[4,96,128]{2,1,0:T(8,128)(2,1)S(1)}, bf16[16,4,96,128]{3,2,1,0:T(8,128)(2,1)}, bf16[2,96,192]{...) custom-call(s32[9]{0:T(128)S(1)} %stack.48.refs_0_, ...), custom_call_target="tpu_custom_call" | custom-call | flops 1811939328 | bytes 16777216 | tf_op jit(solution)/shard_map/attention_head/pallas_call | solution.py:250
  52.2 0.9 collective-permute-start.3
  53.0 0.1 fusion.5
  53.2 1.5 %collective-permute-start.5 = (bf16[4,96,192]{2,1,0:T(8,128)(2,1)S(1)}, bf16[4,96,192]{2,1,0:T(8,128)(2,1)S(1)}, u32[]{:S(2)}, u32[]{:S(2)}) collective-permute-start(bf16[4,96,192]{2,1,0:T(8,128)(2,1)S(1)} %slice.98), channel_id=1, source_target_pairs={{0,48},{16,0},{32,16},{48,32},{64,112},{80,64},{96,80},{112,96},{1... | collective-permute-start | bytes 442376 | tf_op jit(solution)/shard_map/ppermute | solution.py:366
  54.7 4.4 %all-to-all-start.1 = ((bf16[16,4,96,128]{3,2,1,0:T(8,128)(2,1)}), bf16[16,4,96,128]{3,2,1,0:T(8,128)(2,1)}, u32[]{:S(2)}, u32[]{:S(2)}) async-start(bf16[16,4,96,128]{3,2,1,0:T(8,128)(2,1)} %get-tuple-element.55), calls=%async_computation.1 | async-start | bytes 3145728 | tf_op jit(solution)/shard_map/all_to_all | solution.py:388
  59.1 0.0 collective-permute-done.3
  59.1 0.2 collective-permute-start.6
  59.2 2.6 %collective-permute-start.8 = (bf16[2,96,192]{2,1,0:T(8,128)(2,1)S(1)}, bf16[2,96,192]{2,1,0:T(8,128)(2,1)S(1)}, u32[]{:S(2)}, u32[]{:S(2)}) collective-permute-start(bf16[2,96,192]{2,1,0:T(8,128)(2,1)S(1)} %get-tuple-element.54), channel_id=1, source_target_pairs={{0,48},{16,0},{32,16},{48,32},{64,112},{80,64},{96,80},{112,96},{1... | collective-permute-start | bytes 221192 | tf_op jit(solution)/shard_map/ppermute | solution.py:366
  61.8 0.1 add_convert_fusion
  61.9 0.1 collective-permute-start.4
  62.0 0.1 fusion.6
  62.1 0.9 %maximum_select_fusion.2 = (bf16[4,96,128]{2,1,0:T(8,128)(2,1)}, bf16[4,96,128]{2,1,0:T(8,128)(2,1)}) fusion(bf16[4,96,64]{2,1,0:T(8,128)(2,1)S(1)} %get-tuple-element.77, bf16[4,96,64]{2,1,0:T(8,128)(2,1)S(1)} %get-tuple-element.75, pred[]{:T(512)S(6)} %eq.31, bf16[4,96,64]{2,1,0:T(8,128)(2,1)S(1)} %get-tuple-element.74, ...), kind=kLoop, calls=%fused_computation.31 | loop fusion | flops 884736 | bytes 393217 | tf_op jit(solution)/shard_map/jit(_where)/select_n | solution.py:327
  63.0 1.5 %collective-permute-done.6 = bf16[2,96,192]{2,1,0:T(8,128)(2,1)S(1)} collective-permute-done((bf16[2,96,192]{2,1,0:T(8,128)(2,1)S(1)}, bf16[2,96,192]{2,1,0:T(8,128)(2,1)S(1)}, u32[]{:S(2)}, u32[]{:S(2)}) %collective-permute-start.6) | collective-permute-done | bytes 73760 | tf_op jit(solution)/shard_map/ppermute | solution.py:366
  64.5 0.1 add_convert_fusion.2
  64.6 2.5 %collective-permute-start.9 = (bf16[4,96,192]{2,1,0:T(8,128)(2,1)S(1)}, bf16[4,96,192]{2,1,0:T(8,128)(2,1)S(1)}, u32[]{:S(2)}, u32[]{:S(2)}) collective-permute-start(bf16[4,96,192]{2,1,0:T(8,128)(2,1)S(1)} %pad_maximum_fusion.2), channel_id=1, source_target_pairs={{0,48},{16,0},{32,16},{48,32},{64,112},{80,64},{96,80},{112,96},{1... | collective-permute-start | bytes 442376 | tf_op jit(solution)/shard_map/ppermute | solution.py:366
  67.2 0.1 collective-permute-start.7
  67.2 1.6 %collective-permute-done.4 = bf16[4,96,192]{2,1,0:T(8,128)(2,1)S(1)} collective-permute-done((bf16[4,96,192]{2,1,0:T(8,128)(2,1)S(1)}, bf16[4,96,192]{2,1,0:T(8,128)(2,1)S(1)}, u32[]{:S(2)}, u32[]{:S(2)}) %collective-permute-start.4) | collective-permute-done | bytes 147488 | tf_op jit(solution)/shard_map/ppermute | solution.py:366
  68.9 0.1 add_bitcast_fusion.1
  68.9 1.1 %collective-permute-done.9 = bf16[4,96,192]{2,1,0:T(8,128)(2,1)S(1)} collective-permute-done((bf16[4,96,192]{2,1,0:T(8,128)(2,1)S(1)}, bf16[4,96,192]{2,1,0:T(8,128)(2,1)S(1)}, u32[]{:S(2)}, u32[]{:S(2)}) %collective-permute-start.9) | collective-permute-done | bytes 147488 | tf_op jit(solution)/shard_map/ppermute | solution.py:366
  70.1 3.3 %collective-permute-done.7 = bf16[4,96,192]{2,1,0:T(8,128)(2,1)S(1)} collective-permute-done((bf16[4,96,192]{2,1,0:T(8,128)(2,1)S(1)}, bf16[4,96,192]{2,1,0:T(8,128)(2,1)S(1)}, u32[]{:S(2)}, u32[]{:S(2)}) %collective-permute-start.7) | collective-permute-done | bytes 147488 | tf_op jit(solution)/shard_map/ppermute | solution.py:366
  73.4 0.1 add_bitcast_fusion
  73.5 3.4 %collective-permute-start.10 = (bf16[2,96,192]{2,1,0:T(8,128)(2,1)S(1)}, bf16[2,96,192]{2,1,0:T(8,128)(2,1)S(1)}, u32[]{:S(2)}, u32[]{:S(2)}) collective-permute-start(bf16[2,96,192]{2,1,0:T(8,128)(2,1)S(1)} %get-tuple-element.71), channel_id=1, source_target_pairs={{0,64},{16,80},{32,96},{48,112},{64,0},{80,16},{96,32},{112,48},{1... | collective-permute-start | bytes 221192 | tf_op jit(solution)/shard_map/ppermute | solution.py:366
  76.9 2.7 %collective-permute-start.11 = (bf16[2,96,192]{2,1,0:T(8,128)(2,1)S(1)}, bf16[2,96,192]{2,1,0:T(8,128)(2,1)S(1)}, u32[]{:S(2)}, u32[]{:S(2)}) collective-permute-start(bf16[2,96,192]{2,1,0:T(8,128)(2,1)S(1)} %get-tuple-element.70), channel_id=1, source_target_pairs={{0,1},{1,0},{2,3},{3,2},{4,5},{5,4},{6,7},{7,6},{8,9},{9,8},{10,11... | collective-permute-start | bytes 221192 | tf_op jit(solution)/shard_map/ppermute | solution.py:334
  79.5 1.2 %all-to-all-done.1 = bf16[16,4,96,128]{3,2,1,0:T(8,128)(2,1)} async-done(((bf16[16,4,96,128]{3,2,1,0:T(8,128)(2,1)}), bf16[16,4,96,128]{3,2,1,0:T(8,128)(2,1)}, u32[]{:S(2)}, u32[]{:S(2)}) %all-to-all-start.1) | async-done | bytes 1572896 | tf_op jit(solution)/shard_map/all_to_all | solution.py:388
  80.8 1.7 %convert_reduce_fusion = f32[2,4,96,128]{3,2,1,0:T(8,128)S(1)} fusion(bf16[8,2,4,96,128]{4,3,2,1,0:T(8,128)(2,1)} %bitcast.21), kind=kLoop, calls=%fused_computation | loop fusion | flops 1474560 | bytes 1966080 | tf_op jit(solution)/shard_map/reduce_sum | solution.py:390
  82.5 0.1 slice_bitcast_fusion.3
  82.6 0.8 fusion.3
  83.4 0.7 pad_maximum_fusion.5
  84.1 1.3 %collective-permute-done.12 = bf16[2,96,192]{2,1,0:T(8,128)(2,1)S(1)} collective-permute-done((bf16[2,96,192]{2,1,0:T(8,128)(2,1)S(1)}, bf16[2,96,192]{2,1,0:T(8,128)(2,1)S(1)}, u32[]{:S(2)}, u32[]{:S(2)}) %collective-permute-start.12) | collective-permute-done | bytes 73760 | tf_op jit(solution)/shard_map/ppermute | solution.py:407
  85.5 0.8 maximum_select_fusion.1
  (30 shorter events, 0.3 us)
Async XLA Ops:
  3.2 7.3 %copy-start.3 = (bf16[4,96,1536]{2,1,0:T(8,128)(2,1)S(1)}, bf16[4,96,1536]{2,1,0:T(8,128)(2,1)}, u32[]{:S(2)}) copy-start(bf16[4,96,1536]{2,1,0:T(8,128)(2,1)} %param.12) | copy-start | bytes 3538948
  3.2 32.5 %all-to-all-start = ((bf16[16,464,128]{2,1,0:T(8,128)(2,1)}), bf16[16,464,128]{2,1,0:T(8,128)(2,1)S(1)}, u32[]{:S(2)}, u32[]{:S(2)}) async-start(bf16[16,464,128]{2,1,0:T(8,128)(2,1)} %prepare_exchange.1), calls=%async_computation | async-start | bytes 3801088 | tf_op jit(solution)/shard_map/all_to_all | solution.py:340
  10.5 1.3 %copy-start.5 = (bf16[4,96,128]{2,1,0:T(8,128)(2,1)S(1)}, bf16[4,96,128]{2,1,0:T(8,128)(2,1)}, u32[]{:S(2)}) copy-start(bf16[4,96,128]{2,1,0:T(8,128)(2,1)} %param.11) | copy-start | bytes 294916
  10.5 1.4 %copy-start.6 = (bf16[4,96,128]{2,1,0:T(8,128)(2,1)S(1)}, bf16[4,96,128]{2,1,0:T(8,128)(2,1)}, u32[]{:S(2)}) copy-start(bf16[4,96,128]{2,1,0:T(8,128)(2,1)} %param.8) | copy-start | bytes 294916
  10.6 2.0 %copy-start.7 = (bf16[128,128]{1,0:T(8,128)(2,1)S(1)}, bf16[128,128]{1,0:T(8,128)(2,1)}, u32[]{:S(2)}) copy-start(bf16[128,128]{1,0:T(8,128)(2,1)} %param.14) | copy-start | bytes 98308
  11.7 2.2 %collective-permute-start.1 = (bf16[2,96,1536]{2,1,0:T(8,128)(2,1)}, bf16[2,96,1536]{2,1,0:T(8,128)(2,1)S(1)}, u32[]{:S(2)}, u32[]{:S(2)}) collective-permute-start(bf16[2,96,1536]{2,1,0:T(8,128)(2,1)} %get-tuple-element.62), channel_id=1, source_target_pairs={{0,1},{1,0},{2,3},{3,2},{4,5},{5,4},{6,7},{7,6},{8,9},{9,8},{10,11... | collective-permute-start | bytes 1769480 | tf_op jit(solution)/shard_map/ppermute | solution.py:334
  12.1 4.5 %collective-permute-start = (bf16[4,96,128]{2,1,0:T(8,128)(2,1)S(1)}, bf16[4,96,128]{2,1,0:T(8,128)(2,1)S(1)}, u32[]{:S(2)}, u32[]{:S(2)}) collective-permute-start(bf16[4,96,128]{2,1,0:T(8,128)(2,1)S(1)} %pad_maximum_fusion.4), channel_id=1, source_target_pairs={{0,1},{1,0},{2,3},{3,2},{4,5},{5,4},{6,7},{7,6},{8,9},{9,8},{10,11... | collective-permute-start | bytes 294920 | tf_op jit(solution)/shard_map/ppermute | solution.py:334
  13.9 0.8 copy-start.4
  35.7 7.0 %copy-start = (bf16[16,464,128]{2,1,0:T(8,128)(2,1)}, bf16[16,464,128]{2,1,0:T(8,128)(2,1)S(1)}, u32[]{:S(2)}) copy-start(bf16[16,464,128]{2,1,0:T(8,128)(2,1)S(1)} %all-to-all-done.refs_3_.refs_4_.refs_5_) | copy-start | bytes 5701636
  42.7 10.5 %copy-start.1 = (bf16[12,96,192]{2,1,0:T(8,128)(2,1)}, bf16[12,96,192]{2,1,0:T(8,128)(2,1)S(1)}, u32[]{:S(2)}) copy-start(bf16[12,96,192]{2,1,0:T(8,128)(2,1)S(1)} %get-tuple-element.50) | copy-start | bytes 1327108
  42.7 9.5 %collective-permute-start.2 = (bf16[4,96,192]{2,1,0:T(8,128)(2,1)S(1)}, bf16[4,96,192]{2,1,0:T(8,128)(2,1)S(1)}, u32[]{:S(2)}, u32[]{:S(2)}) collective-permute-start(bf16[4,96,192]{2,1,0:T(8,128)(2,1)S(1)} %get-tuple-element.33), channel_id=1, source_target_pairs={{0,16},{16,32},{32,48},{48,0},{64,80},{80,96},{96,112},{112,64},{1... | collective-permute-start | bytes 442376 | tf_op jit(solution)/shard_map/ppermute | solution.py:366
  52.2 6.9 %collective-permute-start.3 = (bf16[4,96,128]{2,1,0:T(8,128)(2,1)S(1)}, bf16[4,96,128]{2,1,0:T(8,128)(2,1)S(1)}, u32[]{:S(2)}, u32[]{:S(2)}) collective-permute-start(bf16[4,96,128]{2,1,0:T(8,128)(2,1)S(1)} %get-tuple-element.48), channel_id=1, source_target_pairs={{0,1},{1,0},{2,3},{3,2},{4,5},{5,4},{6,7},{7,6},{8,9},{9,8},{10,11... | collective-permute-start | bytes 294920 | tf_op jit(solution)/shard_map/ppermute | solution.py:334
  53.2 8.6 %copy-start.2 = (bf16[12,96,192]{2,1,0:T(8,128)(2,1)S(1)}, bf16[12,96,192]{2,1,0:T(8,128)(2,1)}, u32[]{:S(2)}) copy-start(bf16[12,96,192]{2,1,0:T(8,128)(2,1)} %copy-done.1) | copy-start | bytes 1327108
  53.2 14.0 %collective-permute-start.5 = (bf16[4,96,192]{2,1,0:T(8,128)(2,1)S(1)}, bf16[4,96,192]{2,1,0:T(8,128)(2,1)S(1)}, u32[]{:S(2)}, u32[]{:S(2)}) collective-permute-start(bf16[4,96,192]{2,1,0:T(8,128)(2,1)S(1)} %slice.98), channel_id=1, source_target_pairs={{0,48},{16,0},{32,16},{48,32},{64,112},{80,64},{96,80},{112,96},{1... | collective-permute-start | bytes 442376 | tf_op jit(solution)/shard_map/ppermute | solution.py:366
  54.7 26.1 %all-to-all-start.1 = ((bf16[16,4,96,128]{3,2,1,0:T(8,128)(2,1)}), bf16[16,4,96,128]{3,2,1,0:T(8,128)(2,1)}, u32[]{:S(2)}, u32[]{:S(2)}) async-start(bf16[16,4,96,128]{3,2,1,0:T(8,128)(2,1)} %get-tuple-element.55), calls=%async_computation.1 | async-start | bytes 3145728 | tf_op jit(solution)/shard_map/all_to_all | solution.py:388
  59.1 5.4 %collective-permute-start.6 = (bf16[2,96,192]{2,1,0:T(8,128)(2,1)S(1)}, bf16[2,96,192]{2,1,0:T(8,128)(2,1)S(1)}, u32[]{:S(2)}, u32[]{:S(2)}) collective-permute-start(bf16[2,96,192]{2,1,0:T(8,128)(2,1)S(1)} %get-tuple-element.53), channel_id=1, source_target_pairs={{0,16},{16,32},{32,48},{48,0},{64,80},{80,96},{96,112},{112,64},{1... | collective-permute-start | bytes 221192 | tf_op jit(solution)/shard_map/ppermute | solution.py:366
  59.2 5.2 %collective-permute-start.8 = (bf16[2,96,192]{2,1,0:T(8,128)(2,1)S(1)}, bf16[2,96,192]{2,1,0:T(8,128)(2,1)S(1)}, u32[]{:S(2)}, u32[]{:S(2)}) collective-permute-start(bf16[2,96,192]{2,1,0:T(8,128)(2,1)S(1)} %get-tuple-element.54), channel_id=1, source_target_pairs={{0,48},{16,0},{32,16},{48,32},{64,112},{80,64},{96,80},{112,96},{1... | collective-permute-start | bytes 221192 | tf_op jit(solution)/shard_map/ppermute | solution.py:366
  61.9 7.0 %collective-permute-start.4 = (bf16[4,96,192]{2,1,0:T(8,128)(2,1)S(1)}, bf16[4,96,192]{2,1,0:T(8,128)(2,1)S(1)}, u32[]{:S(2)}, u32[]{:S(2)}) collective-permute-start(bf16[4,96,192]{2,1,0:T(8,128)(2,1)S(1)} %add_convert_fusion), channel_id=1, source_target_pairs={{0,16},{16,32},{32,48},{48,0},{64,80},{80,96},{96,112},{112,64},{1... | collective-permute-start | bytes 442376 | tf_op jit(solution)/shard_map/ppermute | solution.py:366
  64.6 5.5 %collective-permute-start.9 = (bf16[4,96,192]{2,1,0:T(8,128)(2,1)S(1)}, bf16[4,96,192]{2,1,0:T(8,128)(2,1)S(1)}, u32[]{:S(2)}, u32[]{:S(2)}) collective-permute-start(bf16[4,96,192]{2,1,0:T(8,128)(2,1)S(1)} %pad_maximum_fusion.2), channel_id=1, source_target_pairs={{0,48},{16,0},{32,16},{48,32},{64,112},{80,64},{96,80},{112,96},{1... | collective-permute-start | bytes 442376 | tf_op jit(solution)/shard_map/ppermute | solution.py:366
  67.2 6.2 %collective-permute-start.7 = (bf16[4,96,192]{2,1,0:T(8,128)(2,1)S(1)}, bf16[4,96,192]{2,1,0:T(8,128)(2,1)S(1)}, u32[]{:S(2)}, u32[]{:S(2)}) collective-permute-start(bf16[4,96,192]{2,1,0:T(8,128)(2,1)S(1)} %pad_maximum_fusion.1), channel_id=1, source_target_pairs={{0,16},{16,32},{32,48},{48,0},{64,80},{80,96},{96,112},{112,64},{1... | collective-permute-start | bytes 442376 | tf_op jit(solution)/shard_map/ppermute | solution.py:366
  73.5 10.7 %collective-permute-start.10 = (bf16[2,96,192]{2,1,0:T(8,128)(2,1)S(1)}, bf16[2,96,192]{2,1,0:T(8,128)(2,1)S(1)}, u32[]{:S(2)}, u32[]{:S(2)}) collective-permute-start(bf16[2,96,192]{2,1,0:T(8,128)(2,1)S(1)} %get-tuple-element.71), channel_id=1, source_target_pairs={{0,64},{16,80},{32,96},{48,112},{64,0},{80,16},{96,32},{112,48},{1... | collective-permute-start | bytes 221192 | tf_op jit(solution)/shard_map/ppermute | solution.py:366
  76.9 7.3 %collective-permute-start.11 = (bf16[2,96,192]{2,1,0:T(8,128)(2,1)S(1)}, bf16[2,96,192]{2,1,0:T(8,128)(2,1)S(1)}, u32[]{:S(2)}, u32[]{:S(2)}) collective-permute-start(bf16[2,96,192]{2,1,0:T(8,128)(2,1)S(1)} %get-tuple-element.70), channel_id=1, source_target_pairs={{0,1},{1,0},{2,3},{3,2},{4,5},{5,4},{6,7},{7,6},{8,9},{9,8},{10,11... | collective-permute-start | bytes 221192 | tf_op jit(solution)/shard_map/ppermute | solution.py:334
  79.5 5.9 %collective-permute-start.12 = (bf16[2,96,192]{2,1,0:T(8,128)(2,1)S(1)}, bf16[2,96,192]{2,1,0:T(8,128)(2,1)S(1)}, u32[]{:S(2)}, u32[]{:S(2)}) collective-permute-start(bf16[2,96,192]{2,1,0:T(8,128)(2,1)S(1)} %get-tuple-element.69), channel_id=1, source_target_pairs={{0,65},{1,64},{2,67},{3,66},{4,69},{5,68},{6,71},{7,70},{8,73},{9,... | collective-permute-start | bytes 221192 | tf_op jit(solution)/shard_map/ppermute | solution.py:407

commit v14 on v13

--- a/solution.py
+++ b/solution.py
@@ -39,7 +39,7 @@
             acc_ref[part, :] = jnp.zeros((CHUNK, keys), jnp.float32)
             return carry
 
-        lax.fori_loop(0, queries // CHUNK, fill, 0)
+        lax.fori_loop(0, queries // CHUNK, fill, 0, unroll=UNROLL)
         sources, _, lanes = cotangent_ref.shape
         cotangent = cotangent_ref[...].astype(jnp.float32)
         cotangent = cotangent.reshape(sources, 2, cap_ref.shape[0], lanes // sources, lanes)

time: 86.6 us -> 86.6 us (level)
  transfers between devices with their start and end apart: 15 -> 15, of which waited for: 8 -> 8; matrix products, arithmetic and copies ran while one was open for 10% -> 10% of each run, Pallas kernels for 10% -> 9%
where the time goes in v14:
time: 86.6 us; the launch traced here: 86.2 us
  waiting for transfers between devices  30.3 us (35%)
  starting transfers between devices  27.4 us (32%)
  Pallas kernels  17.7 us (20%)
  other arithmetic  8.65 us (10%)
  local copies, waits for them, and re-layouts  1.33 us (2%)
  between operations  0.88 us (1%)
    all_to_all x1, waiting for transfers between devices, local(): received = lax.all_to_all(packed, 'col', 0, 0, tiled=True)  19.1 us
    pallas_call x2, Pallas kernels, attend(): pl.pallas_call(functools.partial(attention_kernel, head), grid_spec=pltpu...  15.1 us
    ppermute x8, starting transfers between devices, along_row(): return lax.ppermute(array, 'row', pairs)  11.6 us
    ppermute x8, waiting for transfers between devices, along_row(): return lax.ppermute(array, 'row', pairs)  7.56 us
    all_to_all x1, starting transfers between devices, local(): received = lax.all_to_all(packed, 'col', 0, 0, tiled=True)  7.3 us
    all_to_all x1, starting transfers between devices, local(): kv_parts = lax.all_to_all(kv_grads, 'col', 0, 0, tiled=True)  4.42 us
    ppermute x4, starting transfers between devices, swapped(): return lax.ppermute(array, 'col', swap)  4.14 us
    select_n x3, other arithmetic, in_order(): jnp.where(core == 0, jnp.concatenate([mine, other], axis=axis), jnp.conca...  3.55 us
  transfers between devices with their start and end apart: 15, of which 8 were waited for; matrix products, arithmetic and copies ran while one was open for 10% of the time, Pallas kernels for 9%

profile of v14, /device:TPU:1, one launch (start us, length us, event | category | flops | bytes accessed | tf_op | source)
XLA Modules:
  0.0 86.2 jit_solution(4396805072078202618)
XLA Ops:
  0.6 2.6 %prepare_exchange.1 = bf16[16,464,128]{2,1,0:T(8,128)(2,1)} custom-call(bf16[4,96,128]{2,1,0:T(8,128)(2,1)} %key_ref.1, bf16[4,96,128]{2,1,0:T(8,128)(2,1)} %value_ref.1, s32[4,96]{1,0:T(4,128)} %mask_ref.1, bf16[4,8,1536]{2,1,0:T(8,128)(2,1)} %cotangent_ref.1), custom_call_target="tpu_custom_call" | custom-call | tf_op jit(solution)/shard_map/prepare_exchange/pallas_call | solution.py:217
  3.2 7.3 %all-to-all-start = ((bf16[16,464,128]{2,1,0:T(8,128)(2,1)}), bf16[16,464,128]{2,1,0:T(8,128)(2,1)S(1)}, u32[]{:S(2)}, u32[]{:S(2)}) async-start(bf16[16,464,128]{2,1,0:T(8,128)(2,1)} %prepare_exchange.1), calls=%async_computation | async-start | bytes 3801088 | tf_op jit(solution)/shard_map/all_to_all | solution.py:340
  10.5 0.0 copy-start.6
  10.6 0.0 copy-start.7
  10.6 1.1 %broadcast_select_fusion.1 = (bf16[2,96,1536]{2,1,0:T(8,128)(2,1)}, bf16[2,96,1536]{2,1,0:T(8,128)(2,1)}) fusion(pred[]{:T(512)S(6)} %eq.31, bf16[4,96,1536]{2,1,0:T(8,128)(2,1)S(1)} %copy-done.3), kind=kLoop, calls=%fused_computation.7 | loop fusion | flops 589824 | bytes 2359297 | tf_op jit(solution)/shard_map/jit(_where)/select_n | solution.py:324
  11.7 0.1 collective-permute-start.1
  11.8 0.1 broadcast_select_fusion.2
  11.9 0.1 broadcast_select_fusion.3
  12.0 0.1 pad_maximum_fusion.4
  12.1 0.5 collective-permute-start
  12.6 0.1 stack.48.refs_0_
  12.7 0.1 pad_maximum_fusion.3.refs_1_
  12.8 1.1 %collective-permute-done.1 = bf16[2,96,1536]{2,1,0:T(8,128)(2,1)S(1)} collective-permute-done((bf16[2,96,1536]{2,1,0:T(8,128)(2,1)}, bf16[2,96,1536]{2,1,0:T(8,128)(2,1)S(1)}, u32[]{:S(2)}, u32[]{:S(2)}) %collective-permute-start.1) | collective-permute-done | bytes 589856 | tf_op jit(solution)/shard_map/ppermute | solution.py:334
  13.9 0.8 copy-done.4
  14.7 1.9 %maximum_select_fusion = bf16[2,192,1536]{2,1,0:T(8,128)(2,1)S(1)} fusion(bf16[2,96,1536]{2,1,0:T(8,128)(2,1)} %copy-done.4, bf16[2,96,1536]{2,1,0:T(8,128)(2,1)} %get-tuple-element.61, pred[]{:T(512)S(6)} %eq.31), kind=kLoop, calls=%fused_computation.1 | loop fusion | flops 5308416 | bytes 2359297 | tf_op jit(solution)/shard_map/jit(_where)/select_n | solution.py:327
  16.6 0.0 collective-permute-done.refs_2_
  16.6 19.1 %all-to-all-done.refs_3_.refs_4_.refs_5_ = bf16[16,464,128]{2,1,0:T(8,128)(2,1)S(1)} async-done(((bf16[16,464,128]{2,1,0:T(8,128)(2,1)}), bf16[16,464,128]{2,1,0:T(8,128)(2,1)S(1)}, u32[]{:S(2)}, u32[]{:S(2)}) %all-to-all-start) | async-done | bytes 1900576 | tf_op jit(solution)/shard_map/all_to_all | solution.py:340
  35.7 6.9 %attention_head.2 = (bf16[4,96,128]{2,1,0:T(8,128)(2,1)S(1)}, bf16[4,96,128]{2,1,0:T(8,128)(2,1)S(1)}, bf16[4,64,1536]{2,1,0:T(8,128)(2,1)S(1)}, bf16[4,96,192]{...) custom-call(s32[9]{0:T(128)S(1)} %stack.48.refs_0_, ...), custom_call_target="tpu_custom_call" | custom-call | flops 1811939328 | bytes 16777216 | tf_op jit(solution)/shard_map/attention_head/pallas_call | solution.py:250
  42.6 1.3 %collective-permute-start.2 = (bf16[4,96,192]{2,1,0:T(8,128)(2,1)S(1)}, bf16[4,96,192]{2,1,0:T(8,128)(2,1)S(1)}, u32[]{:S(2)}, u32[]{:S(2)}) collective-permute-start(bf16[4,96,192]{2,1,0:T(8,128)(2,1)S(1)} %get-tuple-element.33), channel_id=1, source_target_pairs={{0,16},{16,32},{32,48},{48,0},{64,80},{80,96},{96,112},{112,64},{1... | collective-permute-start | bytes 442376 | tf_op jit(solution)/shard_map/ppermute | solution.py:366
  43.9 8.2 %attention_head.3 = (bf16[4,96,128]{2,1,0:T(8,128)(2,1)S(1)}, bf16[4,96,128]{2,1,0:T(8,128)(2,1)S(1)}, bf16[16,4,96,128]{3,2,1,0:T(8,128)(2,1)}, bf16[2,96,192]{...) custom-call(s32[9]{0:T(128)S(1)} %stack.48.refs_0_, ...), custom_call_target="tpu_custom_call" | custom-call | flops 1811939328 | bytes 16777216 | tf_op jit(solution)/shard_map/attention_head/pallas_call | solution.py:250
  52.1 0.9 %collective-permute-start.3 = (bf16[4,96,128]{2,1,0:T(8,128)(2,1)S(1)}, bf16[4,96,128]{2,1,0:T(8,128)(2,1)S(1)}, u32[]{:S(2)}, u32[]{:S(2)}) collective-permute-start(bf16[4,96,128]{2,1,0:T(8,128)(2,1)S(1)} %get-tuple-element.48), channel_id=1, source_target_pairs={{0,1},{1,0},{2,3},{3,2},{4,5},{5,4},{6,7},{7,6},{8,9},{9,8},{10,11... | collective-permute-start | bytes 294920 | tf_op jit(solution)/shard_map/ppermute | solution.py:334
  53.0 0.1 fusion.5
  53.2 1.4 %collective-permute-start.5 = (bf16[4,96,192]{2,1,0:T(8,128)(2,1)S(1)}, bf16[4,96,192]{2,1,0:T(8,128)(2,1)S(1)}, u32[]{:S(2)}, u32[]{:S(2)}) collective-permute-start(bf16[4,96,192]{2,1,0:T(8,128)(2,1)S(1)} %slice.98), channel_id=1, source_target_pairs={{0,48},{16,0},{32,16},{48,32},{64,112},{80,64},{96,80},{112,96},{1... | collective-permute-start | bytes 442376 | tf_op jit(solution)/shard_map/ppermute | solution.py:366
  54.6 4.4 %all-to-all-start.1 = ((bf16[16,4,96,128]{3,2,1,0:T(8,128)(2,1)}), bf16[16,4,96,128]{3,2,1,0:T(8,128)(2,1)}, u32[]{:S(2)}, u32[]{:S(2)}) async-start(bf16[16,4,96,128]{3,2,1,0:T(8,128)(2,1)} %get-tuple-element.55), calls=%async_computation.1 | async-start | bytes 3145728 | tf_op jit(solution)/shard_map/all_to_all | solution.py:388
  59.0 0.2 collective-permute-start.6
  59.2 2.6 %collective-permute-start.8 = (bf16[2,96,192]{2,1,0:T(8,128)(2,1)S(1)}, bf16[2,96,192]{2,1,0:T(8,128)(2,1)S(1)}, u32[]{:S(2)}, u32[]{:S(2)}) collective-permute-start(bf16[2,96,192]{2,1,0:T(8,128)(2,1)S(1)} %get-tuple-element.54), channel_id=1, source_target_pairs={{0,48},{16,0},{32,16},{48,32},{64,112},{80,64},{96,80},{112,96},{1... | collective-permute-start | bytes 221192 | tf_op jit(solution)/shard_map/ppermute | solution.py:366
  61.8 0.1 add_convert_fusion
  61.8 0.1 collective-permute-start.4
  61.9 0.1 fusion.6
  62.0 0.9 %maximum_select_fusion.2 = (bf16[4,96,128]{2,1,0:T(8,128)(2,1)}, bf16[4,96,128]{2,1,0:T(8,128)(2,1)}) fusion(bf16[4,96,64]{2,1,0:T(8,128)(2,1)S(1)} %get-tuple-element.77, bf16[4,96,64]{2,1,0:T(8,128)(2,1)S(1)} %get-tuple-element.75, pred[]{:T(512)S(6)} %eq.31, bf16[4,96,64]{2,1,0:T(8,128)(2,1)S(1)} %get-tuple-element.74, ...), kind=kLoop, calls=%fused_computation.31 | loop fusion | flops 884736 | bytes 393217 | tf_op jit(solution)/shard_map/jit(_where)/select_n | solution.py:327
  62.9 1.5 %collective-permute-done.6 = bf16[2,96,192]{2,1,0:T(8,128)(2,1)S(1)} collective-permute-done((bf16[2,96,192]{2,1,0:T(8,128)(2,1)S(1)}, bf16[2,96,192]{2,1,0:T(8,128)(2,1)S(1)}, u32[]{:S(2)}, u32[]{:S(2)}) %collective-permute-start.6) | collective-permute-done | bytes 73760 | tf_op jit(solution)/shard_map/ppermute | solution.py:366
  64.4 0.1 add_convert_fusion.2
  64.5 2.5 %collective-permute-start.9 = (bf16[4,96,192]{2,1,0:T(8,128)(2,1)S(1)}, bf16[4,96,192]{2,1,0:T(8,128)(2,1)S(1)}, u32[]{:S(2)}, u32[]{:S(2)}) collective-permute-start(bf16[4,96,192]{2,1,0:T(8,128)(2,1)S(1)} %pad_maximum_fusion.2), channel_id=1, source_target_pairs={{0,48},{16,0},{32,16},{48,32},{64,112},{80,64},{96,80},{112,96},{1... | collective-permute-start | bytes 442376 | tf_op jit(solution)/shard_map/ppermute | solution.py:366
  67.1 0.1 collective-permute-start.7
  67.2 1.6 %collective-permute-done.4 = bf16[4,96,192]{2,1,0:T(8,128)(2,1)S(1)} collective-permute-done((bf16[4,96,192]{2,1,0:T(8,128)(2,1)S(1)}, bf16[4,96,192]{2,1,0:T(8,128)(2,1)S(1)}, u32[]{:S(2)}, u32[]{:S(2)}) %collective-permute-start.4) | collective-permute-done | bytes 147488 | tf_op jit(solution)/shard_map/ppermute | solution.py:366
  68.8 0.1 add_bitcast_fusion.1
  68.9 1.1 %collective-permute-done.9 = bf16[4,96,192]{2,1,0:T(8,128)(2,1)S(1)} collective-permute-done((bf16[4,96,192]{2,1,0:T(8,128)(2,1)S(1)}, bf16[4,96,192]{2,1,0:T(8,128)(2,1)S(1)}, u32[]{:S(2)}, u32[]{:S(2)}) %collective-permute-start.9) | collective-permute-done | bytes 147488 | tf_op jit(solution)/shard_map/ppermute | solution.py:366
  70.0 3.3 %collective-permute-done.7 = bf16[4,96,192]{2,1,0:T(8,128)(2,1)S(1)} collective-permute-done((bf16[4,96,192]{2,1,0:T(8,128)(2,1)S(1)}, bf16[4,96,192]{2,1,0:T(8,128)(2,1)S(1)}, u32[]{:S(2)}, u32[]{:S(2)}) %collective-permute-start.7) | collective-permute-done | bytes 147488 | tf_op jit(solution)/shard_map/ppermute | solution.py:366
  73.3 0.1 add_bitcast_fusion
  73.4 3.4 %collective-permute-start.10 = (bf16[2,96,192]{2,1,0:T(8,128)(2,1)S(1)}, bf16[2,96,192]{2,1,0:T(8,128)(2,1)S(1)}, u32[]{:S(2)}, u32[]{:S(2)}) collective-permute-start(bf16[2,96,192]{2,1,0:T(8,128)(2,1)S(1)} %get-tuple-element.71), channel_id=1, source_target_pairs={{0,64},{16,80},{32,96},{48,112},{64,0},{80,16},{96,32},{112,48},{1... | collective-permute-start | bytes 221192 | tf_op jit(solution)/shard_map/ppermute | solution.py:366
  76.8 2.7 %collective-permute-start.11 = (bf16[2,96,192]{2,1,0:T(8,128)(2,1)S(1)}, bf16[2,96,192]{2,1,0:T(8,128)(2,1)S(1)}, u32[]{:S(2)}, u32[]{:S(2)}) collective-permute-start(bf16[2,96,192]{2,1,0:T(8,128)(2,1)S(1)} %get-tuple-element.70), channel_id=1, source_target_pairs={{0,1},{1,0},{2,3},{3,2},{4,5},{5,4},{6,7},{7,6},{8,9},{9,8},{10,11... | collective-permute-start | bytes 221192 | tf_op jit(solution)/shard_map/ppermute | solution.py:334
  79.5 1.2 %all-to-all-done.1 = bf16[16,4,96,128]{3,2,1,0:T(8,128)(2,1)} async-done(((bf16[16,4,96,128]{3,2,1,0:T(8,128)(2,1)}), bf16[16,4,96,128]{3,2,1,0:T(8,128)(2,1)}, u32[]{:S(2)}, u32[]{:S(2)}) %all-to-all-start.1) | async-done | bytes 1572896 | tf_op jit(solution)/shard_map/all_to_all | solution.py:388
  80.7 1.7 %convert_reduce_fusion = f32[2,4,96,128]{3,2,1,0:T(8,128)S(1)} fusion(bf16[8,2,4,96,128]{4,3,2,1,0:T(8,128)(2,1)} %bitcast.21), kind=kLoop, calls=%fused_computation | loop fusion | flops 1474560 | bytes 1966080 | tf_op jit(solution)/shard_map/reduce_sum | solution.py:390
  82.4 0.1 slice_bitcast_fusion.3
  82.6 0.8 fusion.3
  83.3 0.7 pad_maximum_fusion.5
  84.1 1.3 %collective-permute-done.12 = bf16[2,96,192]{2,1,0:T(8,128)(2,1)S(1)} collective-permute-done((bf16[2,96,192]{2,1,0:T(8,128)(2,1)S(1)}, bf16[2,96,192]{2,1,0:T(8,128)(2,1)S(1)}, u32[]{:S(2)}, u32[]{:S(2)}) %collective-permute-start.12) | collective-permute-done | bytes 73760 | tf_op jit(solution)/shard_map/ppermute | solution.py:407
  85.4 0.8 maximum_select_fusion.1
  (30 shorter events, 0.3 us)
Async XLA Ops:
  3.2 7.3 %copy-start.3 = (bf16[4,96,1536]{2,1,0:T(8,128)(2,1)S(1)}, bf16[4,96,1536]{2,1,0:T(8,128)(2,1)}, u32[]{:S(2)}) copy-start(bf16[4,96,1536]{2,1,0:T(8,128)(2,1)} %param.12) | copy-start | bytes 3538948
  3.2 32.5 %all-to-all-start = ((bf16[16,464,128]{2,1,0:T(8,128)(2,1)}), bf16[16,464,128]{2,1,0:T(8,128)(2,1)S(1)}, u32[]{:S(2)}, u32[]{:S(2)}) async-start(bf16[16,464,128]{2,1,0:T(8,128)(2,1)} %prepare_exchange.1), calls=%async_computation | async-start | bytes 3801088 | tf_op jit(solution)/shard_map/all_to_all | solution.py:340
  10.5 1.3 %copy-start.5 = (bf16[4,96,128]{2,1,0:T(8,128)(2,1)S(1)}, bf16[4,96,128]{2,1,0:T(8,128)(2,1)}, u32[]{:S(2)}) copy-start(bf16[4,96,128]{2,1,0:T(8,128)(2,1)} %param.11) | copy-start | bytes 294916
  10.5 1.4 %copy-start.6 = (bf16[4,96,128]{2,1,0:T(8,128)(2,1)S(1)}, bf16[4,96,128]{2,1,0:T(8,128)(2,1)}, u32[]{:S(2)}) copy-start(bf16[4,96,128]{2,1,0:T(8,128)(2,1)} %param.8) | copy-start | bytes 294916
  10.6 2.0 %copy-start.7 = (bf16[128,128]{1,0:T(8,128)(2,1)S(1)}, bf16[128,128]{1,0:T(8,128)(2,1)}, u32[]{:S(2)}) copy-start(bf16[128,128]{1,0:T(8,128)(2,1)} %param.14) | copy-start | bytes 98308
  11.7 2.2 %collective-permute-start.1 = (bf16[2,96,1536]{2,1,0:T(8,128)(2,1)}, bf16[2,96,1536]{2,1,0:T(8,128)(2,1)S(1)}, u32[]{:S(2)}, u32[]{:S(2)}) collective-permute-start(bf16[2,96,1536]{2,1,0:T(8,128)(2,1)} %get-tuple-element.62), channel_id=1, source_target_pairs={{0,1},{1,0},{2,3},{3,2},{4,5},{5,4},{6,7},{7,6},{8,9},{9,8},{10,11... | collective-permute-start | bytes 1769480 | tf_op jit(solution)/shard_map/ppermute | solution.py:334
  12.1 4.5 %collective-permute-start = (bf16[4,96,128]{2,1,0:T(8,128)(2,1)S(1)}, bf16[4,96,128]{2,1,0:T(8,128)(2,1)S(1)}, u32[]{:S(2)}, u32[]{:S(2)}) collective-permute-start(bf16[4,96,128]{2,1,0:T(8,128)(2,1)S(1)} %pad_maximum_fusion.4), channel_id=1, source_target_pairs={{0,1},{1,0},{2,3},{3,2},{4,5},{5,4},{6,7},{7,6},{8,9},{9,8},{10,11... | collective-permute-start | bytes 294920 | tf_op jit(solution)/shard_map/ppermute | solution.py:334
  13.9 0.8 copy-start.4
  35.7 6.9 %copy-start = (bf16[16,464,128]{2,1,0:T(8,128)(2,1)}, bf16[16,464,128]{2,1,0:T(8,128)(2,1)S(1)}, u32[]{:S(2)}) copy-start(bf16[16,464,128]{2,1,0:T(8,128)(2,1)S(1)} %all-to-all-done.refs_3_.refs_4_.refs_5_) | copy-start | bytes 5701636
  42.6 10.5 %copy-start.1 = (bf16[12,96,192]{2,1,0:T(8,128)(2,1)}, bf16[12,96,192]{2,1,0:T(8,128)(2,1)S(1)}, u32[]{:S(2)}) copy-start(bf16[12,96,192]{2,1,0:T(8,128)(2,1)S(1)} %get-tuple-element.50) | copy-start | bytes 1327108
  42.6 9.5 %collective-permute-start.2 = (bf16[4,96,192]{2,1,0:T(8,128)(2,1)S(1)}, bf16[4,96,192]{2,1,0:T(8,128)(2,1)S(1)}, u32[]{:S(2)}, u32[]{:S(2)}) collective-permute-start(bf16[4,96,192]{2,1,0:T(8,128)(2,1)S(1)} %get-tuple-element.33), channel_id=1, source_target_pairs={{0,16},{16,32},{32,48},{48,0},{64,80},{80,96},{96,112},{112,64},{1... | collective-permute-start | bytes 442376 | tf_op jit(solution)/shard_map/ppermute | solution.py:366
  52.1 6.9 %collective-permute-start.3 = (bf16[4,96,128]{2,1,0:T(8,128)(2,1)S(1)}, bf16[4,96,128]{2,1,0:T(8,128)(2,1)S(1)}, u32[]{:S(2)}, u32[]{:S(2)}) collective-permute-start(bf16[4,96,128]{2,1,0:T(8,128)(2,1)S(1)} %get-tuple-element.48), channel_id=1, source_target_pairs={{0,1},{1,0},{2,3},{3,2},{4,5},{5,4},{6,7},{7,6},{8,9},{9,8},{10,11... | collective-permute-start | bytes 294920 | tf_op jit(solution)/shard_map/ppermute | solution.py:334
  53.1 8.6 %copy-start.2 = (bf16[12,96,192]{2,1,0:T(8,128)(2,1)S(1)}, bf16[12,96,192]{2,1,0:T(8,128)(2,1)}, u32[]{:S(2)}) copy-start(bf16[12,96,192]{2,1,0:T(8,128)(2,1)} %copy-done.1) | copy-start | bytes 1327108
  53.2 14.0 %collective-permute-start.5 = (bf16[4,96,192]{2,1,0:T(8,128)(2,1)S(1)}, bf16[4,96,192]{2,1,0:T(8,128)(2,1)S(1)}, u32[]{:S(2)}, u32[]{:S(2)}) collective-permute-start(bf16[4,96,192]{2,1,0:T(8,128)(2,1)S(1)} %slice.98), channel_id=1, source_target_pairs={{0,48},{16,0},{32,16},{48,32},{64,112},{80,64},{96,80},{112,96},{1... | collective-permute-start | bytes 442376 | tf_op jit(solution)/shard_map/ppermute | solution.py:366
  54.6 26.1 %all-to-all-start.1 = ((bf16[16,4,96,128]{3,2,1,0:T(8,128)(2,1)}), bf16[16,4,96,128]{3,2,1,0:T(8,128)(2,1)}, u32[]{:S(2)}, u32[]{:S(2)}) async-start(bf16[16,4,96,128]{3,2,1,0:T(8,128)(2,1)} %get-tuple-element.55), calls=%async_computation.1 | async-start | bytes 3145728 | tf_op jit(solution)/shard_map/all_to_all | solution.py:388
  59.0 5.4 %collective-permute-start.6 = (bf16[2,96,192]{2,1,0:T(8,128)(2,1)S(1)}, bf16[2,96,192]{2,1,0:T(8,128)(2,1)S(1)}, u32[]{:S(2)}, u32[]{:S(2)}) collective-permute-start(bf16[2,96,192]{2,1,0:T(8,128)(2,1)S(1)} %get-tuple-element.53), channel_id=1, source_target_pairs={{0,16},{16,32},{32,48},{48,0},{64,80},{80,96},{96,112},{112,64},{1... | collective-permute-start | bytes 221192 | tf_op jit(solution)/shard_map/ppermute | solution.py:366
  59.2 5.2 %collective-permute-start.8 = (bf16[2,96,192]{2,1,0:T(8,128)(2,1)S(1)}, bf16[2,96,192]{2,1,0:T(8,128)(2,1)S(1)}, u32[]{:S(2)}, u32[]{:S(2)}) collective-permute-start(bf16[2,96,192]{2,1,0:T(8,128)(2,1)S(1)} %get-tuple-element.54), channel_id=1, source_target_pairs={{0,48},{16,0},{32,16},{48,32},{64,112},{80,64},{96,80},{112,96},{1... | collective-permute-start | bytes 221192 | tf_op jit(solution)/shard_map/ppermute | solution.py:366
  61.8 7.0 %collective-permute-start.4 = (bf16[4,96,192]{2,1,0:T(8,128)(2,1)S(1)}, bf16[4,96,192]{2,1,0:T(8,128)(2,1)S(1)}, u32[]{:S(2)}, u32[]{:S(2)}) collective-permute-start(bf16[4,96,192]{2,1,0:T(8,128)(2,1)S(1)} %add_convert_fusion), channel_id=1, source_target_pairs={{0,16},{16,32},{32,48},{48,0},{64,80},{80,96},{96,112},{112,64},{1... | collective-permute-start | bytes 442376 | tf_op jit(solution)/shard_map/ppermute | solution.py:366
  64.5 5.5 %collective-permute-start.9 = (bf16[4,96,192]{2,1,0:T(8,128)(2,1)S(1)}, bf16[4,96,192]{2,1,0:T(8,128)(2,1)S(1)}, u32[]{:S(2)}, u32[]{:S(2)}) collective-permute-start(bf16[4,96,192]{2,1,0:T(8,128)(2,1)S(1)} %pad_maximum_fusion.2), channel_id=1, source_target_pairs={{0,48},{16,0},{32,16},{48,32},{64,112},{80,64},{96,80},{112,96},{1... | collective-permute-start | bytes 442376 | tf_op jit(solution)/shard_map/ppermute | solution.py:366
  67.1 6.2 %collective-permute-start.7 = (bf16[4,96,192]{2,1,0:T(8,128)(2,1)S(1)}, bf16[4,96,192]{2,1,0:T(8,128)(2,1)S(1)}, u32[]{:S(2)}, u32[]{:S(2)}) collective-permute-start(bf16[4,96,192]{2,1,0:T(8,128)(2,1)S(1)} %pad_maximum_fusion.1), channel_id=1, source_target_pairs={{0,16},{16,32},{32,48},{48,0},{64,80},{80,96},{96,112},{112,64},{1... | collective-permute-start | bytes 442376 | tf_op jit(solution)/shard_map/ppermute | solution.py:366
  73.4 10.7 %collective-permute-start.10 = (bf16[2,96,192]{2,1,0:T(8,128)(2,1)S(1)}, bf16[2,96,192]{2,1,0:T(8,128)(2,1)S(1)}, u32[]{:S(2)}, u32[]{:S(2)}) collective-permute-start(bf16[2,96,192]{2,1,0:T(8,128)(2,1)S(1)} %get-tuple-element.71), channel_id=1, source_target_pairs={{0,64},{16,80},{32,96},{48,112},{64,0},{80,16},{96,32},{112,48},{1... | collective-permute-start | bytes 221192 | tf_op jit(solution)/shard_map/ppermute | solution.py:366
  76.8 7.3 %collective-permute-start.11 = (bf16[2,96,192]{2,1,0:T(8,128)(2,1)S(1)}, bf16[2,96,192]{2,1,0:T(8,128)(2,1)S(1)}, u32[]{:S(2)}, u32[]{:S(2)}) collective-permute-start(bf16[2,96,192]{2,1,0:T(8,128)(2,1)S(1)} %get-tuple-element.70), channel_id=1, source_target_pairs={{0,1},{1,0},{2,3},{3,2},{4,5},{5,4},{6,7},{7,6},{8,9},{9,8},{10,11... | collective-permute-start | bytes 221192 | tf_op jit(solution)/shard_map/ppermute | solution.py:334
  79.5 5.9 %collective-permute-start.12 = (bf16[2,96,192]{2,1,0:T(8,128)(2,1)S(1)}, bf16[2,96,192]{2,1,0:T(8,128)(2,1)S(1)}, u32[]{:S(2)}, u32[]{:S(2)}) collective-permute-start(bf16[2,96,192]{2,1,0:T(8,128)(2,1)S(1)} %get-tuple-element.69), channel_id=1, source_target_pairs={{0,65},{1,64},{2,67},{3,66},{4,69},{5,68},{6,71},{7,70},{8,73},{9,... | collective-permute-start | bytes 221192 | tf_op jit(solution)/shard_map/ppermute | solution.py:407
